TPU v7x, 32 devices: a whole 2x2x4 slice. The times are simulated.
32 devices in a mesh: wide: 8 (over z, y), narrow: 4 (over x, core).
Axes of the slice: x: 2, y: 2, z: 4, core: 2. Of those that a mesh axis runs over, the one named last changes fastest.
Arguments:
- tokens: bfloat16 [96, 256, 512], P('wide'), may hold values from -6 to 6
- cotangent: bfloat16 [96, 256, 512], P('wide'), may hold values from -6 to 6
- counts: int32 [8], replicated, may hold values from 1 to 12, 64 in all
- group_order: int32 [64], replicated, may hold values from 0 to 63, each once
- query_weight: bfloat16 [512, 512], P(None, 'narrow'), may hold values from -0.25 to 0.25
- key_weight: bfloat16 [512, 512], P(None, 'narrow'), may hold values from -0.25 to 0.25
- value_weight: bfloat16 [512, 512], P(None, 'narrow'), may hold values from -0.25 to 0.25
- output_weight: bfloat16 [512, 512], P('narrow'), may hold values from -1 to 1
- gain_attn: float32 [512], replicated, may hold values from 0.5 to 1.5
- gain_mix: float32 [512], replicated, may hold values from 0.5 to 1.5
- controller: bfloat16 [512, 32], P(None, 'narrow'), may hold values from -0.375 to 0.375
- w_in: bfloat16 [32, 512, 2048], P('narrow'), may hold values from -0.25 to 0.25
- b_in: float32 [32, 2048], P('narrow'), may hold values from -0.625 to 0.625
- w_out: bfloat16 [32, 2048, 512], P('narrow'), may hold values from -5 to 5
- b_out: float32 [32, 512], P('narrow'), may hold values from -3 to 3
Outputs:
- mixed_out: bfloat16 [96, 256, 512], P('wide')
- d_tokens: bfloat16 [96, 256, 512], P('wide')
- query_weight_gradient: float32 [512, 512], P(None, 'narrow')
- key_weight_gradient: float32 [512, 512], P(None, 'narrow')
- value_weight_gradient: float32 [512, 512], P(None, 'narrow')
- output_weight_gradient: float32 [512, 512], P('narrow')
- g_gain_attn: float32 [512], replicated
- g_gain_mix: float32 [512], replicated
- g_controller: float32 [512, 32], P(None, 'narrow')
- g_w_in: float32 [32, 512, 2048], P('narrow', 'wide')
- g_b_in: float32 [32, 2048], P('narrow')
- g_w_out: float32 [32, 2048, 512], P('narrow', 'wide')
- g_b_out: float32 [32, 512], P('narrow')
Inputs may be any that keep to these rules, and one draw needn't show every extreme that they name: Index i of wide holds counts[i] sequences, in its first slots; the counts sum to 64 and the largest is 12. `group_order`: each sequence once.
All inputs are finite; a program needn't handle non-finite values.
Results may differ from a plain program's by a relative error of at most 0.04.
Values may be sent and summed in bfloat16 or wider, within the bound.
No kernel may reach another device: no remote copies, remote signals or barrier semaphores. Data moves between devices by JAX's collectives and lax.ppermute only.
A program may use at most 256 MiB of HBM per device.

v0:
```python
import jax
import jax.numpy as jnp
from jax import lax
from jax.sharding import PartitionSpec as P

HEAD_WIDTH = 64
GROUP = 32
GROUPS = 2


EPSILON = 1e-05
NEGATIVE = -1e30


def body(
    tokens,
    cotangent,
    counts,
    group_order,
    query_weight,
    key_weight,
    value_weight,
    output_weight,
    gain_attn,
    gain_mix,
    controller,
    w_in,
    b_in,
    w_out,
    b_out,
):
    slot_count, seq_len, model_width = tokens.shape
    wide_count = lax.axis_size("wide")
    wide_index = lax.axis_index("wide")
    head_count = query_weight.shape[1] // HEAD_WIDTH
    score_scale = float(HEAD_WIDTH) ** (-0.5)
    seq_ends = jnp.cumsum(counts)
    seq_starts = seq_ends - counts
    device_ids = jnp.arange(wide_count, dtype=jnp.int32)
    owner_dev = jnp.sum((seq_ends[None, :] <= group_order[:, None]).astype(jnp.int32), axis=1)
    first_seq = jnp.sum(
        jnp.where(owner_dev[:, None] == device_ids[None, :], seq_starts[None, :], 0), axis=1
    )
    members = owner_dev * slot_count + group_order - first_seq
    own_count = jnp.sum(jnp.where(device_ids == wide_index, counts, 0))
    live_rows = (jnp.arange(slot_count) < own_count).astype(jnp.float32)[:, None, None]
    complete_tokens = tokens.astype(jnp.float32)
    inverse_one = lax.rsqrt(
        jnp.mean(complete_tokens * complete_tokens, axis=-1, keepdims=True) + EPSILON
    )
    normed_one = complete_tokens * inverse_one
    attention_input = (normed_one * gain_attn).astype(jnp.bfloat16)

    def project(weight_matrix):
        built_result = jnp.einsum(
            "pza,aq->pzq", attention_input, weight_matrix, preferred_element_type=jnp.float32
        )
        return built_result.astype(jnp.bfloat16).reshape(
            slot_count, seq_len, head_count, HEAD_WIDTH
        )

    def flatten_heads(head_rows):
        return head_rows.reshape(slot_count, seq_len, head_count * HEAD_WIDTH)

    query_rows = project(query_weight)
    keys_low = project(key_weight)
    values_low = project(value_weight)
    causal = jnp.arange(seq_len)[:, None] >= jnp.arange(seq_len)[None, :]
    scores = (
        jnp.einsum("bqhc,bkhc->bhqk", query_rows, keys_low, preferred_element_type=jnp.float32)
        * score_scale
    )
    scores = jnp.where(causal, scores, NEGATIVE)
    weights_attn = jax.nn.softmax(scores, axis=-1)
    weights_low = weights_attn.astype(jnp.bfloat16)
    context_rows = jnp.einsum(
        "bhqk,bkhc->bqhc", weights_low, values_low, preferred_element_type=jnp.float32
    )
    context_rows = flatten_heads(context_rows.astype(jnp.bfloat16))
    attention_terms = jnp.einsum(
        "pza,aq->pzq", context_rows, output_weight, preferred_element_type=jnp.float32
    )
    attention = lax.psum(attention_terms.astype(jnp.bfloat16), "narrow").astype(jnp.float32)
    block_len = seq_len // wide_count
    hidden_state = complete_tokens + attention
    inverse_two = lax.rsqrt(jnp.mean(hidden_state * hidden_state, axis=-1, keepdims=True) + EPSILON)
    normed_two = hidden_state * inverse_two
    mix_in = (normed_two * gain_mix).astype(jnp.bfloat16)
    mix_rows, cot_rows = (
        lax.all_to_all(mix_in, "wide", split_axis=1, concat_axis=0, tiled=True),
        lax.all_to_all(cotangent, "wide", split_axis=1, concat_axis=0, tiled=True),
    )
    mix_len = mix_rows.shape[1]
    group_shape = (GROUPS, GROUP, mix_len, model_width)
    grouped = jnp.take(mix_rows, members, axis=0).reshape(group_shape)
    logits = jnp.einsum("grpd,de->grpe", grouped, controller, preferred_element_type=jnp.float32)
    mix_weights = jax.nn.softmax(logits, axis=1)
    mix_low = mix_weights.astype(jnp.bfloat16)
    mixed_rows = jnp.einsum(
        "grpe,grpd->gped", mix_low, grouped, preferred_element_type=jnp.float32
    ).astype(jnp.bfloat16)
    pre_act = (
        jnp.einsum("gped,edf->gpef", mixed_rows, w_in, preferred_element_type=jnp.float32) + b_in
    )
    activation, gelu_back = jax.vjp(jax.nn.gelu, pre_act)
    activation_low = activation.astype(jnp.bfloat16)
    expert_out = (
        jnp.einsum("gpef,efd->gped", activation_low, w_out, preferred_element_type=jnp.float32)
        + b_out
    ).astype(jnp.bfloat16)
    combined = jnp.einsum(
        "grpe,gped->grpd", mix_low, expert_out, preferred_element_type=jnp.float32
    )
    combined = lax.psum(combined.astype(jnp.bfloat16), "narrow").astype(jnp.float32)
    placed = jnp.zeros((wide_count * slot_count, block_len, model_width), jnp.bfloat16)
    placed = placed.at[members].set(
        combined.astype(jnp.bfloat16).reshape(-1, block_len, model_width)
    )
    mix_back = lax.all_to_all(placed, "wide", split_axis=0, concat_axis=1, tiled=True).astype(
        jnp.float32
    )
    mixed_part = (live_rows * (hidden_state + mix_back)).astype(jnp.bfloat16)
    cot_group = jnp.take(cot_rows, members, axis=0).reshape(group_shape)
    d_mixw = jnp.einsum(
        "grpd,gped->grpe", cot_group, expert_out, preferred_element_type=jnp.float32
    )
    d_expert = jnp.einsum(
        "grpe,grpd->gped", mix_low, cot_group, preferred_element_type=jnp.float32
    ).astype(jnp.bfloat16)
    g_w_out = jnp.einsum(
        "gpef,gped->efd", activation_low, d_expert, preferred_element_type=jnp.float32
    )
    g_b_out = jnp.sum(d_expert.astype(jnp.float32), axis=(0, 1))
    d_activation = jnp.einsum("gped,efd->gpef", d_expert, w_out, preferred_element_type=jnp.float32)
    d_pre = gelu_back(d_activation)[0].astype(jnp.bfloat16)
    g_w_in = jnp.einsum("gped,gpef->edf", mixed_rows, d_pre, preferred_element_type=jnp.float32)
    g_b_in = jnp.sum(d_pre.astype(jnp.float32), axis=(0, 1))
    d_mixed = jnp.einsum("gpef,edf->gped", d_pre, w_in, preferred_element_type=jnp.float32).astype(
        jnp.bfloat16
    )
    d_mixw = d_mixw + jnp.einsum(
        "gped,grpd->grpe", d_mixed, grouped, preferred_element_type=jnp.float32
    )
    d_mixw = d_mixw.astype(jnp.bfloat16).astype(jnp.float32)
    d_logits = (
        mix_weights * (d_mixw - jnp.sum(mix_weights * d_mixw, axis=1, keepdims=True))
    ).astype(jnp.bfloat16)
    g_controller = jnp.einsum(
        "grpd,grpe->de", grouped, d_logits, preferred_element_type=jnp.float32
    )
    d_grouped = jnp.einsum("grpe,gped->grpd", mix_low, d_mixed, preferred_element_type=jnp.float32)
    d_grouped = d_grouped + jnp.einsum(
        "grpe,de->grpd", d_logits, controller, preferred_element_type=jnp.float32
    )
    d_grouped = lax.psum(d_grouped.astype(jnp.bfloat16), "narrow").astype(jnp.float32)
    grad_placed = jnp.zeros((wide_count * slot_count, block_len, model_width), jnp.bfloat16)
    grad_placed = grad_placed.at[members].set(
        d_grouped.astype(jnp.bfloat16).reshape(-1, block_len, model_width)
    )
    grad_mix = lax.all_to_all(grad_placed, "wide", split_axis=0, concat_axis=1, tiled=True).astype(
        jnp.float32
    )
    g_gain_mix = jnp.sum(grad_mix * normed_two, axis=(0, 1))
    d_normed_two = grad_mix * gain_mix
    d_hidden = cotangent.astype(jnp.float32) * live_rows + inverse_two * (
        d_normed_two - normed_two * jnp.mean(d_normed_two * normed_two, axis=-1, keepdims=True)
    )
    attention_gradient = d_hidden.astype(jnp.bfloat16)
    output_weight_gradient = jnp.einsum(
        "uca,uch->ah", context_rows, attention_gradient, preferred_element_type=jnp.float32
    )
    context_gradient = jnp.einsum(
        "gmt,ot->gmo", attention_gradient, output_weight, preferred_element_type=jnp.float32
    )
    context_gradient = context_gradient.astype(jnp.bfloat16).reshape(
        slot_count, seq_len, head_count, HEAD_WIDTH
    )
    d_weights = jnp.einsum(
        "bqhc,bkhc->bhqk", context_gradient, values_low, preferred_element_type=jnp.float32
    )
    d_weights = d_weights.astype(jnp.bfloat16).astype(jnp.float32)
    value_gradient = jnp.einsum(
        "bhqk,bqhc->bkhc", weights_low, context_gradient, preferred_element_type=jnp.float32
    ).astype(jnp.bfloat16)
    d_scores = (
        weights_attn * (d_weights - jnp.sum(weights_attn * d_weights, axis=-1, keepdims=True))
    ).astype(jnp.bfloat16)
    query_gradient = (
        jnp.einsum("bhqk,bkhc->bqhc", d_scores, keys_low, preferred_element_type=jnp.float32)
        * score_scale
    ).astype(jnp.bfloat16)
    key_gradient = (
        jnp.einsum("bhqk,bqhc->bkhc", d_scores, query_rows, preferred_element_type=jnp.float32)
        * score_scale
    ).astype(jnp.bfloat16)
    query_gradient = flatten_heads(query_gradient)
    key_gradient = flatten_heads(key_gradient)
    value_gradient = flatten_heads(value_gradient)
    query_weight_gradient = jnp.einsum(
        "uca,uch->ah", attention_input, query_gradient, preferred_element_type=jnp.float32
    )
    key_weight_gradient = jnp.einsum(
        "uca,uch->ah", attention_input, key_gradient, preferred_element_type=jnp.float32
    )
    value_weight_gradient = jnp.einsum(
        "uca,uch->ah", attention_input, value_gradient, preferred_element_type=jnp.float32
    )
    attention_input_gradient = jnp.einsum(
        "gmt,ot->gmo", query_gradient, query_weight, preferred_element_type=jnp.float32
    )
    attention_input_gradient = attention_input_gradient + jnp.einsum(
        "gmt,ot->gmo", key_gradient, key_weight, preferred_element_type=jnp.float32
    )
    attention_input_gradient = attention_input_gradient + jnp.einsum(
        "gmt,ot->gmo", value_gradient, value_weight, preferred_element_type=jnp.float32
    )
    attention_input_gradient = lax.psum(
        attention_input_gradient.astype(jnp.bfloat16), "narrow"
    ).astype(jnp.float32)
    attention_input_gradient = attention_input_gradient.astype(jnp.bfloat16).astype(jnp.float32)
    g_gain_attn = jnp.sum(attention_input_gradient * normed_one, axis=(0, 1))
    d_normed_one = attention_input_gradient * gain_attn
    d_tokens = d_hidden + inverse_one * (
        d_normed_one - normed_one * jnp.mean(d_normed_one * normed_one, axis=-1, keepdims=True)
    )
    d_tokens = (d_tokens * live_rows).astype(jnp.bfloat16)
    wide_sums = (
        lax.psum(query_weight_gradient.astype(jnp.bfloat16), "wide").astype(jnp.float32),
        lax.psum(key_weight_gradient.astype(jnp.bfloat16), "wide").astype(jnp.float32),
        lax.psum(value_weight_gradient.astype(jnp.bfloat16), "wide").astype(jnp.float32),
        lax.psum(output_weight_gradient.astype(jnp.bfloat16), "wide").astype(jnp.float32),
        lax.psum(g_controller.astype(jnp.bfloat16), "wide").astype(jnp.float32),
        lax.psum(g_gain_attn.astype(jnp.bfloat16), "wide").astype(jnp.float32),
        lax.psum(g_gain_mix.astype(jnp.bfloat16), "wide").astype(jnp.float32),
        lax.psum(g_b_in.astype(jnp.bfloat16), "wide").astype(jnp.float32),
        lax.psum(g_b_out.astype(jnp.bfloat16), "wide").astype(jnp.float32),
    )
    g_w_in, g_w_out = (
        lax.psum_scatter(
            g_w_in.astype(jnp.bfloat16), "wide", scatter_dimension=1, tiled=True
        ).astype(jnp.float32),
        lax.psum_scatter(
            g_w_out.astype(jnp.bfloat16), "wide", scatter_dimension=1, tiled=True
        ).astype(jnp.float32),
    )
    return (
        mixed_part,
        d_tokens,
        wide_sums[0],
        wide_sums[1],
        wide_sums[2],
        wide_sums[3],
        wide_sums[5],
        wide_sums[6],
        wide_sums[4],
        g_w_in,
        wide_sums[7],
        g_w_out,
        wide_sums[8],
    )


def solution(mesh):
    placed = (
        P("wide", None, None),
        P("wide", None, None),
        P(),
        P(),
        P(None, "narrow"),
        P(None, "narrow"),
        P(None, "narrow"),
        P("narrow", None),
        P(),
        P(),
        P(None, "narrow"),
        P("narrow", None, None),
        P("narrow", None),
        P("narrow", None, None),
        P("narrow", None),
    )
    return jax.shard_map(
        body,
        mesh=mesh,
        in_specs=placed,
        out_specs=(
            P("wide", None, None),
            P("wide", None, None),
            P(None, "narrow"),
            P(None, "narrow"),
            P(None, "narrow"),
            P("narrow", None),
            P(),
            P(),
            P(None, "narrow"),
            P("narrow", "wide", None),
            P("narrow", None),
            P("narrow", "wide", None),
            P("narrow", None),
        ),
        check_vma=False,
    )
```

profile of v0, /device:TPU:0, one launch (start us, length us, event | category | flops | bytes accessed | tf_op | source)
XLA Modules:
  0.0 1274.4 jit_solution(12969634011759792426)
XLA Ops:
  7.2 5.8 copy.252
  13.0 7.5 all-to-all-start.2
  29.3 6.2 fusion.146
  35.5 3.7 fusion.63
  40.1 2.7 convolution_convert_fusion
  42.8 70.0 %all-reduce.8.cloned.1.call-done = bf16[12,256,512]{2,1,0:T(8,128)(2,1)} async-done(((bf16[12,256,512]{2,1,0:T(8,128)(2,1)}), bf16[12,256,512]{2,1,0:T(8,128)(2,1)}) %all-reduce.8.cloned.1.call-update) | async-done | bytes 3145744 | tf_op jit(solution)/shard_map/psum | solution.py:83
  112.8 3.1 multiply_reduce_fusion.1
  117.2 3.9 copy.242
  121.2 5.6 all-to-all-start
  128.6 5.7 copy.254
  134.3 3.9 gather_fusion.1
  138.2 81.8 %all-to-all-done = bf16[12,256,512]{2,0,1:T(8,128)(2,1)} async-done(((bf16[12,256,512]{2,0,1:T(8,128)(2,1)}), bf16[12,256,512]{2,0,1:T(8,128)(2,1)}, u32[]{:S(2)}, u32[]{:S(2)}) %all-to-all-start) | async-done | bytes 3145760 | tf_op jit(solution)/shard_map/all_to_all | solution.py:90
  220.0 5.7 copy.244
  225.7 3.9 gather_fusion
  229.6 4.0 broadcast_select_fusion
  240.0 2.9 fusion.75
  242.9 3.7 fusion.149
  246.6 9.1 fusion.3
  255.8 12.5 fusion.148
  268.3 12.4 fusion.90
  280.7 4.0 fusion.49
  284.7 3.8 fusion.106
  288.6 8.9 fusion.87
  307.7 3.0 fusion.37
  310.7 2.7 copy.267
  313.4 50.0 %all-reduce.10.cloned.1.call-done = bf16[64,32,512]{2,1,0:T(8,128)(2,1)} async-done(((bf16[64,32,512]{2,1,0:T(8,128)(2,1)}), bf16[64,32,512]{2,1,0:T(8,128)(2,1)}) %all-reduce.10.cloned.1.call-update) | async-done | bytes 2097168 | tf_op jit(solution)/shard_map/psum | solution.py:155
  365.4 9.9 scatter_fusion.1
  375.3 5.6 all-to-all-start.3
  386.0 65.7 %all-to-all-done.3 = bf16[96,32,512]{2,1,0:T(8,128)(2,1)} async-done(((bf16[96,32,512]{2,1,0:T(8,128)(2,1)}), bf16[96,32,512]{2,1,0:T(8,128)(2,1)}, u32[]{:S(2)}, u32[]{:S(2)}) %all-to-all-start.3) | async-done | bytes 3145760 | tf_op jit(solution)/shard_map/all_to_all | solution.py:160
  451.7 2.8 convert_bitcast_fusion
  456.4 2.6 fusion.25
  459.1 2.9 multiply_add_fusion
  471.7 2.7 add_convert_fusion
  475.2 3.5 fusion.101
  484.6 10.1 bitcast_convert_fusion
  495.0 12.1 bitcast_convert_fusion.1
  507.1 68.6 %all-reduce.14.cloned.1.call-done = (bf16[64,32,512]{2,1,0:T(8,128)(2,1)}, bf16[12,256,512]{2,1,0:T(8,128)(2,1)}) async-done(((bf16[64,32,512]{2,1,0:T(8,128)(2,1)}, bf16[12,256,512]{2,1,0:T(8,128)(2,1)}), (bf16[64,32,512]{2,1,0:T(8,128)(2,1)}, bf16[12,256,512]{2,1,0:T(8,128)(2,1)})) %all-reduce.14.cloned.1.call-update) | async-done | bytes 5242896 | tf_op jit(solution)/shard_map/psum | solution.py:114
  577.8 10.0 scatter_fusion
  587.7 5.6 all-to-all-start.1
  595.4 96.8 %all-reduce.12.cloned.1.call-done = (bf16[512,128]{1,0:T(8,128)(2,1)}, bf16[512,128]{1,0:T(8,128)(2,1)}, bf16[512,128]{1,0:T(8,128)(2,1)}, bf16[128,512]{1,0:T(8,128)(2,1)}) async-done(((bf16[512,128]{1,0:T(8,128)(2,1)}, bf16[512,128]{1,0:T(8,128)(2,1)}, bf16[512,128]{1,0:T(8,128)(2,1)}, bf16[128,512]{1,0:T(8,128)(2,1)}), (bf16[512,128]{1,0:T(8,128)(2,1)}, bf16[512,128]{1,0:T(8,128)(2,1)}, ...) | async-done | bytes 524304 | tf_op jit(solution)/shard_map/psum | solution.py:228
  698.8 3.8 fusion.23
  702.6 38.9 %all-reduce = (bf16[512]{0:T(512)(128)(2,1)S(1)}, bf16[512]{0:T(512)(128)(2,1)S(1)}, bf16[512,8]{0,1:T(8,128)(2,1)S(1)}, bf16[8,2048]{1,0:T(8,128)(2,1)S(1)}, bf16[8,512]{1,0:T(8,128)(2,1)S(1)}) all-reduce(bf16[512]{0:T(512)(128)(2,1)S(1)} %get-tuple-element.16, ...), channel_id=1, replica_groups=mesh['wide'=8,'narrow'=4] {'wide'}, use_global_device_ids=true, to_apply=%region_25.27 | all-reduce | flops 25600 | bytes 102400 | tf_op jit(solution)/shard_map/psum | solution.py:233
  744.4 3.0 convert_bitcast_fusion.1
  750.9 5.0 fusion.17
  755.9 222.1 %reduce-scatter.5.cloned.1.call-done = bf16[8,256,512]{2,1,0:T(8,128)(2,1)} async-done(((bf16[8,2048,512]{2,1,0:T(8,128)(2,1)}), bf16[8,256,512]{2,1,0:T(8,128)(2,1)}) %reduce-scatter.5.cloned.1.call-update) | async-done | bytes 2097168 | tf_op jit(solution)/shard_map/reduce_scatter | solution.py:242
  978.1 4.2 convert_element_type.300
  982.3 280.9 %reduce-scatter.3.cloned.1.call-done = bf16[8,64,2048]{2,1,0:T(8,128)(2,1)} async-done(((bf16[8,512,2048]{2,1,0:T(8,128)(2,1)}), bf16[8,64,2048]{2,1,0:T(8,128)(2,1)}) %reduce-scatter.3.cloned.1.call-update) | async-done | bytes 2097168 | tf_op jit(solution)/shard_map/reduce_scatter | solution.py:239
  1263.1 4.1 convert_element_type.297
  (195 shorter events, 71.7 us)
Async XLA Ops:
  7.2 33.0 %copy-start = (bf16[128,512]{1,0:T(8,128)(2,1)S(1)}, bf16[128,512]{1,0:T(8,128)(2,1)}, u32[]{:S(2)}) copy-start(bf16[128,512]{1,0:T(8,128)(2,1)} %param.24) | copy-start | bytes 393220
  13.0 7.8 copy-start.2
  13.0 9.2 copy-start.32
  13.0 9.2 copy-start.45
  13.0 108.1 %all-to-all-start.2 = ((bf16[12,256,512]{2,0,1:T(8,128)(2,1)}), bf16[12,256,512]{2,0,1:T(8,128)(2,1)}, u32[]{:S(2)}, u32[]{:S(2)}) async-start(bf16[12,256,512]{2,0,1:T(8,128)(2,1)} %copy.252), calls=%async_computation.2 | async-start | bytes 8388608 | tf_op jit(solution)/shard_map/all_to_all | solution.py:91
  20.6 4.0 copy-start.30
  20.6 92.2 %all-reduce.8.cloned.1.call-start = ((), (), s32[]{:S(2)}) async-start(), calls=%async_computation.6 | async-start | bytes 6291456 | tf_op jit(solution)/shard_map/psum | solution.py:83
  21.5 5.4 copy-start.28
  26.9 2.4 copy-start.37
  35.5 3.7 copy-start.41
  42.8 73.1 %copy-start.43 = (f32[512]{0:T(512)S(1)}, f32[512]{0:T(512)}, u32[]{:S(2)}) copy-start(f32[512]{0:T(512)} %param.26) | copy-start | bytes 6148
  112.8 3.2 copy-start.4
  121.2 5.9 copy-start.49
  121.2 6.1 copy-start.50
  121.2 98.8 %all-to-all-start = ((bf16[12,256,512]{2,0,1:T(8,128)(2,1)}), bf16[12,256,512]{2,0,1:T(8,128)(2,1)}, u32[]{:S(2)}, u32[]{:S(2)}) async-start(bf16[12,256,512]{2,0,1:T(8,128)(2,1)} %copy.242), calls=%async_computation | async-start | bytes 8388608 | tf_op jit(solution)/shard_map/all_to_all | solution.py:90
  126.8 236.5 %all-reduce.10.cloned.1.call-start = ((), (), s32[]{:S(2)}) async-start(), calls=%async_computation.7 | async-start | bytes 4194304 | tf_op jit(solution)/shard_map/psum | solution.py:155
  229.6 5.3 copy-start.38
  242.9 12.8 %copy-start.11 = (bf16[2,32,8,512]{3,2,1,0:T(8,128)(2,1)}, bf16[2,32,8,512]{3,2,1,0:T(8,128)(2,1)S(1)}, u32[]{:S(2)}) copy-start(bf16[2,32,8,512]{3,2,1,0:T(8,128)(2,1)S(1)} %fusion.75) | copy-start | bytes 1572868
  246.6 9.2 copy-start.25
  246.6 9.2 copy-start.51
  255.8 12.6 copy-start.12
  280.7 7.8 copy-start.13
  280.7 7.8 copy-start.52
  280.7 7.8 copy-start.54
  288.6 9.7 copy-start.10
  310.7 54.7 %copy-start.48 = (s32[64]{0:T(128)S(1)}, s32[64]{0:T(128)}, u32[]{:S(2)}) copy-start(s32[64]{0:T(128)} %copy-done.47) | copy-start | bytes 772
  375.3 6.4 copy-start.14
  375.3 76.4 %all-to-all-start.3 = ((bf16[96,32,512]{2,1,0:T(8,128)(2,1)}), bf16[96,32,512]{2,1,0:T(8,128)(2,1)}, u32[]{:S(2)}, u32[]{:S(2)}) async-start(bf16[96,32,512]{2,1,0:T(8,128)(2,1)} %scatter_fusion.1), calls=%async_computation.3 | async-start | bytes 6291456 | tf_op jit(solution)/shard_map/all_to_all | solution.py:160
  381.0 194.7 %all-reduce.14.cloned.1.call-start = ((), (), s32[]{:S(2)}) async-start(), calls=%async_computation.11 | async-start | bytes 10485760 | tf_op jit(solution)/shard_map/psum | solution.py:114
  456.4 2.7 copy-start.8
  456.4 6.8 slice-start.4
  459.1 4.2 slice-start.5
  462.0 2.6 copy-start.3
  465.0 6.7 copy-start.22
  474.5 217.8 %all-reduce.12.cloned.1.call-start = ((), (), s32[]{:S(2)}) async-start(), calls=%async_computation.10 | async-start | bytes 1048576 | tf_op jit(solution)/shard_map/psum | solution.py:228
  475.2 3.5 copy-start.16
  475.2 8.1 slice-start
  478.7 4.6 slice-start.1
  484.5 493.5 %reduce-scatter.5.cloned.1.call-start = ((), (), s32[]{:S(2)}) async-start(), calls=%async_computation.9 | async-start | bytes 18874368 | tf_op jit(solution)/shard_map/reduce_scatter | solution.py:242
  494.7 768.4 %reduce-scatter.3.cloned.1.call-start = ((), (), s32[]{:S(2)}) async-start(), calls=%async_computation.8 | async-start | bytes 18874368 | tf_op jit(solution)/shard_map/reduce_scatter | solution.py:239
  587.7 5.7 copy-start.21
  587.7 156.7 %all-to-all-start.1 = ((bf16[96,32,512]{2,1,0:T(8,128)(2,1)}), bf16[96,32,512]{2,1,0:T(8,128)(2,1)}, u32[]{:S(2)}, u32[]{:S(2)}) async-start(bf16[96,32,512]{2,1,0:T(8,128)(2,1)} %scatter_fusion), calls=%async_computation.1 | async-start | bytes 6291456 | tf_op jit(solution)/shard_map/all_to_all | solution.py:119
  595.4 107.1 %copy-start.39 = (bf16[8,512]{1,0:T(8,128)(2,1)S(1)}, bf16[8,512]{1,0:T(8,128)(2,1)}, u32[]{:S(2)}) copy-start(bf16[8,512]{1,0:T(8,128)(2,1)} %get-tuple-element.47) | copy-start | bytes 24580
  595.4 107.1 %copy-start.40 = (bf16[8,2048]{1,0:T(8,128)(2,1)S(1)}, bf16[8,2048]{1,0:T(8,128)(2,1)}, u32[]{:S(2)}) copy-start(bf16[8,2048]{1,0:T(8,128)(2,1)} %get-tuple-element.45) | copy-start | bytes 98308
  744.4 3.8 slice-start.2
  747.5 2.6 copy-start.6
  747.5 3.4 copy-start.9
  978.0 289.2 %copy-start.1 = (bf16[128,512]{1,0:T(8,128)(2,1)S(1)}, bf16[128,512]{1,0:T(8,128)(2,1)}, u32[]{:S(2)}) copy-start(bf16[128,512]{1,0:T(8,128)(2,1)} %param.24) | copy-start | bytes 393220
  (24 other events, 32.2 us)
Sparse Core Ops, SparseCore 0:
  43.0 69.7 all-reduce.7
  313.5 49.8 all-reduce.9
  474.6 101.0 all-reduce.13
  580.4 111.8 all-reduce.11
  695.9 282.1 reduce-scatter.4
  982.1 280.9 reduce-scatter.2
where the time goes:
time: 1280 us; the launch traced here: 1270 us
  waiting for transfers between devices  936 us (73%)
  matrix products  129 us (10%)
  local copies, waits for them, and re-layouts  75.7 us (6%)
  other arithmetic  54.2 us (4%)
  blocking collectives  38.9 us (3%)
  starting transfers between devices  25.6 us (2%)
  between operations  15.1 us (1%)
    reduce_scatter x1, waiting for transfers between devices, body(): lax.psum_scatter(g_w_in.astype(jnp.bfloat16), 'wide', scatter_dimension=1...  281 us
    reduce_scatter x1, waiting for transfers between devices, body(): lax.psum_scatter(g_w_out.astype(jnp.bfloat16), 'wide', scatter_dimension=...  222 us
    psum x1, waiting for transfers between devices, body(): lax.psum(query_weight_gradient.astype(jnp.bfloat16), 'wide')  96.8 us
    all_to_all x1, waiting for transfers between devices, body(): lax.all_to_all(mix_in, 'wide', split_axis=1, concat_axis=0, tiled=True)  81.8 us
    psum x1, waiting for transfers between devices, body(): lax.psum(attention_terms.astype(jnp.bfloat16), 'narrow').astype(jnp.float32)  70 us
    psum x1, waiting for transfers between devices, body(): lax.psum(combined.astype(jnp.bfloat16), 'narrow').astype(jnp.float32)  68.6 us
    all_to_all x1, waiting for transfers between devices, body(): lax.all_to_all(grad_placed, 'wide', split_axis=0, concat_axis=1, tiled=True)  65.7 us
    psum x1, waiting for transfers between devices, body(): lax.psum(d_grouped.astype(jnp.bfloat16), 'narrow').astype(jnp.float32)  50 us
  transfers between devices with their start and end apart: 10, of which 8 were waited for; matrix products, arithmetic and copies ran while one was open for 9% of the time, Pallas kernels for 0%

commit v1 on v0

v1 whole, which is shorter than its diff:
```python
import functools

import jax
import jax.numpy as jnp
from jax import lax
from jax.experimental import pallas as pl
from jax.experimental.pallas import tpu as pltpu
from jax.sharding import PartitionSpec as P

HEAD_WIDTH = 64
GROUP = 32
GROUPS = 2
LANES = 128

EPSILON = 1e-05
NEGATIVE = -1e30
BOTH = ("wide", "narrow")
F32 = jnp.float32
BF16 = jnp.bfloat16
VMEM_LIMIT = 56 * 1024 * 1024


def mm(a, b):
    return lax.dot_general(a, b, (((1,), (0,)), ((), ())), preferred_element_type=F32)


def mm_nt(a, b):
    return lax.dot_general(a, b, (((1,), (1,)), ((), ())), preferred_element_type=F32)


def mm_tn(a, b):
    return lax.dot_general(a, b, (((0,), (0,)), ((), ())), preferred_element_type=F32)


def params(*semantics):
    return pltpu.CompilerParams(dimension_semantics=semantics or None, vmem_limit_bytes=VMEM_LIMIT)


def whole(shape):
    zeros = (0,) * len(shape)
    return pl.BlockSpec(tuple(shape), lambda *_: zeros)


def head_masks(rows):
    lane = lax.broadcasted_iota(jnp.int32, (rows, LANES), 1)
    return [(lane >= h * HEAD_WIDTH) & (lane < (h + 1) * HEAD_WIDTH) for h in range(LANES // HEAD_WIDTH)]


def keep(mask, rows):
    return jnp.where(mask, rows, jnp.zeros_like(rows))


def causal_probs(query_head, keys, causal):
    scores = mm_nt(query_head, keys) * (float(HEAD_WIDTH) ** -0.5)
    scores = jnp.where(causal, scores, NEGATIVE)
    powers = jnp.exp(scores - jnp.max(scores, axis=-1, keepdims=True))
    return powers / jnp.sum(powers, axis=-1, keepdims=True)


def causal_mask(length):
    return lax.broadcasted_iota(jnp.int32, (length, length), 0) >= lax.broadcasted_iota(
        jnp.int32, (length, length), 1
    )


def inverse_rms(rows):
    return lax.rsqrt(jnp.mean(rows * rows, axis=-1, keepdims=True) + EPSILON)


def attention_kernel(blocks, place, tokens, *refs):
    packs = refs[:blocks]
    gain_attn, gain_mix, mix_out, hidden_out, q_out, k_out, v_out, context_out = refs[blocks:]
    rows = tokens[0].astype(F32)
    length, width = rows.shape
    entry = (rows * inverse_rms(rows) * gain_attn[...]).astype(BF16)
    causal = causal_mask(length)
    masks = head_masks(length)
    attention = jnp.zeros((length, width), F32)
    for j in range(blocks):
        at = slice(j * LANES, (j + 1) * LANES)
        joint = mm(entry, packs[j][:, : 3 * LANES]).astype(BF16)
        q, k, v = (joint[:, i * LANES : (i + 1) * LANES] for i in range(3))
        context = jnp.zeros((length, LANES), F32)
        for mask in masks:
            probs = causal_probs(keep(mask, q), k, causal)
            context = context + mm(probs.astype(BF16), keep(mask, v))
        context = context.astype(BF16)
        attention = attention + mm_nt(context, packs[j][:, 3 * LANES :])
        q_out[0, :, at] = q
        k_out[0, :, at] = k
        v_out[0, :, at] = v
        context_out[0, :, at] = context
    hidden = rows + attention
    mixed = hidden * inverse_rms(hidden) * gain_mix[...]
    mix_out[...] = mixed.reshape(mix_out.shape).astype(BF16)
    hidden_out[0] = hidden


def attention_forward(place, tokens, packs, gain_attn, gain_mix, slots, spread):
    total, length, width = tokens.shape
    inner = packs[0].shape[1] // 4 * len(packs)
    part = length // spread

    def own(i, place):
        return (jnp.minimum(place[0] + i, total - 1), 0, 0)

    def local(i, place):
        return (i, 0, 0)

    saved = jax.ShapeDtypeStruct((slots, length, inner), BF16)
    return pl.pallas_call(
        functools.partial(attention_kernel, len(packs)),
        grid_spec=pltpu.PrefetchScalarGridSpec(
            num_scalar_prefetch=1,
            grid=(slots,),
            in_specs=[pl.BlockSpec((1, length, width), own)]
            + [whole(p.shape) for p in packs]
            + [whole((1, width))] * 2,
            out_specs=[
                pl.BlockSpec((spread, 1, part, width), lambda i, place: (0, i, 0, 0)),
                pl.BlockSpec((1, length, width), local),
            ]
            + [pl.BlockSpec((1, length, inner), local)] * 4,
        ),
        out_shape=[
            jax.ShapeDtypeStruct((spread, slots, part, width), BF16),
            jax.ShapeDtypeStruct((slots, length, width), F32),
        ]
        + [saved] * 4,
        compiler_params=params("arbitrary"),
        cost_estimate=pl.CostEstimate(
            flops=slots * 2 * length * (4 * width * inner + 4 * length * inner),
            bytes_accessed=slots * length * width * 16 + 4 * width * inner * 2,
            transcendentals=slots * length * length * inner // HEAD_WIDTH,
        ),
        name="attention_forward",
    )(place, tokens, *packs, gain_attn, gain_mix)


def slot_softmax(logits, codes, part):
    experts = logits.shape[1]
    logits = logits.reshape(-1, part, experts)
    codes = jnp.broadcast_to(codes, (codes.shape[0], experts)).reshape(-1, part, experts)
    total = jnp.zeros_like(logits)
    for g in range(GROUPS):
        inside = (codes >= g * part) & (codes < (g + 1) * part)
        held = jnp.where(inside, logits, NEGATIVE)
        powers = jnp.where(inside, jnp.exp(held - jnp.max(held, axis=0, keepdims=True)), 0.0)
        total = total + powers / jnp.sum(powers, axis=0, keepdims=True)
    return total.reshape(-1, experts)


def group_totals(terms, codes, part):
    experts = terms.shape[1]
    terms = terms.reshape(-1, part, experts)
    codes = jnp.broadcast_to(codes, (codes.shape[0], experts)).reshape(-1, part, experts)
    total = jnp.zeros_like(terms)
    for g in range(GROUPS):
        inside = (codes >= g * part) & (codes < (g + 1) * part)
        total = jnp.where(inside, jnp.sum(jnp.where(inside, terms, 0.0), axis=0, keepdims=True), total)
    return total.reshape(-1, experts)


def mix_kernel(part, rows, cots, controller, row_code, col_code, tile, probs_out, spread_out, sent):
    held = rows[...]
    probs = slot_softmax(mm(held, controller[...]), row_code[...], part)
    probs_out[...] = probs
    wide = mm(probs.astype(BF16), tile[...])
    spread = jnp.where(row_code[...] == col_code[...], wide, 0.0).astype(BF16)
    spread_out[...] = spread
    block = sent.shape[2]
    merged = mm_tn(spread, held).astype(BF16)
    grads = mm_tn(spread, cots[...]).astype(BF16)
    for n in range(sent.shape[0]):
        sent[n, 0] = merged[n * block : (n + 1) * block]
        sent[n, 1] = grads[n * block : (n + 1) * block]


def mix_forward(part, rows, cots, controller, row_code, col_code, tile, narrow):
    count, width = rows.shape
    experts, columns = tile.shape
    return pl.pallas_call(
        functools.partial(mix_kernel, part),
        out_shape=[
            jax.ShapeDtypeStruct((count, experts), F32),
            jax.ShapeDtypeStruct((count, columns), BF16),
            jax.ShapeDtypeStruct((narrow, 2, columns // narrow, width), BF16),
        ],
        compiler_params=params(),
        cost_estimate=pl.CostEstimate(
            flops=4 * count * columns * width,
            bytes_accessed=6 * count * width * 2,
            transcendentals=count * experts * 2,
        ),
        name="mix_forward",
    )(rows, cots, controller, row_code, col_code, tile)


def unmix_kernel(
    part, spread, rows, cots, probs, back, controller, row_code, col_code, tile, grad_out, mixed_out, gain_out
):
    columns = spread.shape[1]
    outs = back[:, 0].reshape(columns, -1)
    grads = back[:, 1].reshape(columns, -1)
    held = rows[...]
    pairs = (mm_nt(cots[...], outs) + mm_nt(held, grads)).astype(BF16)
    pairs = jnp.where(row_code[...] == col_code[...], pairs, jnp.zeros_like(pairs))
    d_weights = mm_nt(pairs, tile[...])
    p = probs[...]
    d_logits = (p * (d_weights - group_totals(p * d_weights, row_code[...], part))).astype(BF16)
    grad_out[...] = (mm(spread[...], grads) + mm_nt(d_logits, controller[...])).astype(BF16)
    mixed_out[...] = mm(spread[...], outs).astype(BF16)
    gain_out[...] = mm_tn(d_logits, held)


def mix_backward(part, spread, rows, cots, probs, back, controller, row_code, col_code, tile):
    count, width = rows.shape
    experts, columns = tile.shape
    return pl.pallas_call(
        functools.partial(unmix_kernel, part),
        out_shape=[
            jax.ShapeDtypeStruct((count, width), BF16),
            jax.ShapeDtypeStruct((count, width), BF16),
            jax.ShapeDtypeStruct((experts, width), F32),
        ],
        compiler_params=params(),
        cost_estimate=pl.CostEstimate(
            flops=8 * count * columns * width,
            bytes_accessed=8 * count * width * 2,
            transcendentals=0,
        ),
        name="mix_backward",
    )(spread, rows, cots, probs, back, controller, row_code, col_code, tile)


GELU_SLOPE = 0.7978845608028654
GELU_CUBE = 0.044715


def gelu_pair(x):
    square = x * x
    bend = jnp.tanh(GELU_SLOPE * x * (1.0 + GELU_CUBE * square))
    gate = 0.5 * (1.0 + bend)
    slope = gate + 0.5 * x * (1.0 - bend * bend) * (GELU_SLOPE * (1.0 + 3.0 * GELU_CUBE * square))
    return x * gate, slope


def expert_kernel(both, w_in, b_in, w_out, b_out, sent):
    block = both.shape
    merged = both[:, 0].reshape(-1, block[-1])
    grads = both[:, 1].reshape(-1, block[-1])
    act, slope = gelu_pair(mm(merged, w_in[0]) + b_in[0])
    outs = mm(act.astype(BF16), w_out[0]) + b_out[0]
    d_pre = (mm_nt(grads, w_out[0]) * slope).astype(BF16)
    d_merged = mm_nt(d_pre, w_in[0])
    shape = (block[0],) + block[2:]
    sent[:, 0] = outs.astype(BF16).reshape(shape)
    sent[:, 1] = d_merged.astype(BF16).reshape(shape)


def experts_at_positions(both, w_in, b_in, w_out, b_out):
    sources, _, count, width = both.shape
    experts, _, inner = w_in.shape
    rows = count // experts
    tokens = pl.BlockSpec((sources, 2, rows, width), lambda e: (0, 0, e, 0))
    return pl.pallas_call(
        expert_kernel,
        grid=(experts,),
        in_specs=[
            tokens,
            pl.BlockSpec((1, width, inner), lambda e: (e, 0, 0)),
            pl.BlockSpec((1, 1, inner), lambda e: (e, 0, 0)),
            pl.BlockSpec((1, inner, width), lambda e: (e, 0, 0)),
            pl.BlockSpec((1, 1, width), lambda e: (e, 0, 0)),
        ],
        out_specs=tokens,
        out_shape=jax.ShapeDtypeStruct(both.shape, BF16),
        compiler_params=params("arbitrary"),
        cost_estimate=pl.CostEstimate(
            flops=8 * sources * count * width * inner,
            bytes_accessed=4 * experts * width * inner + 4 * sources * count * width * 2,
            transcendentals=sources * count * inner,
        ),
        name="experts",
    )(both, w_in, b_in[:, None], w_out, b_out[:, None])


def weight_kernel(expert, both, w_in, b_in, w_out, g_in, g_out, merged, grads):
    width = both.shape[-1]

    @pl.when(pl.program_id(0) == 0)
    def _():
        merged[...] = both[:, :, 0].reshape(merged.shape)
        grads[...] = both[:, :, 1].reshape(grads.shape)

    act, slope = gelu_pair(mm(merged[...], w_in[0]) + b_in[0])
    d_pre = (mm_nt(grads[...], w_out[0]) * slope).astype(BF16)
    g_in[...] = mm_tn(merged[...], d_pre).astype(BF16)
    block = w_out.shape[1]
    g_out[0, :block] = mm_tn(act.astype(BF16), grads[...]).astype(BF16)
    bias_out = jnp.sum(grads[...].astype(F32), axis=0, keepdims=True)
    bias_in = jnp.sum(d_pre.astype(F32), axis=0, keepdims=True)
    g_out[0, block:] = jnp.zeros((g_out.shape[1] - block, width), BF16)
    g_out[0, block : block + 1] = bias_out.astype(BF16)
    g_out[0, block + 1 : block + 2] = jnp.concatenate(
        [bias_in, jnp.zeros((1, width - bias_in.shape[1]), F32)], axis=1
    ).astype(BF16)


def expert_weights(expert, both, w_in, b_in, w_out, wide):
    sources, inner_sources, _, rows, width = both.shape
    inner = w_in.shape[2]
    block = inner // wide
    count = sources * inner_sources * rows
    return pl.pallas_call(
        weight_kernel,
        grid_spec=pltpu.PrefetchScalarGridSpec(
            num_scalar_prefetch=1,
            grid=(wide,),
            in_specs=[
                whole(both.shape),
                pl.BlockSpec((1, width, block), lambda i, e: (e[0], 0, i)),
                pl.BlockSpec((1, 1, block), lambda i, e: (e[0], 0, i)),
                pl.BlockSpec((1, block, width), lambda i, e: (e[0], i, 0)),
            ],
            out_specs=[
                pl.BlockSpec((width, block), lambda i, e: (0, i)),
                pl.BlockSpec((1, block + 16, width), lambda i, e: (i, 0, 0)),
            ],
            scratch_shapes=[pltpu.VMEM((count, width), BF16)] * 2,
        ),
        out_shape=[
            jax.ShapeDtypeStruct((width, inner), BF16),
            jax.ShapeDtypeStruct((wide, block + 16, width), BF16),
        ],
        compiler_params=params("arbitrary"),
        cost_estimate=pl.CostEstimate(
            flops=8 * count * width * inner,
            bytes_accessed=8 * width * inner + 4 * count * width,
            transcendentals=count * inner,
        ),
        name="expert_weights",
    )(expert, both, w_in, b_in[:, None], w_out)


def hidden_kernel(blocks, place, cots, grads, hidden, context, gain_mix, d_hidden_out, weight_out, gain_out):
    i = pl.program_id(0)
    length, width = hidden.shape[1:]
    live = (place[0] + i < place[1]).astype(F32)
    rows = hidden[0]
    inverse = inverse_rms(rows)
    normed = rows * inverse
    grad = grads[...].astype(F32).reshape(length, width)
    d_normed = grad * gain_mix[...]
    d_hidden = cots[0].astype(F32) * live + inverse * (
        d_normed - normed * jnp.mean(d_normed * normed, axis=-1, keepdims=True)
    )
    d_hidden_out[0] = d_hidden
    gain = jnp.sum(grad * normed, axis=0, keepdims=True)
    d_low = d_hidden.astype(BF16)

    @pl.when(i == 0)
    def _():
        weight_out[...] = jnp.zeros_like(weight_out)
        gain_out[...] = jnp.zeros_like(gain_out)

    gain_out[0:1] += gain
    for j in range(blocks):
        weight_out[j] += mm_tn(context[0, :, j * LANES : (j + 1) * LANES], d_low)


def hidden_backward(place, cotangent, grads, hidden, context, gain_mix):
    spread, slots, part, width = grads.shape
    total, length, _ = cotangent.shape
    inner = context.shape[2]
    blocks = inner // LANES

    def own(i, place):
        return (jnp.minimum(place[0] + i, total - 1), 0, 0)

    def local(i, place):
        return (i, 0, 0)

    return pl.pallas_call(
        functools.partial(hidden_kernel, blocks),
        grid_spec=pltpu.PrefetchScalarGridSpec(
            num_scalar_prefetch=1,
            grid=(slots,),
            in_specs=[
                pl.BlockSpec((1, length, width), own),
                pl.BlockSpec((spread, 1, part, width), lambda i, place: (0, i, 0, 0)),
                pl.BlockSpec((1, length, width), local),
                pl.BlockSpec((1, length, inner), local),
                whole((1, width)),
            ],
            out_specs=[
                pl.BlockSpec((1, length, width), local),
                whole((blocks, LANES, width)),
                whole((8, width)),
            ],
        ),
        out_shape=[
            jax.ShapeDtypeStruct((slots, length, width), F32),
            jax.ShapeDtypeStruct((blocks, LANES, width), F32),
            jax.ShapeDtypeStruct((8, width), F32),
        ],
        compiler_params=params("arbitrary"),
        cost_estimate=pl.CostEstimate(
            flops=slots * 2 * length * width * inner,
            bytes_accessed=slots * length * width * 14,
            transcendentals=0,
        ),
        name="hidden_backward",
    )(place, cotangent, grads, hidden, context, gain_mix)


def attention_back_kernel(blocks, place, tokens, d_hidden, q_in, k_in, v_in, *refs):
    packs = refs[:blocks]
    gain_attn, d_tokens_out, weight_out, total, gain = refs[blocks:]
    i = pl.program_id(0)
    rows = tokens[0].astype(F32)
    length, width = rows.shape
    scale = float(HEAD_WIDTH) ** -0.5
    inverse = inverse_rms(rows)
    normed = rows * inverse
    entry = (normed * gain_attn[...]).astype(BF16)
    d_low = d_hidden[0].astype(BF16)
    causal = causal_mask(length)
    masks = head_masks(length)

    @pl.when(i == 0)
    def _():
        total[...] = jnp.zeros_like(total)
        gain[...] = jnp.zeros_like(gain)

    d_entry = jnp.zeros((length, width), F32)
    for j in range(blocks):
        at = slice(j * LANES, (j + 1) * LANES)
        q, k, v = q_in[0, :, at], k_in[0, :, at], v_in[0, :, at]
        d_context = mm(d_low, packs[j][:, 3 * LANES :]).astype(BF16)
        d_q = jnp.zeros((length, LANES), F32)
        d_k = jnp.zeros((length, LANES), F32)
        d_v = jnp.zeros((length, LANES), F32)
        for mask in masks:
            q_head = keep(mask, q)
            d_head = keep(mask, d_context)
            probs = causal_probs(q_head, k, causal)
            d_probs = mm_nt(d_head, v).astype(BF16).astype(F32)
            d_scores = probs * (d_probs - jnp.sum(probs * d_probs, axis=-1, keepdims=True))
            d_scores = d_scores.astype(BF16)
            d_v = d_v + mm_tn(probs.astype(BF16), d_head)
            d_q = d_q + mm(d_scores, keep(mask, k))
            d_k = d_k + mm_tn(d_scores, q_head)
        joint = jnp.concatenate([d_q * scale, d_k * scale, d_v], axis=1).astype(BF16)
        d_entry = d_entry + mm_nt(joint, packs[j][:, : 3 * LANES])
        grad = mm_tn(entry, joint)
        for c in range(3):
            total[j, c * width : (c + 1) * width] += grad[:, c * LANES : (c + 1) * LANES]
    d_entry = d_entry.astype(BF16).astype(F32)
    gain[0:1] += jnp.sum(d_entry * normed, axis=0, keepdims=True)
    d_normed = d_entry * gain_attn[...]
    d_tokens = d_hidden[0] + inverse * (
        d_normed - normed * jnp.mean(d_normed * normed, axis=-1, keepdims=True)
    )
    live = (place[0] + i < place[1]).astype(F32)
    d_tokens_out[0] = (d_tokens * live).astype(BF16)

    @pl.when(i == pl.num_programs(0) - 1)
    def _():
        height = 3 * width
        for j in range(blocks):
            weight_out[j, :height] = total[j].astype(BF16)
            weight_out[j, height:] = jnp.zeros((weight_out.shape[1] - height, LANES), BF16)
            tail = jnp.concatenate(
                [gain[0:1, c * LANES : (c + 1) * LANES] for c in range(width // LANES)]
                + [jnp.zeros((16 - width // LANES, LANES), F32)],
                axis=0,
            )
            weight_out[j, height : height + 16] = tail.astype(BF16)


def attention_backward(place, tokens, d_hidden, q, k, v, packs, gain_attn, extra):
    total, length, width = tokens.shape
    slots, _, inner = q.shape
    blocks = len(packs)

    def own(i, place):
        return (jnp.minimum(place[0] + i, total - 1), 0, 0)

    def local(i, place):
        return (i, 0, 0)

    return pl.pallas_call(
        functools.partial(attention_back_kernel, blocks),
        grid_spec=pltpu.PrefetchScalarGridSpec(
            num_scalar_prefetch=1,
            grid=(slots,),
            in_specs=[pl.BlockSpec((1, length, width), own), pl.BlockSpec((1, length, width), local)]
            + [pl.BlockSpec((1, length, inner), local)] * 3
            + [whole(p.shape) for p in packs]
            + [whole((1, width))],
            out_specs=[
                pl.BlockSpec((1, length, width), local),
                whole((blocks, 3 * width + extra, LANES)),
            ],
            scratch_shapes=[
                pltpu.VMEM((blocks, 3 * width, LANES), F32),
                pltpu.VMEM((8, width), F32),
            ],
        ),
        out_shape=[
            jax.ShapeDtypeStruct((slots, length, width), BF16),
            jax.ShapeDtypeStruct((blocks, 3 * width + extra, LANES), BF16),
        ],
        compiler_params=params("arbitrary"),
        cost_estimate=pl.CostEstimate(
            flops=slots * 2 * length * (7 * width * inner + 10 * length * inner),
            bytes_accessed=slots * length * width * 14 + 8 * width * inner * 2,
            transcendentals=slots * length * length * inner // HEAD_WIDTH,
        ),
        name="attention_backward",
    )(place, tokens, d_hidden, q, k, v, *packs, gain_attn)


def output_kernel(place, hidden, mixed, out):
    live = (place[0] + pl.program_id(0) < place[1]).astype(F32)
    rows = mixed[...].astype(F32).reshape(hidden.shape[1:])
    out[0] = (live * (hidden[0] + rows)).astype(BF16)


def layer_output(place, hidden, mixed):
    spread, slots, part, width = mixed.shape
    length = hidden.shape[1]
    return pl.pallas_call(
        output_kernel,
        grid_spec=pltpu.PrefetchScalarGridSpec(
            num_scalar_prefetch=1,
            grid=(slots,),
            in_specs=[
                pl.BlockSpec((1, length, width), lambda i, place: (i, 0, 0)),
                pl.BlockSpec((spread, 1, part, width), lambda i, place: (0, i, 0, 0)),
            ],
            out_specs=pl.BlockSpec((1, length, width), lambda i, place: (i, 0, 0)),
        ),
        out_shape=jax.ShapeDtypeStruct((slots, length, width), BF16),
        compiler_params=params("arbitrary"),
        cost_estimate=pl.CostEstimate(
            flops=slots * length * width * 3, bytes_accessed=slots * length * width * 8, transcendentals=0
        ),
        name="layer_output",
    )(place, hidden, mixed)


def swap_core(x):
    narrow = lax.axis_size("narrow")
    return lax.ppermute(x, "narrow", [(n, n ^ 1) for n in range(narrow)])


def from_chip(x, k):
    narrow = lax.axis_size("narrow")
    return lax.ppermute(x, "narrow", [((n + 2 * k) % narrow, n) for n in range(narrow)])


def to_chip(x, k):
    narrow = lax.axis_size("narrow")
    return lax.ppermute(x, "narrow", [(n, (n + 2 * k) % narrow) for n in range(narrow)])


def relative_narrow():
    narrow = lax.axis_size("narrow")
    me = lax.axis_index("narrow")
    chips = [lax.rem(me + 2 * k, narrow) for k in range(narrow // 2)]
    return chips + [lax.bitwise_xor(n, 1) for n in chips]


def gather_narrow(x):
    chips = [x] + [from_chip(x, k) for k in range(1, lax.axis_size("narrow") // 2)]
    return chips + [swap_core(piece) for piece in chips]


def scatter_narrow(x):
    chips = x.shape[0] // 2
    summed = x[:chips].astype(F32) + swap_core(x[chips:]).astype(F32)
    low = summed.astype(BF16)
    result = summed[0]
    for k in range(1, chips):
        result = result + to_chip(low[k], k).astype(F32)
    return result


def sum_wide(x):
    wide = lax.axis_size("wide")
    parts = x.astype(BF16).reshape(wide, x.shape[0] // wide, x.shape[1])
    parts = lax.all_to_all(parts, "wide", split_axis=0, concat_axis=0, tiled=True)
    part = jnp.sum(parts.astype(F32), axis=0).astype(BF16)
    parts = jnp.broadcast_to(part[None], parts.shape)
    parts = lax.all_to_all(parts, "wide", split_axis=0, concat_axis=0, tiled=True)
    return parts.reshape(x.shape).astype(F32)


def place_kernel(count, where, *refs):
    pieces, out, sems = refs[:count], refs[count], refs[count + 1]
    slots = pieces[0].shape[0]
    copies = [
        pltpu.make_async_copy(piece, out.at[pl.ds(where[j] * slots, slots)], sems.at[j])
        for j, piece in enumerate(pieces)
    ]
    for copy in copies:
        copy.start()
    for copy in copies:
        copy.wait()


def place_narrow(pieces, where):
    count = len(pieces)
    slots = pieces[0].shape[0]
    shape = (count * slots,) + pieces[0].shape[1:]
    size = pieces[0].size * 4 * count
    return pl.pallas_call(
        functools.partial(place_kernel, count),
        grid_spec=pltpu.PrefetchScalarGridSpec(
            num_scalar_prefetch=1,
            in_specs=[pl.BlockSpec(memory_space=pl.ANY)] * count,
            out_specs=pl.BlockSpec(memory_space=pl.ANY),
            scratch_shapes=[pltpu.SemaphoreType.DMA((count,))],
        ),
        out_shape=jax.ShapeDtypeStruct(shape, pieces[0].dtype),
        compiler_params=pltpu.CompilerParams(vmem_limit_bytes=1 << 20),
        cost_estimate=pl.CostEstimate(flops=0, bytes_accessed=size, transcendentals=0),
        name="place_narrow",
    )(where, *pieces)


def body(
    tokens,
    cotangent,
    counts,
    group_order,
    query_weight,
    key_weight,
    value_weight,
    output_weight,
    gain_attn,
    gain_mix,
    controller,
    w_in,
    b_in,
    w_out,
    b_out,
):
    slot_count, seq_len, model_width = tokens.shape
    wide, narrow = lax.axis_size("wide"), lax.axis_size("narrow")
    spread = wide * narrow
    wide_index, narrow_index = lax.axis_index("wide"), lax.axis_index("narrow")
    slots = -(-slot_count // narrow)
    part = seq_len // spread
    padded_part = -(-part // 8) * 8
    local_experts = w_in.shape[0]
    experts = local_experts * narrow
    share = wide // local_experts
    relative = jnp.stack(relative_narrow())
    head_columns = query_weight.shape[1]

    seq_ends = jnp.cumsum(counts)
    seq_starts = seq_ends - counts
    own_count = counts[wide_index]
    place = jnp.stack([narrow_index * slots, own_count]).astype(jnp.int32)
    slot_ids = jnp.arange(slots * narrow)
    slot_seqs = jnp.where(slot_ids[None] < counts[:, None], seq_starts[:, None] + slot_ids[None], -1)
    matches = slot_seqs.reshape(-1, 1) == group_order[None]
    slot_group = jnp.sum(jnp.where(matches, 1 + jnp.arange(group_order.shape[0]) // GROUP, 0), axis=1) - 1
    positions = jnp.arange(padded_part)
    row_code = jnp.where(slot_group[:, None] >= 0, slot_group[:, None] * padded_part + positions, -1)
    row_code = row_code.reshape(-1, 1).astype(jnp.int32)
    per_expert = GROUPS * padded_part
    col_code = (jnp.arange(experts * per_expert) % per_expert).astype(jnp.int32)[None]
    tile = jnp.repeat(jnp.eye(experts, dtype=BF16), per_expert, axis=1)

    pack = jnp.stack([query_weight, key_weight, value_weight, output_weight.T], axis=1)
    joined = LANES // head_columns
    packs = gather_narrow(pack.reshape(model_width, -1))
    if joined > 1:
        packs = [p.reshape(model_width, 4, head_columns) for p in packs]
        packs = [
            jnp.concatenate(packs[i : i + joined], axis=2).reshape(model_width, -1)
            for i in range(0, narrow, joined)
        ]
    controllers = jnp.stack(gather_narrow(controller.T))
    controllers = controllers[jnp.argsort(relative)].reshape(experts, model_width).T

    gain_attn_row, gain_mix_row = gain_attn[None], gain_mix[None]

    def own_slots(x):
        x = jnp.pad(x, ((0, slots * narrow - slot_count), (0, 0), (0, 0)))
        return lax.dynamic_slice_in_dim(x, narrow_index * slots, slots)

    def to_positions(x):
        x = lax.all_to_all(x, BOTH, split_axis=0, concat_axis=0, tiled=True)
        x = jnp.pad(x, ((0, 0), (0, 0), (0, padded_part - part), (0, 0)))
        return x.reshape(-1, model_width)

    def to_slots(x):
        x = x.reshape(spread, slots, padded_part, model_width)[:, :, :part]
        return lax.all_to_all(x, BOTH, split_axis=0, concat_axis=0, tiled=True)

    cot_sent = own_slots(cotangent).reshape(slots, spread, part, model_width).transpose(1, 0, 2, 3)
    cot_rows = to_positions(cot_sent)

    mix_sent, hidden, q, k, v, context = attention_forward(
        place, tokens, packs, gain_attn_row, gain_mix_row, slots, spread
    )
    mix_rows = to_positions(mix_sent)
    probs, spread_probs, both = mix_forward(
        padded_part, mix_rows, cot_rows, controllers, row_code, col_code, tile, narrow
    )

    both = both.reshape(narrow, 2, -1, padded_part, model_width)[:, :, :, :part]
    both = both.reshape(narrow, 2, -1, model_width)
    both = lax.all_to_all(both, "narrow", split_axis=0, concat_axis=0, tiled=True)
    rows = GROUPS * part
    by_expert = both.reshape(narrow, 2, local_experts, rows, model_width)
    if rows % 16 == 0:
        back = experts_at_positions(both, w_in, b_in, w_out, b_out)
    else:
        lines = by_expert.transpose(1, 2, 0, 3, 4).reshape(1, 2, -1, model_width)
        back = experts_at_positions(lines, w_in, b_in, w_out, b_out)
        back = back.reshape(2, local_experts, narrow, rows, model_width).transpose(2, 0, 1, 3, 4)
        back = back.reshape(both.shape)

    tokens_sent = by_expert.transpose(2, 0, 1, 3, 4).reshape(
        wide, narrow // share, 2, rows, model_width
    )
    tokens_all = lax.all_to_all(tokens_sent, "wide", split_axis=0, concat_axis=0, tiled=True)
    expert_index = (wide_index // share).astype(jnp.int32)[None]
    grad_in, grad_out = expert_weights(expert_index, tokens_all, w_in, b_in, w_out, wide)
    grad_in = lax.all_to_all(
        grad_in.reshape(wide, model_width // wide, -1), "wide", split_axis=0, concat_axis=0, tiled=True
    )
    hidden_units = w_in.shape[2]
    block = hidden_units // wide
    biases = grad_out[:, block : block + 2]
    grad_out = lax.all_to_all(grad_out[:, :block], "wide", split_axis=0, concat_axis=0, tiled=True)
    bias_out = biases[0, 0]
    bias_in = biases[:, 1, :block].reshape(-1)
    bias = jnp.concatenate([bias_in, bias_out])
    bias = lax.all_to_all(
        jnp.broadcast_to(bias[None, None], (wide, 1, bias.shape[0])),
        "wide",
        split_axis=0,
        concat_axis=0,
        tiled=True,
    )

    def over_share(x):
        x = x.astype(F32).reshape((local_experts, share) + x.shape[1:])
        return jnp.sum(x, axis=1)

    g_w_in, g_w_out = over_share(grad_in), over_share(grad_out)
    bias = over_share(bias)[:, 0]
    g_b_in, g_b_out = bias[:, :hidden_units], bias[:, hidden_units:]

    back = lax.all_to_all(back, "narrow", split_axis=0, concat_axis=0, tiled=True)
    back = back.reshape(narrow, 2, -1, part, model_width)
    back = jnp.pad(back, ((0, 0), (0, 0), (0, 0), (0, padded_part - part), (0, 0)))
    back = back.reshape(narrow, 2, -1, model_width)
    grad_rows, mixed_rows, grad_controller = mix_backward(
        padded_part, spread_probs, mix_rows, cot_rows, probs, back, controllers, row_code, col_code, tile
    )
    grads = to_slots(grad_rows)
    mixed = to_slots(mixed_rows)
    mixed_part = layer_output(place, hidden, mixed)
    mixed_part = place_narrow(gather_narrow(mixed_part), relative)[:slot_count]

    d_hidden, grad_output, grad_gain_mix = hidden_backward(
        place, cotangent, grads, hidden, context, gain_mix_row
    )
    grad_controller = grad_controller.reshape(narrow, local_experts, model_width)[relative]
    grad_output = grad_output.reshape(narrow, head_columns, model_width)
    gain_rows = jnp.broadcast_to(grad_gain_mix[None], (narrow,) + grad_gain_mix.shape)
    first = jnp.concatenate([grad_output, grad_controller, gain_rows], axis=1)
    height = first.shape[1]
    padding = -height % (16 * wide)
    first = jnp.pad(first, ((0, 0), (0, padding), (0, 0))).astype(BF16)
    first = sum_wide(scatter_narrow(first))
    output_weight_gradient = first[:head_columns]
    g_controller = first[head_columns : head_columns + local_experts].T
    g_gain_mix = first[head_columns + local_experts]

    extra = -(3 * model_width + 16) % (16 * wide) + 16
    d_tokens, second = attention_backward(
        place, tokens, d_hidden, q, k, v, packs, gain_attn_row, extra
    )
    d_tokens = place_narrow(gather_narrow(d_tokens), relative)[:slot_count]
    if joined > 1:
        tail = second[:, 3 * model_width :]
        second = second[:, : 3 * model_width].reshape(narrow // joined, 3 * model_width, joined, -1)
        second = second.transpose(0, 2, 1, 3).reshape(narrow, 3 * model_width, head_columns)
        second = jnp.pad(second, ((0, 0), (0, 0), (0, LANES - head_columns)))
        second = jnp.concatenate([second, jnp.repeat(tail, joined, axis=0)], axis=1)
    second = sum_wide(scatter_narrow(second))
    projections = second[: 3 * model_width, :head_columns].reshape(3, model_width, head_columns)
    g_gain_attn = second[3 * model_width : 3 * model_width + model_width // LANES].reshape(-1)

    return (
        mixed_part,
        d_tokens,
        projections[0],
        projections[1],
        projections[2],
        output_weight_gradient,
        g_gain_attn,
        g_gain_mix,
        g_controller,
        g_w_in,
        g_b_in,
        g_w_out,
        g_b_out,
    )


def solution(mesh):
    placed = (
        P("wide", None, None),
        P("wide", None, None),
        P(),
        P(),
        P(None, "narrow"),
        P(None, "narrow"),
        P(None, "narrow"),
        P("narrow", None),
        P(),
        P(),
        P(None, "narrow"),
        P("narrow", None, None),
        P("narrow", None),
        P("narrow", None, None),
        P("narrow", None),
    )
    return jax.shard_map(
        body,
        mesh=mesh,
        in_specs=placed,
        out_specs=(
            P("wide", None, None),
            P("wide", None, None),
            P(None, "narrow"),
            P(None, "narrow"),
            P(None, "narrow"),
            P("narrow", None),
            P(),
            P(),
            P(None, "narrow"),
            P("narrow", "wide", None),
            P("narrow", None),
            P("narrow", "wide", None),
            P("narrow", None),
        ),
        check_vma=False,
    )
```

time: 1280 us -> 500 us (0.39)
  waiting for transfers between devices: 936 us -> 212 us
  Pallas kernels: 0 us -> 162 us
  matrix products: 129 us -> 0 us
  local copies, waits for them, and re-layouts: 75.7 us -> 29.3 us
  other arithmetic: 54.2 us -> 17.6 us
  starting transfers between devices: 25.6 us -> 59.5 us
  blocking collectives: 38.9 us -> 15.5 us
  between operations: 15.1 us -> 1.24 us
    reduce_scatter x2 -> x0, waiting for transfers between devices: 503 us -> none  [the longest x1 281 us: body(): lax.psum_scatter(g_w_in.astype(jnp.bfloat16), 'wide', scatter_dimension=1...]
    psum x4 -> x0, waiting for transfers between devices: 285 us -> none  [the longest x1 96.8 us: body(): lax.psum(query_weight_gradient.astype(jnp.bfloat16), 'wide')]
    pallas_call x0 -> x10, Pallas kernels: none -> 162 us  [the longest x2 74.8 us: place_narrow(): pl.pallas_call(functools.partial(place_kernel, count), grid_spec=pltpu.Pr...]
    dot_general x32 -> x0, matrix products: 123 us -> none  [the longest x1 12.5 us: body(): jnp.einsum('gped,efd->gpef', d_expert, w_out, preferred_element_type=jnp....]
    ppermute x0 -> x16, waiting for transfers between devices: none -> 61.7 us  [the longest x4 48.2 us: from_chip(): lax.ppermute(x, 'narrow', [((n + 2 * k) % narrow, n) for n in range(narro...]
    psum x1 -> x0, blocking collectives: 38.9 us -> none  [body(): lax.psum(g_gain_attn.astype(jnp.bfloat16), 'wide').astype(jnp.float32)]
    all_to_all x4 -> x13, starting transfers between devices: 24.5 us -> 50.7 us  [the longest x2 11.9 us: to_positions(): x = lax.all_to_all(x, BOTH, split_axis=0, concat_axis=0, tiled=True)]
    convert_element_type x19 -> x7, other arithmetic: 34.2 us -> 9.51 us  [the longest x2 6.72 us: over_share(): x = x.astype(F32).reshape((local_experts, share) + x.shape[1:])]
  transfers between devices with their start and end apart: 10 -> 29, of which waited for: 8 -> 16; matrix products, arithmetic and copies ran while one was open for 9% -> 7% of each run, Pallas kernels for 0% -> 26%
where the time goes in v1:
time: 500 us; the launch traced here: 497 us
  waiting for transfers between devices  212 us (42%)
  Pallas kernels  162 us (32%)
  starting transfers between devices  59.5 us (12%)
  local copies, waits for them, and re-layouts  29.3 us (6%)
  other arithmetic  17.6 us (4%)
  blocking collectives  15.5 us (3%)
    pallas_call x2, Pallas kernels, place_narrow(): pl.pallas_call(functools.partial(place_kernel, count), grid_spec=pltpu.Pr...  74.8 us
    ppermute x4, waiting for transfers between devices, from_chip(): lax.ppermute(x, 'narrow', [((n + 2 * k) % narrow, n) for n in range(narro...  48.2 us
    all_to_all x1, waiting for transfers between devices, body(): lax.all_to_all(grad_in.reshape(wide, model_width // wide, -1), 'wide', sp...  44.4 us
    all_to_all x3, waiting for transfers between devices, sum_wide(): lax.all_to_all(parts, 'wide', split_axis=0, concat_axis=0, tiled=True)  25.8 us
    pallas_call x1, Pallas kernels, experts_at_positions(): pl.pallas_call(expert_kernel, grid=(experts,), in_specs=[tokens, pl.Block...  20.7 us
    pallas_call x1, Pallas kernels, attention_backward(): pl.pallas_call(functools.partial(attention_back_kernel, blocks), grid_spe...  20.5 us
    all_to_all x1, waiting for transfers between devices, body(): lax.all_to_all(tokens_sent, 'wide', split_axis=0, concat_axis=0, tiled=True)  19.7 us
    all_to_all x2, waiting for transfers between devices, to_positions(): x = lax.all_to_all(x, BOTH, split_axis=0, concat_axis=0, tiled=True)  16.5 us
  transfers between devices with their start and end apart: 29, of which 16 were waited for; matrix products, arithmetic and copies ran while one was open for 7% of the time, Pallas kernels for 26%

profile of v1, /device:TPU:0, one launch (start us, length us, event | category | flops | bytes accessed | tf_op | source)
XLA Modules:
  0.0 497.4 jit_solution(10715277062426298497)
XLA Ops:
  2.9 7.3 %all-to-all-start.1 = ((bf16[32,3,8,512]{3,2,1,0:T(8,128)(2,1)}), bf16[32,3,8,512]{3,2,1,0:T(8,128)(2,1)S(1)}, u32[]{:S(2)}, u32[]{:S(2)}) async-start(bf16[32,3,8,512]{3,2,1,0:T(8,128)(2,1)} %copy.59), calls=%async_computation.1 | async-start | bytes 1572864 | tf_op jit(solution)/shard_map/all_to_all | solution.py:698
  10.9 1.8 collective-permute-start
  13.7 19.1 %collective-permute-done.refs_1_ = bf16[512,512]{1,0:T(8,128)(2,1)S(1)} collective-permute-done((bf16[512,512]{1,0:T(8,128)(2,1)S(1)}, bf16[512,512]{1,0:T(8,128)(2,1)S(1)}, u32[]{:S(2)}, u32[]{:S(2)}) %collective-permute-start) | collective-permute-done | bytes 524320 | tf_op jit(solution)/shard_map/ppermute | solution.py:561
  36.5 14.0 %attention_forward.1 = (bf16[32,3,8,512]{3,2,1,0:T(8,128)(2,1)}, f32[3,256,512]{2,1,0:T(8,128)}, bf16[3,256,512]{2,1,0:T(8,128)(2,1)}, bf16[3,256,512]{2,1,0:T(8...) custom-call(s32[2]{0:T(128)} %pad_add_fusion.1.place, bf16[12,256,512]{2,1,0:T(8,128)(2,1)} %tokens.3, ...), custom_call_target="tpu_custom_call" | custom-call | flops 2415919104 | bytes 8388608 | tf_op jit(solution)/shard_map/attention_forward/pallas_call | solution.py:111
  50.5 4.6 all-to-all-start
  59.3 16.5 %all-to-all-done = bf16[32,3,8,512]{3,2,1,0:T(8,128)(2,1)S(1)} async-done(((bf16[32,3,8,512]{3,2,1,0:T(8,128)(2,1)}), bf16[32,3,8,512]{3,2,1,0:T(8,128)(2,1)S(1)}, u32[]{:S(2)}, u32[]{:S(2)}) %all-to-all-start) | async-done | bytes 786464 | tf_op jit(solution)/shard_map/all_to_all | solution.py:698
  76.7 4.7 mix_forward.1
  81.4 3.5 all-to-all-start.2
  86.2 13.1 %all-to-all-done.2.both = bf16[4,2,128,512]{3,2,1,0:T(8,128)(2,1)S(1)} async-done(((bf16[4,2,128,512]{3,2,1,0:T(8,128)(2,1)}), bf16[4,2,128,512]{3,2,1,0:T(8,128)(2,1)S(1)}, u32[]{:S(2)}, u32[]{:S(2)}) %all-to-all-start.2) | async-done | bytes 1048608 | tf_op jit(solution)/shard_map/all_to_all | solution.py:719
  100.3 20.7 %experts.1 = bf16[4,2,128,512]{3,2,1,0:T(8,128)(2,1)} custom-call(bf16[4,2,128,512]{3,2,1,0:T(8,128)(2,1)} %copy-done.2, bf16[8,512,2048]{2,1,0:T(8,128)(2,1)} %w_in.3, f32[8,1,2048]{2,1,0:T(1,128)} %broadcast_in_dim.94.b_in, bf16[8,2048,512]{2,1,0:T(8,128)(2,1)} %w_out.3, f32[8,1,512]{2,1,0:T(1,128)} %broadcast_in_dim.95.b_out), custom_call_target="tpu_custom_call" | custom-call | flops 4294967296 | bytes 35651584 | tf_op jit(solution)/shard_map/experts/pallas_call | solution.py:266
  121.1 3.6 all-to-all-start.3
  125.8 13.4 %all-to-all-done.3.back = bf16[4,2,128,512]{3,2,1,0:T(8,128)(2,1)S(1)} async-done(((bf16[4,2,128,512]{3,2,1,0:T(8,128)(2,1)}), bf16[4,2,128,512]{3,2,1,0:T(8,128)(2,1)S(1)}, u32[]{:S(2)}, u32[]{:S(2)}) %all-to-all-start.3) | async-done | bytes 1048608 | tf_op jit(solution)/shard_map/all_to_all | solution.py:762
  139.1 3.7 all-to-all-start.10
  142.8 6.0 %mix_backward.1 = (bf16[768,512]{1,0:T(8,128)(2,1)}, bf16[768,512]{1,0:T(8,128)(2,1)}, f32[32,512]{1,0:T(8,128)}) custom-call(bf16[768,512]{1,0:T(8,128)(2,1)} %get-tuple-element.36.spread, bf16[768,512]{1,0:T(8,128)(2,1)} %bitcast.88, bf16[768,512]{1,0:T(8,128)(2,1)} %bitcast.85, f32[768,32]{1,0:T(8,128)} %get-tuple-element.37.probs, ...), custom_call_target="tpu_custom_call" | custom-call | flops 1610612736 | bytes 6291456 | tf_op jit(solution)/shard_map/mix_backward/pallas_call | solution.py:219
  148.8 19.7 %all-to-all-done.10.both = bf16[8,4,2,16,512]{4,3,2,1,0:T(8,128)(2,1)S(1)} async-done(((bf16[8,4,2,16,512]{4,3,2,1,0:T(8,128)(2,1)}), bf16[8,4,2,16,512]{4,3,2,1,0:T(8,128)(2,1)S(1)}, u32[]{:S(2)}, u32[]{:S(2)}) %all-to-all-start.10) | async-done | bytes 1048608 | tf_op jit(solution)/shard_map/all_to_all | solution.py:733
  168.5 2.9 all-to-all-start.5
  172.9 11.4 %expert_weights.1 = (bf16[512,2048]{1,0:T(8,128)(2,1)}, bf16[8,272,512]{2,1,0:T(8,128)(2,1)}) custom-call(s32[1]{0:T(128)} %bitcast.48.expert, bf16[8,4,2,16,512]{4,3,2,1,0:T(8,128)(2,1)} %copy-done.6, bf16[8,512,2048]{2,1,0:T(8,128)(2,1)} %w_in.3, f32[8,1,2048]{2,1,0:T(1,128)} %broadcast_in_dim.94.b_in, bf16[8,2048,512]{2,1,0:T(8,128)(2,1)} %w_out.3), custom_call_target="tpu_custom_call" | custom-call | flops 4294967296 | bytes 9437184 | tf_op jit(solution)/shard_map/expert_weights/pallas_call | solution.py:315
  184.4 7.5 %all-to-all-done.5.grads = bf16[32,3,8,512]{3,2,1,0:T(8,128)(2,1)S(1)} async-done(((bf16[32,3,8,512]{3,2,1,0:T(8,128)(2,1)}), bf16[32,3,8,512]{3,2,1,0:T(8,128)(2,1)S(1)}, u32[]{:S(2)}, u32[]{:S(2)}) %all-to-all-start.5) | async-done | bytes 786464 | tf_op jit(solution)/shard_map/all_to_all | solution.py:704
  192.8 5.7 %hidden_backward.1 = (f32[3,256,512]{2,1,0:T(8,128)}, f32[4,128,512]{2,1,0:T(8,128)}, f32[8,512]{1,0:T(8,128)}) custom-call(s32[2]{0:T(128)} %pad_add_fusion.1.place, bf16[12,256,512]{2,1,0:T(8,128)(2,1)} %cots.1, bf16[32,3,8,512]{3,2,1,0:T(8,128)(2,1)} %copy-done.7, f32[3,256,512]{2,1,0:T(8,128)} %get-tuple-element.33.hidden, ...), custom_call_target="tpu_custom_call" | custom-call | flops 402653184 | bytes 5505024 | tf_op jit(solution)/shard_map/hidden_backward/pallas_call | solution.py:384
  200.7 20.5 %attention_backward.1 = (bf16[3,256,512]{2,1,0:T(8,128)(2,1)}, bf16[4,1664,128]{2,1,0:T(8,128)(2,1)}) custom-call(s32[2]{0:T(128)} %pad_add_fusion.1.place, bf16[12,256,512]{2,1,0:T(8,128)(2,1)} %tokens.3, f32[3,256,512]{2,1,0:T(8,128)} %get-tuple-element.42.d_hidden, bf16[3,256,512]{2,1,0:T(8,128)(2,1)} %get-tuple-element.43.q_in, ...), custom_call_target="tpu_custom_call" | custom-call | flops 4831838208 | bytes 9699328 | tf_op jit(solution)/shard_map/attention_backward/pallas_call | solution.py:493
  221.2 2.1 slice.74
  227.4 3.7 all-to-all-start.12
  231.3 6.6 %all-to-all-done.12 = bf16[8,2,1280]{2,1,0:T(2,128)(2,1)S(1)} async-done(((bf16[8,2,1280]{2,1,0:T(2,128)(2,1)}), bf16[8,2,1280]{2,1,0:T(2,128)(2,1)S(1)}, u32[]{:S(2)}, u32[]{:S(2)}) %all-to-all-start.12) | async-done | bytes 40992 | tf_op jit(solution)/shard_map/all_to_all | solution.py:746
  237.9 2.6 all-to-all-start.4
  240.5 1.7 collective-permute-start.15
  245.0 11.7 %collective-permute-done.15 = bf16[256,512]{1,0:T(8,128)(2,1)S(1)} collective-permute-done((bf16[256,512]{1,0:T(8,128)(2,1)S(1)}, bf16[256,512]{1,0:T(8,128)(2,1)S(1)}, u32[]{:S(2)}, u32[]{:S(2)}) %collective-permute-start.15) | collective-permute-done | bytes 262176 | tf_op jit(solution)/shard_map/ppermute | solution.py:566
  257.5 3.6 all-to-all-done.4.mixed
  261.1 3.5 all-to-all-start.8
  264.6 1.9 collective-permute-done.13
  266.5 1.9 fusion.6
  268.4 5.4 %all-to-all-done.8 = bf16[8,32,512]{2,1,0:T(8,128)(2,1)S(1)} async-done(((bf16[8,32,512]{2,1,0:T(8,128)(2,1)}), bf16[8,32,512]{2,1,0:T(8,128)(2,1)S(1)}, u32[]{:S(2)}, u32[]{:S(2)}) %all-to-all-start.8) | async-done | bytes 262176 | tf_op jit(solution)/shard_map/all_to_all | solution.py:594
  273.7 3.6 all-to-all-start.6
  277.4 12.0 %all-to-all-done.6 = bf16[8,208,128]{2,1,0:T(8,128)(2,1)S(1)} async-done(((bf16[8,208,128]{2,1,0:T(8,128)(2,1)}), bf16[8,208,128]{2,1,0:T(8,128)(2,1)S(1)}, u32[]{:S(2)}, u32[]{:S(2)}) %all-to-all-start.6) | async-done | bytes 426016 | tf_op jit(solution)/shard_map/all_to_all | solution.py:594
  290.1 3.6 all-to-all-start.9
  293.8 8.4 %all-to-all-done.9 = bf16[8,32,512]{2,1,0:T(8,128)(2,1)S(1)} async-done(((bf16[8,32,512]{2,1,0:T(8,128)(2,1)}), bf16[8,32,512]{2,1,0:T(8,128)(2,1)S(1)}, u32[]{:S(2)}, u32[]{:S(2)}) %all-to-all-start.9) | async-done | bytes 262176 | tf_op jit(solution)/shard_map/all_to_all | solution.py:597
  302.3 15.5 %all_to_all.70 = bf16[8,208,128]{2,1,0:T(8,128)(2,1)} all-to-all(bf16[8,208,128]{2,1,0:T(8,128)(2,1)S(1)} %broadcast_in_dim.96), channel_id=1, replica_groups=mesh['wide'=8,'narrow'=4] {'wide'}, dimensions={0} | all-to-all | bytes 851968 | tf_op jit(solution)/shard_map/all_to_all | solution.py:597
  317.8 3.6 all-to-all-start.11
  321.4 3.1 slice.92
  324.5 44.4 %all-to-all-done.11 = bf16[8,64,2048]{2,1,0:T(8,128)(2,1)S(1)} async-done(((bf16[8,64,2048]{2,1,0:T(8,128)(2,1)}), bf16[8,64,2048]{2,1,0:T(8,128)(2,1)S(1)}, u32[]{:S(2)}, u32[]{:S(2)}) %all-to-all-start.11) | async-done | bytes 2097184 | tf_op jit(solution)/shard_map/all_to_all | solution.py:736
  370.2 4.3 all-to-all-start.13
  374.6 2.7 collective-permute-start.9
  377.4 4.0 layer_output.1.refs_0_
  381.3 14.5 %collective-permute-done.9.refs_1_ = bf16[3,256,512]{2,1,0:T(8,128)(2,1)S(1)} collective-permute-done((bf16[3,256,512]{2,1,0:T(8,128)(2,1)S(1)}, bf16[3,256,512]{2,1,0:T(8,128)(2,1)S(1)}, u32[]{:S(2)}, u32[]{:S(2)}) %collective-permute-start.9) | collective-permute-done | bytes 786464 | tf_op jit(solution)/shard_map/ppermute | solution.py:561
  396.3 14.6 %collective-permute-done.6.refs_1_ = bf16[3,256,512]{2,1,0:T(8,128)(2,1)S(1)} collective-permute-done((bf16[3,256,512]{2,1,0:T(8,128)(2,1)}, bf16[3,256,512]{2,1,0:T(8,128)(2,1)S(1)}, u32[]{:S(2)}, u32[]{:S(2)}) %collective-permute-start.6) | collective-permute-done | bytes 786464 | tf_op jit(solution)/shard_map/ppermute | solution.py:561
  412.2 49.3 %place_narrow.3 = bf16[12,256,512]{2,1,0:T(8,128)(2,1)} custom-call(s32[4]{0:T(128)S(1)} %pad_add_fusion.where, bf16[3,256,512]{2,1,0:T(8,128)(2,1)S(1)} %copy-done.1, bf16[3,256,512]{2,1,0:T(8,128)(2,1)S(1)} %collective-permute-done.9.refs_1_, bf16[3,256,512]{2,1,0:T(8,128)(2,1)} %collective-permute-done.10.refs_2_, ...), custom_call_target="tpu_custom_call" | custom-call | bytes 6291456 | tf_op jit(solution)/shard_map/place_narrow/pallas_call | solution.py:619
  461.6 25.5 %place_narrow.2 = bf16[12,256,512]{2,1,0:T(8,128)(2,1)} custom-call(s32[4]{0:T(128)S(1)} %pad_add_fusion.where, bf16[3,256,512]{2,1,0:T(8,128)(2,1)S(1)} %copy-done, bf16[3,256,512]{2,1,0:T(8,128)(2,1)S(1)} %collective-permute-done.6.refs_1_, bf16[3,256,512]{2,1,0:T(8,128)(2,1)S(1)} %collective-permute-done.7.refs_2_, ...), custom_call_target="tpu_custom_call" | custom-call | bytes 6291456 | tf_op jit(solution)/shard_map/place_narrow/pallas_call | solution.py:619
  490.7 2.5 convert_element_type.76
  493.2 4.2 convert_element_type.77
  (154 shorter events, 35.8 us)
Async XLA Ops:
  0.6 9.5 %copy-start.18 = (bf16[512,128]{1,0:T(8,128)(2,1)S(1)}, bf16[512,128]{1,0:T(8,128)(2,1)}, u32[]{:S(2)}) copy-start(bf16[512,128]{1,0:T(8,128)(2,1)} %param.19) | copy-start | bytes 393220
  1.9 8.4 %copy-start.19 = (bf16[512,128]{1,0:T(8,128)(2,1)S(1)}, bf16[512,128]{1,0:T(8,128)(2,1)}, u32[]{:S(2)}) copy-start(bf16[512,128]{1,0:T(8,128)(2,1)} %param.20) | copy-start | bytes 393220
  1.9 8.5 %copy-start.20 = (bf16[512,128]{1,0:T(8,128)(2,1)S(1)}, bf16[512,128]{1,0:T(8,128)(2,1)}, u32[]{:S(2)}) copy-start(bf16[512,128]{1,0:T(8,128)(2,1)} %param.21) | copy-start | bytes 393220
  1.9 8.7 %copy-start.21 = (bf16[128,512]{1,0:T(8,128)(2,1)S(1)}, bf16[128,512]{1,0:T(8,128)(2,1)}, u32[]{:S(2)}) copy-start(bf16[128,512]{1,0:T(8,128)(2,1)} %param.22) | copy-start | bytes 393220
  2.9 9.9 %copy-start.24 = (bf16[512,8]{0,1:T(8,128)(2,1)S(1)}, bf16[512,8]{0,1:T(8,128)(2,1)}, u32[]{:S(2)}) copy-start(bf16[512,8]{0,1:T(8,128)(2,1)} %param.25) | copy-start | bytes 24580
  2.9 10.6 %copy-start.25 = (s32[8]{0:T(128)S(1)}, s32[8]{0:T(128)}, u32[]{:S(2)}) copy-start(s32[8]{0:T(128)} %param.17) | copy-start | bytes 100
  2.9 47.7 %all-to-all-start.1 = ((bf16[32,3,8,512]{3,2,1,0:T(8,128)(2,1)}), bf16[32,3,8,512]{3,2,1,0:T(8,128)(2,1)S(1)}, u32[]{:S(2)}, u32[]{:S(2)}) async-start(bf16[32,3,8,512]{3,2,1,0:T(8,128)(2,1)} %copy.59), calls=%async_computation.1 | async-start | bytes 1572864 | tf_op jit(solution)/shard_map/all_to_all | solution.py:698
  10.9 24.8 %copy-start.15 = (bf16[512,512]{1,0:T(8,128)(2,1)}, bf16[512,512]{1,0:T(8,128)(2,1)S(1)}, u32[]{:S(2)}) copy-start(bf16[512,512]{1,0:T(8,128)(2,1)S(1)} %copy.66.refs_0_) | copy-start | bytes 1572868
  10.9 21.9 %collective-permute-start = (bf16[512,512]{1,0:T(8,128)(2,1)S(1)}, bf16[512,512]{1,0:T(8,128)(2,1)S(1)}, u32[]{:S(2)}, u32[]{:S(2)}) collective-permute-start(bf16[512,512]{1,0:T(8,128)(2,1)S(1)} %copy.66.refs_0_), channel_id=1, source_target_pairs={{2,0},{3,1},{0,2},{1,3},{6,4},{7,5},{4,6},{5,7},{10,8},{11,9},{8,1... | collective-permute-start | bytes 1572872 | tf_op jit(solution)/shard_map/ppermute | solution.py:561
  12.7 42.7 %collective-permute-start.3 = (bf16[8,512]{1,0:T(8,128)(2,1)S(1)}, bf16[8,512]{1,0:T(8,128)(2,1)S(1)}, u32[]{:S(2)}, u32[]{:S(2)}) collective-permute-start(bf16[8,512]{1,0:T(8,128)(2,1)S(1)} %bitcast.106), channel_id=1, source_target_pairs={{2,0},{3,1},{0,2},{1,3},{6,4},{7,5},{4,6},{5,7},{10,8},{11,9},{8,1... | collective-permute-start | bytes 24584 | tf_op jit(solution)/shard_map/ppermute | solution.py:561
  13.0 45.0 %collective-permute-start.4 = (bf16[8,512]{1,0:T(8,128)(2,1)S(1)}, bf16[8,512]{1,0:T(8,128)(2,1)S(1)}, u32[]{:S(2)}, u32[]{:S(2)}) collective-permute-start(bf16[8,512]{1,0:T(8,128)(2,1)S(1)} %bitcast.107), channel_id=1, source_target_pairs={{0,1},{1,0},{2,3},{3,2},{4,5},{5,4},{6,7},{7,6},{8,9},{9,8},{10,11... | collective-permute-start | bytes 24584 | tf_op jit(solution)/shard_map/ppermute | solution.py:556
  13.0 22.7 %collective-permute-start.1 = (bf16[512,512]{1,0:T(8,128)(2,1)S(1)}, bf16[512,512]{1,0:T(8,128)(2,1)S(1)}, u32[]{:S(2)}, u32[]{:S(2)}) collective-permute-start(bf16[512,512]{1,0:T(8,128)(2,1)S(1)} %copy.66.refs_0_), channel_id=1, source_target_pairs={{0,1},{1,0},{2,3},{3,2},{4,5},{5,4},{6,7},{7,6},{8,9},{9,8},{10,11... | collective-permute-start | bytes 1572872 | tf_op jit(solution)/shard_map/ppermute | solution.py:556
  32.8 2.9 collective-permute-start.2
  36.5 18.7 %copy-start.26 = (s32[64]{0:T(128)S(1)}, s32[64]{0:T(128)}, u32[]{:S(2)}) copy-start(s32[64]{0:T(128)} %param.18) | copy-start | bytes 772
  50.5 25.3 %copy-start.13 = (bf16[32,3,8,512]{3,2,1,0:T(8,128)(2,1)}, bf16[32,3,8,512]{3,2,1,0:T(8,128)(2,1)S(1)}, u32[]{:S(2)}) copy-start(bf16[32,3,8,512]{3,2,1,0:T(8,128)(2,1)S(1)} %all-to-all-done.1) | copy-start | bytes 2359300
  50.5 25.2 %all-to-all-start = ((bf16[32,3,8,512]{3,2,1,0:T(8,128)(2,1)}), bf16[32,3,8,512]{3,2,1,0:T(8,128)(2,1)S(1)}, u32[]{:S(2)}, u32[]{:S(2)}) async-start(bf16[32,3,8,512]{3,2,1,0:T(8,128)(2,1)} %get-tuple-element.34), calls=%async_computation | async-start | bytes 1572864 | tf_op jit(solution)/shard_map/all_to_all | solution.py:698
  55.4 2.5 collective-permute-start.5
  76.7 8.2 %copy-start.23 = (f32[8,512]{1,0:T(8,128)S(1)}, f32[8,512]{1,0:T(8,128)}, u32[]{:S(2)}) copy-start(f32[8,512]{1,0:T(8,128)} %param.29) | copy-start | bytes 49156
  76.7 8.9 %copy-start.22 = (f32[8,2048]{1,0:T(8,128)S(1)}, f32[8,2048]{1,0:T(8,128)}, u32[]{:S(2)}) copy-start(f32[8,2048]{1,0:T(8,128)} %param.27) | copy-start | bytes 196612
  81.4 18.0 %all-to-all-start.2 = ((bf16[4,2,128,512]{3,2,1,0:T(8,128)(2,1)}), bf16[4,2,128,512]{3,2,1,0:T(8,128)(2,1)S(1)}, u32[]{:S(2)}, u32[]{:S(2)}) async-start(bf16[4,2,128,512]{3,2,1,0:T(8,128)(2,1)} %get-tuple-element.38), calls=%async_computation.2 | async-start | bytes 2097152 | tf_op jit(solution)/shard_map/all_to_all | solution.py:719
  121.1 18.1 %all-to-all-start.3 = ((bf16[4,2,128,512]{3,2,1,0:T(8,128)(2,1)}), bf16[4,2,128,512]{3,2,1,0:T(8,128)(2,1)S(1)}, u32[]{:S(2)}, u32[]{:S(2)}) async-start(bf16[4,2,128,512]{3,2,1,0:T(8,128)(2,1)} %experts.1), calls=%async_computation.3 | async-start | bytes 2097152 | tf_op jit(solution)/shard_map/all_to_all | solution.py:762
  139.1 29.3 %all-to-all-start.10 = ((bf16[8,4,2,16,512]{4,3,2,1,0:T(8,128)(2,1)}), bf16[8,4,2,16,512]{4,3,2,1,0:T(8,128)(2,1)S(1)}, u32[]{:S(2)}, u32[]{:S(2)}) async-start(bf16[8,4,2,16,512]{4,3,2,1,0:T(8,128)(2,1)} %bitcast.78), calls=%async_computation.10 | async-start | bytes 2097152 | tf_op jit(solution)/shard_map/all_to_all | solution.py:733
  168.5 4.4 copy-start.6
  168.5 23.4 %all-to-all-start.5 = ((bf16[32,3,8,512]{3,2,1,0:T(8,128)(2,1)}), bf16[32,3,8,512]{3,2,1,0:T(8,128)(2,1)S(1)}, u32[]{:S(2)}, u32[]{:S(2)}) async-start(bf16[32,3,8,512]{3,2,1,0:T(8,128)(2,1)} %bitcast.89), calls=%async_computation.5 | async-start | bytes 1572864 | tf_op jit(solution)/shard_map/all_to_all | solution.py:704
  200.7 30.5 %collective-permute-start.14 = (bf16[2,256,512]{2,1,0:T(8,128)(2,1)S(1)}, bf16[2,256,512]{2,1,0:T(8,128)(2,1)S(1)}, u32[]{:S(2)}, u32[]{:S(2)}) collective-permute-start(bf16[2,256,512]{2,1,0:T(8,128)(2,1)S(1)} %slice.104), channel_id=1, source_target_pairs={{0,1},{1,0},{2,3},{3,2},{4,5},{5,4},{6,7},{7,6},{8,9},{9,8},{10,11... | collective-permute-start | bytes 1572872 | tf_op jit(solution)/shard_map/ppermute | solution.py:556
  223.3 18.9 %collective-permute-start.12 = (bf16[2,1664,128]{2,1,0:T(8,128)(2,1)}, bf16[2,1664,128]{2,1,0:T(8,128)(2,1)}, u32[]{:S(2)}, u32[]{:S(2)}) collective-permute-start(bf16[2,1664,128]{2,1,0:T(8,128)(2,1)} %slice.74), channel_id=1, source_target_pairs={{0,1},{1,0},{2,3},{3,2},{4,5},{5,4},{6,7},{7,6},{8,9},{9,8},{10,11... | collective-permute-start | bytes 2555912 | tf_op jit(solution)/shard_map/ppermute | solution.py:556
  227.4 10.4 %all-to-all-start.12 = ((bf16[8,2,1280]{2,1,0:T(2,128)(2,1)}), bf16[8,2,1280]{2,1,0:T(2,128)(2,1)S(1)}, u32[]{:S(2)}, u32[]{:S(2)}) async-start(bf16[8,2,1280]{2,1,0:T(2,128)(2,1)} %reshape.428), calls=%async_computation.12 | async-start | bytes 81920 | tf_op jit(solution)/shard_map/all_to_all | solution.py:746
  237.9 23.2 %all-to-all-start.4 = ((bf16[32,3,8,512]{3,2,1,0:T(8,128)(2,1)}), bf16[32,3,8,512]{3,2,1,0:T(8,128)(2,1)S(1)}, u32[]{:S(2)}, u32[]{:S(2)}) async-start(bf16[32,3,8,512]{3,2,1,0:T(8,128)(2,1)} %bitcast.86), calls=%async_computation.4 | async-start | bytes 1572864 | tf_op jit(solution)/shard_map/all_to_all | solution.py:704
  240.5 16.2 %collective-permute-start.15 = (bf16[256,512]{1,0:T(8,128)(2,1)S(1)}, bf16[256,512]{1,0:T(8,128)(2,1)S(1)}, u32[]{:S(2)}, u32[]{:S(2)}) collective-permute-start(bf16[256,512]{1,0:T(8,128)(2,1)S(1)} %fusion.10), channel_id=1, source_target_pairs={{0,2},{1,3},{2,0},{3,1},{4,6},{5,7},{6,4},{7,5},{8,10},{9,11},{10,... | collective-permute-start | bytes 786440 | tf_op jit(solution)/shard_map/ppermute | solution.py:566
  244.6 21.9 %collective-permute-start.13 = (bf16[1664,128]{1,0:T(8,128)(2,1)}, bf16[1664,128]{1,0:T(8,128)(2,1)}, u32[]{:S(2)}, u32[]{:S(2)}) collective-permute-start(bf16[1664,128]{1,0:T(8,128)(2,1)} %fusion.9), channel_id=1, source_target_pairs={{0,2},{1,3},{2,0},{3,1},{4,6},{5,7},{6,4},{7,5},{8,10},{9,11},{10,... | collective-permute-start | bytes 1277960 | tf_op jit(solution)/shard_map/ppermute | solution.py:566
  261.1 29.0 %copy-start.8 = (bf16[32,3,8,512]{3,2,1,0:T(8,128)(2,1)}, bf16[32,3,8,512]{3,2,1,0:T(8,128)(2,1)S(1)}, u32[]{:S(2)}) copy-start(bf16[32,3,8,512]{3,2,1,0:T(8,128)(2,1)S(1)} %all-to-all-done.4.mixed) | copy-start | bytes 2359300
  261.1 12.7 %all-to-all-start.8 = ((bf16[8,32,512]{2,1,0:T(8,128)(2,1)}), bf16[8,32,512]{2,1,0:T(8,128)(2,1)S(1)}, u32[]{:S(2)}, u32[]{:S(2)}) async-start(bf16[8,32,512]{2,1,0:T(8,128)(2,1)} %bitcast.83), calls=%async_computation.8 | async-start | bytes 524288 | tf_op jit(solution)/shard_map/all_to_all | solution.py:594
  273.7 15.7 %all-to-all-start.6 = ((bf16[8,208,128]{2,1,0:T(8,128)(2,1)}), bf16[8,208,128]{2,1,0:T(8,128)(2,1)S(1)}, u32[]{:S(2)}, u32[]{:S(2)}) async-start(bf16[8,208,128]{2,1,0:T(8,128)(2,1)} %bitcast.31), calls=%async_computation.6 | async-start | bytes 851968 | tf_op jit(solution)/shard_map/all_to_all | solution.py:594
  290.1 12.1 %all-to-all-start.9 = ((bf16[8,32,512]{2,1,0:T(8,128)(2,1)}), bf16[8,32,512]{2,1,0:T(8,128)(2,1)S(1)}, u32[]{:S(2)}, u32[]{:S(2)}) async-start(bf16[8,32,512]{2,1,0:T(8,128)(2,1)} %broadcast_in_dim.98), calls=%async_computation.9 | async-start | bytes 524288 | tf_op jit(solution)/shard_map/all_to_all | solution.py:597
  302.2 15.6 %copy-start.9 = (bf16[8,32,512]{2,1,0:T(8,128)(2,1)}, bf16[8,32,512]{2,1,0:T(8,128)(2,1)S(1)}, u32[]{:S(2)}) copy-start(bf16[8,32,512]{2,1,0:T(8,128)(2,1)S(1)} %all-to-all-done.9) | copy-start | bytes 786436
  317.8 51.1 %all-to-all-start.11 = ((bf16[8,64,2048]{2,1,0:T(8,128)(2,1)}), bf16[8,64,2048]{2,1,0:T(8,128)(2,1)S(1)}, u32[]{:S(2)}, u32[]{:S(2)}) async-start(bf16[8,64,2048]{2,1,0:T(8,128)(2,1)} %bitcast.81), calls=%async_computation.11 | async-start | bytes 4194304 | tf_op jit(solution)/shard_map/all_to_all | solution.py:736
  324.5 50.1 %copy-start.1 = (bf16[3,256,512]{2,1,0:T(8,128)(2,1)S(1)}, bf16[3,256,512]{2,1,0:T(8,128)(2,1)}, u32[]{:S(2)}) copy-start(bf16[3,256,512]{2,1,0:T(8,128)(2,1)} %get-tuple-element.46.refs_0_) | copy-start | bytes 2359300
  370.2 123.0 %all-to-all-start.13 = ((bf16[8,256,512]{2,1,0:T(8,128)(2,1)}), bf16[8,256,512]{2,1,0:T(8,128)(2,1)}, u32[]{:S(2)}, u32[]{:S(2)}) async-start(bf16[8,256,512]{2,1,0:T(8,128)(2,1)} %slice.92), calls=%async_computation.13 | async-start | bytes 4194304 | tf_op jit(solution)/shard_map/all_to_all | solution.py:742
  374.6 36.3 %copy-start.17 = (bf16[8,2,1280]{2,1,0:T(2,128)(2,1)S(1)}, bf16[8,2,1280]{2,1,0:T(2,128)(2,1)}, u32[]{:S(2)}) copy-start(bf16[8,2,1280]{2,1,0:T(2,128)(2,1)} %copy-done.16) | copy-start | bytes 122884
  374.6 21.2 %collective-permute-start.9 = (bf16[3,256,512]{2,1,0:T(8,128)(2,1)S(1)}, bf16[3,256,512]{2,1,0:T(8,128)(2,1)S(1)}, u32[]{:S(2)}, u32[]{:S(2)}) collective-permute-start(bf16[3,256,512]{2,1,0:T(8,128)(2,1)S(1)} %copy-done.1), channel_id=1, source_target_pairs={{2,0},{3,1},{0,2},{1,3},{6,4},{7,5},{4,6},{5,7},{10,8},{11,9},{8,1... | collective-permute-start | bytes 2359304 | tf_op jit(solution)/shard_map/ppermute | solution.py:561
  381.3 29.6 %collective-permute-start.6 = (bf16[3,256,512]{2,1,0:T(8,128)(2,1)}, bf16[3,256,512]{2,1,0:T(8,128)(2,1)S(1)}, u32[]{:S(2)}, u32[]{:S(2)}) collective-permute-start(bf16[3,256,512]{2,1,0:T(8,128)(2,1)} %layer_output.1.refs_0_), channel_id=1, source_target_pairs={{2,0},{3,1},{0,2},{1,3},{6,4},{7,5},{4,6},{5,7},{10,8},{11,9},{8,1... | collective-permute-start | bytes 2359304 | tf_op jit(solution)/shard_map/ppermute | solution.py:561
  381.3 30.9 %collective-permute-start.10 = (bf16[3,256,512]{2,1,0:T(8,128)(2,1)S(1)}, bf16[3,256,512]{2,1,0:T(8,128)(2,1)}, u32[]{:S(2)}, u32[]{:S(2)}) collective-permute-start(bf16[3,256,512]{2,1,0:T(8,128)(2,1)S(1)} %copy-done.1), channel_id=1, source_target_pairs={{0,1},{1,0},{2,3},{3,2},{4,5},{5,4},{6,7},{7,6},{8,9},{9,8},{10,11... | collective-permute-start | bytes 2359304 | tf_op jit(solution)/shard_map/ppermute | solution.py:556
  395.8 16.4 %collective-permute-start.11 = (bf16[3,256,512]{2,1,0:T(8,128)(2,1)S(1)}, bf16[3,256,512]{2,1,0:T(8,128)(2,1)}, u32[]{:S(2)}, u32[]{:S(2)}) collective-permute-start(bf16[3,256,512]{2,1,0:T(8,128)(2,1)S(1)} %collective-permute-done.9.refs_1_), channel_id=1, source_target_pairs={{0,1},{1,0},{2,3},{3,2},{4,5},{5,4},{6,7},{7,6},{8,9},{9,8},{10,11... | collective-permute-start | bytes 2359304 | tf_op jit(solution)/shard_map/ppermute | solution.py:556
  395.8 65.8 %collective-permute-start.7 = (bf16[3,256,512]{2,1,0:T(8,128)(2,1)}, bf16[3,256,512]{2,1,0:T(8,128)(2,1)S(1)}, u32[]{:S(2)}, u32[]{:S(2)}) collective-permute-start(bf16[3,256,512]{2,1,0:T(8,128)(2,1)} %layer_output.1.refs_0_), channel_id=1, source_target_pairs={{0,1},{1,0},{2,3},{3,2},{4,5},{5,4},{6,7},{7,6},{8,9},{9,8},{10,11... | collective-permute-start | bytes 2359304 | tf_op jit(solution)/shard_map/ppermute | solution.py:556
  410.9 50.7 %collective-permute-start.8 = (bf16[3,256,512]{2,1,0:T(8,128)(2,1)S(1)}, bf16[3,256,512]{2,1,0:T(8,128)(2,1)}, u32[]{:S(2)}, u32[]{:S(2)}) collective-permute-start(bf16[3,256,512]{2,1,0:T(8,128)(2,1)S(1)} %collective-permute-done.6.refs_1_), channel_id=1, source_target_pairs={{0,1},{1,0},{2,3},{3,2},{4,5},{5,4},{6,7},{7,6},{8,9},{9,8},{10,11... | collective-permute-start | bytes 2359304 | tf_op jit(solution)/shard_map/ppermute | solution.py:556
  412.2 49.4 %copy-start = (bf16[3,256,512]{2,1,0:T(8,128)(2,1)S(1)}, bf16[3,256,512]{2,1,0:T(8,128)(2,1)}, u32[]{:S(2)}) copy-start(bf16[3,256,512]{2,1,0:T(8,128)(2,1)} %layer_output.1.refs_0_) | copy-start | bytes 2359300
  461.6 25.6 %copy-start.10 = (bf16[8,32,512]{2,1,0:T(8,128)(2,1)S(1)}, bf16[8,32,512]{2,1,0:T(8,128)(2,1)}, u32[]{:S(2)}) copy-start(bf16[8,32,512]{2,1,0:T(8,128)(2,1)} %copy-done.9) | copy-start | bytes 786436
  461.6 27.6 %copy-start.11 = (bf16[8,208,128]{2,1,0:T(8,128)(2,1)S(1)}, bf16[8,208,128]{2,1,0:T(8,128)(2,1)}, u32[]{:S(2)}) copy-start(bf16[8,208,128]{2,1,0:T(8,128)(2,1)} %all_to_all.70) | copy-start | bytes 1277956
  (10 other events, 23.1 us)

commit v2 on v1

v2 whole, which is shorter than its diff:
```python
import functools

import jax
import jax.numpy as jnp
from jax import lax
from jax.experimental import pallas as pl
from jax.experimental.pallas import tpu as pltpu
from jax.sharding import PartitionSpec as P

HEAD_WIDTH = 64
GROUP = 32
GROUPS = 2
LANES = 128

EPSILON = 1e-05
NEGATIVE = -1e30
BOTH = ("wide", "narrow")
F32 = jnp.float32
BF16 = jnp.bfloat16
VMEM_LIMIT = 56 * 1024 * 1024


def mm(a, b):
    return lax.dot_general(a, b, (((1,), (0,)), ((), ())), preferred_element_type=F32)


def mm_nt(a, b):
    return lax.dot_general(a, b, (((1,), (1,)), ((), ())), preferred_element_type=F32)


def mm_tn(a, b):
    return lax.dot_general(a, b, (((0,), (0,)), ((), ())), preferred_element_type=F32)


def params(*semantics):
    return pltpu.CompilerParams(dimension_semantics=semantics or None, vmem_limit_bytes=VMEM_LIMIT)


def whole(shape):
    zeros = (0,) * len(shape)
    return pl.BlockSpec(tuple(shape), lambda *_: zeros)


def head_masks(rows):
    lane = lax.broadcasted_iota(jnp.int32, (rows, LANES), 1)
    return [(lane >= h * HEAD_WIDTH) & (lane < (h + 1) * HEAD_WIDTH) for h in range(LANES // HEAD_WIDTH)]


def keep(mask, rows):
    return jnp.where(mask, rows, jnp.zeros_like(rows))


def causal_probs(query_head, keys, causal):
    scores = mm_nt(query_head, keys) * (float(HEAD_WIDTH) ** -0.5)
    scores = jnp.where(causal, scores, NEGATIVE)
    powers = jnp.exp(scores - jnp.max(scores, axis=-1, keepdims=True))
    return powers / jnp.sum(powers, axis=-1, keepdims=True)


def causal_mask(length):
    return lax.broadcasted_iota(jnp.int32, (length, length), 0) >= lax.broadcasted_iota(
        jnp.int32, (length, length), 1
    )


def inverse_rms(rows):
    return lax.rsqrt(jnp.mean(rows * rows, axis=-1, keepdims=True) + EPSILON)


def attention_kernel(blocks, place, tokens, *refs):
    packs = refs[:blocks]
    gain_attn, gain_mix, mix_out, hidden_out, q_out, k_out, v_out, context_out = refs[blocks:]
    rows = tokens[0].astype(F32)
    length, width = rows.shape
    entry = (rows * inverse_rms(rows) * gain_attn[...]).astype(BF16)
    causal = causal_mask(length)
    masks = head_masks(length)
    attention = jnp.zeros((length, width), F32)
    for j in range(blocks):
        at = slice(j * LANES, (j + 1) * LANES)
        joint = mm(entry, packs[j][:, : 3 * LANES]).astype(BF16)
        q, k, v = (joint[:, i * LANES : (i + 1) * LANES] for i in range(3))
        context = jnp.zeros((length, LANES), F32)
        for mask in masks:
            probs = causal_probs(keep(mask, q), k, causal)
            context = context + mm(probs.astype(BF16), keep(mask, v))
        context = context.astype(BF16)
        attention = attention + mm_nt(context, packs[j][:, 3 * LANES :])
        q_out[0, :, at] = q
        k_out[0, :, at] = k
        v_out[0, :, at] = v
        context_out[0, :, at] = context
    hidden = rows + attention
    mixed = hidden * inverse_rms(hidden) * gain_mix[...]
    mix_out[...] = mixed.reshape(mix_out.shape).astype(BF16)
    hidden_out[0] = hidden


def attention_forward(place, tokens, packs, gain_attn, gain_mix, slots, spread):
    total, length, width = tokens.shape
    inner = packs[0].shape[1] // 4 * len(packs)
    part = length // spread

    def own(i, place):
        return (jnp.minimum(place[0] + i, total - 1), 0, 0)

    def local(i, place):
        return (i, 0, 0)

    saved = jax.ShapeDtypeStruct((slots, length, inner), BF16)
    return pl.pallas_call(
        functools.partial(attention_kernel, len(packs)),
        grid_spec=pltpu.PrefetchScalarGridSpec(
            num_scalar_prefetch=1,
            grid=(slots,),
            in_specs=[pl.BlockSpec((1, length, width), own)]
            + [whole(p.shape) for p in packs]
            + [whole((1, width))] * 2,
            out_specs=[
                pl.BlockSpec((spread, 1, part, width), lambda i, place: (0, i, 0, 0)),
                pl.BlockSpec((1, length, width), local),
            ]
            + [pl.BlockSpec((1, length, inner), local)] * 4,
        ),
        out_shape=[
            jax.ShapeDtypeStruct((spread, slots, part, width), BF16),
            jax.ShapeDtypeStruct((slots, length, width), F32),
        ]
        + [saved] * 4,
        compiler_params=params("arbitrary"),
        cost_estimate=pl.CostEstimate(
            flops=slots * 2 * length * (4 * width * inner + 4 * length * inner),
            bytes_accessed=slots * length * width * 16 + 4 * width * inner * 2,
            transcendentals=slots * length * length * inner // HEAD_WIDTH,
        ),
        name="attention_forward",
    )(place, tokens, *packs, gain_attn, gain_mix)


def slot_softmax(logits, codes, part):
    experts = logits.shape[1]
    logits = logits.reshape(-1, part, experts)
    codes = jnp.broadcast_to(codes, (codes.shape[0], experts)).reshape(-1, part, experts)
    total = jnp.zeros_like(logits)
    for g in range(GROUPS):
        inside = (codes >= g * part) & (codes < (g + 1) * part)
        held = jnp.where(inside, logits, NEGATIVE)
        powers = jnp.where(inside, jnp.exp(held - jnp.max(held, axis=0, keepdims=True)), 0.0)
        total = total + powers / jnp.sum(powers, axis=0, keepdims=True)
    return total.reshape(-1, experts)


def group_totals(terms, codes, part):
    experts = terms.shape[1]
    terms = terms.reshape(-1, part, experts)
    codes = jnp.broadcast_to(codes, (codes.shape[0], experts)).reshape(-1, part, experts)
    total = jnp.zeros_like(terms)
    for g in range(GROUPS):
        inside = (codes >= g * part) & (codes < (g + 1) * part)
        total = jnp.where(inside, jnp.sum(jnp.where(inside, terms, 0.0), axis=0, keepdims=True), total)
    return total.reshape(-1, experts)


def mix_kernel(part, relative, rows, cots, controller, row_code, col_code, tile, probs_out, spread_out, *refs):
    sent, (merged, grads) = refs[:-2], refs[-2:]
    held = rows[...]
    probs = slot_softmax(mm(held, controller[...]), row_code[...], part)
    probs_out[...] = probs
    wide = mm(probs.astype(BF16), tile[...])
    spread = jnp.where(row_code[...] == col_code[...], wide, 0.0).astype(BF16)
    spread_out[...] = spread
    block = sent[0].shape[1]
    merged[...] = mm_tn(spread, held).astype(BF16)
    grads[...] = mm_tn(spread, cots[...]).astype(BF16)
    for j, out in enumerate(sent):
        at = pl.ds(pl.multiple_of(relative[j] * block, block), block)
        out[0] = merged[at]
        out[1] = grads[at]


def mix_forward(part, relative, rows, cots, controller, row_code, col_code, tile, narrow):
    count, width = rows.shape
    experts, columns = tile.shape
    block = columns // narrow
    return pl.pallas_call(
        functools.partial(mix_kernel, part),
        grid_spec=pltpu.PrefetchScalarGridSpec(
            num_scalar_prefetch=1,
            grid=(1,),
            in_specs=[whole(x.shape) for x in (rows, cots, controller, row_code, col_code, tile)],
            out_specs=[whole((count, experts)), whole((count, columns))]
            + [whole((2, block, width))] * narrow,
            scratch_shapes=[pltpu.VMEM((columns, width), BF16)] * 2,
        ),
        out_shape=[
            jax.ShapeDtypeStruct((count, experts), F32),
            jax.ShapeDtypeStruct((count, columns), BF16),
        ]
        + [jax.ShapeDtypeStruct((2, block, width), BF16)] * narrow,
        compiler_params=params("arbitrary"),
        cost_estimate=pl.CostEstimate(
            flops=4 * count * columns * width,
            bytes_accessed=6 * count * width * 2,
            transcendentals=count * experts * 2,
        ),
        name="mix_forward",
    )(relative, rows, cots, controller, row_code, col_code, tile)


def unmix_kernel(
    part, narrow, relative, spread, rows, cots, probs, controller, row_code, col_code, tile, *refs
):
    back, (grad_out, mixed_out, gain_out, outs, grads) = refs[:narrow], refs[narrow:]
    block = back[0].shape[1]
    for j, piece in enumerate(back):
        at = pl.ds(pl.multiple_of(relative[j] * block, block), block)
        outs[at] = piece[0]
        grads[at] = piece[1]
    held = rows[...]
    pairs = (mm_nt(cots[...], outs[...]) + mm_nt(held, grads[...])).astype(BF16)
    pairs = jnp.where(row_code[...] == col_code[...], pairs, jnp.zeros_like(pairs))
    d_weights = mm_nt(pairs, tile[...])
    p = probs[...]
    d_logits = (p * (d_weights - group_totals(p * d_weights, row_code[...], part))).astype(BF16)
    grad_out[...] = (mm(spread[...], grads[...]) + mm_nt(d_logits, controller[...])).astype(BF16)
    mixed_out[...] = mm(spread[...], outs[...]).astype(BF16)
    gain_out[...] = mm_tn(d_logits, held)


def mix_backward(part, relative, spread, rows, cots, probs, back, controller, row_code, col_code, tile):
    count, width = rows.shape
    experts, columns = tile.shape
    operands = (spread, rows, cots, probs, controller, row_code, col_code, tile) + tuple(back)
    outs = [
        jax.ShapeDtypeStruct((count, width), BF16),
        jax.ShapeDtypeStruct((count, width), BF16),
        jax.ShapeDtypeStruct((experts, width), F32),
    ]
    return pl.pallas_call(
        functools.partial(unmix_kernel, part, len(back)),
        grid_spec=pltpu.PrefetchScalarGridSpec(
            num_scalar_prefetch=1,
            grid=(1,),
            in_specs=[whole(x.shape) for x in operands],
            out_specs=[whole(x.shape) for x in outs],
            scratch_shapes=[pltpu.VMEM((columns, width), BF16)] * 2,
        ),
        out_shape=outs,
        compiler_params=params("arbitrary"),
        cost_estimate=pl.CostEstimate(
            flops=8 * count * columns * width,
            bytes_accessed=8 * count * width * 2,
            transcendentals=0,
        ),
        name="mix_backward",
    )(relative, *operands)


GELU_SLOPE = 0.7978845608028654
GELU_CUBE = 0.044715


def gelu_pair(x):
    square = x * x
    bend = jnp.tanh(GELU_SLOPE * x * (1.0 + GELU_CUBE * square))
    gate = 0.5 * (1.0 + bend)
    slope = gate + 0.5 * x * (1.0 - bend * bend) * (GELU_SLOPE * (1.0 + 3.0 * GELU_CUBE * square))
    return x * gate, slope


def expert_kernel(count, *refs):
    both, (w_in, b_in, w_out, b_out), sent = refs[:count], refs[count : count + 4], refs[count + 4 :]
    rows = both[0].shape[1]
    merged = jnp.concatenate([x[0] for x in both], axis=0)
    grads = jnp.concatenate([x[1] for x in both], axis=0)
    act, slope = gelu_pair(mm(merged, w_in[0]) + b_in[0])
    outs = mm(act.astype(BF16), w_out[0]) + b_out[0]
    d_pre = (mm_nt(grads, w_out[0]) * slope).astype(BF16)
    d_merged = mm_nt(d_pre, w_in[0])
    for j, out in enumerate(sent):
        at = slice(j * rows, (j + 1) * rows)
        out[0] = outs[at].astype(BF16)
        out[1] = d_merged[at].astype(BF16)


def experts_at_positions(both, w_in, b_in, w_out, b_out):
    _, count, width = both[0].shape
    experts, _, inner = w_in.shape
    sources = len(both)
    tokens = pl.BlockSpec((2, count // experts, width), lambda e: (0, e, 0))
    return pl.pallas_call(
        functools.partial(expert_kernel, sources),
        grid=(experts,),
        in_specs=[tokens] * sources
        + [
            pl.BlockSpec((1, width, inner), lambda e: (e, 0, 0)),
            pl.BlockSpec((1, 1, inner), lambda e: (e, 0, 0)),
            pl.BlockSpec((1, inner, width), lambda e: (e, 0, 0)),
            pl.BlockSpec((1, 1, width), lambda e: (e, 0, 0)),
        ],
        out_specs=[tokens] * sources,
        out_shape=[jax.ShapeDtypeStruct(x.shape, BF16) for x in both],
        compiler_params=params("arbitrary"),
        cost_estimate=pl.CostEstimate(
            flops=8 * sources * count * width * inner,
            bytes_accessed=4 * experts * width * inner + 4 * sources * count * width * 2,
            transcendentals=sources * count * inner,
        ),
        name="experts",
    )(*both, w_in, b_in[:, None], w_out, b_out[:, None])


def weight_kernel(units, where, both, w_in, b_in, w_out, g_in, g_out, bias_out, merged, grads, total):
    i = pl.program_id(1)
    width = both.shape[-1]
    half, unit = where[0], where[1]
    span = total.shape[0]
    block = w_out.shape[1]

    @pl.when(i == 0)
    def _():
        merged[...] = both[:, 0, :, 0].reshape(merged.shape)
        grads[...] = both[:, 0, :, 1].reshape(grads.shape)
        bias_out[...] = jnp.zeros_like(bias_out)
        sums = jnp.sum(grads[...].astype(F32), axis=0, keepdims=True)
        bias_out[0, 1:2, :width] = sums

    act, slope = gelu_pair(mm(merged[...], w_in[0]) + b_in[0])
    d_pre = (mm_nt(grads[...], w_out[0]) * slope).astype(BF16)
    bias_out[0, 0:1, pl.ds(pl.multiple_of(i * block, block), block)] = jnp.sum(
        d_pre.astype(F32), axis=0, keepdims=True
    )
    total[...] = mm_tn(merged[:, pl.ds(pl.multiple_of(half * span, span), span)], d_pre)
    rows = span // units
    for d in range(units):
        at = pl.ds(pl.multiple_of(lax.bitwise_xor(unit, d) * rows, rows), rows)
        g_in[d, 0] = total[at].astype(BF16)

    @pl.when((i >= half * units) & (i < (half + 1) * units))
    def _():
        g_out[0, 0] = mm_tn(act.astype(BF16), grads[...]).astype(BF16)


def expert_weights(where, first, both, w_in, b_in, w_out, wide, units):
    sources, held, inner_sources, _, rows, width = both.shape
    inner = w_in.shape[2]
    block = inner // wide
    count = sources * inner_sources * rows
    span = width * units // wide

    def out_block(p, i, where, first):
        return (lax.bitwise_xor(jnp.clip(i - where[0] * units, 0, units - 1), where[1]), p, 0, 0)

    return pl.pallas_call(
        lambda where, first, *refs: weight_kernel(units, where, *refs),
        grid_spec=pltpu.PrefetchScalarGridSpec(
            num_scalar_prefetch=2,
            grid=(held, wide),
            in_specs=[
                pl.BlockSpec(
                    (sources, 1, inner_sources, 2, rows, width), lambda p, i, w, f: (0, p, 0, 0, 0, 0)
                ),
                pl.BlockSpec((1, width, block), lambda p, i, w, f: (f[0] + p, 0, i)),
                pl.BlockSpec((1, 1, block), lambda p, i, w, f: (f[0] + p, 0, i)),
                pl.BlockSpec((1, block, width), lambda p, i, w, f: (f[0] + p, i, 0)),
            ],
            out_specs=[
                pl.BlockSpec((units, 1, span // units, block), lambda p, i, w, f: (0, p, 0, i)),
                pl.BlockSpec((1, 1, block, width), out_block),
                pl.BlockSpec((1, 8, inner), lambda p, i, w, f: (p, 0, 0)),
            ],
            scratch_shapes=[pltpu.VMEM((count, width), BF16)] * 2 + [pltpu.VMEM((span, block), F32)],
        ),
        out_shape=[
            jax.ShapeDtypeStruct((units, held, span // units, inner), BF16),
            jax.ShapeDtypeStruct((units, held, block, width), BF16),
            jax.ShapeDtypeStruct((held, 8, inner), F32),
        ],
        compiler_params=params("arbitrary", "arbitrary"),
        cost_estimate=pl.CostEstimate(
            flops=held * 6 * count * width * inner,
            bytes_accessed=held * (8 * width * inner + 4 * count * width),
            transcendentals=held * count * inner,
        ),
        name="expert_weights",
    )(where, first, both, w_in, b_in[:, None], w_out)


def attention_back_kernel(blocks, place, tokens, cots, grads, hidden, q_in, k_in, v_in, context, *refs):
    packs = refs[:blocks]
    gain_attn, gain_mix, d_tokens_out, weight_out, total, gains = refs[blocks:]
    i = pl.program_id(0)
    length, width = hidden.shape[1:]
    scale = float(HEAD_WIDTH) ** -0.5
    live = (place[0] + i < place[1]).astype(F32)

    @pl.when(i == 0)
    def _():
        total[...] = jnp.zeros_like(total)
        gains[...] = jnp.zeros_like(gains)

    rows = hidden[0]
    inverse = inverse_rms(rows)
    normed = rows * inverse
    grad = grads[...].astype(F32).reshape(length, width)
    gains[1:2] += jnp.sum(grad * normed, axis=0, keepdims=True)
    d_normed = grad * gain_mix[...]
    d_hidden = cots[0].astype(F32) * live + inverse * (
        d_normed - normed * jnp.mean(d_normed * normed, axis=-1, keepdims=True)
    )
    d_low = d_hidden.astype(BF16)

    rows = tokens[0].astype(F32)
    inverse = inverse_rms(rows)
    normed = rows * inverse
    entry = (normed * gain_attn[...]).astype(BF16)
    causal = causal_mask(length)
    masks = head_masks(length)
    d_entry = jnp.zeros((length, width), F32)
    for j in range(blocks):
        at = slice(j * LANES, (j + 1) * LANES)
        q, k, v = q_in[0, :, at], k_in[0, :, at], v_in[0, :, at]
        d_context = mm(d_low, packs[j][:, 3 * LANES :]).astype(BF16)
        d_q = jnp.zeros((length, LANES), F32)
        d_k = jnp.zeros((length, LANES), F32)
        d_v = jnp.zeros((length, LANES), F32)
        for mask in masks:
            q_head = keep(mask, q)
            d_head = keep(mask, d_context)
            probs = causal_probs(q_head, k, causal)
            d_probs = mm_nt(d_head, v).astype(BF16).astype(F32)
            d_scores = probs * (d_probs - jnp.sum(probs * d_probs, axis=-1, keepdims=True))
            d_scores = d_scores.astype(BF16)
            d_v = d_v + mm_tn(probs.astype(BF16), d_head)
            d_q = d_q + mm(d_scores, keep(mask, k))
            d_k = d_k + mm_tn(d_scores, q_head)
        joint = jnp.concatenate([d_q * scale, d_k * scale, d_v], axis=1).astype(BF16)
        d_entry = d_entry + mm_nt(joint, packs[j][:, : 3 * LANES])
        grad = mm_tn(entry, joint)
        for c in range(3):
            total[j, c * width : (c + 1) * width] += grad[:, c * LANES : (c + 1) * LANES]
        total[j, 3 * width : 4 * width] += mm_tn(d_low, context[0, :, at])
    d_entry = d_entry.astype(BF16).astype(F32)
    gains[0:1] += jnp.sum(d_entry * normed, axis=0, keepdims=True)
    d_normed = d_entry * gain_attn[...]
    d_tokens = d_hidden + inverse * (
        d_normed - normed * jnp.mean(d_normed * normed, axis=-1, keepdims=True)
    )
    d_tokens_out[0] = (d_tokens * live).astype(BF16)

    @pl.when(i == pl.num_programs(0) - 1)
    def _():
        height = 4 * width
        pieces = width // LANES
        tail = [gains[r : r + 1, c * LANES : (c + 1) * LANES] for r in range(2) for c in range(pieces)]
        tail = jnp.concatenate(tail + [jnp.zeros((16 - 2 * pieces, LANES), F32)], axis=0).astype(BF16)
        for j in range(blocks):
            weight_out[j, :height] = total[j].astype(BF16)
            weight_out[j, height:] = tail


def attention_backward(place, tokens, cotangent, grads, hidden, q, k, v, context, packs, gain_attn, gain_mix):
    total, length, width = tokens.shape
    spread, slots, part, _ = grads.shape
    inner = q.shape[2]
    blocks = len(packs)

    def own(i, place):
        return (jnp.minimum(place[0] + i, total - 1), 0, 0)

    def local(i, place):
        return (i, 0, 0)

    return pl.pallas_call(
        functools.partial(attention_back_kernel, blocks),
        grid_spec=pltpu.PrefetchScalarGridSpec(
            num_scalar_prefetch=1,
            grid=(slots,),
            in_specs=[
                pl.BlockSpec((1, length, width), own),
                pl.BlockSpec((1, length, width), own),
                pl.BlockSpec((spread, 1, part, width), lambda i, place: (0, i, 0, 0)),
                pl.BlockSpec((1, length, width), local),
            ]
            + [pl.BlockSpec((1, length, inner), local)] * 4
            + [whole(p.shape) for p in packs]
            + [whole((1, width))] * 2,
            out_specs=[
                pl.BlockSpec((1, length, width), local),
                whole((blocks, 4 * width + 16, LANES)),
            ],
            scratch_shapes=[
                pltpu.VMEM((blocks, 4 * width, LANES), F32),
                pltpu.VMEM((8, width), F32),
            ],
        ),
        out_shape=[
            jax.ShapeDtypeStruct((slots, length, width), BF16),
            jax.ShapeDtypeStruct((blocks, 4 * width + 16, LANES), BF16),
        ],
        compiler_params=params("arbitrary"),
        cost_estimate=pl.CostEstimate(
            flops=slots * 2 * length * (8 * width * inner + 10 * length * inner),
            bytes_accessed=slots * length * width * 18 + 8 * width * inner * 2,
            transcendentals=slots * length * length * inner // HEAD_WIDTH,
        ),
        name="attention_backward",
    )(place, tokens, cotangent, grads, hidden, q, k, v, context, *packs, gain_attn, gain_mix)


def output_kernel(place, hidden, mixed, out):
    live = (place[0] + pl.program_id(0) < place[1]).astype(F32)
    rows = mixed[...].astype(F32).reshape(hidden.shape[1:])
    out[0] = (live * (hidden[0] + rows)).astype(BF16)


def layer_output(place, hidden, mixed):
    spread, slots, part, width = mixed.shape
    length = hidden.shape[1]
    return pl.pallas_call(
        output_kernel,
        grid_spec=pltpu.PrefetchScalarGridSpec(
            num_scalar_prefetch=1,
            grid=(slots,),
            in_specs=[
                pl.BlockSpec((1, length, width), lambda i, place: (i, 0, 0)),
                pl.BlockSpec((spread, 1, part, width), lambda i, place: (0, i, 0, 0)),
            ],
            out_specs=pl.BlockSpec((1, length, width), lambda i, place: (i, 0, 0)),
        ),
        out_shape=jax.ShapeDtypeStruct((slots, length, width), BF16),
        compiler_params=params("arbitrary"),
        cost_estimate=pl.CostEstimate(
            flops=slots * length * width * 3, bytes_accessed=slots * length * width * 8, transcendentals=0
        ),
        name="layer_output",
    )(place, hidden, mixed)


def swap_core(x):
    narrow = lax.axis_size("narrow")
    return lax.ppermute(x, "narrow", [(n, n ^ 1) for n in range(narrow)])


def from_chip(x, k):
    narrow = lax.axis_size("narrow")
    return lax.ppermute(x, "narrow", [((n + 2 * k) % narrow, n) for n in range(narrow)])


def to_chip(x, k):
    narrow = lax.axis_size("narrow")
    return lax.ppermute(x, "narrow", [(n, (n + 2 * k) % narrow) for n in range(narrow)])


def relative_narrow():
    narrow = lax.axis_size("narrow")
    me = lax.axis_index("narrow")
    chips = [lax.rem(me + 2 * k, narrow) for k in range(narrow // 2)]
    return chips + [lax.bitwise_xor(n, 1) for n in chips]


def gather_narrow(x):
    chips = [x] + [from_chip(x, k) for k in range(1, lax.axis_size("narrow") // 2)]
    return chips + [swap_core(piece) for piece in chips]


def scatter_narrow(x):
    chips = x.shape[0] // 2
    summed = x[:chips].astype(F32) + swap_core(x[chips:]).astype(F32)
    low = summed.astype(BF16)
    result = summed[0]
    for k in range(1, chips):
        result = result + to_chip(low[k], k).astype(F32)
    return result


def sum_wide(x):
    wide = lax.axis_size("wide")
    parts = x.astype(BF16).reshape(wide, x.shape[0] // wide, x.shape[1])
    parts = lax.all_to_all(parts, "wide", split_axis=0, concat_axis=0, tiled=True)
    part = jnp.sum(parts.astype(F32), axis=0).astype(BF16)
    parts = jnp.broadcast_to(part[None], parts.shape)
    parts = lax.all_to_all(parts, "wide", split_axis=0, concat_axis=0, tiled=True)
    return parts.reshape(x.shape).astype(F32)


def to_relative(x, j):
    narrow = lax.axis_size("narrow")
    k, other = j % (narrow // 2), j // (narrow // 2)
    return lax.ppermute(x, "narrow", [(n, ((n + 2 * k) % narrow) ^ other) for n in range(narrow)])


def from_relative(x, j):
    narrow = lax.axis_size("narrow")
    k, other = j % (narrow // 2), j // (narrow // 2)
    return lax.ppermute(x, "narrow", [(((n + 2 * k) % narrow) ^ other, n) for n in range(narrow)])


def to_unit(x, d):
    wide = lax.axis_size("wide")
    return lax.ppermute(x, "wide", [(w, w ^ d) for w in range(wide)])


def place_kernel(count, where, *refs):
    out = refs[count]
    for j in range(count):

        @pl.when(pl.program_id(0) == j)
        def _(j=j):
            out[...] = refs[j][...].astype(out.dtype)


def place_blocks(pieces, where, dtype):
    count = len(pieces)
    shape = pieces[0].shape
    zeros = (0,) * (len(shape) - 1)
    return pl.pallas_call(
        functools.partial(place_kernel, count),
        grid_spec=pltpu.PrefetchScalarGridSpec(
            num_scalar_prefetch=1,
            grid=(count,),
            in_specs=[whole(shape)] * count,
            out_specs=pl.BlockSpec(shape, lambda i, where: (where[i],) + zeros),
        ),
        out_shape=jax.ShapeDtypeStruct((count * shape[0],) + shape[1:], dtype),
        compiler_params=params("arbitrary"),
        cost_estimate=pl.CostEstimate(
            flops=0, bytes_accessed=pieces[0].size * 8 * count, transcendentals=0
        ),
        name="place_blocks",
    )(where, *pieces)


def body(
    tokens,
    cotangent,
    counts,
    group_order,
    query_weight,
    key_weight,
    value_weight,
    output_weight,
    gain_attn,
    gain_mix,
    controller,
    w_in,
    b_in,
    w_out,
    b_out,
):
    slot_count, seq_len, model_width = tokens.shape
    wide, narrow = lax.axis_size("wide"), lax.axis_size("narrow")
    spread = wide * narrow
    wide_index, narrow_index = lax.axis_index("wide"), lax.axis_index("narrow")
    slots = -(-slot_count // narrow)
    part = seq_len // spread
    padded_part = -(-part // 8) * 8
    local_experts = w_in.shape[0]
    experts = local_experts * narrow
    relative = jnp.stack(relative_narrow())
    head_columns = query_weight.shape[1]

    seq_ends = jnp.cumsum(counts)
    seq_starts = seq_ends - counts
    own_count = counts[wide_index]
    place = jnp.stack([narrow_index * slots, own_count]).astype(jnp.int32)
    slot_ids = jnp.arange(slots * narrow)
    slot_seqs = jnp.where(slot_ids[None] < counts[:, None], seq_starts[:, None] + slot_ids[None], -1)
    matches = slot_seqs.reshape(-1, 1) == group_order[None]
    slot_group = jnp.sum(jnp.where(matches, 1 + jnp.arange(group_order.shape[0]) // GROUP, 0), axis=1) - 1
    positions = jnp.arange(padded_part)
    row_code = jnp.where(slot_group[:, None] >= 0, slot_group[:, None] * padded_part + positions, -1)
    row_code = row_code.reshape(-1, 1).astype(jnp.int32)
    per_expert = GROUPS * padded_part
    col_code = (jnp.arange(experts * per_expert) % per_expert).astype(jnp.int32)[None]
    tile = jnp.repeat(jnp.eye(experts, dtype=BF16), per_expert, axis=1)

    pack = jnp.stack([query_weight, key_weight, value_weight, output_weight.T], axis=1)
    joined = LANES // head_columns
    packs = gather_narrow(pack.reshape(model_width, -1))
    if joined > 1:
        packs = [p.reshape(model_width, 4, head_columns) for p in packs]
        packs = [
            jnp.concatenate(packs[i : i + joined], axis=2).reshape(model_width, -1)
            for i in range(0, narrow, joined)
        ]
    controllers = jnp.stack(gather_narrow(controller.T))
    controllers = controllers[jnp.argsort(relative)].reshape(experts, model_width).T

    gain_attn_row, gain_mix_row = gain_attn[None], gain_mix[None]

    def own_slots(x):
        x = jnp.pad(x, ((0, slots * narrow - slot_count), (0, 0), (0, 0)))
        return lax.dynamic_slice_in_dim(x, narrow_index * slots, slots)

    def to_positions(x):
        x = lax.all_to_all(x, BOTH, split_axis=0, concat_axis=0, tiled=True)
        x = jnp.pad(x, ((0, 0), (0, 0), (0, padded_part - part), (0, 0)))
        return x.reshape(-1, model_width)

    def to_slots(x):
        x = x.reshape(spread, slots, padded_part, model_width)[:, :, :part]
        return lax.all_to_all(x, BOTH, split_axis=0, concat_axis=0, tiled=True)

    cot_sent = own_slots(cotangent).reshape(slots, spread, part, model_width).transpose(1, 0, 2, 3)
    cot_rows = to_positions(cot_sent)

    mix_sent, hidden, q, k, v, context = attention_forward(
        place, tokens, packs, gain_attn_row, gain_mix_row, slots, spread
    )
    mix_rows = to_positions(mix_sent)
    probs, spread_probs, *both = mix_forward(
        padded_part, relative, mix_rows, cot_rows, controllers, row_code, col_code, tile, narrow
    )

    def trim(x):
        return x.reshape(2, -1, padded_part, model_width)[:, :, :part].reshape(2, -1, model_width)

    def untrim(x):
        x = x.reshape(2, -1, part, model_width)
        x = jnp.pad(x, ((0, 0), (0, 0), (0, padded_part - part), (0, 0)))
        return x.reshape(2, -1, model_width)

    both = [trim(x) for x in both]
    both = both[:1] + [to_relative(x, j) for j, x in enumerate(both) if j]
    rows = GROUPS * part
    by_expert = jnp.stack(both).reshape(narrow, 2, local_experts, rows, model_width)
    halves = 2 if wide % 4 == 0 else 1
    units = wide // halves
    held, share = max(local_experts // units, 1), max(units // local_experts, 1)
    unit = lax.rem(wide_index, units)
    tokens_sent = by_expert.transpose(2, 0, 1, 3, 4).reshape(
        units, held, narrow // share, 2, rows, model_width
    )
    tokens_sent = jnp.concatenate([tokens_sent] * halves)
    tokens_sent, both = lax.optimization_barrier((tokens_sent, both))
    tokens_all = lax.all_to_all(tokens_sent, "wide", split_axis=0, concat_axis=0, tiled=True)
    if rows % 16 == 0:
        back = experts_at_positions(both, w_in, b_in, w_out, b_out)
    else:
        lines = by_expert.transpose(1, 2, 0, 3, 4).reshape(2, -1, model_width)
        (back,) = experts_at_positions([lines], w_in, b_in, w_out, b_out)
        back = back.reshape(2, local_experts, narrow, rows, model_width).transpose(2, 0, 1, 3, 4)
        back = list(back.reshape(narrow, 2, -1, model_width))

    where = jnp.stack([wide_index // units, unit]).astype(jnp.int32)
    first = (unit * held // share).astype(jnp.int32)[None]
    grad_in, grad_out, bias = expert_weights(
        where, first, tokens_all, w_in, b_in, w_out, wide, units
    )

    back = [untrim(x if j == 0 else from_relative(x, j)) for j, x in enumerate(back)]
    grad_rows, mixed_rows, grad_controller = mix_backward(
        padded_part, relative, spread_probs, mix_rows, cot_rows, probs, back, controllers, row_code, col_code, tile
    )
    grads = to_slots(grad_rows)
    mixed_rows, grad_in, grad_out, bias, grads = lax.optimization_barrier(
        (mixed_rows, grad_in, grad_out, bias, grads)
    )
    mixed = to_slots(mixed_rows)

    def by_unit(pieces, dtype):
        pieces = [pieces[0]] + [to_unit(pieces[d], d) for d in range(1, units)]
        order = lax.bitwise_xor(unit, jnp.arange(units))
        if share == 1:
            return place_blocks(pieces, order, dtype)
        pieces = jnp.stack(pieces)[order].astype(F32)
        return jnp.sum(pieces.reshape((local_experts, share) + pieces.shape[2:]), axis=1)

    g_w_in, g_w_out = by_unit(grad_in, F32), by_unit(grad_out, F32)
    bias = by_unit([bias] * units, F32)
    g_b_in, g_b_out = bias[:, 0], bias[:, 1, :model_width]

    mixed_part = layer_output(place, hidden, mixed)
    mixed_part = place_blocks(gather_narrow(mixed_part), relative, BF16)[:slot_count]

    d_tokens, weights = attention_backward(
        place, tokens, cotangent, grads, hidden, q, k, v, context, packs, gain_attn_row, gain_mix_row
    )
    d_tokens = place_blocks(gather_narrow(d_tokens), relative, BF16)[:slot_count]
    height = 4 * model_width
    if joined > 1:
        tail = weights[:, height:]
        weights = weights[:, :height].reshape(narrow // joined, height, joined, -1)
        weights = weights.transpose(0, 2, 1, 3).reshape(narrow, height, head_columns)
        weights = jnp.pad(weights, ((0, 0), (0, 0), (0, LANES - head_columns)))
        weights = jnp.concatenate([weights, jnp.repeat(tail, joined, axis=0)], axis=1)
    grad_controller = grad_controller.astype(BF16).reshape(narrow, -1, LANES)[relative]
    end = height + 16 + grad_controller.shape[1]
    weights = jnp.concatenate([weights, grad_controller], axis=1)
    weights = jnp.pad(weights, ((0, 0), (0, -end % (16 * wide)), (0, 0)))
    weights = sum_wide(scatter_narrow(weights))
    projections = weights[:height, :head_columns].reshape(4, model_width, head_columns)
    pieces = model_width // LANES
    g_gain_attn = weights[height : height + pieces].reshape(-1)
    g_gain_mix = weights[height + pieces : height + 2 * pieces].reshape(-1)
    g_controller = weights[height + 16 : end].reshape(local_experts, model_width).T
    output_weight_gradient = projections[3].T

    return (
        mixed_part,
        d_tokens,
        projections[0],
        projections[1],
        projections[2],
        output_weight_gradient,
        g_gain_attn,
        g_gain_mix,
        g_controller,
        g_w_in,
        g_b_in,
        g_w_out,
        g_b_out,
    )


def solution(mesh):
    placed = (
        P("wide", None, None),
        P("wide", None, None),
        P(),
        P(),
        P(None, "narrow"),
        P(None, "narrow"),
        P(None, "narrow"),
        P("narrow", None),
        P(),
        P(),
        P(None, "narrow"),
        P("narrow", None, None),
        P("narrow", None),
        P("narrow", None, None),
        P("narrow", None),
    )
    return jax.shard_map(
        body,
        mesh=mesh,
        in_specs=placed,
        out_specs=(
            P("wide", None, None),
            P("wide", None, None),
            P(None, "narrow"),
            P(None, "narrow"),
            P(None, "narrow"),
            P("narrow", None),
            P(),
            P(),
            P(None, "narrow"),
            P("narrow", "wide", None),
            P("narrow", None),
            P("narrow", "wide", None),
            P("narrow", None),
        ),
        check_vma=False,
    )
```

time: 500 us -> 343 us (0.69)
  waiting for transfers between devices: 212 us -> 126 us
  Pallas kernels: 162 us -> 116 us
  blocking collectives: 15.5 us -> 0 us
  other arithmetic: 17.6 us -> 12.2 us
    all_to_all x5 -> x0, waiting for transfers between devices: 77.5 us -> none  [the longest x1 44.4 us: body(): lax.all_to_all(grad_in.reshape(wide, model_width // wide, -1), 'wide', sp...]
    ppermute x0 -> x15, waiting for transfers between devices: none -> 64.7 us  [the longest x9 41.7 us: to_unit(): return lax.ppermute(x, 'wide', [(w, w ^ d) for w in range(wide)])]
    pallas_call x7 -> x9, Pallas kernels: 123 us -> 76.2 us  [the longest x5 21.8 us: place_blocks(): pl.pallas_call(functools.partial(place_kernel, count), grid_spec=pltpu.Pr...]
    ppermute x4, waiting for transfers between devices: 48.2 us -> 19.1 us  [from_chip(): lax.ppermute(x, 'narrow', [((n + 2 * k) % narrow, n) for n in range(narro...]
    all_to_all x3 -> x2, waiting for transfers between devices: 25.8 us -> 0.01 us  [sum_wide(): lax.all_to_all(parts, 'wide', split_axis=0, concat_axis=0, tiled=True)]
    all_to_all x5 -> x0, starting transfers between devices: 18.8 us -> none  [the longest x1 4.35 us: body(): lax.all_to_all(grad_out[:, :block], 'wide', split_axis=0, concat_axis=0,...]
    ppermute x0 -> x15, starting transfers between devices: none -> 16.5 us  [the longest x9 12.1 us: to_unit(): return lax.ppermute(x, 'wide', [(w, w ^ d) for w in range(wide)])]
    all_to_all x1 -> x0, blocking collectives: 15.5 us -> none  [sum_wide(): lax.all_to_all(parts, 'wide', split_axis=0, concat_axis=0, tiled=True)]
  transfers between devices with their start and end apart: 29 -> 36, of which waited for: 16 -> 13; matrix products, arithmetic and copies ran while one was open for 7% -> 6% of each run, Pallas kernels for 26% -> 26%
where the time goes in v2:
time: 343 us; the launch traced here: 342 us
  waiting for transfers between devices  126 us (37%)
  Pallas kernels  116 us (34%)
  starting transfers between devices  58.3 us (17%)
  local copies, waits for them, and re-layouts  28.3 us (8%)
  other arithmetic  12.2 us (4%)
    ppermute x9, waiting for transfers between devices, to_unit(): return lax.ppermute(x, 'wide', [(w, w ^ d) for w in range(wide)])  41.7 us
    pallas_call x1, Pallas kernels, attention_backward(): pl.pallas_call(functools.partial(attention_back_kernel, blocks), grid_spe...  21.9 us
    pallas_call x5, Pallas kernels, place_blocks(): pl.pallas_call(functools.partial(place_kernel, count), grid_spec=pltpu.Pr...  21.8 us
    pallas_call x1, Pallas kernels, expert_weights(): pl.pallas_call(lambda where, first, *refs: weight_kernel(units, where, *r...  21.5 us
    pallas_call x1, Pallas kernels, experts_at_positions(): pl.pallas_call(functools.partial(expert_kernel, sources), grid=(experts,)...  20.9 us
    ppermute x1, waiting for transfers between devices, to_chip(): lax.ppermute(x, 'narrow', [(n, (n + 2 * k) % narrow) for n in range(narro...  19.8 us
    ppermute x4, waiting for transfers between devices, from_chip(): lax.ppermute(x, 'narrow', [((n + 2 * k) % narrow, n) for n in range(narro...  19.1 us
    all_to_all x2, waiting for transfers between devices, to_positions(): x = lax.all_to_all(x, BOTH, split_axis=0, concat_axis=0, tiled=True)  16.5 us
  transfers between devices with their start and end apart: 36, of which 13 were waited for; matrix products, arithmetic and copies ran while one was open for 6% of the time, Pallas kernels for 26%

profile of v2, /device:TPU:0, one launch (start us, length us, event | category | flops | bytes accessed | tf_op | source)
XLA Modules:
  0.0 341.6 jit_solution(17858666218855000946)
XLA Ops:
  0.7 1.2 dynamic-slice_bitcast_fusion
  2.9 7.3 %all-to-all-start.1 = ((bf16[32,3,8,512]{3,2,1,0:T(8,128)(2,1)}), bf16[32,3,8,512]{3,2,1,0:T(8,128)(2,1)S(1)}, u32[]{:S(2)}, u32[]{:S(2)}) async-start(bf16[32,3,8,512]{3,2,1,0:T(8,128)(2,1)} %copy.75), calls=%async_computation.1 | async-start | bytes 1572864 | tf_op jit(solution)/shard_map/all_to_all | solution.py:697
  10.9 1.8 collective-permute-start
  13.7 19.1 %collective-permute-done.refs_1_ = bf16[512,512]{1,0:T(8,128)(2,1)S(1)} collective-permute-done((bf16[512,512]{1,0:T(8,128)(2,1)S(1)}, bf16[512,512]{1,0:T(8,128)(2,1)S(1)}, u32[]{:S(2)}, u32[]{:S(2)}) %collective-permute-start) | collective-permute-done | bytes 524320 | tf_op jit(solution)/shard_map/ppermute | solution.py:547
  34.4 1.2 pad_add_fusion.1.place
  36.5 14.0 %attention_forward.1 = (bf16[32,3,8,512]{3,2,1,0:T(8,128)(2,1)}, f32[3,256,512]{2,1,0:T(8,128)}, bf16[3,256,512]{2,1,0:T(8,128)(2,1)}, bf16[3,256,512]{2,1,0:T(8...) custom-call(s32[2]{0:T(128)} %pad_add_fusion.1.place, bf16[12,256,512]{2,1,0:T(8,128)(2,1)} %tokens.3, ...), custom_call_target="tpu_custom_call" | custom-call | flops 2415919104 | bytes 8388608 | tf_op jit(solution)/shard_map/attention_forward/pallas_call | solution.py:111
  50.6 4.6 %all-to-all-start = ((bf16[32,3,8,512]{3,2,1,0:T(8,128)(2,1)}), bf16[32,3,8,512]{3,2,1,0:T(8,128)(2,1)S(1)}, u32[]{:S(2)}, u32[]{:S(2)}) async-start(bf16[32,3,8,512]{3,2,1,0:T(8,128)(2,1)} %get-tuple-element.49), calls=%async_computation | async-start | bytes 1572864 | tf_op jit(solution)/shard_map/all_to_all | solution.py:697
  59.4 16.4 %all-to-all-done = bf16[32,3,8,512]{3,2,1,0:T(8,128)(2,1)S(1)} async-done(((bf16[32,3,8,512]{3,2,1,0:T(8,128)(2,1)}), bf16[32,3,8,512]{3,2,1,0:T(8,128)(2,1)S(1)}, u32[]{:S(2)}, u32[]{:S(2)}) %all-to-all-start) | async-done | bytes 786464 | tf_op jit(solution)/shard_map/all_to_all | solution.py:697
  76.7 5.4 %mix_forward.1 = (f32[768,32]{1,0:T(8,128)}, bf16[768,512]{1,0:T(8,128)(2,1)}, bf16[2,128,512]{2,1,0:T(8,128)(2,1)}, bf16[2,128,512]{2,1,0:T(8,128)(2,1)}, bf16[...) custom-call(s32[4]{0:T(128)} %copy-done.31, bf16[768,512]{1,0:T(8,128)(2,1)} %bitcast.99, ...), custom_call_target="tpu_custom_call" | custom-call | flops 805306368 | bytes 4718592 | tf_op jit(solution)/shard_map/mix_forward/pallas_call | solution.py:185
  82.0 1.5 collective-permute-start.6
  84.2 7.3 %collective-permute-done.6.refs_1_ = bf16[2,128,512]{2,1,0:T(8,128)(2,1)S(1)} collective-permute-done((bf16[2,128,512]{2,1,0:T(8,128)(2,1)}, bf16[2,128,512]{2,1,0:T(8,128)(2,1)S(1)}, u32[]{:S(2)}, u32[]{:S(2)}) %collective-permute-start.6) | collective-permute-done | bytes 262176 | tf_op jit(solution)/shard_map/ppermute | solution.py:590
  91.5 3.9 %collective-permute-done.8.refs_3_ = bf16[2,128,512]{2,1,0:T(8,128)(2,1)S(1)} collective-permute-done((bf16[2,128,512]{2,1,0:T(8,128)(2,1)}, bf16[2,128,512]{2,1,0:T(8,128)(2,1)S(1)}, u32[]{:S(2)}, u32[]{:S(2)}) %collective-permute-start.8) | collective-permute-done | bytes 262176 | tf_op jit(solution)/shard_map/ppermute | solution.py:590
  96.6 1.5 pad_maximum_fusion
  98.1 3.7 %all-to-all-start.2 = ((bf16[8,2,4,2,16,512]{5,4,3,2,1,0:T(8,128)(2,1)}), bf16[8,2,4,2,16,512]{5,4,3,2,1,0:T(8,128)(2,1)S(1)}, u32[]{:S(2)}, u32[]{:S(2)}) async-start(bf16[8,2,4,2,16,512]{5,4,3,2,1,0:T(8,128)(2,1)} %pad_maximum_fusion), calls=%async_computation.2 | async-start | bytes 4194304 | tf_op jit(solution)/shard_map/all_to_all | solution.py:737
  103.2 20.9 %experts.1 = (bf16[2,128,512]{2,1,0:T(8,128)(2,1)}, bf16[2,128,512]{2,1,0:T(8,128)(2,1)}, bf16[2,128,512]{2,1,0:T(8,128)(2,1)}, bf16[2,128,512]{2,1,0:T(8,128)(2,1)}) custom-call(bf16[2,128,512]{2,1,0:T(8,128)(2,1)} %get-tuple-element.57.refs_0_, bf16[2,128,512]{2,1,0:T(8,128)(2,1)} %copy-done.5, bf16[2,128,512]{2,1,0:T(8,128)(2,1)} %copy-done.6, ...), custom_call_target="tpu_custom_call" | custom-call | flops 4294967296 | bytes 35651584 | tf_op jit(solution)/shard_map/experts/pallas_call | solution.py:291
  124.1 1.7 collective-permute-start.9
  126.3 7.2 %collective-permute-done.9.refs_1_ = bf16[2,128,512]{2,1,0:T(8,128)(2,1)S(1)} collective-permute-done((bf16[2,128,512]{2,1,0:T(8,128)(2,1)}, bf16[2,128,512]{2,1,0:T(8,128)(2,1)S(1)}, u32[]{:S(2)}, u32[]{:S(2)}) %collective-permute-start.9) | collective-permute-done | bytes 262176 | tf_op jit(solution)/shard_map/ppermute | solution.py:596
  133.5 4.7 %collective-permute-done.11.refs_3_ = bf16[2,128,512]{2,1,0:T(8,128)(2,1)S(1)} collective-permute-done((bf16[2,128,512]{2,1,0:T(8,128)(2,1)}, bf16[2,128,512]{2,1,0:T(8,128)(2,1)S(1)}, u32[]{:S(2)}, u32[]{:S(2)}) %collective-permute-start.11) | collective-permute-done | bytes 262176 | tf_op jit(solution)/shard_map/ppermute | solution.py:596
  138.9 6.7 %mix_backward.1 = (bf16[768,512]{1,0:T(8,128)(2,1)}, bf16[768,512]{1,0:T(8,128)(2,1)}, f32[32,512]{1,0:T(8,128)}) custom-call(s32[4]{0:T(128)} %copy-done.31, bf16[768,512]{1,0:T(8,128)(2,1)} %get-tuple-element.51.spread, bf16[768,512]{1,0:T(8,128)(2,1)} %bitcast.100, bf16[768,512]{1,0:T(8,128)(2,1)} %bitcast.98, f32[768,32]{1,0:T(8,128)} %get-tuple-element.52.probs, ...), custom_call_target="tpu_custom_call" | custom-call | flops 1610612736 | bytes 6291456 | tf_op jit(solution)/shard_map/mix_backward/pallas_call | solution.py:239
  145.6 5.4 %all-to-all-done.2.refs_0_ = bf16[8,2,4,2,16,512]{5,4,3,2,1,0:T(8,128)(2,1)S(1)} async-done(((bf16[8,2,4,2,16,512]{5,4,3,2,1,0:T(8,128)(2,1)}), bf16[8,2,4,2,16,512]{5,4,3,2,1,0:T(8,128)(2,1)S(1)}, u32[]{:S(2)}, u32[]{:S(2)}) %all-to-all-start.2) | async-done | bytes 2097184 | tf_op jit(solution)/shard_map/all_to_all | solution.py:737
  151.0 4.0 %all-to-all-start.3 = ((bf16[32,3,8,512]{3,2,1,0:T(8,128)(2,1)}), bf16[32,3,8,512]{3,2,1,0:T(8,128)(2,1)S(1)}, u32[]{:S(2)}, u32[]{:S(2)}) async-start(bf16[32,3,8,512]{3,2,1,0:T(8,128)(2,1)} %bitcast.102), calls=%async_computation.3 | async-start | bytes 1572864 | tf_op jit(solution)/shard_map/all_to_all | solution.py:703
  157.2 21.5 %expert_weights.1 = (bf16[4,2,64,2048]{3,2,1,0:T(8,128)(2,1)}, bf16[4,2,256,512]{3,2,1,0:T(8,128)(2,1)}, f32[2,8,2048]{2,1,0:T(8,128)}) custom-call(s32[2]{0:T(128)} %pad_add_fusion.2.where, s32[1]{0:T(128)} %bitcast.35.first, bf16[8,2,4,2,16,512]{5,4,3,2,1,0:T(8,128)(2,1)} %copy-done, bf16[8,512,2048]{2,1,0:T(8,128)(2,1)} %refs_1_.1, ...), custom_call_target="tpu_custom_call" | custom-call | flops 6442450944 | bytes 18874368 | tf_op jit(solution)/shard_map/expert_weights/pallas_call | solution.py:354
  179.5 21.9 %attention_backward.1 = (bf16[3,256,512]{2,1,0:T(8,128)(2,1)}, bf16[4,2064,128]{2,1,0:T(8,128)(2,1)}) custom-call(s32[2]{0:T(128)} %pad_add_fusion.1.place, bf16[12,256,512]{2,1,0:T(8,128)(2,1)} %tokens.3, bf16[12,256,512]{2,1,0:T(8,128)(2,1)} %cots.1, bf16[32,3,8,512]{3,2,1,0:T(8,128)(2,1)} %copy-done.16, f32[3,256,512]{2,1,0:T(8,128)} %get-tuple-element.48.hidden, ...), custom_call_target="tpu_custom_call" | custom-call | flops 5234491392 | bytes 11272192 | tf_op jit(solution)/shard_map/attention_backward/pallas_call | solution.py:474
  201.4 1.7 fusion.2
  204.3 5.6 %all-to-all-start.4 = ((bf16[32,3,8,512]{3,2,1,0:T(8,128)(2,1)}), bf16[32,3,8,512]{3,2,1,0:T(8,128)(2,1)S(1)}, u32[]{:S(2)}, u32[]{:S(2)}) async-start(bf16[32,3,8,512]{3,2,1,0:T(8,128)(2,1)} %bitcast.101), calls=%async_computation.4 | async-start | bytes 1572864 | tf_op jit(solution)/shard_map/all_to_all | solution.py:703
  210.0 1.5 convert_add_fusion
  211.5 1.8 collective-permute-start.19
  213.3 19.8 %collective-permute-done.19 = bf16[2176,128]{1,0:T(8,128)(2,1)S(1)} collective-permute-done((bf16[2176,128]{1,0:T(8,128)(2,1)S(1)}, bf16[2176,128]{1,0:T(8,128)(2,1)S(1)}, u32[]{:S(2)}, u32[]{:S(2)}) %collective-permute-start.19) | collective-permute-done | bytes 557088 | tf_op jit(solution)/shard_map/ppermute | solution.py:552
  234.1 5.5 %all-to-all-start.5 = ((bf16[8,272,128]{2,1,0:T(8,128)(2,1)}), bf16[8,272,128]{2,1,0:T(8,128)(2,1)S(1)}, u32[]{:S(2)}, u32[]{:S(2)}) async-start(bf16[8,272,128]{2,1,0:T(8,128)(2,1)} %bitcast.45), calls=%async_computation.5 | async-start | bytes 1114112 | tf_op jit(solution)/shard_map/all_to_all | solution.py:580
  240.7 2.9 collective-permute-start.22
  243.7 1.9 collective-permute-start.24
  245.7 1.5 collective-permute-start.23
  247.7 4.0 %layer_output.1.refs_0_ = bf16[3,256,512]{2,1,0:T(8,128)(2,1)} custom-call(s32[2]{0:T(128)} %pad_add_fusion.1.place, f32[3,256,512]{2,1,0:T(8,128)} %get-tuple-element.48.hidden, bf16[32,3,8,512]{3,2,1,0:T(8,128)(2,1)} %copy-done.2), custom_call_target="tpu_custom_call" | custom-call | flops 1179648 | bytes 3145728 | tf_op jit(solution)/shard_map/layer_output/pallas_call | solution.py:520
  251.6 15.3 %collective-permute-done.25.refs_3_ = f32[2,8,2048]{2,1,0:T(8,128)S(1)} collective-permute-done((f32[2,8,2048]{2,1,0:T(8,128)S(1)}, f32[2,8,2048]{2,1,0:T(8,128)S(1)}, u32[]{:S(2)}, u32[]{:S(2)}) %collective-permute-start.25) | collective-permute-done | bytes 131104 | tf_op jit(solution)/shard_map/ppermute | solution.py:601
  267.6 1.4 collective-permute-start.21
  270.3 1.4 slice_bitcast_fusion.1
  271.7 1.7 collective-permute-start.28
  273.3 9.1 %collective-permute-done.21.refs_2_ = bf16[2,64,2048]{2,1,0:T(8,128)(2,1)S(1)} collective-permute-done((bf16[2,64,2048]{2,1,0:T(8,128)(2,1)S(1)}, bf16[2,64,2048]{2,1,0:T(8,128)(2,1)S(1)}, u32[]{:S(2)}, u32[]{:S(2)}) %collective-permute-start.21) | collective-permute-done | bytes 524320 | tf_op jit(solution)/shard_map/ppermute | solution.py:601
  283.3 1.4 collective-permute-start.27
  285.7 4.1 %all-to-all-start.6 = ((bf16[8,272,128]{2,1,0:T(8,128)(2,1)}), bf16[8,272,128]{2,1,0:T(8,128)(2,1)S(1)}, u32[]{:S(2)}, u32[]{:S(2)}) async-start(bf16[8,272,128]{2,1,0:T(8,128)(2,1)} %broadcast_in_dim.79), calls=%async_computation.6 | async-start | bytes 1114112 | tf_op jit(solution)/shard_map/all_to_all | solution.py:583
  289.8 2.6 collective-permute-done.20.refs_1_
  292.9 2.3 collective-permute-done.28.refs_3_
  295.7 12.3 %collective-permute-done.27.refs_2_ = bf16[2,256,512]{2,1,0:T(8,128)(2,1)} collective-permute-done((bf16[2,256,512]{2,1,0:T(8,128)(2,1)}, bf16[2,256,512]{2,1,0:T(8,128)(2,1)}, u32[]{:S(2)}, u32[]{:S(2)}) %collective-permute-start.27) | collective-permute-done | bytes 524320 | tf_op jit(solution)/shard_map/ppermute | solution.py:601
  309.1 3.2 place_blocks.8
  315.6 4.6 %place_blocks.7 = f32[8,64,2048]{2,1,0:T(8,128)} custom-call(s32[4]{0:T(128)} %iota_xor_fusion.where, bf16[2,64,2048]{2,1,0:T(8,128)(2,1)} %get-tuple-element.142.refs_0_, bf16[2,64,2048]{2,1,0:T(8,128)(2,1)} %collective-permute-done.20.refs_1_, bf16[2,64,2048]{2,1,0:T(8,128)(2,1)} %copy-done.18, bf16[2,64,2048]{2,1,0:T(8,128)(2,1)} %copy-done.17), custom_call_target="tpu_custom_call" | custom-call | bytes 8388608 | tf_op jit(solution)/shard_map/place_blocks/pallas_call | solution.py:617
  321.0 4.6 %place_blocks.9 = f32[8,256,512]{2,1,0:T(8,128)} custom-call(s32[4]{0:T(128)} %iota_xor_fusion.where, bf16[2,256,512]{2,1,0:T(8,128)(2,1)} %get-tuple-element.138.refs_0_, bf16[2,256,512]{2,1,0:T(8,128)(2,1)} %copy-done.19, bf16[2,256,512]{2,1,0:T(8,128)(2,1)} %collective-permute-done.27.refs_2_, bf16[2,256,512]{2,1,0:T(8,128)(2,1)} %collective-permute-done.28.refs_3_), custom_call_target="tpu_custom_call" | custom-call | bytes 8388608 | tf_op jit(solution)/shard_map/place_blocks/pallas_call | solution.py:617
  327.4 4.7 %place_blocks.6 = bf16[12,256,512]{2,1,0:T(8,128)(2,1)} custom-call(s32[4]{0:T(128)} %copy-done.31, bf16[3,256,512]{2,1,0:T(8,128)(2,1)} %get-tuple-element.77.refs_0_, bf16[3,256,512]{2,1,0:T(8,128)(2,1)} %copy-done.8, bf16[3,256,512]{2,1,0:T(8,128)(2,1)} %copy-done.10, bf16[3,256,512]{2,1,0:T(8,128)(2,1)} %copy-done.12), custom_call_target="tpu_custom_call" | custom-call | bytes 12582912 | tf_op jit(solution)/shard_map/place_blocks/pallas_call | solution.py:617
  333.9 4.7 %place_blocks.5 = bf16[12,256,512]{2,1,0:T(8,128)(2,1)} custom-call(s32[4]{0:T(128)} %copy-done.31, bf16[3,256,512]{2,1,0:T(8,128)(2,1)} %layer_output.1.refs_0_, bf16[3,256,512]{2,1,0:T(8,128)(2,1)} %copy-done.9, bf16[3,256,512]{2,1,0:T(8,128)(2,1)} %copy-done.11, bf16[3,256,512]{2,1,0:T(8,128)(2,1)} %copy-done.13), custom_call_target="tpu_custom_call" | custom-call | bytes 12582912 | tf_op jit(solution)/shard_map/place_blocks/pallas_call | solution.py:617
  (176 shorter events, 37.8 us)
Async XLA Ops:
  2.9 9.9 %copy-start.30 = (bf16[512,8]{0,1:T(8,128)(2,1)S(1)}, bf16[512,8]{0,1:T(8,128)(2,1)}, u32[]{:S(2)}) copy-start(bf16[512,8]{0,1:T(8,128)(2,1)} %param.25) | copy-start | bytes 24580
  2.9 10.6 %copy-start.32 = (s32[8]{0:T(128)S(1)}, s32[8]{0:T(128)}, u32[]{:S(2)}) copy-start(s32[8]{0:T(128)} %param.17) | copy-start | bytes 100
  2.9 47.7 %all-to-all-start.1 = ((bf16[32,3,8,512]{3,2,1,0:T(8,128)(2,1)}), bf16[32,3,8,512]{3,2,1,0:T(8,128)(2,1)S(1)}, u32[]{:S(2)}, u32[]{:S(2)}) async-start(bf16[32,3,8,512]{3,2,1,0:T(8,128)(2,1)} %copy.75), calls=%async_computation.1 | async-start | bytes 1572864 | tf_op jit(solution)/shard_map/all_to_all | solution.py:697
  10.9 24.8 %copy-start.20 = (bf16[512,512]{1,0:T(8,128)(2,1)}, bf16[512,512]{1,0:T(8,128)(2,1)S(1)}, u32[]{:S(2)}) copy-start(bf16[512,512]{1,0:T(8,128)(2,1)S(1)} %copy.86.refs_0_) | copy-start | bytes 1572868
  10.9 21.9 %collective-permute-start = (bf16[512,512]{1,0:T(8,128)(2,1)S(1)}, bf16[512,512]{1,0:T(8,128)(2,1)S(1)}, u32[]{:S(2)}, u32[]{:S(2)}) collective-permute-start(bf16[512,512]{1,0:T(8,128)(2,1)S(1)} %copy.86.refs_0_), channel_id=1, source_target_pairs={{2,0},{3,1},{0,2},{1,3},{6,4},{7,5},{4,6},{5,7},{10,8},{11,9},{8,1... | collective-permute-start | bytes 1572872 | tf_op jit(solution)/shard_map/ppermute | solution.py:547
  12.7 42.8 %collective-permute-start.3 = (bf16[8,512]{1,0:T(8,128)(2,1)S(1)}, bf16[8,512]{1,0:T(8,128)(2,1)S(1)}, u32[]{:S(2)}, u32[]{:S(2)}) collective-permute-start(bf16[8,512]{1,0:T(8,128)(2,1)S(1)} %bitcast.114), channel_id=1, source_target_pairs={{2,0},{3,1},{0,2},{1,3},{6,4},{7,5},{4,6},{5,7},{10,8},{11,9},{8,1... | collective-permute-start | bytes 24584 | tf_op jit(solution)/shard_map/ppermute | solution.py:547
  13.0 45.1 %collective-permute-start.4 = (bf16[8,512]{1,0:T(8,128)(2,1)S(1)}, bf16[8,512]{1,0:T(8,128)(2,1)S(1)}, u32[]{:S(2)}, u32[]{:S(2)}) collective-permute-start(bf16[8,512]{1,0:T(8,128)(2,1)S(1)} %bitcast.115), channel_id=1, source_target_pairs={{0,1},{1,0},{2,3},{3,2},{4,5},{5,4},{6,7},{7,6},{8,9},{9,8},{10,11... | collective-permute-start | bytes 24584 | tf_op jit(solution)/shard_map/ppermute | solution.py:542
  13.0 22.7 %collective-permute-start.1 = (bf16[512,512]{1,0:T(8,128)(2,1)S(1)}, bf16[512,512]{1,0:T(8,128)(2,1)S(1)}, u32[]{:S(2)}, u32[]{:S(2)}) collective-permute-start(bf16[512,512]{1,0:T(8,128)(2,1)S(1)} %copy.86.refs_0_), channel_id=1, source_target_pairs={{0,1},{1,0},{2,3},{3,2},{4,5},{5,4},{6,7},{7,6},{8,9},{9,8},{10,11... | collective-permute-start | bytes 1572872 | tf_op jit(solution)/shard_map/ppermute | solution.py:542
  32.8 2.9 collective-permute-start.2
  33.7 16.9 %copy-start.31 = (s32[4]{0:T(128)}, s32[4]{0:T(128)S(1)}, u32[]{:S(2)}) copy-start(s32[4]{0:T(128)S(1)} %pad_add_fusion.relative.where) | copy-start | bytes 52
  36.5 18.7 %copy-start.33 = (s32[64]{0:T(128)S(1)}, s32[64]{0:T(128)}, u32[]{:S(2)}) copy-start(s32[64]{0:T(128)} %param.18) | copy-start | bytes 772
  50.6 25.3 %copy-start.14 = (bf16[32,3,8,512]{3,2,1,0:T(8,128)(2,1)}, bf16[32,3,8,512]{3,2,1,0:T(8,128)(2,1)S(1)}, u32[]{:S(2)}) copy-start(bf16[32,3,8,512]{3,2,1,0:T(8,128)(2,1)S(1)} %all-to-all-done.1) | copy-start | bytes 2359300
  50.6 25.2 %all-to-all-start = ((bf16[32,3,8,512]{3,2,1,0:T(8,128)(2,1)}), bf16[32,3,8,512]{3,2,1,0:T(8,128)(2,1)S(1)}, u32[]{:S(2)}, u32[]{:S(2)}) async-start(bf16[32,3,8,512]{3,2,1,0:T(8,128)(2,1)} %get-tuple-element.49), calls=%async_computation | async-start | bytes 1572864 | tf_op jit(solution)/shard_map/all_to_all | solution.py:697
  55.5 2.6 collective-permute-start.5
  82.0 9.4 %collective-permute-start.6 = (bf16[2,128,512]{2,1,0:T(8,128)(2,1)}, bf16[2,128,512]{2,1,0:T(8,128)(2,1)S(1)}, u32[]{:S(2)}, u32[]{:S(2)}) collective-permute-start(bf16[2,128,512]{2,1,0:T(8,128)(2,1)} %get-tuple-element.54), channel_id=1, source_target_pairs={{0,2},{1,3},{2,0},{3,1},{4,6},{5,7},{6,4},{7,5},{8,10},{9,11},{10,... | collective-permute-start | bytes 786440 | tf_op jit(solution)/shard_map/ppermute | solution.py:590
  83.5 7.9 %collective-permute-start.7 = (bf16[2,128,512]{2,1,0:T(8,128)(2,1)}, bf16[2,128,512]{2,1,0:T(8,128)(2,1)S(1)}, u32[]{:S(2)}, u32[]{:S(2)}) collective-permute-start(bf16[2,128,512]{2,1,0:T(8,128)(2,1)} %get-tuple-element.55), channel_id=1, source_target_pairs={{0,1},{1,0},{2,3},{3,2},{4,5},{5,4},{6,7},{7,6},{8,9},{9,8},{10,11... | collective-permute-start | bytes 786440 | tf_op jit(solution)/shard_map/ppermute | solution.py:590
  83.5 11.8 %collective-permute-start.8 = (bf16[2,128,512]{2,1,0:T(8,128)(2,1)}, bf16[2,128,512]{2,1,0:T(8,128)(2,1)S(1)}, u32[]{:S(2)}, u32[]{:S(2)}) collective-permute-start(bf16[2,128,512]{2,1,0:T(8,128)(2,1)} %get-tuple-element.56), channel_id=1, source_target_pairs={{0,3},{1,2},{2,1},{3,0},{4,7},{5,6},{6,5},{7,4},{8,11},{9,10},{10,... | collective-permute-start | bytes 786440 | tf_op jit(solution)/shard_map/ppermute | solution.py:590
  98.1 52.9 %all-to-all-start.2 = ((bf16[8,2,4,2,16,512]{5,4,3,2,1,0:T(8,128)(2,1)}), bf16[8,2,4,2,16,512]{5,4,3,2,1,0:T(8,128)(2,1)S(1)}, u32[]{:S(2)}, u32[]{:S(2)}) async-start(bf16[8,2,4,2,16,512]{5,4,3,2,1,0:T(8,128)(2,1)} %pad_maximum_fusion), calls=%async_computation.2 | async-start | bytes 4194304 | tf_op jit(solution)/shard_map/all_to_all | solution.py:737
  124.1 9.4 %collective-permute-start.9 = (bf16[2,128,512]{2,1,0:T(8,128)(2,1)}, bf16[2,128,512]{2,1,0:T(8,128)(2,1)S(1)}, u32[]{:S(2)}, u32[]{:S(2)}) collective-permute-start(bf16[2,128,512]{2,1,0:T(8,128)(2,1)} %get-tuple-element.62), channel_id=1, source_target_pairs={{2,0},{3,1},{0,2},{1,3},{6,4},{7,5},{4,6},{5,7},{10,8},{11,9},{8,1... | collective-permute-start | bytes 786440 | tf_op jit(solution)/shard_map/ppermute | solution.py:596
  125.8 7.7 %collective-permute-start.10 = (bf16[2,128,512]{2,1,0:T(8,128)(2,1)}, bf16[2,128,512]{2,1,0:T(8,128)(2,1)S(1)}, u32[]{:S(2)}, u32[]{:S(2)}) collective-permute-start(bf16[2,128,512]{2,1,0:T(8,128)(2,1)} %get-tuple-element.63), channel_id=1, source_target_pairs={{1,0},{0,1},{3,2},{2,3},{5,4},{4,5},{7,6},{6,7},{9,8},{8,9},{11,10... | collective-permute-start | bytes 786440 | tf_op jit(solution)/shard_map/ppermute | solution.py:596
  126.1 12.1 %collective-permute-start.11 = (bf16[2,128,512]{2,1,0:T(8,128)(2,1)}, bf16[2,128,512]{2,1,0:T(8,128)(2,1)S(1)}, u32[]{:S(2)}, u32[]{:S(2)}) collective-permute-start(bf16[2,128,512]{2,1,0:T(8,128)(2,1)} %get-tuple-element.64), channel_id=1, source_target_pairs={{3,0},{2,1},{1,2},{0,3},{7,4},{6,5},{5,6},{4,7},{11,8},{10,9},{9,1... | collective-permute-start | bytes 786440 | tf_op jit(solution)/shard_map/ppermute | solution.py:596
  151.0 27.6 %all-to-all-start.3 = ((bf16[32,3,8,512]{3,2,1,0:T(8,128)(2,1)}), bf16[32,3,8,512]{3,2,1,0:T(8,128)(2,1)S(1)}, u32[]{:S(2)}, u32[]{:S(2)}) async-start(bf16[32,3,8,512]{3,2,1,0:T(8,128)(2,1)} %bitcast.102), calls=%async_computation.3 | async-start | bytes 1572864 | tf_op jit(solution)/shard_map/all_to_all | solution.py:703
  204.2 5.7 %collective-permute-start.18 = (bf16[2,2176,128]{2,1,0:T(8,128)(2,1)}, bf16[2,2176,128]{2,1,0:T(8,128)(2,1)}, u32[]{:S(2)}, u32[]{:S(2)}) collective-permute-start(bf16[2,2176,128]{2,1,0:T(8,128)(2,1)} %slice.98), channel_id=1, source_target_pairs={{0,1},{1,0},{2,3},{3,2},{4,5},{5,4},{6,7},{7,6},{8,9},{9,8},{10,11... | collective-permute-start | bytes 3342344 | tf_op jit(solution)/shard_map/ppermute | solution.py:542
  204.3 29.8 %all-to-all-start.4 = ((bf16[32,3,8,512]{3,2,1,0:T(8,128)(2,1)}), bf16[32,3,8,512]{3,2,1,0:T(8,128)(2,1)S(1)}, u32[]{:S(2)}, u32[]{:S(2)}) async-start(bf16[32,3,8,512]{3,2,1,0:T(8,128)(2,1)} %bitcast.101), calls=%async_computation.4 | async-start | bytes 1572864 | tf_op jit(solution)/shard_map/all_to_all | solution.py:703
  211.4 28.2 %copy-start.4 = (bf16[4,2,64,2048]{3,2,1,0:T(8,128)(2,1)S(1)}, bf16[4,2,64,2048]{3,2,1,0:T(8,128)(2,1)}, u32[]{:S(2)}) copy-start(bf16[4,2,64,2048]{3,2,1,0:T(8,128)(2,1)} %get-tuple-element.80) | copy-start | bytes 6291460
  211.5 21.7 %collective-permute-start.19 = (bf16[2176,128]{1,0:T(8,128)(2,1)S(1)}, bf16[2176,128]{1,0:T(8,128)(2,1)S(1)}, u32[]{:S(2)}, u32[]{:S(2)}) collective-permute-start(bf16[2176,128]{1,0:T(8,128)(2,1)S(1)} %fusion.5), channel_id=1, source_target_pairs={{0,2},{1,3},{2,0},{3,1},{4,6},{5,7},{6,4},{7,5},{8,10},{9,11},{10,... | collective-permute-start | bytes 1671176 | tf_op jit(solution)/shard_map/ppermute | solution.py:552
  234.1 50.6 %all-to-all-start.5 = ((bf16[8,272,128]{2,1,0:T(8,128)(2,1)}), bf16[8,272,128]{2,1,0:T(8,128)(2,1)S(1)}, u32[]{:S(2)}, u32[]{:S(2)}) async-start(bf16[8,272,128]{2,1,0:T(8,128)(2,1)} %bitcast.45), calls=%async_computation.5 | async-start | bytes 1114112 | tf_op jit(solution)/shard_map/all_to_all | solution.py:580
  240.7 29.5 %copy-start.3 = (bf16[4,2,256,512]{3,2,1,0:T(8,128)(2,1)S(1)}, bf16[4,2,256,512]{3,2,1,0:T(8,128)(2,1)}, u32[]{:S(2)}) copy-start(bf16[4,2,256,512]{3,2,1,0:T(8,128)(2,1)} %get-tuple-element.82) | copy-start | bytes 6291460
  240.7 30.9 %collective-permute-start.22 = (bf16[2,64,2048]{2,1,0:T(8,128)(2,1)S(1)}, bf16[2,64,2048]{2,1,0:T(8,128)(2,1)S(1)}, u32[]{:S(2)}, u32[]{:S(2)}) collective-permute-start(bf16[2,64,2048]{2,1,0:T(8,128)(2,1)S(1)} %get-tuple-element.139), channel_id=1, source_target_pairs={{0,12},{4,8},{8,4},{12,0},{16,28},{20,24},{24,20},{28,16},{1,13},{... | collective-permute-start | bytes 1572872 | tf_op jit(solution)/shard_map/ppermute | solution.py:601
  243.6 23.3 %collective-permute-start.25 = (f32[2,8,2048]{2,1,0:T(8,128)S(1)}, f32[2,8,2048]{2,1,0:T(8,128)S(1)}, u32[]{:S(2)}, u32[]{:S(2)}) collective-permute-start(f32[2,8,2048]{2,1,0:T(8,128)S(1)} %copy-done.25), channel_id=1, source_target_pairs={{0,12},{4,8},{8,4},{12,0},{16,28},{20,24},{24,20},{28,16},{1,13},{... | collective-permute-start | bytes 393224 | tf_op jit(solution)/shard_map/ppermute | solution.py:601
  243.7 25.3 %collective-permute-start.24 = (f32[2,8,2048]{2,1,0:T(8,128)S(1)}, f32[2,8,2048]{2,1,0:T(8,128)S(1)}, u32[]{:S(2)}, u32[]{:S(2)}) collective-permute-start(f32[2,8,2048]{2,1,0:T(8,128)S(1)} %copy-done.25), channel_id=1, source_target_pairs={{0,8},{4,12},{8,0},{12,4},{16,24},{20,28},{24,16},{28,20},{1,9},{5... | collective-permute-start | bytes 393224 | tf_op jit(solution)/shard_map/ppermute | solution.py:601
  245.7 24.0 %collective-permute-start.23 = (f32[2,8,2048]{2,1,0:T(8,128)S(1)}, f32[2,8,2048]{2,1,0:T(8,128)}, u32[]{:S(2)}, u32[]{:S(2)}) collective-permute-start(f32[2,8,2048]{2,1,0:T(8,128)S(1)} %copy-done.25), channel_id=1, source_target_pairs={{0,4},{4,0},{8,12},{12,8},{16,20},{20,16},{24,28},{28,24},{1,5},{5... | collective-permute-start | bytes 393224 | tf_op jit(solution)/shard_map/ppermute | solution.py:601
  247.1 45.3 %collective-permute-start.15 = (bf16[3,256,512]{2,1,0:T(8,128)(2,1)}, bf16[3,256,512]{2,1,0:T(8,128)(2,1)S(1)}, u32[]{:S(2)}, u32[]{:S(2)}) collective-permute-start(bf16[3,256,512]{2,1,0:T(8,128)(2,1)} %get-tuple-element.77.refs_0_), channel_id=1, source_target_pairs={{2,0},{3,1},{0,2},{1,3},{6,4},{7,5},{4,6},{5,7},{10,8},{11,9},{8,1... | collective-permute-start | bytes 2359304 | tf_op jit(solution)/shard_map/ppermute | solution.py:547
  267.6 14.9 %collective-permute-start.21 = (bf16[2,64,2048]{2,1,0:T(8,128)(2,1)S(1)}, bf16[2,64,2048]{2,1,0:T(8,128)(2,1)S(1)}, u32[]{:S(2)}, u32[]{:S(2)}) collective-permute-start(bf16[2,64,2048]{2,1,0:T(8,128)(2,1)S(1)} %get-tuple-element.140), channel_id=1, source_target_pairs={{0,8},{4,12},{8,0},{12,4},{16,24},{20,28},{24,16},{28,20},{1,9},{5... | collective-permute-start | bytes 1572872 | tf_op jit(solution)/shard_map/ppermute | solution.py:601
  269.0 23.4 %collective-permute-start.20 = (bf16[2,64,2048]{2,1,0:T(8,128)(2,1)}, bf16[2,64,2048]{2,1,0:T(8,128)(2,1)}, u32[]{:S(2)}, u32[]{:S(2)}) collective-permute-start(bf16[2,64,2048]{2,1,0:T(8,128)(2,1)} %get-tuple-element.141), channel_id=1, source_target_pairs={{0,4},{4,0},{8,12},{12,8},{16,20},{20,16},{24,28},{28,24},{1,5},{5... | collective-permute-start | bytes 1572872 | tf_op jit(solution)/shard_map/ppermute | solution.py:601
  269.7 25.5 %collective-permute-start.12 = (bf16[3,256,512]{2,1,0:T(8,128)(2,1)}, bf16[3,256,512]{2,1,0:T(8,128)(2,1)S(1)}, u32[]{:S(2)}, u32[]{:S(2)}) collective-permute-start(bf16[3,256,512]{2,1,0:T(8,128)(2,1)} %layer_output.1.refs_0_), channel_id=1, source_target_pairs={{2,0},{3,1},{0,2},{1,3},{6,4},{7,5},{4,6},{5,7},{10,8},{11,9},{8,1... | collective-permute-start | bytes 2359304 | tf_op jit(solution)/shard_map/ppermute | solution.py:547
  271.6 23.5 %copy-start.1 = (bf16[3,256,512]{2,1,0:T(8,128)(2,1)S(1)}, bf16[3,256,512]{2,1,0:T(8,128)(2,1)}, u32[]{:S(2)}) copy-start(bf16[3,256,512]{2,1,0:T(8,128)(2,1)} %layer_output.1.refs_0_) | copy-start | bytes 2359300
  271.7 43.9 %copy-start.17 = (bf16[2,64,2048]{2,1,0:T(8,128)(2,1)}, bf16[2,64,2048]{2,1,0:T(8,128)(2,1)S(1)}, u32[]{:S(2)}) copy-start(bf16[2,64,2048]{2,1,0:T(8,128)(2,1)S(1)} %collective-permute-done.22.refs_3_) | copy-start | bytes 1572868
  271.7 23.5 %collective-permute-start.28 = (bf16[2,256,512]{2,1,0:T(8,128)(2,1)}, bf16[2,256,512]{2,1,0:T(8,128)(2,1)}, u32[]{:S(2)}, u32[]{:S(2)}) collective-permute-start(bf16[2,256,512]{2,1,0:T(8,128)(2,1)} %get-tuple-element.135), channel_id=1, source_target_pairs={{0,12},{4,8},{8,4},{12,0},{16,28},{20,24},{24,20},{28,16},{1,13},{... | collective-permute-start | bytes 1572872 | tf_op jit(solution)/shard_map/ppermute | solution.py:601
  283.3 24.8 %collective-permute-start.27 = (bf16[2,256,512]{2,1,0:T(8,128)(2,1)}, bf16[2,256,512]{2,1,0:T(8,128)(2,1)}, u32[]{:S(2)}, u32[]{:S(2)}) collective-permute-start(bf16[2,256,512]{2,1,0:T(8,128)(2,1)} %get-tuple-element.136), channel_id=1, source_target_pairs={{0,8},{4,12},{8,0},{12,4},{16,24},{20,28},{24,16},{28,20},{1,9},{5... | collective-permute-start | bytes 1572872 | tf_op jit(solution)/shard_map/ppermute | solution.py:601
  285.7 52.9 %all-to-all-start.6 = ((bf16[8,272,128]{2,1,0:T(8,128)(2,1)}), bf16[8,272,128]{2,1,0:T(8,128)(2,1)S(1)}, u32[]{:S(2)}, u32[]{:S(2)}) async-start(bf16[8,272,128]{2,1,0:T(8,128)(2,1)} %broadcast_in_dim.79), calls=%async_computation.6 | async-start | bytes 1114112 | tf_op jit(solution)/shard_map/all_to_all | solution.py:583
  292.4 33.3 %collective-permute-start.16 = (bf16[3,256,512]{2,1,0:T(8,128)(2,1)}, bf16[3,256,512]{2,1,0:T(8,128)(2,1)S(1)}, u32[]{:S(2)}, u32[]{:S(2)}) collective-permute-start(bf16[3,256,512]{2,1,0:T(8,128)(2,1)} %get-tuple-element.77.refs_0_), channel_id=1, source_target_pairs={{0,1},{1,0},{2,3},{3,2},{4,5},{5,4},{6,7},{7,6},{8,9},{9,8},{10,11... | collective-permute-start | bytes 2359304 | tf_op jit(solution)/shard_map/ppermute | solution.py:542
  292.4 27.8 %copy-start.8 = (bf16[3,256,512]{2,1,0:T(8,128)(2,1)}, bf16[3,256,512]{2,1,0:T(8,128)(2,1)S(1)}, u32[]{:S(2)}) copy-start(bf16[3,256,512]{2,1,0:T(8,128)(2,1)S(1)} %collective-permute-done.15.refs_1_) | copy-start | bytes 2359300
  292.4 33.3 %collective-permute-start.17 = (bf16[3,256,512]{2,1,0:T(8,128)(2,1)S(1)}, bf16[3,256,512]{2,1,0:T(8,128)(2,1)S(1)}, u32[]{:S(2)}, u32[]{:S(2)}) collective-permute-start(bf16[3,256,512]{2,1,0:T(8,128)(2,1)S(1)} %collective-permute-done.15.refs_1_), channel_id=1, source_target_pairs={{0,1},{1,0},{2,3},{3,2},{4,5},{5,4},{6,7},{7,6},{8,9},{9,8},{10,11... | collective-permute-start | bytes 2359304 | tf_op jit(solution)/shard_map/ppermute | solution.py:542
  295.2 36.9 %collective-permute-start.13 = (bf16[3,256,512]{2,1,0:T(8,128)(2,1)S(1)}, bf16[3,256,512]{2,1,0:T(8,128)(2,1)S(1)}, u32[]{:S(2)}, u32[]{:S(2)}) collective-permute-start(bf16[3,256,512]{2,1,0:T(8,128)(2,1)S(1)} %copy-done.1), channel_id=1, source_target_pairs={{0,1},{1,0},{2,3},{3,2},{4,5},{5,4},{6,7},{7,6},{8,9},{9,8},{10,11... | collective-permute-start | bytes 2359304 | tf_op jit(solution)/shard_map/ppermute | solution.py:542
  295.2 25.0 %copy-start.9 = (bf16[3,256,512]{2,1,0:T(8,128)(2,1)}, bf16[3,256,512]{2,1,0:T(8,128)(2,1)S(1)}, u32[]{:S(2)}) copy-start(bf16[3,256,512]{2,1,0:T(8,128)(2,1)S(1)} %collective-permute-done.12.refs_1_) | copy-start | bytes 2359300
  295.2 36.9 %collective-permute-start.14 = (bf16[3,256,512]{2,1,0:T(8,128)(2,1)S(1)}, bf16[3,256,512]{2,1,0:T(8,128)(2,1)S(1)}, u32[]{:S(2)}, u32[]{:S(2)}) collective-permute-start(bf16[3,256,512]{2,1,0:T(8,128)(2,1)S(1)} %collective-permute-done.12.refs_1_), channel_id=1, source_target_pairs={{0,1},{1,0},{2,3},{3,2},{4,5},{5,4},{6,7},{7,6},{8,9},{9,8},{10,11... | collective-permute-start | bytes 2359304 | tf_op jit(solution)/shard_map/ppermute | solution.py:542
  308.0 12.2 %collective-permute-start.26 = (bf16[2,256,512]{2,1,0:T(8,128)(2,1)}, bf16[2,256,512]{2,1,0:T(8,128)(2,1)S(1)}, u32[]{:S(2)}, u32[]{:S(2)}) collective-permute-start(bf16[2,256,512]{2,1,0:T(8,128)(2,1)} %get-tuple-element.137), channel_id=1, source_target_pairs={{0,4},{4,0},{8,12},{12,8},{16,20},{20,16},{24,28},{28,24},{1,5},{5... | collective-permute-start | bytes 1572872 | tf_op jit(solution)/shard_map/ppermute | solution.py:601
  (27 other events, 99.5 us)

commit v3 on v2

v3 whole, which is shorter than its diff:
```python
import functools

import jax
import jax.numpy as jnp
from jax import lax
from jax.experimental import pallas as pl
from jax.experimental.pallas import tpu as pltpu
from jax.sharding import PartitionSpec as P

HEAD_WIDTH = 64
GROUP = 32
GROUPS = 2
LANES = 128

EPSILON = 1e-05
NEGATIVE = -1e30
BOTH = ("wide", "narrow")
F32 = jnp.float32
BF16 = jnp.bfloat16
VMEM_LIMIT = 56 * 1024 * 1024


def mm(a, b):
    return lax.dot_general(a, b, (((1,), (0,)), ((), ())), preferred_element_type=F32)


def mm_nt(a, b):
    return lax.dot_general(a, b, (((1,), (1,)), ((), ())), preferred_element_type=F32)


def mm_tn(a, b):
    return lax.dot_general(a, b, (((0,), (0,)), ((), ())), preferred_element_type=F32)


def params(*semantics):
    return pltpu.CompilerParams(dimension_semantics=semantics or None, vmem_limit_bytes=VMEM_LIMIT)


def whole(shape):
    zeros = (0,) * len(shape)
    return pl.BlockSpec(tuple(shape), lambda *_: zeros)


def head_masks(rows):
    lane = lax.broadcasted_iota(jnp.int32, (rows, LANES), 1)
    return [(lane >= h * HEAD_WIDTH) & (lane < (h + 1) * HEAD_WIDTH) for h in range(LANES // HEAD_WIDTH)]


def keep(mask, rows):
    return jnp.where(mask, rows, jnp.zeros_like(rows))


def causal_probs(query_head, keys, causal):
    scores = mm_nt(query_head, keys) * (float(HEAD_WIDTH) ** -0.5)
    scores = jnp.where(causal, scores, NEGATIVE)
    powers = jnp.exp(scores - jnp.max(scores, axis=-1, keepdims=True))
    return powers * (1.0 / jnp.sum(powers, axis=-1, keepdims=True))


def causal_mask(length):
    return lax.broadcasted_iota(jnp.int32, (length, length), 0) >= lax.broadcasted_iota(
        jnp.int32, (length, length), 1
    )


def inverse_rms(rows):
    return lax.rsqrt(jnp.mean(rows * rows, axis=-1, keepdims=True) + EPSILON)


def attend(entry, packs, causal, masks, joint_out, context_out):
    attention = None
    for j, pack in enumerate(packs):
        joint = mm(entry, pack[:, : 3 * LANES]).astype(BF16)
        joint_out[0, :, j * 3 * LANES : (j + 1) * 3 * LANES] = joint
        q, k, v = (joint[:, i * LANES : (i + 1) * LANES] for i in range(3))
        context = None
        for mask in masks:
            probs = causal_probs(keep(mask, q), k, causal)
            term = mm(probs.astype(BF16), keep(mask, v))
            context = term if context is None else context + term
        context = context.astype(BF16)
        context_out[0, :, j * LANES : (j + 1) * LANES] = context
        term = mm_nt(context, pack[:, 3 * LANES :])
        attention = term if attention is None else attention + term
    return attention


def near_kernel(blocks, place, tokens, *refs):
    packs, (gain_attn, partial_out, joint_out, context_out) = refs[:blocks], refs[blocks:]
    rows = tokens[0].astype(F32)
    entry = (rows * inverse_rms(rows) * gain_attn[...]).astype(BF16)
    length = rows.shape[0]
    partial_out[0] = rows + attend(
        entry, packs, causal_mask(length), head_masks(length), joint_out, context_out
    )


def far_kernel(blocks, place, tokens, partial, *refs):
    packs = refs[:blocks]
    gain_attn, gain_mix, mix_out, hidden_out, joint_out, context_out = refs[blocks:]
    rows = tokens[0].astype(F32)
    entry = (rows * inverse_rms(rows) * gain_attn[...]).astype(BF16)
    length = rows.shape[0]
    hidden = partial[0] + attend(
        entry, packs, causal_mask(length), head_masks(length), joint_out, context_out
    )
    mixed = hidden * inverse_rms(hidden) * gain_mix[...]
    mix_out[...] = mixed.reshape(mix_out.shape).astype(BF16)
    hidden_out[0] = hidden


def local_block(i, place):
    return (i, 0, 0)


def attention_near(place, tokens, packs, gain_attn, slots):
    total, length, width = tokens.shape
    inner = len(packs) * LANES
    return pl.pallas_call(
        functools.partial(near_kernel, len(packs)),
        grid_spec=pltpu.PrefetchScalarGridSpec(
            num_scalar_prefetch=1,
            grid=(slots,),
            in_specs=[
                pl.BlockSpec((1, length, width), lambda i, place: (jnp.minimum(place[0] + i, total - 1), 0, 0))
            ]
            + [whole(p.shape) for p in packs]
            + [whole((1, width))],
            out_specs=[
                pl.BlockSpec((1, length, width), local_block),
                pl.BlockSpec((1, length, 3 * inner), local_block),
                pl.BlockSpec((1, length, inner), local_block),
            ],
        ),
        out_shape=[
            jax.ShapeDtypeStruct((slots, length, width), F32),
            jax.ShapeDtypeStruct((slots, length, 3 * inner), BF16),
            jax.ShapeDtypeStruct((slots, length, inner), BF16),
        ],
        compiler_params=params("arbitrary"),
        cost_estimate=pl.CostEstimate(
            flops=slots * 2 * length * (4 * width * inner + 4 * length * inner),
            bytes_accessed=slots * length * (width * 6 + inner * 8) + 8 * width * inner,
            transcendentals=slots * length * length * inner // HEAD_WIDTH,
        ),
        name="attention_near",
    )(place, tokens, *packs, gain_attn)


def attention_far(place, tokens, partial, packs, gain_attn, gain_mix, slots, spread):
    total, length, width = tokens.shape
    inner = len(packs) * LANES
    part = length // spread
    return pl.pallas_call(
        functools.partial(far_kernel, len(packs)),
        grid_spec=pltpu.PrefetchScalarGridSpec(
            num_scalar_prefetch=1,
            grid=(slots,),
            in_specs=[
                pl.BlockSpec((1, length, width), lambda i, place: (jnp.minimum(place[0] + i, total - 1), 0, 0)),
                pl.BlockSpec((1, length, width), local_block),
            ]
            + [whole(p.shape) for p in packs]
            + [whole((1, width))] * 2,
            out_specs=[
                pl.BlockSpec((spread, 1, part, width), lambda i, place: (0, i, 0, 0)),
                pl.BlockSpec((1, length, width), local_block),
                pl.BlockSpec((1, length, 3 * inner), local_block),
                pl.BlockSpec((1, length, inner), local_block),
            ],
        ),
        out_shape=[
            jax.ShapeDtypeStruct((spread, slots, part, width), BF16),
            jax.ShapeDtypeStruct((slots, length, width), F32),
            jax.ShapeDtypeStruct((slots, length, 3 * inner), BF16),
            jax.ShapeDtypeStruct((slots, length, inner), BF16),
        ],
        compiler_params=params("arbitrary"),
        cost_estimate=pl.CostEstimate(
            flops=slots * 2 * length * (4 * width * inner + 4 * length * inner),
            bytes_accessed=slots * length * (width * 12 + inner * 8) + 8 * width * inner,
            transcendentals=slots * length * length * inner // HEAD_WIDTH,
        ),
        name="attention_far",
    )(place, tokens, partial, *packs, gain_attn, gain_mix)


def pack_kernel(query, key, value, output, out):
    width = query.shape[1]
    for i, ref in enumerate((query, key, value)):
        out[:, i * width : (i + 1) * width] = ref[...]
    out[:, 3 * width :] = output[...].T


def pack_weights(query, key, value, output):
    width, columns = query.shape
    if columns % LANES:
        return jnp.concatenate([query, key, value, output.T], axis=1)
    return pl.pallas_call(
        pack_kernel,
        out_shape=jax.ShapeDtypeStruct((width, 4 * columns), BF16),
        compiler_params=params(),
        cost_estimate=pl.CostEstimate(flops=0, bytes_accessed=16 * width * columns, transcendentals=0),
        name="pack_weights",
    )(query, key, value, output)


def slot_softmax(logits, codes, part):
    experts = logits.shape[1]
    logits = logits.reshape(-1, part, experts)
    codes = jnp.broadcast_to(codes, (codes.shape[0], experts)).reshape(-1, part, experts)
    total = jnp.zeros_like(logits)
    for g in range(GROUPS):
        inside = (codes >= g * part) & (codes < (g + 1) * part)
        held = jnp.where(inside, logits, NEGATIVE)
        powers = jnp.where(inside, jnp.exp(held - jnp.max(held, axis=0, keepdims=True)), 0.0)
        total = total + powers / jnp.sum(powers, axis=0, keepdims=True)
    return total.reshape(-1, experts)


def group_totals(terms, codes, part):
    experts = terms.shape[1]
    terms = terms.reshape(-1, part, experts)
    codes = jnp.broadcast_to(codes, (codes.shape[0], experts)).reshape(-1, part, experts)
    total = jnp.zeros_like(terms)
    for g in range(GROUPS):
        inside = (codes >= g * part) & (codes < (g + 1) * part)
        total = jnp.where(inside, jnp.sum(jnp.where(inside, terms, 0.0), axis=0, keepdims=True), total)
    return total.reshape(-1, experts)


def mix_kernel(part, relative, rows, cots, controller, row_code, col_code, tile, probs_out, spread_out, *refs):
    sent, (merged, grads) = refs[:-2], refs[-2:]
    held = rows[...]
    probs = slot_softmax(mm(held, controller[...]), row_code[...], part)
    probs_out[...] = probs
    wide = mm(probs.astype(BF16), tile[...])
    spread = jnp.where(row_code[...] == col_code[...], wide, 0.0).astype(BF16)
    spread_out[...] = spread
    count, _, lines, _ = sent[0].shape
    merged[...] = mm_tn(spread, held).astype(BF16)
    grads[...] = mm_tn(spread, cots[...]).astype(BF16)
    for j, out in enumerate(sent):
        for e in range(count):
            at = pl.ds(pl.multiple_of((relative[j] * count + e) * lines, lines), lines)
            out[e, 0] = merged[at]
            out[e, 1] = grads[at]


def mix_forward(part, relative, rows, cots, controller, row_code, col_code, tile, narrow):
    count, width = rows.shape
    experts, columns = tile.shape
    sent = (experts // narrow, 2, columns // experts, width)
    return pl.pallas_call(
        functools.partial(mix_kernel, part),
        grid_spec=pltpu.PrefetchScalarGridSpec(
            num_scalar_prefetch=1,
            grid=(1,),
            in_specs=[whole(x.shape) for x in (rows, cots, controller, row_code, col_code, tile)],
            out_specs=[whole((count, experts)), whole((count, columns))]
            + [whole(sent)] * narrow,
            scratch_shapes=[pltpu.VMEM((columns, width), BF16)] * 2,
        ),
        out_shape=[
            jax.ShapeDtypeStruct((count, experts), F32),
            jax.ShapeDtypeStruct((count, columns), BF16),
        ]
        + [jax.ShapeDtypeStruct(sent, BF16)] * narrow,
        compiler_params=params("arbitrary"),
        cost_estimate=pl.CostEstimate(
            flops=4 * count * columns * width,
            bytes_accessed=6 * count * width * 2,
            transcendentals=count * experts * 2,
        ),
        name="mix_forward",
    )(relative, rows, cots, controller, row_code, col_code, tile)


def unmix_kernel(
    part, narrow, relative, spread, rows, cots, probs, controller, row_code, col_code, tile, *refs
):
    back, (grad_out, mixed_out, gain_out, outs, grads) = refs[:narrow], refs[narrow:]
    count, _, lines, _ = back[0].shape
    for j, piece in enumerate(back):
        for e in range(count):
            at = pl.ds(pl.multiple_of((relative[j] * count + e) * lines, lines), lines)
            outs[at] = piece[e, 0]
            grads[at] = piece[e, 1]
    held = rows[...]
    pairs = (mm_nt(cots[...], outs[...]) + mm_nt(held, grads[...])).astype(BF16)
    pairs = jnp.where(row_code[...] == col_code[...], pairs, jnp.zeros_like(pairs))
    d_weights = mm_nt(pairs, tile[...])
    p = probs[...]
    d_logits = (p * (d_weights - group_totals(p * d_weights, row_code[...], part))).astype(BF16)
    grad_out[...] = (mm(spread[...], grads[...]) + mm_nt(d_logits, controller[...])).astype(BF16)
    mixed_out[...] = mm(spread[...], outs[...]).astype(BF16)
    gain_out[...] = mm_tn(d_logits, held)


def mix_backward(part, relative, spread, rows, cots, probs, back, controller, row_code, col_code, tile):
    count, width = rows.shape
    experts, columns = tile.shape
    operands = (spread, rows, cots, probs, controller, row_code, col_code, tile) + tuple(back)
    outs = [
        jax.ShapeDtypeStruct((count, width), BF16),
        jax.ShapeDtypeStruct((count, width), BF16),
        jax.ShapeDtypeStruct((experts, width), F32),
    ]
    return pl.pallas_call(
        functools.partial(unmix_kernel, part, len(back)),
        grid_spec=pltpu.PrefetchScalarGridSpec(
            num_scalar_prefetch=1,
            grid=(1,),
            in_specs=[whole(x.shape) for x in operands],
            out_specs=[whole(x.shape) for x in outs],
            scratch_shapes=[pltpu.VMEM((columns, width), BF16)] * 2,
        ),
        out_shape=outs,
        compiler_params=params("arbitrary"),
        cost_estimate=pl.CostEstimate(
            flops=8 * count * columns * width,
            bytes_accessed=8 * count * width * 2,
            transcendentals=0,
        ),
        name="mix_backward",
    )(relative, *operands)


GELU_SLOPE = 0.7978845608028654
GELU_CUBE = 0.044715


def gelu_pair(x):
    square = x * x
    bend = jnp.tanh(GELU_SLOPE * x * (1.0 + GELU_CUBE * square))
    gate = 0.5 * (1.0 + bend)
    slope = gate + 0.5 * x * (1.0 - bend * bend) * (GELU_SLOPE * (1.0 + 3.0 * GELU_CUBE * square))
    return x * gate, slope


def expert_kernel(count, *refs):
    both, (w_in, b_in, w_out, b_out), sent = refs[:count], refs[count : count + 4], refs[count + 4 :]
    rows = both[0].shape[2]
    merged = jnp.concatenate([x[0, 0] for x in both], axis=0)
    grads = jnp.concatenate([x[0, 1] for x in both], axis=0)
    act, slope = gelu_pair(mm(merged, w_in[0]) + b_in[0])
    outs = mm(act.astype(BF16), w_out[0]) + b_out[0]
    d_pre = (mm_nt(grads, w_out[0]) * slope).astype(BF16)
    d_merged = mm_nt(d_pre, w_in[0])
    for j, out in enumerate(sent):
        at = slice(j * rows, (j + 1) * rows)
        out[0, 0] = outs[at].astype(BF16)
        out[0, 1] = d_merged[at].astype(BF16)


def experts_at_positions(both, w_in, b_in, w_out, b_out):
    experts, _, rows, width = both[0].shape
    inner = w_in.shape[2]
    sources, count = len(both), experts * rows
    tokens = pl.BlockSpec((1, 2, rows, width), lambda e: (e, 0, 0, 0))
    return pl.pallas_call(
        functools.partial(expert_kernel, sources),
        grid=(experts,),
        in_specs=[tokens] * sources
        + [
            pl.BlockSpec((1, width, inner), lambda e: (e, 0, 0)),
            pl.BlockSpec((1, 1, inner), lambda e: (e, 0, 0)),
            pl.BlockSpec((1, inner, width), lambda e: (e, 0, 0)),
            pl.BlockSpec((1, 1, width), lambda e: (e, 0, 0)),
        ],
        out_specs=[tokens] * sources,
        out_shape=[jax.ShapeDtypeStruct(x.shape, BF16) for x in both],
        compiler_params=params("arbitrary"),
        cost_estimate=pl.CostEstimate(
            flops=8 * sources * count * width * inner,
            bytes_accessed=4 * experts * width * inner + 4 * sources * count * width * 2,
            transcendentals=sources * count * inner,
        ),
        name="experts",
    )(*both, w_in, b_in[:, None], w_out, b_out[:, None])


def weight_kernel(units, where, first, both, w_in, b_in, w_out, *refs):
    refs, (merged, grads, turned, total) = refs[:-4], refs[-4:]
    outs = list(refs[: units - 1]) + [refs[units - 1 :]]
    p, i = pl.program_id(0), pl.program_id(1)
    half, unit = where[0], where[1]
    width = both.shape[-1]
    block = w_out.shape[1]
    span = turned.shape[0]
    rows = span // units
    fold = width // block
    height = refs[0].shape[1]

    def put(lines, at, values, d=None):
        for u in range(units) if d is None else [d]:
            if u < units - 1:
                outs[u][p, lines, at] = values
            else:
                for expert, out in enumerate(outs[u]):

                    @pl.when(p == expert)
                    def _(out=out):
                        out[0, lines, at] = values

    @pl.when(i == 0)
    def _():
        merged[...] = both[:, :, 0, 0].reshape(merged.shape)
        grads[...] = both[:, :, 0, 1].reshape(grads.shape)
        turned[...] = merged[:, pl.ds(pl.multiple_of(half * span, span), span)].T
        sums = jnp.sum(grads[...].astype(F32), axis=0, keepdims=True).astype(BF16)
        put(slice(height - 16, height), slice(0, width), jnp.zeros((16, width), BF16))
        put(slice(height - 1, height), slice(0, width), sums)

    act, slope = gelu_pair(mm(merged[...], w_in[0]) + b_in[0])
    d_pre = (mm_nt(grads[...], w_out[0]) * slope).astype(BF16)
    bias = jnp.sum(d_pre.astype(F32), axis=0, keepdims=True).astype(BF16)
    total[...] = mm(turned[...], d_pre)
    for part in range(fold):

        @pl.when(lax.rem(i, fold) == part)
        def _(part=part):
            at = slice(part * block, (part + 1) * block)
            base = pl.ds(pl.multiple_of(i // fold * rows, rows), rows)
            for d in range(units):
                own = pl.multiple_of(lax.bitwise_xor(unit, d) * rows, rows)
                put(base, at, total[pl.ds(own, rows)].astype(BF16), d)

    for step in range(pl.num_programs(1)):

        @pl.when(i == step)
        def _(step=step):
            line = height - 16 + step // fold
            put(slice(line, line + 1), slice(step % fold * block, (step % fold + 1) * block), bias)

    @pl.when((i >= half * units) & (i < (half + 1) * units))
    def _():
        grad = mm_tn(act.astype(BF16), grads[...]).astype(BF16)
        start = height - 16 - block
        for d in range(units):

            @pl.when(i - half * units == lax.bitwise_xor(unit, d))
            def _(d=d):
                put(slice(start, start + block), slice(0, width), grad, d)


def expert_weights(where, first, both, w_in, b_in, w_out, wide, units):
    sources, inner_sources, held, _, rows, width = both.shape
    inner = w_in.shape[2]
    block = inner // wide
    count = sources * inner_sources * rows
    span = width * units // wide
    height = inner // width * (width // wide) + block + 16
    shapes = [(held, height, width)] * (units - 1) + [(1, height, width)] * held
    return pl.pallas_call(
        functools.partial(weight_kernel, units),
        grid_spec=pltpu.PrefetchScalarGridSpec(
            num_scalar_prefetch=2,
            grid=(held, wide),
            in_specs=[
                pl.BlockSpec(
                    (sources, inner_sources, 1, 2, rows, width), lambda p, i, w, f: (0, 0, p, 0, 0, 0)
                ),
                pl.BlockSpec((1, width, block), lambda p, i, w, f: (f[0] + p, 0, i)),
                pl.BlockSpec((1, 1, block), lambda p, i, w, f: (f[0] + p, 0, i)),
                pl.BlockSpec((1, block, width), lambda p, i, w, f: (f[0] + p, i, 0)),
            ],
            out_specs=[whole(x) for x in shapes],
            scratch_shapes=[pltpu.VMEM((count, width), BF16)] * 2
            + [pltpu.VMEM((span, count), BF16), pltpu.VMEM((span, block), F32)],
        ),
        out_shape=[jax.ShapeDtypeStruct(x, BF16) for x in shapes],
        compiler_params=params("arbitrary", "arbitrary"),
        cost_estimate=pl.CostEstimate(
            flops=held * 6 * count * width * inner,
            bytes_accessed=held * (8 * width * inner + 4 * count * width),
            transcendentals=held * count * inner,
        ),
        name="expert_weights",
    )(where, first, both, w_in, b_in[:, None], w_out)


def owner_kernel(units, held, where, *refs):
    pieces, (g_in, g_out, bias) = refs[:-3], refs[-3:]
    rows, block = g_in.shape[1], g_out.shape[1]
    width = g_out.shape[2]
    start = pieces[0].shape[1] - 16 - block
    for d in range(units):
        for p in range(held):

            @pl.when((pl.program_id(0) == d) & (pl.program_id(1) == p))
            def _(d=d, p=p):
                ref, e = (pieces[d], p) if d < units - 1 else (pieces[d + p], 0)
                for c in range(g_in.shape[2] // width):
                    at = slice(c * width, (c + 1) * width)
                    g_in[0, :, at] = ref[e, c * rows : (c + 1) * rows].astype(F32)
                g_out[0] = ref[e, start : start + block].astype(F32)
                bias[0] = ref[e, start + block :].astype(F32)


def owned_weights(pieces, where, inner, wide, units):
    width = pieces[0].shape[2]
    held = len(pieces) - units + 1
    count = units * held
    shapes = [(1, width // wide, inner), (1, inner // wide, width), (1, 16, width)]
    return pl.pallas_call(
        functools.partial(owner_kernel, units, held),
        grid_spec=pltpu.PrefetchScalarGridSpec(
            num_scalar_prefetch=1,
            grid=(units, held),
            in_specs=[whole(x.shape) for x in pieces],
            out_specs=[pl.BlockSpec(x, lambda d, p, where: (where[d] * held + p, 0, 0)) for x in shapes],
        ),
        out_shape=[jax.ShapeDtypeStruct((count,) + x[1:], F32) for x in shapes],
        compiler_params=params("arbitrary", "arbitrary"),
        cost_estimate=pl.CostEstimate(
            flops=0, bytes_accessed=sum(x.size for x in pieces) * 6, transcendentals=0
        ),
        name="owned_weights",
    )(where, *pieces)


def attend_back(entry, d_low, packs, joint_in, context_in, causal, masks, total):
    width = entry.shape[1]
    scale = float(HEAD_WIDTH) ** -0.5
    d_entry = None
    for j, pack in enumerate(packs):
        base = j * 3 * LANES
        q, k, v = (joint_in[0, :, base + i * LANES : base + (i + 1) * LANES] for i in range(3))
        context = context_in[0, :, j * LANES : (j + 1) * LANES]
        d_context = mm(d_low, pack[:, 3 * LANES :]).astype(BF16)
        d_q, d_k, d_v = [], [], []
        for mask in masks:
            q_head = keep(mask, q)
            d_head = keep(mask, d_context)
            probs = causal_probs(q_head, k, causal)
            d_probs = mm_nt(d_head, v).astype(BF16).astype(F32)
            d_scores = probs * (d_probs - jnp.sum(probs * d_probs, axis=-1, keepdims=True))
            d_scores = d_scores.astype(BF16)
            d_v.append(mm_tn(probs.astype(BF16), d_head))
            d_q.append(mm(d_scores, keep(mask, k)))
            d_k.append(mm_tn(d_scores, q_head))
        joint = [sum(d_q) * scale, sum(d_k) * scale, sum(d_v)]
        joint = jnp.concatenate(joint, axis=1).astype(BF16)
        term = mm_nt(joint, pack[:, : 3 * LANES])
        d_entry = term if d_entry is None else d_entry + term
        grad = mm_tn(entry, joint)
        for c in range(3):
            total[j, c * width : (c + 1) * width] += grad[:, c * LANES : (c + 1) * LANES]
        grad = mm_tn(context, d_low)
        for c in range(width // LANES):
            at = slice(3 * width + c * LANES, 3 * width + (c + 1) * LANES)
            total[j, at] += grad[:, c * LANES : (c + 1) * LANES]
    return d_entry


def store_weights(total, controllers, outs, lanes, gains=None):
    height = total.shape[1]
    for o, out in enumerate(outs):
        j, at = divmod(o, LANES // lanes)
        piece = total[j].astype(BF16)
        if lanes < LANES:
            own = slice(at * lanes, (at + 1) * lanes)
            split = height // 4 * 3
            piece = [jnp.pad(piece[:split, own], ((0, 0), (0, LANES - lanes)))] + [
                jnp.pad(piece[c : c + LANES][own], ((0, LANES - lanes), (0, 0)))
                for c in range(split, height, LANES)
            ]
            piece = jnp.concatenate(piece, axis=0)
        out[:height] = piece
        tail = [controllers[o]]
        if gains is not None:
            tail.append(gains)
        left = out.shape[0] - height - sum(x.shape[0] for x in tail)
        out[height:] = jnp.concatenate(tail + [jnp.zeros((left, LANES), BF16)], axis=0)


def back_far_kernel(blocks, lanes, place, tokens, cots, grads, hidden, joint, context, *refs):
    packs, (gain_attn, gain_mix, controllers), refs = refs[:blocks], refs[blocks : blocks + 3], refs[blocks + 3 :]
    (partial_out, d_hidden_out, gain_out), outs, total = refs[:3], refs[3:-1], refs[-1]
    i = pl.program_id(0)
    length, width = hidden.shape[1:]
    live = (place[0] + i < place[1]).astype(F32)

    @pl.when(i == 0)
    def _():
        total[...] = jnp.zeros_like(total)
        gain_out[...] = jnp.zeros_like(gain_out)

    rows = hidden[0]
    inverse = inverse_rms(rows)
    normed = rows * inverse
    grad = grads[...].astype(F32).reshape(length, width)
    gain_out[0:1] += jnp.sum(grad * normed, axis=0, keepdims=True)
    d_normed = grad * gain_mix[...]
    d_hidden = cots[0].astype(F32) * live + inverse * (
        d_normed - normed * jnp.mean(d_normed * normed, axis=-1, keepdims=True)
    )
    d_hidden_out[0] = d_hidden
    rows = tokens[0].astype(F32)
    entry = (rows * inverse_rms(rows) * gain_attn[...]).astype(BF16)
    partial_out[0] = attend_back(
        entry, d_hidden.astype(BF16), packs, joint, context, causal_mask(length), head_masks(length), total
    )

    @pl.when(i == pl.num_programs(0) - 1)
    def _():
        store_weights(total, controllers, outs, lanes)


def back_near_kernel(blocks, lanes, place, tokens, d_hidden, partial, joint, context, *refs):
    packs, (gain_attn, gain_in, controllers), refs = refs[:blocks], refs[blocks : blocks + 3], refs[blocks + 3 :]
    d_tokens_out, outs, (total, gain) = refs[0], refs[1:-2], refs[-2:]
    i = pl.program_id(0)
    length, width = d_hidden.shape[1:]

    @pl.when(i == 0)
    def _():
        total[...] = jnp.zeros_like(total)
        gain[...] = jnp.zeros_like(gain)

    rows = tokens[0].astype(F32)
    inverse = inverse_rms(rows)
    normed = rows * inverse
    entry = (normed * gain_attn[...]).astype(BF16)
    d_entry = partial[0] + attend_back(
        entry, d_hidden[0].astype(BF16), packs, joint, context, causal_mask(length), head_masks(length), total
    )
    d_entry = d_entry.astype(BF16).astype(F32)
    gain[0:1] += jnp.sum(d_entry * normed, axis=0, keepdims=True)
    d_normed = d_entry * gain_attn[...]
    d_tokens = d_hidden[0] + inverse * (
        d_normed - normed * jnp.mean(d_normed * normed, axis=-1, keepdims=True)
    )
    live = (place[0] + i < place[1]).astype(F32)
    d_tokens_out[0] = (d_tokens * live).astype(BF16)

    @pl.when(i == pl.num_programs(0) - 1)
    def _():
        pieces = width // LANES
        tail = [x[0:1, c * LANES : (c + 1) * LANES] for x in (gain, gain_in) for c in range(pieces)]
        tail.append(jnp.zeros((16 - 2 * pieces, LANES), F32))
        store_weights(total, controllers, outs, lanes, jnp.concatenate(tail, axis=0).astype(BF16))


def attention_back_far(
    place, tokens, cotangent, grads, hidden, joint, context, packs, gain_attn, gain_mix, controllers, height
):
    total, length, width = tokens.shape
    spread, slots, part, _ = grads.shape
    inner = context.shape[2]
    blocks = len(packs)
    count = controllers.shape[0]

    def own(i, place):
        return (jnp.minimum(place[0] + i, total - 1), 0, 0)

    rows = pl.BlockSpec((1, length, width), local_block)
    return pl.pallas_call(
        functools.partial(back_far_kernel, blocks, inner // count),
        grid_spec=pltpu.PrefetchScalarGridSpec(
            num_scalar_prefetch=1,
            grid=(slots,),
            in_specs=[
                pl.BlockSpec((1, length, width), own),
                pl.BlockSpec((1, length, width), own),
                pl.BlockSpec((spread, 1, part, width), lambda i, place: (0, i, 0, 0)),
                rows,
                pl.BlockSpec((1, length, 3 * inner), local_block),
                pl.BlockSpec((1, length, inner), local_block),
            ]
            + [whole(p.shape) for p in packs]
            + [whole((1, width))] * 2
            + [whole(controllers.shape)],
            out_specs=[rows, rows, whole((8, width))] + [whole((height, LANES))] * count,
            scratch_shapes=[pltpu.VMEM((blocks, 4 * width, LANES), F32)],
        ),
        out_shape=[
            jax.ShapeDtypeStruct((slots, length, width), F32),
            jax.ShapeDtypeStruct((slots, length, width), F32),
            jax.ShapeDtypeStruct((8, width), F32),
        ]
        + [jax.ShapeDtypeStruct((height, LANES), BF16)] * count,
        compiler_params=params("arbitrary"),
        cost_estimate=pl.CostEstimate(
            flops=0,
            bytes_accessed=slots * length * (width * 18 + inner * 8) + 16 * width * inner,
            transcendentals=slots * length * length * inner // HEAD_WIDTH,
        ),
        name="attention_back_far",
    )(place, tokens, cotangent, grads, hidden, joint, context, *packs, gain_attn, gain_mix, controllers)


def attention_back_near(
    place, tokens, d_hidden, partial, joint, context, packs, gain_attn, gain_in, controllers, height
):
    total, length, width = tokens.shape
    slots, _, inner = context.shape
    blocks = len(packs)
    count = controllers.shape[0]

    def own(i, place):
        return (jnp.minimum(place[0] + i, total - 1), 0, 0)

    rows = pl.BlockSpec((1, length, width), local_block)
    return pl.pallas_call(
        functools.partial(back_near_kernel, blocks, inner // count),
        grid_spec=pltpu.PrefetchScalarGridSpec(
            num_scalar_prefetch=1,
            grid=(slots,),
            in_specs=[
                pl.BlockSpec((1, length, width), own),
                rows,
                rows,
                pl.BlockSpec((1, length, 3 * inner), local_block),
                pl.BlockSpec((1, length, inner), local_block),
            ]
            + [whole(p.shape) for p in packs]
            + [whole((1, width)), whole((8, width)), whole(controllers.shape)],
            out_specs=[rows] + [whole((height, LANES))] * count,
            scratch_shapes=[
                pltpu.VMEM((blocks, 4 * width, LANES), F32),
                pltpu.VMEM((8, width), F32),
            ],
        ),
        out_shape=[
            jax.ShapeDtypeStruct((slots, length, width), BF16),
        ]
        + [jax.ShapeDtypeStruct((height, LANES), BF16)] * count,
        compiler_params=params("arbitrary"),
        cost_estimate=pl.CostEstimate(
            flops=0,
            bytes_accessed=slots * length * (width * 12 + inner * 8) + 16 * width * inner,
            transcendentals=slots * length * length * inner // HEAD_WIDTH,
        ),
        name="attention_back_near",
    )(place, tokens, d_hidden, partial, joint, context, *packs, gain_attn, gain_in, controllers)


def output_kernel(place, hidden, mixed, out):
    live = (place[0] + pl.program_id(0) < place[1]).astype(F32)
    rows = mixed[...].astype(F32).reshape(hidden.shape[1:])
    out[0] = (live * (hidden[0] + rows)).astype(BF16)


def layer_output(place, hidden, mixed):
    spread, slots, part, width = mixed.shape
    length = hidden.shape[1]
    return pl.pallas_call(
        output_kernel,
        grid_spec=pltpu.PrefetchScalarGridSpec(
            num_scalar_prefetch=1,
            grid=(slots,),
            in_specs=[
                pl.BlockSpec((1, length, width), lambda i, place: (i, 0, 0)),
                pl.BlockSpec((spread, 1, part, width), lambda i, place: (0, i, 0, 0)),
            ],
            out_specs=pl.BlockSpec((1, length, width), lambda i, place: (i, 0, 0)),
        ),
        out_shape=jax.ShapeDtypeStruct((slots, length, width), BF16),
        compiler_params=params("arbitrary"),
        cost_estimate=pl.CostEstimate(
            flops=slots * length * width * 3, bytes_accessed=slots * length * width * 8, transcendentals=0
        ),
        name="layer_output",
    )(place, hidden, mixed)


def swap_core(x):
    narrow = lax.axis_size("narrow")
    return lax.ppermute(x, "narrow", [(n, n ^ 1) for n in range(narrow)])


def from_chip(x, k):
    narrow = lax.axis_size("narrow")
    return lax.ppermute(x, "narrow", [((n + 2 * k) % narrow, n) for n in range(narrow)])


def to_chip(x, k):
    narrow = lax.axis_size("narrow")
    return lax.ppermute(x, "narrow", [(n, (n + 2 * k) % narrow) for n in range(narrow)])


def relative_narrow():
    narrow = lax.axis_size("narrow")
    me = lax.axis_index("narrow")
    return [lax.bitwise_xor(lax.rem(me + 2 * (j // 2), narrow), j % 2) for j in range(narrow)]


def gather_narrow(x):
    blocks = []
    for k in range(lax.axis_size("narrow") // 2):
        piece = from_chip(x, k) if k else x
        blocks += [piece, swap_core(piece)]
    return blocks


def far_sums(pieces):
    pairs = [(pieces[2 * k], swap_core(pieces[2 * k + 1])) for k in range(len(pieces) // 2)]
    return [(x.astype(F32) + y.astype(F32)).astype(BF16) for x, y in pairs]


def sum_wide(x, *others):
    wide = lax.axis_size("wide")
    parts = x.astype(BF16).reshape(wide, x.shape[0] // wide, x.shape[1])
    parts = lax.all_to_all(parts, "wide", split_axis=0, concat_axis=0, tiled=True)
    part = jnp.sum(parts.astype(F32), axis=0).astype(BF16)
    part, others = lax.optimization_barrier((part, others))
    parts = jnp.broadcast_to(part[None], parts.shape)
    parts = lax.all_to_all(parts, "wide", split_axis=0, concat_axis=0, tiled=True)
    return parts.reshape(x.shape).astype(F32), others


def to_relative(x, j):
    narrow = lax.axis_size("narrow")
    k, other = j // 2, j % 2
    return lax.ppermute(x, "narrow", [(n, ((n + 2 * k) % narrow) ^ other) for n in range(narrow)])


def from_relative(x, j):
    narrow = lax.axis_size("narrow")
    k, other = j // 2, j % 2
    return lax.ppermute(x, "narrow", [(((n + 2 * k) % narrow) ^ other, n) for n in range(narrow)])


def to_unit(x, d):
    wide = lax.axis_size("wide")
    return lax.ppermute(x, "wide", [(w, w ^ d) for w in range(wide)])


def place_kernel(count, where, *refs):
    out = refs[count]
    for j in range(count):

        @pl.when(pl.program_id(0) == j)
        def _(j=j):
            out[...] = refs[j][...].astype(out.dtype)


def place_blocks(pieces, where, dtype):
    count = len(pieces)
    shape = pieces[0].shape
    zeros = (0,) * (len(shape) - 1)
    return pl.pallas_call(
        functools.partial(place_kernel, count),
        grid_spec=pltpu.PrefetchScalarGridSpec(
            num_scalar_prefetch=1,
            grid=(count,),
            in_specs=[whole(shape)] * count,
            out_specs=pl.BlockSpec(shape, lambda i, where: (where[i],) + zeros),
        ),
        out_shape=jax.ShapeDtypeStruct((count * shape[0],) + shape[1:], dtype),
        compiler_params=params("arbitrary"),
        cost_estimate=pl.CostEstimate(
            flops=0, bytes_accessed=pieces[0].size * 8 * count, transcendentals=0
        ),
        name="place_blocks",
    )(where, *pieces)


def body(
    tokens,
    cotangent,
    counts,
    group_order,
    query_weight,
    key_weight,
    value_weight,
    output_weight,
    gain_attn,
    gain_mix,
    controller,
    w_in,
    b_in,
    w_out,
    b_out,
):
    slot_count, seq_len, model_width = tokens.shape
    wide, narrow = lax.axis_size("wide"), lax.axis_size("narrow")
    spread = wide * narrow
    wide_index, narrow_index = lax.axis_index("wide"), lax.axis_index("narrow")
    slots = -(-slot_count // narrow)
    part = seq_len // spread
    padded_part = -(-part // 8) * 8
    local_experts = w_in.shape[0]
    experts = local_experts * narrow
    relative = jnp.stack(relative_narrow())
    head_columns = query_weight.shape[1]

    seq_ends = jnp.cumsum(counts)
    seq_starts = seq_ends - counts
    own_count = counts[wide_index]
    place = jnp.stack([narrow_index * slots, own_count]).astype(jnp.int32)
    slot_ids = jnp.arange(slots * narrow)
    slot_seqs = jnp.where(slot_ids[None] < counts[:, None], seq_starts[:, None] + slot_ids[None], -1)
    matches = slot_seqs.reshape(-1, 1) == group_order[None]
    slot_group = jnp.sum(jnp.where(matches, 1 + jnp.arange(group_order.shape[0]) // GROUP, 0), axis=1) - 1
    positions = jnp.arange(padded_part)
    row_code = jnp.where(slot_group[:, None] >= 0, slot_group[:, None] * padded_part + positions, -1)
    row_code = row_code.reshape(-1, 1).astype(jnp.int32)
    per_expert = GROUPS * padded_part
    col_code = (jnp.arange(experts * per_expert) % per_expert).astype(jnp.int32)[None]
    tile = jnp.repeat(jnp.eye(experts, dtype=BF16), per_expert, axis=1)

    pack = pack_weights(query_weight, key_weight, value_weight, output_weight)
    packs = [pack, swap_core(pack)]
    far_packs = [from_chip(pack, k) for k in range(1, narrow // 2)]
    joined = LANES // head_columns

    def join(packs):
        if joined == 1:
            return packs
        packs = [p.reshape(model_width, 4, head_columns) for p in packs]
        return [
            jnp.concatenate(packs[i : i + joined], axis=2).reshape(model_width, -1)
            for i in range(0, len(packs), joined)
        ]

    controllers = jnp.stack(gather_narrow(controller.T))
    controllers = controllers[jnp.argsort(relative)].reshape(experts, model_width).T

    gain_attn_row, gain_mix_row = gain_attn[None], gain_mix[None]

    def to_positions(x):
        x = lax.all_to_all(x, BOTH, split_axis=0, concat_axis=0, tiled=True)
        x = jnp.pad(x, ((0, 0), (0, 0), (0, padded_part - part), (0, 0)))
        return x.reshape(-1, model_width)

    def to_slots(x):
        x = x.reshape(spread, slots, padded_part, model_width)[:, :, :part]
        return lax.all_to_all(x, BOTH, split_axis=0, concat_axis=0, tiled=True)

    cots, *packs = lax.optimization_barrier((cotangent, *packs))
    cots = jnp.pad(cots, ((0, slots * narrow - slot_count), (0, 0), (0, 0)))
    cots = cots.reshape(slots * narrow, wide, narrow, part, model_width)
    cots = lax.dynamic_index_in_dim(cots, narrow_index, axis=2, keepdims=False).transpose(1, 0, 2, 3)
    cots = lax.all_to_all(cots, "wide", split_axis=0, concat_axis=0, tiled=True)
    cots = jnp.pad(cots, ((0, 0), (0, 0), (0, padded_part - part), (0, 0)))
    cot_rows = cots.reshape(-1, model_width)

    packs = join(packs)
    partial, joint_near, context_near = attention_near(place, tokens, packs, gain_attn_row, slots)
    partial, far_packs = lax.optimization_barrier((partial, far_packs))
    far_packs = join([x for piece in far_packs for x in (piece, swap_core(piece))])
    mix_sent, hidden, joint_far, context_far = attention_far(
        place, tokens, partial, far_packs, gain_attn_row, gain_mix_row, slots, spread
    )
    mix_rows = to_positions(mix_sent)
    probs, spread_probs, *both = mix_forward(
        padded_part, relative, mix_rows, cot_rows, controllers, row_code, col_code, tile, narrow
    )

    rows = GROUPS * part

    def trim(x):
        x = x.reshape(local_experts, 2, GROUPS, padded_part, model_width)[:, :, :, :part]
        return x.reshape(local_experts, 2, rows, model_width)

    def untrim(x):
        x = x.reshape(local_experts, 2, GROUPS, part, model_width)
        x = jnp.pad(x, ((0, 0), (0, 0), (0, 0), (0, padded_part - part), (0, 0)))
        return x.reshape(local_experts, 2, -1, model_width)

    both = [trim(x) for x in both]
    both = both[:1] + [to_relative(x, j) for j, x in enumerate(both) if j]
    halves = 2 if wide % 4 == 0 else 1
    units = wide // halves
    held, share = max(local_experts // units, 1), max(units // local_experts, 1)
    unit = lax.rem(wide_index, units)
    shape = (held, 2, rows, model_width)
    tokens_sent = jnp.stack(both).reshape((share, narrow // share, units // share) + shape)
    tokens_sent = tokens_sent.transpose(2, 0, 1, 3, 4, 5, 6).reshape((units, narrow // share) + shape)
    tokens_sent = jnp.concatenate([tokens_sent] * halves)
    tokens_sent, both = lax.optimization_barrier((tokens_sent, both))
    tokens_all = lax.all_to_all(tokens_sent, "wide", split_axis=0, concat_axis=0, tiled=True)
    if rows % 16 == 0:
        back = experts_at_positions(both, w_in, b_in, w_out, b_out)
    else:
        lines = jnp.stack(both, axis=2).reshape(local_experts, 2, narrow * rows, model_width)
        (back,) = experts_at_positions([lines], w_in, b_in, w_out, b_out)
        back = back.reshape(local_experts, 2, narrow, rows, model_width)
        back = [back[:, :, j] for j in range(narrow)]

    where = jnp.stack([wide_index // units, unit]).astype(jnp.int32)
    first = (unit * held // share).astype(jnp.int32)[None]
    expert_grads = expert_weights(where, first, tokens_all, w_in, b_in, w_out, wide, units)

    back = [untrim(x if j == 0 else from_relative(x, j)) for j, x in enumerate(back)]
    grad_rows, mixed_rows, grad_controller = mix_backward(
        padded_part, relative, spread_probs, mix_rows, cot_rows, probs, back, controllers, row_code, col_code, tile
    )
    grads = to_slots(grad_rows)
    mixed_rows, expert_grads, grads = lax.optimization_barrier((mixed_rows, expert_grads, grads))
    mixed = to_slots(mixed_rows)

    expert_grads = list(expert_grads[:1]) + [
        to_unit(x, min(d, units - 1)) for d, x in enumerate(expert_grads) if d
    ]

    height = 4 * model_width
    grad_controller = grad_controller.astype(BF16).reshape(narrow, -1, LANES)[relative]
    end = height + grad_controller.shape[1]
    rows_sent = -(-(end + 16) // (16 * wide)) * 16 * wide
    partial, d_hidden, gain_mix_part, *far = attention_back_far(
        place,
        tokens,
        cotangent,
        grads,
        hidden,
        joint_far,
        context_far,
        far_packs,
        gain_attn_row,
        gain_mix_row,
        grad_controller[2:],
        rows_sent,
    )
    partial, far = lax.optimization_barrier((partial, far_sums(far)))
    far = sum([to_chip(x, k + 1).astype(F32) for k, x in enumerate(far)], 0.0)
    d_tokens, kept, sent = attention_back_near(
        place,
        tokens,
        d_hidden,
        partial,
        joint_near,
        context_near,
        packs,
        gain_attn_row,
        gain_mix_part,
        grad_controller[:2],
        rows_sent,
    )
    d_tokens, kept, sent, mixed, expert_grads[:3] = lax.optimization_barrier(
        (d_tokens, kept, sent, mixed, expert_grads[:3])
    )
    weights = kept.astype(F32) + swap_core(sent).astype(F32) + far
    weights, expert_grads = sum_wide(weights, *expert_grads)
    gains = weights[end : end + 16].astype(BF16)
    gains = sum([to_chip(gains, k).astype(F32) for k in range(1, narrow // 2)], gains.astype(F32))
    projections = weights[: 3 * model_width, :head_columns].reshape(3, model_width, head_columns)
    output_weight_gradient = weights[3 * model_width : height].reshape(-1, LANES, LANES)[:, :head_columns]
    output_weight_gradient = output_weight_gradient.transpose(1, 0, 2).reshape(head_columns, -1)
    g_controller = weights[height:end].reshape(local_experts, model_width).T
    pieces = model_width // LANES
    g_gain_attn = gains[:pieces].reshape(-1)
    g_gain_mix = gains[pieces : 2 * pieces].reshape(-1)

    d_tokens = place_blocks(gather_narrow(d_tokens), relative, BF16)[:slot_count]
    mixed_part = layer_output(place, hidden, mixed)
    mixed_part = place_blocks(gather_narrow(mixed_part), relative, BF16)[:slot_count]

    order = lax.bitwise_xor(unit, jnp.arange(units))
    g_w_in, g_w_out, bias = owned_weights(expert_grads, order, w_in.shape[2], wide, units)

    def over_share(x):
        return jnp.sum(x.reshape((local_experts, share) + x.shape[1:]), axis=1)

    g_w_in, g_w_out, bias = (over_share(x) for x in (g_w_in, g_w_out, bias))
    g_b_in = bias[:, : w_in.shape[2] // model_width].reshape(local_experts, -1)
    g_b_out = bias[:, -1]

    return (
        mixed_part,
        d_tokens,
        projections[0],
        projections[1],
        projections[2],
        output_weight_gradient,
        g_gain_attn,
        g_gain_mix,
        g_controller,
        g_w_in,
        g_b_in,
        g_w_out,
        g_b_out,
    )


def solution(mesh):
    placed = (
        P("wide", None, None),
        P("wide", None, None),
        P(),
        P(),
        P(None, "narrow"),
        P(None, "narrow"),
        P(None, "narrow"),
        P("narrow", None),
        P(),
        P(),
        P(None, "narrow"),
        P("narrow", None, None),
        P("narrow", None),
        P("narrow", None, None),
        P("narrow", None),
    )
    return jax.shard_map(
        body,
        mesh=mesh,
        in_specs=placed,
        out_specs=(
            P("wide", None, None),
            P("wide", None, None),
            P(None, "narrow"),
            P(None, "narrow"),
            P(None, "narrow"),
            P("narrow", None),
            P(),
            P(),
            P(None, "narrow"),
            P("narrow", "wide", None),
            P("narrow", None),
            P("narrow", "wide", None),
            P("narrow", None),
        ),
        check_vma=False,
    )
```

time: 343 us -> 300 us (0.87)
  waiting for transfers between devices: 126 us -> 88.4 us
  local copies, waits for them, and re-layouts: 28.3 us -> 21.5 us
  Pallas kernels: 116 us -> 122 us
  starting transfers between devices: 58.3 us -> 54 us
    ppermute x1 -> x2, waiting for transfers between devices: 19.8 us -> 0.01 us  [to_chip(): lax.ppermute(x, 'narrow', [(n, (n + 2 * k) % narrow) for n in range(narro...]
    pallas_call x3 -> x7, Pallas kernels: 57.4 us -> 76.2 us  [the longest x1 23.7 us: expert_weights(): pl.pallas_call(functools.partial(weight_kernel, units), grid_spec=pltpu.P...]
    ppermute x4, waiting for transfers between devices: 19.1 us -> 1.45 us  [from_chip(): lax.ppermute(x, 'narrow', [((n + 2 * k) % narrow, n) for n in range(narro...]
    pallas_call x5 -> x2, Pallas kernels: 21.8 us -> 9.35 us  [place_blocks(): pl.pallas_call(functools.partial(place_kernel, count), grid_spec=pltpu.Pr...]
    ppermute x9 -> x4, waiting for transfers between devices: 41.7 us -> 29.7 us  [to_unit(): return lax.ppermute(x, 'wide', [(w, w ^ d) for w in range(wide)])]
    all_to_all x0 -> x1, starting transfers between devices: none -> 7.2 us  [body(): cots = lax.all_to_all(cots, 'wide', split_axis=0, concat_axis=0, tiled=True)]
    all_to_all x2, waiting for transfers between devices: 0.01 us -> 6.63 us  [sum_wide(): lax.all_to_all(parts, 'wide', split_axis=0, concat_axis=0, tiled=True)]
    all_to_all x2 -> x1, starting transfers between devices: 11.9 us -> 5.66 us  [to_positions(): x = lax.all_to_all(x, BOTH, split_axis=0, concat_axis=0, tiled=True)]
  transfers between devices with their start and end apart: 36 -> 33, of which waited for: 13 -> 15; matrix products, arithmetic and copies ran while one was open for 6% -> 6% of each run, Pallas kernels for 26% -> 39%
where the time goes in v3:
time: 300 us; the launch traced here: 299 us
  Pallas kernels  122 us (41%)
  waiting for transfers between devices  88.4 us (29%)
  starting transfers between devices  54 us (18%)
  local copies, waits for them, and re-layouts  21.5 us (7%)
  other arithmetic  11.3 us (4%)
    ppermute x4, waiting for transfers between devices, to_unit(): return lax.ppermute(x, 'wide', [(w, w ^ d) for w in range(wide)])  29.7 us
    pallas_call x1, Pallas kernels, expert_weights(): pl.pallas_call(functools.partial(weight_kernel, units), grid_spec=pltpu.P...  23.7 us
    pallas_call x1, Pallas kernels, experts_at_positions(): pl.pallas_call(functools.partial(expert_kernel, sources), grid=(experts,)...  20.8 us
    all_to_all x1, waiting for transfers between devices, to_positions(): x = lax.all_to_all(x, BOTH, split_axis=0, concat_axis=0, tiled=True)  16.5 us
    pallas_call x1, Pallas kernels, attention_back_far(): pl.pallas_call(functools.partial(back_far_kernel, blocks, inner // count)...  13.4 us
    pallas_call x1, Pallas kernels, attention_back_near(): pl.pallas_call(functools.partial(back_near_kernel, blocks, inner // count...  12.5 us
    ppermute x3, waiting for transfers between devices, to_relative(): lax.ppermute(x, 'narrow', [(n, (n + 2 * k) % narrow ^ other) for n in ran...  12.3 us
    ppermute x3, waiting for transfers between devices, from_relative(): lax.ppermute(x, 'narrow', [((n + 2 * k) % narrow ^ other, n) for n in ran...  11.4 us
  transfers between devices with their start and end apart: 33, of which 15 were waited for; matrix products, arithmetic and copies ran while one was open for 6% of the time, Pallas kernels for 39%

profile of v3, /device:TPU:0, one launch (start us, length us, event | category | flops | bytes accessed | tf_op | source)
XLA Modules:
  0.0 298.6 jit_solution(7552319981884184697)
XLA Ops:
  0.6 2.0 pack_weights.1.refs_0_
  3.1 1.7 collective-permute-done.refs_1_
  4.8 2.3 copy_bitcast_fusion
  7.1 7.2 %all-to-all-start.1 = ((bf16[8,12,8,512]{3,2,1,0:T(8,128)(2,1)}), bf16[8,12,8,512]{3,2,1,0:T(8,128)(2,1)S(1)}, u32[]{:S(2)}, u32[]{:S(2)}) async-start(bf16[8,12,8,512]{3,2,1,0:T(8,128)(2,1)} %copy_bitcast_fusion), calls=%async_computation.1 | async-start | bytes 1572864 | tf_op jit(solution)/shard_map/all_to_all | solution.py:937
  14.4 1.6 collective-permute-start.1
  17.2 1.3 pad_add_fusion.1.place
  18.5 8.2 %attention_near.1 = (f32[3,256,512]{2,1,0:T(8,128)}, bf16[3,256,768]{2,1,0:T(8,128)(2,1)}, bf16[3,256,256]{2,1,0:T(8,128)(2,1)}) custom-call(s32[2]{0:T(128)} %pad_add_fusion.1.place, bf16[12,256,512]{2,1,0:T(8,128)(2,1)} %tokens.7, bf16[512,512]{1,0:T(8,128)(2,1)} %pack_weights.1.refs_0_, bf16[512,512]{1,0:T(8,128)(2,1)} %copy-done.20, f32[1,512]{1,0:T(1,128)} %bitcast.86), custom_call_target="tpu_custom_call" | custom-call | flops 1207959552 | bytes 4980736 | tf_op jit(solution)/shard_map/attention_near/pallas_call | solution.py:119
  26.8 1.4 collective-permute-done.1.refs_0_
  30.9 8.9 %attention_far.1 = (bf16[32,3,8,512]{3,2,1,0:T(8,128)(2,1)}, f32[3,256,512]{2,1,0:T(8,128)}, bf16[3,256,768]{2,1,0:T(8,128)(2,1)}, bf16[3,256,256]{2,1,0:T(8,128)(2,1)}) custom-call(s32[2]{0:T(128)} %pad_add_fusion.1.place, bf16[12,256,512]{2,1,0:T(8,128)(2,1)} %tokens.7, f32[3,256,512]{2,1,0:T(8,128)} %get-tuple-element.85.partial, ...), custom_call_target="tpu_custom_call" | custom-call | flops 1207959552 | bytes 7340032 | tf_op jit(solution)/shard_map/attention_far/pallas_call | solution.py:154
  39.8 5.7 %all-to-all-start = ((bf16[32,3,8,512]{3,2,1,0:T(8,128)(2,1)}), bf16[32,3,8,512]{3,2,1,0:T(8,128)(2,1)S(1)}, u32[]{:S(2)}, u32[]{:S(2)}) async-start(bf16[32,3,8,512]{3,2,1,0:T(8,128)(2,1)} %get-tuple-element.88), calls=%async_computation | async-start | bytes 1572864 | tf_op jit(solution)/shard_map/all_to_all | solution.py:925
  49.6 16.5 %all-to-all-done = bf16[32,3,8,512]{3,2,1,0:T(8,128)(2,1)S(1)} async-done(((bf16[32,3,8,512]{3,2,1,0:T(8,128)(2,1)}), bf16[32,3,8,512]{3,2,1,0:T(8,128)(2,1)S(1)}, u32[]{:S(2)}, u32[]{:S(2)}) %all-to-all-start) | async-done | bytes 786464 | tf_op jit(solution)/shard_map/all_to_all | solution.py:925
  67.0 5.4 %mix_forward.1 = (f32[768,32]{1,0:T(8,128)}, bf16[768,512]{1,0:T(8,128)(2,1)}, bf16[8,2,16,512]{3,2,1,0:T(8,128)(2,1)}, bf16[8,2,16,512]{3,2,1,0:T(8,128)(2,1)},...) custom-call(s32[4]{0:T(128)} %copy-done.25, bf16[768,512]{1,0:T(8,128)(2,1)} %bitcast.77, ...), custom_call_target="tpu_custom_call" | custom-call | flops 805306368 | bytes 4718592 | tf_op jit(solution)/shard_map/mix_forward/pallas_call | solution.py:254
  72.3 1.6 collective-permute-start.7
  74.2 7.5 %collective-permute-done.7.refs_2_ = bf16[8,2,16,512]{3,2,1,0:T(8,128)(2,1)S(1)} collective-permute-done((bf16[8,2,16,512]{3,2,1,0:T(8,128)(2,1)}, bf16[8,2,16,512]{3,2,1,0:T(8,128)(2,1)S(1)}, u32[]{:S(2)}, u32[]{:S(2)}) %collective-permute-start.7) | collective-permute-done | bytes 262176 | tf_op jit(solution)/shard_map/ppermute | solution.py:817
  81.7 4.8 %collective-permute-done.8.refs_3_ = bf16[8,2,16,512]{3,2,1,0:T(8,128)(2,1)S(1)} collective-permute-done((bf16[8,2,16,512]{3,2,1,0:T(8,128)(2,1)}, bf16[8,2,16,512]{3,2,1,0:T(8,128)(2,1)S(1)}, u32[]{:S(2)}, u32[]{:S(2)}) %collective-permute-start.8) | collective-permute-done | bytes 262176 | tf_op jit(solution)/shard_map/ppermute | solution.py:817
  87.7 1.5 pad_maximum_fusion
  89.2 3.8 %all-to-all-start.2 = ((bf16[8,4,2,2,16,512]{5,4,3,2,1,0:T(8,128)(2,1)}), bf16[8,4,2,2,16,512]{5,4,3,2,1,0:T(8,128)(2,1)S(1)}, u32[]{:S(2)}, u32[]{:S(2)}) async-start(bf16[8,4,2,2,16,512]{5,4,3,2,1,0:T(8,128)(2,1)} %pad_maximum_fusion), calls=%async_computation.2 | async-start | bytes 4194304 | tf_op jit(solution)/shard_map/all_to_all | solution.py:975
  94.3 20.8 %experts.1 = (bf16[8,2,16,512]{3,2,1,0:T(8,128)(2,1)}, bf16[8,2,16,512]{3,2,1,0:T(8,128)(2,1)}, bf16[8,2,16,512]{3,2,1,0:T(8,128)(2,1)}, bf16[8,2,16,512]{3,2,1,0:T(8,128)(2,1)}) custom-call(bf16[8,2,16,512]{3,2,1,0:T(8,128)(2,1)} %get-tuple-element.97.refs_0_, bf16[8,2,16,512]{3,2,1,0:T(8,128)(2,1)} %copy-done.9, bf16[8,2,16,512]{3,2,1,0:T(8,128)(2,1)} %copy-done.10, ...), custom_call_target="tpu_custom_call" | custom-call | flops 4294967296 | bytes 35651584 | tf_op jit(solution)/shard_map/experts/pallas_call | solution.py:361
  115.1 1.5 collective-permute-start.10
  117.3 7.2 %collective-permute-done.10.refs_2_ = bf16[8,2,16,512]{3,2,1,0:T(8,128)(2,1)S(1)} collective-permute-done((bf16[8,2,16,512]{3,2,1,0:T(8,128)(2,1)}, bf16[8,2,16,512]{3,2,1,0:T(8,128)(2,1)S(1)}, u32[]{:S(2)}, u32[]{:S(2)}) %collective-permute-start.10) | collective-permute-done | bytes 262176 | tf_op jit(solution)/shard_map/ppermute | solution.py:823
  124.5 4.2 %collective-permute-done.11.refs_3_ = bf16[8,2,16,512]{3,2,1,0:T(8,128)(2,1)S(1)} collective-permute-done((bf16[8,2,16,512]{3,2,1,0:T(8,128)(2,1)}, bf16[8,2,16,512]{3,2,1,0:T(8,128)(2,1)S(1)}, u32[]{:S(2)}, u32[]{:S(2)}) %collective-permute-start.11) | collective-permute-done | bytes 262176 | tf_op jit(solution)/shard_map/ppermute | solution.py:823
  129.5 6.7 %mix_backward.1 = (bf16[768,512]{1,0:T(8,128)(2,1)}, bf16[768,512]{1,0:T(8,128)(2,1)}, f32[32,512]{1,0:T(8,128)}) custom-call(s32[4]{0:T(128)} %copy-done.25, bf16[768,512]{1,0:T(8,128)(2,1)} %get-tuple-element.91.spread, bf16[768,512]{1,0:T(8,128)(2,1)} %bitcast.78, bf16[768,512]{1,0:T(8,128)(2,1)} %bitcast.75, f32[768,32]{1,0:T(8,128)} %get-tuple-element.92.probs, ...), custom_call_target="tpu_custom_call" | custom-call | flops 1610612736 | bytes 6291456 | tf_op jit(solution)/shard_map/mix_backward/pallas_call | solution.py:309
  136.2 5.6 %all-to-all-done.2.both = bf16[8,4,2,2,16,512]{5,4,3,2,1,0:T(8,128)(2,1)S(1)} async-done(((bf16[8,4,2,2,16,512]{5,4,3,2,1,0:T(8,128)(2,1)}), bf16[8,4,2,2,16,512]{5,4,3,2,1,0:T(8,128)(2,1)S(1)}, u32[]{:S(2)}, u32[]{:S(2)}) %all-to-all-start.2) | async-done | bytes 2097184 | tf_op jit(solution)/shard_map/all_to_all | solution.py:975
  141.8 3.8 %all-to-all-start.3 = ((bf16[32,3,8,512]{3,2,1,0:T(8,128)(2,1)}), bf16[32,3,8,512]{3,2,1,0:T(8,128)(2,1)S(1)}, u32[]{:S(2)}, u32[]{:S(2)}) async-start(bf16[32,3,8,512]{3,2,1,0:T(8,128)(2,1)} %bitcast.79), calls=%async_computation.3 | async-start | bytes 1572864 | tf_op jit(solution)/shard_map/all_to_all | solution.py:931
  146.3 23.7 %expert_weights.1 = (bf16[2,528,512]{2,1,0:T(8,128)(2,1)}, bf16[2,528,512]{2,1,0:T(8,128)(2,1)}, bf16[2,528,512]{2,1,0:T(8,128)(2,1)}, bf16[1,528,512]{2,1,0:T(8,128)(2,1)}, bf16[1,528,512]{2,1,0:T(8,128)(2,1)}) custom-call(s32[2]{0:T(128)} %pad_add_fusion.2.where, s32[1]{0:T(128)} %bitcast.30.first, bf16[8,4,2,2,16,512]{5,4,3,2,1,0:T(8,128)(2,1)} %copy-done, ...), custom_call_target="tpu_custom_call" | custom-call | flops 6442450944 | bytes 18874368 | tf_op jit(solution)/shard_map/expert_weights/pallas_call | solution.py:455
  170.0 5.4 %all-to-all-start.4 = ((bf16[32,3,8,512]{3,2,1,0:T(8,128)(2,1)}), bf16[32,3,8,512]{3,2,1,0:T(8,128)(2,1)S(1)}, u32[]{:S(2)}, u32[]{:S(2)}) async-start(bf16[32,3,8,512]{3,2,1,0:T(8,128)(2,1)} %bitcast.76), calls=%async_computation.4 | async-start | bytes 1572864 | tf_op jit(solution)/shard_map/all_to_all | solution.py:931
  176.7 13.4 %attention_back_far.1 = (f32[3,256,512]{2,1,0:T(8,128)}, f32[3,256,512]{2,1,0:T(8,128)}, f32[8,512]{1,0:T(8,128)}, bf16[2176,128]{1,0:T(8,128)(2,1)}, bf16[2176,128]{1,0:T(8,128)(2,1)}) custom-call(s32[2]{0:T(128)} %pad_add_fusion.1.place, bf16[12,256,512]{2,1,0:T(8,128)(2,1)} %tokens.7, bf16[12,256,512]{2,1,0:T(8,128)(2,1)} %cots.1, ...), custom_call_target="tpu_custom_call" | custom-call | bytes 10747904 | tf_op jit(solution)/shard_map/attention_back_far/pallas_call | solution.py:659
  190.3 1.7 collective-permute-start.13
  192.0 1.5 collective-permute-start.14
  193.5 2.0 add_convert_fusion.1
  195.5 1.5 collective-permute-start.22
  197.0 12.5 %attention_back_near.1 = (bf16[3,256,512]{2,1,0:T(8,128)(2,1)}, bf16[2176,128]{1,0:T(8,128)(2,1)}, bf16[2176,128]{1,0:T(8,128)(2,1)}) custom-call(s32[2]{0:T(128)} %pad_add_fusion.1.place, bf16[12,256,512]{2,1,0:T(8,128)(2,1)} %tokens.7, f32[3,256,512]{2,1,0:T(8,128)} %get-tuple-element.117.d_hidden, f32[3,256,512]{2,1,0:T(8,128)} %get-tuple-element.121.partial, ...), custom_call_target="tpu_custom_call" | custom-call | bytes 8388608 | tf_op jit(solution)/shard_map/attention_back_near/pallas_call | solution.py:706
  209.5 7.9 %collective-permute-done.13.refs_1_ = bf16[2,528,512]{2,1,0:T(8,128)(2,1)S(1)} collective-permute-done((bf16[2,528,512]{2,1,0:T(8,128)(2,1)S(1)}, bf16[2,528,512]{2,1,0:T(8,128)(2,1)S(1)}, u32[]{:S(2)}, u32[]{:S(2)}) %collective-permute-start.13) | collective-permute-done | bytes 1081376 | tf_op jit(solution)/shard_map/ppermute | solution.py:828
  217.4 1.4 collective-permute-done.14.refs_2_
  218.9 2.1 collective-permute-done.21
  221.1 2.1 add_convert_fusion
  223.1 4.1 %all-to-all-start.5 = ((bf16[8,272,128]{2,1,0:T(8,128)(2,1)}), bf16[8,272,128]{2,1,0:T(8,128)(2,1)S(1)}, u32[]{:S(2)}, u32[]{:S(2)}) async-start(bf16[8,272,128]{2,1,0:T(8,128)(2,1)} %bitcast.38), calls=%async_computation.5 | async-start | bytes 1114112 | tf_op jit(solution)/shard_map/all_to_all | solution.py:806
  227.2 1.4 collective-permute-start.19
  228.6 4.0 %layer_output.1.refs_0_ = bf16[3,256,512]{2,1,0:T(8,128)(2,1)} custom-call(s32[2]{0:T(128)} %pad_add_fusion.1.place, f32[3,256,512]{2,1,0:T(8,128)} %get-tuple-element.87.hidden, bf16[32,3,8,512]{3,2,1,0:T(8,128)(2,1)} %copy-done.2), custom_call_target="tpu_custom_call" | custom-call | flops 1179648 | bytes 3145728 | tf_op jit(solution)/shard_map/layer_output/pallas_call | solution.py:749
  233.2 2.9 collective-permute-start.23
  236.2 6.6 %all-to-all-done.5 = bf16[8,272,128]{2,1,0:T(8,128)(2,1)S(1)} async-done(((bf16[8,272,128]{2,1,0:T(8,128)(2,1)}), bf16[8,272,128]{2,1,0:T(8,128)(2,1)S(1)}, u32[]{:S(2)}, u32[]{:S(2)}) %all-to-all-start.5) | async-done | bytes 557088 | tf_op jit(solution)/shard_map/all_to_all | solution.py:806
  242.9 9.6 %collective-permute-done.23.refs_3_ = bf16[1,528,512]{2,1,0:T(8,128)(2,1)S(1)} collective-permute-done((bf16[1,528,512]{2,1,0:T(8,128)(2,1)}, bf16[1,528,512]{2,1,0:T(8,128)(2,1)S(1)}, u32[]{:S(2)}, u32[]{:S(2)}) %collective-permute-start.23) | collective-permute-done | bytes 540704 | tf_op jit(solution)/shard_map/ppermute | solution.py:828
  252.5 10.8 %collective-permute-done.24.refs_4_ = bf16[1,528,512]{2,1,0:T(8,128)(2,1)} collective-permute-done((bf16[1,528,512]{2,1,0:T(8,128)(2,1)}, bf16[1,528,512]{2,1,0:T(8,128)(2,1)}, u32[]{:S(2)}, u32[]{:S(2)}) %collective-permute-start.24) | collective-permute-done | bytes 540704 | tf_op jit(solution)/shard_map/ppermute | solution.py:828
  264.2 4.7 %all-to-all-start.6 = ((bf16[8,272,128]{2,1,0:T(8,128)(2,1)}), bf16[8,272,128]{2,1,0:T(8,128)(2,1)S(1)}, u32[]{:S(2)}, u32[]{:S(2)}) async-start(bf16[8,272,128]{2,1,0:T(8,128)(2,1)} %broadcast_in_dim.79), calls=%async_computation.6 | async-start | bytes 1114112 | tf_op jit(solution)/shard_map/all_to_all | solution.py:810
  270.5 7.5 %owned_weights.1 = (f32[8,64,2048]{2,1,0:T(8,128)}, f32[8,256,512]{2,1,0:T(8,128)}, f32[8,16,512]{2,1,0:T(8,128)}) custom-call(s32[4]{0:T(128)} %iota_xor_fusion.where, bf16[2,528,512]{2,1,0:T(8,128)(2,1)} %get-tuple-element.143.refs_0_, bf16[2,528,512]{2,1,0:T(8,128)(2,1)} %copy-done.7, bf16[2,528,512]{2,1,0:T(8,128)(2,1)} %copy-done.8, ...), custom_call_target="tpu_custom_call" | custom-call | bytes 12976128 | tf_op jit(solution)/shard_map/owned_weights/pallas_call | solution.py:506
  283.0 4.7 %place_blocks.3 = bf16[12,256,512]{2,1,0:T(8,128)(2,1)} custom-call(s32[4]{0:T(128)} %copy-done.25, bf16[3,256,512]{2,1,0:T(8,128)(2,1)} %get-tuple-element.133.refs_0_, bf16[3,256,512]{2,1,0:T(8,128)(2,1)} %copy-done.14, bf16[3,256,512]{2,1,0:T(8,128)(2,1)} %collective-permute-done.19.refs_2_, bf16[3,256,512]{2,1,0:T(8,128)(2,1)} %copy-done.16), custom_call_target="tpu_custom_call" | custom-call | bytes 12582912 | tf_op jit(solution)/shard_map/place_blocks/pallas_call | solution.py:844
  289.4 4.7 %place_blocks.2 = bf16[12,256,512]{2,1,0:T(8,128)(2,1)} custom-call(s32[4]{0:T(128)} %copy-done.25, bf16[3,256,512]{2,1,0:T(8,128)(2,1)} %layer_output.1.refs_0_, bf16[3,256,512]{2,1,0:T(8,128)(2,1)} %copy-done.13, bf16[3,256,512]{2,1,0:T(8,128)(2,1)} %collective-permute-done.16.refs_2_, bf16[3,256,512]{2,1,0:T(8,128)(2,1)} %copy-done.15), custom_call_target="tpu_custom_call" | custom-call | bytes 12582912 | tf_op jit(solution)/shard_map/place_blocks/pallas_call | solution.py:844
  294.1 1.4 collective-permute-start.25
  (151 shorter events, 29.0 us)
Async XLA Ops:
  2.6 2.2 collective-permute-start
  4.8 9.5 %copy-start.4 = (bf16[512,512]{1,0:T(8,128)(2,1)S(1)}, bf16[512,512]{1,0:T(8,128)(2,1)}, u32[]{:S(2)}) copy-start(bf16[512,512]{1,0:T(8,128)(2,1)} %pack_weights.1.refs_0_) | copy-start | bytes 1572868
  4.8 11.1 %copy-start.24 = (bf16[512,8]{0,1:T(8,128)(2,1)S(1)}, bf16[512,8]{0,1:T(8,128)(2,1)}, u32[]{:S(2)}) copy-start(bf16[512,8]{0,1:T(8,128)(2,1)} %param.25) | copy-start | bytes 24580
  4.8 11.6 %copy-start.26 = (s32[8]{0:T(128)S(1)}, s32[8]{0:T(128)}, u32[]{:S(2)}) copy-start(s32[8]{0:T(128)} %param.17) | copy-start | bytes 100
  7.1 32.7 %all-to-all-start.1 = ((bf16[8,12,8,512]{3,2,1,0:T(8,128)(2,1)}), bf16[8,12,8,512]{3,2,1,0:T(8,128)(2,1)S(1)}, u32[]{:S(2)}, u32[]{:S(2)}) async-start(bf16[8,12,8,512]{3,2,1,0:T(8,128)(2,1)} %copy_bitcast_fusion), calls=%async_computation.1 | async-start | bytes 1572864 | tf_op jit(solution)/shard_map/all_to_all | solution.py:937
  14.4 13.8 %collective-permute-start.1 = (bf16[512,512]{1,0:T(8,128)(2,1)S(1)}, bf16[512,512]{1,0:T(8,128)(2,1)S(1)}, u32[]{:S(2)}, u32[]{:S(2)}) collective-permute-start(bf16[512,512]{1,0:T(8,128)(2,1)S(1)} %copy-done.4), channel_id=1, source_target_pairs={{2,0},{3,1},{0,2},{1,3},{6,4},{7,5},{4,6},{5,7},{10,8},{11,9},{8,1... | collective-permute-start | bytes 1572872 | tf_op jit(solution)/shard_map/ppermute | solution.py:776
  15.9 29.9 %collective-permute-start.4 = (bf16[8,512]{1,0:T(8,128)(2,1)S(1)}, bf16[8,512]{1,0:T(8,128)(2,1)S(1)}, u32[]{:S(2)}, u32[]{:S(2)}) collective-permute-start(bf16[8,512]{1,0:T(8,128)(2,1)S(1)} %bitcast.92), channel_id=1, source_target_pairs={{2,0},{3,1},{0,2},{1,3},{6,4},{7,5},{4,6},{5,7},{10,8},{11,9},{8,1... | collective-permute-start | bytes 24584 | tf_op jit(solution)/shard_map/ppermute | solution.py:776
  16.4 31.9 %collective-permute-start.3 = (bf16[8,512]{1,0:T(8,128)(2,1)S(1)}, bf16[8,512]{1,0:T(8,128)(2,1)S(1)}, u32[]{:S(2)}, u32[]{:S(2)}) collective-permute-start(bf16[8,512]{1,0:T(8,128)(2,1)S(1)} %bitcast.93), channel_id=1, source_target_pairs={{0,1},{1,0},{2,3},{3,2},{4,5},{5,4},{6,7},{7,6},{8,9},{9,8},{10,11... | collective-permute-start | bytes 24584 | tf_op jit(solution)/shard_map/ppermute | solution.py:771
  28.2 1.9 collective-permute-start.2
  28.4 11.3 %copy-start.25 = (s32[4]{0:T(128)}, s32[4]{0:T(128)S(1)}, u32[]{:S(2)}) copy-start(s32[4]{0:T(128)S(1)} %pad_add_fusion.relative.where) | copy-start | bytes 52
  39.8 5.7 %copy-start.27 = (s32[64]{0:T(128)S(1)}, s32[64]{0:T(128)}, u32[]{:S(2)}) copy-start(s32[64]{0:T(128)} %param.18) | copy-start | bytes 772
  39.8 26.3 %copy-start.17 = (bf16[8,12,8,512]{3,2,1,0:T(8,128)(2,1)}, bf16[8,12,8,512]{3,2,1,0:T(8,128)(2,1)S(1)}, u32[]{:S(2)}) copy-start(bf16[8,12,8,512]{3,2,1,0:T(8,128)(2,1)S(1)} %all-to-all-done.1) | copy-start | bytes 2359300
  39.8 26.3 %all-to-all-start = ((bf16[32,3,8,512]{3,2,1,0:T(8,128)(2,1)}), bf16[32,3,8,512]{3,2,1,0:T(8,128)(2,1)S(1)}, u32[]{:S(2)}, u32[]{:S(2)}) async-start(bf16[32,3,8,512]{3,2,1,0:T(8,128)(2,1)} %get-tuple-element.88), calls=%async_computation | async-start | bytes 1572864 | tf_op jit(solution)/shard_map/all_to_all | solution.py:925
  45.8 2.5 collective-permute-start.5
  72.3 1.9 collective-permute-start.6
  72.3 9.3 %collective-permute-start.7 = (bf16[8,2,16,512]{3,2,1,0:T(8,128)(2,1)}, bf16[8,2,16,512]{3,2,1,0:T(8,128)(2,1)S(1)}, u32[]{:S(2)}, u32[]{:S(2)}) collective-permute-start(bf16[8,2,16,512]{3,2,1,0:T(8,128)(2,1)} %get-tuple-element.95), channel_id=1, source_target_pairs={{0,2},{1,3},{2,0},{3,1},{4,6},{5,7},{6,4},{7,5},{8,10},{9,11},{10,... | collective-permute-start | bytes 786440 | tf_op jit(solution)/shard_map/ppermute | solution.py:817
  74.0 12.5 %collective-permute-start.8 = (bf16[8,2,16,512]{3,2,1,0:T(8,128)(2,1)}, bf16[8,2,16,512]{3,2,1,0:T(8,128)(2,1)S(1)}, u32[]{:S(2)}, u32[]{:S(2)}) collective-permute-start(bf16[8,2,16,512]{3,2,1,0:T(8,128)(2,1)} %get-tuple-element.96), channel_id=1, source_target_pairs={{0,3},{1,2},{2,1},{3,0},{4,7},{5,6},{6,5},{7,4},{8,11},{9,10},{10,... | collective-permute-start | bytes 786440 | tf_op jit(solution)/shard_map/ppermute | solution.py:817
  74.2 15.0 %copy-start.9 = (bf16[8,2,16,512]{3,2,1,0:T(8,128)(2,1)}, bf16[8,2,16,512]{3,2,1,0:T(8,128)(2,1)S(1)}, u32[]{:S(2)}) copy-start(bf16[8,2,16,512]{3,2,1,0:T(8,128)(2,1)S(1)} %collective-permute-done.6.refs_1_) | copy-start | bytes 786436
  81.7 7.5 %copy-start.10 = (bf16[8,2,16,512]{3,2,1,0:T(8,128)(2,1)}, bf16[8,2,16,512]{3,2,1,0:T(8,128)(2,1)S(1)}, u32[]{:S(2)}) copy-start(bf16[8,2,16,512]{3,2,1,0:T(8,128)(2,1)S(1)} %collective-permute-done.7.refs_2_) | copy-start | bytes 786436
  89.2 52.6 %all-to-all-start.2 = ((bf16[8,4,2,2,16,512]{5,4,3,2,1,0:T(8,128)(2,1)}), bf16[8,4,2,2,16,512]{5,4,3,2,1,0:T(8,128)(2,1)S(1)}, u32[]{:S(2)}, u32[]{:S(2)}) async-start(bf16[8,4,2,2,16,512]{5,4,3,2,1,0:T(8,128)(2,1)} %pad_maximum_fusion), calls=%async_computation.2 | async-start | bytes 4194304 | tf_op jit(solution)/shard_map/all_to_all | solution.py:975
  115.1 9.4 %collective-permute-start.10 = (bf16[8,2,16,512]{3,2,1,0:T(8,128)(2,1)}, bf16[8,2,16,512]{3,2,1,0:T(8,128)(2,1)S(1)}, u32[]{:S(2)}, u32[]{:S(2)}) collective-permute-start(bf16[8,2,16,512]{3,2,1,0:T(8,128)(2,1)} %get-tuple-element.103), channel_id=1, source_target_pairs={{2,0},{3,1},{0,2},{1,3},{6,4},{7,5},{4,6},{5,7},{10,8},{11,9},{8,1... | collective-permute-start | bytes 786440 | tf_op jit(solution)/shard_map/ppermute | solution.py:823
  116.6 12.1 %collective-permute-start.11 = (bf16[8,2,16,512]{3,2,1,0:T(8,128)(2,1)}, bf16[8,2,16,512]{3,2,1,0:T(8,128)(2,1)S(1)}, u32[]{:S(2)}, u32[]{:S(2)}) collective-permute-start(bf16[8,2,16,512]{3,2,1,0:T(8,128)(2,1)} %get-tuple-element.104), channel_id=1, source_target_pairs={{3,0},{2,1},{1,2},{0,3},{7,4},{6,5},{5,6},{4,7},{11,8},{10,9},{9,1... | collective-permute-start | bytes 786440 | tf_op jit(solution)/shard_map/ppermute | solution.py:823
  116.7 12.0 %collective-permute-start.9 = (bf16[8,2,16,512]{3,2,1,0:T(8,128)(2,1)}, bf16[8,2,16,512]{3,2,1,0:T(8,128)(2,1)S(1)}, u32[]{:S(2)}, u32[]{:S(2)}) collective-permute-start(bf16[8,2,16,512]{3,2,1,0:T(8,128)(2,1)} %get-tuple-element.102), channel_id=1, source_target_pairs={{1,0},{0,1},{3,2},{2,3},{5,4},{4,5},{7,6},{6,7},{9,8},{8,9},{11,10... | collective-permute-start | bytes 786440 | tf_op jit(solution)/shard_map/ppermute | solution.py:823
  141.8 28.2 %all-to-all-start.3 = ((bf16[32,3,8,512]{3,2,1,0:T(8,128)(2,1)}), bf16[32,3,8,512]{3,2,1,0:T(8,128)(2,1)S(1)}, u32[]{:S(2)}, u32[]{:S(2)}) async-start(bf16[32,3,8,512]{3,2,1,0:T(8,128)(2,1)} %bitcast.79), calls=%async_computation.3 | async-start | bytes 1572864 | tf_op jit(solution)/shard_map/all_to_all | solution.py:931
  170.0 6.7 %copy-start.3 = (bf16[32,3,8,512]{3,2,1,0:T(8,128)(2,1)}, bf16[32,3,8,512]{3,2,1,0:T(8,128)(2,1)S(1)}, u32[]{:S(2)}) copy-start(bf16[32,3,8,512]{3,2,1,0:T(8,128)(2,1)S(1)} %all-to-all-done.3.grads) | copy-start | bytes 2359300
  170.0 48.8 %all-to-all-start.4 = ((bf16[32,3,8,512]{3,2,1,0:T(8,128)(2,1)}), bf16[32,3,8,512]{3,2,1,0:T(8,128)(2,1)S(1)}, u32[]{:S(2)}, u32[]{:S(2)}) async-start(bf16[32,3,8,512]{3,2,1,0:T(8,128)(2,1)} %bitcast.76), calls=%async_computation.4 | async-start | bytes 1572864 | tf_op jit(solution)/shard_map/all_to_all | solution.py:931
  176.7 13.7 %copy-start.29 = (bf16[2,528,512]{2,1,0:T(8,128)(2,1)S(1)}, bf16[2,528,512]{2,1,0:T(8,128)(2,1)}, u32[]{:S(2)}) copy-start(bf16[2,528,512]{2,1,0:T(8,128)(2,1)} %get-tuple-element.130) | copy-start | bytes 3244036
  176.7 15.4 %copy-start.28 = (bf16[2,528,512]{2,1,0:T(8,128)(2,1)S(1)}, bf16[2,528,512]{2,1,0:T(8,128)(2,1)}, u32[]{:S(2)}) copy-start(bf16[2,528,512]{2,1,0:T(8,128)(2,1)} %get-tuple-element.131) | copy-start | bytes 3244036
  190.0 3.5 %collective-permute-start.12 = (bf16[2176,128]{1,0:T(8,128)(2,1)}, bf16[2176,128]{1,0:T(8,128)(2,1)S(1)}, u32[]{:S(2)}, u32[]{:S(2)}) collective-permute-start(bf16[2176,128]{1,0:T(8,128)(2,1)} %get-tuple-element.120), channel_id=1, source_target_pairs={{0,1},{1,0},{2,3},{3,2},{4,5},{5,4},{6,7},{7,6},{8,9},{9,8},{10,11... | collective-permute-start | bytes 1671176 | tf_op jit(solution)/shard_map/ppermute | solution.py:771
  190.3 27.0 %collective-permute-start.13 = (bf16[2,528,512]{2,1,0:T(8,128)(2,1)S(1)}, bf16[2,528,512]{2,1,0:T(8,128)(2,1)S(1)}, u32[]{:S(2)}, u32[]{:S(2)}) collective-permute-start(bf16[2,528,512]{2,1,0:T(8,128)(2,1)S(1)} %copy-done.29), channel_id=1, source_target_pairs={{0,4},{4,0},{8,12},{12,8},{16,20},{20,16},{24,28},{28,24},{1,5},{5... | collective-permute-start | bytes 3244040 | tf_op jit(solution)/shard_map/ppermute | solution.py:828
  192.0 26.8 %collective-permute-start.14 = (bf16[2,528,512]{2,1,0:T(8,128)(2,1)S(1)}, bf16[2,528,512]{2,1,0:T(8,128)(2,1)S(1)}, u32[]{:S(2)}, u32[]{:S(2)}) collective-permute-start(bf16[2,528,512]{2,1,0:T(8,128)(2,1)S(1)} %copy-done.28), channel_id=1, source_target_pairs={{0,8},{4,12},{8,0},{12,4},{16,24},{20,28},{24,16},{28,20},{1,9},{5... | collective-permute-start | bytes 3244040 | tf_op jit(solution)/shard_map/ppermute | solution.py:828
  195.5 23.4 %collective-permute-start.22 = (bf16[2176,128]{1,0:T(8,128)(2,1)}, bf16[2176,128]{1,0:T(8,128)(2,1)S(1)}, u32[]{:S(2)}, u32[]{:S(2)}) collective-permute-start(bf16[2176,128]{1,0:T(8,128)(2,1)} %add_convert_fusion.1), channel_id=1, source_target_pairs={{0,2},{1,3},{2,0},{3,1},{4,6},{5,7},{6,4},{7,5},{8,10},{9,11},{10,... | collective-permute-start | bytes 1671176 | tf_op jit(solution)/shard_map/ppermute | solution.py:781
  217.4 5.7 %copy-start.7 = (bf16[2,528,512]{2,1,0:T(8,128)(2,1)}, bf16[2,528,512]{2,1,0:T(8,128)(2,1)S(1)}, u32[]{:S(2)}) copy-start(bf16[2,528,512]{2,1,0:T(8,128)(2,1)S(1)} %collective-permute-done.13.refs_1_) | copy-start | bytes 3244036
  218.8 2.2 collective-permute-start.21
  223.1 19.6 %all-to-all-start.5 = ((bf16[8,272,128]{2,1,0:T(8,128)(2,1)}), bf16[8,272,128]{2,1,0:T(8,128)(2,1)S(1)}, u32[]{:S(2)}, u32[]{:S(2)}) async-start(bf16[8,272,128]{2,1,0:T(8,128)(2,1)} %bitcast.38), calls=%async_computation.5 | async-start | bytes 1114112 | tf_op jit(solution)/shard_map/all_to_all | solution.py:806
  227.2 41.8 %collective-permute-start.19 = (bf16[3,256,512]{2,1,0:T(8,128)(2,1)}, bf16[3,256,512]{2,1,0:T(8,128)(2,1)}, u32[]{:S(2)}, u32[]{:S(2)}) collective-permute-start(bf16[3,256,512]{2,1,0:T(8,128)(2,1)} %get-tuple-element.133.refs_0_), channel_id=1, source_target_pairs={{2,0},{3,1},{0,2},{1,3},{6,4},{7,5},{4,6},{5,7},{10,8},{11,9},{8,1... | collective-permute-start | bytes 2359304 | tf_op jit(solution)/shard_map/ppermute | solution.py:776
  232.6 36.3 %copy-start.12 = (bf16[3,256,512]{2,1,0:T(8,128)(2,1)S(1)}, bf16[3,256,512]{2,1,0:T(8,128)(2,1)}, u32[]{:S(2)}) copy-start(bf16[3,256,512]{2,1,0:T(8,128)(2,1)} %get-tuple-element.133.refs_0_) | copy-start | bytes 2359300
  232.6 36.9 %copy-start.1 = (bf16[3,256,512]{2,1,0:T(8,128)(2,1)S(1)}, bf16[3,256,512]{2,1,0:T(8,128)(2,1)}, u32[]{:S(2)}) copy-start(bf16[3,256,512]{2,1,0:T(8,128)(2,1)} %layer_output.1.refs_0_) | copy-start | bytes 2359300
  232.6 37.0 %collective-permute-start.16 = (bf16[3,256,512]{2,1,0:T(8,128)(2,1)}, bf16[3,256,512]{2,1,0:T(8,128)(2,1)}, u32[]{:S(2)}, u32[]{:S(2)}) collective-permute-start(bf16[3,256,512]{2,1,0:T(8,128)(2,1)} %layer_output.1.refs_0_), channel_id=1, source_target_pairs={{2,0},{3,1},{0,2},{1,3},{6,4},{7,5},{4,6},{5,7},{10,8},{11,9},{8,1... | collective-permute-start | bytes 2359304 | tf_op jit(solution)/shard_map/ppermute | solution.py:776
  233.2 19.3 %collective-permute-start.23 = (bf16[1,528,512]{2,1,0:T(8,128)(2,1)}, bf16[1,528,512]{2,1,0:T(8,128)(2,1)S(1)}, u32[]{:S(2)}, u32[]{:S(2)}) collective-permute-start(bf16[1,528,512]{2,1,0:T(8,128)(2,1)} %get-tuple-element.140), channel_id=1, source_target_pairs={{0,12},{4,8},{8,4},{12,0},{16,28},{20,24},{24,20},{28,16},{1,13},{... | collective-permute-start | bytes 1622024 | tf_op jit(solution)/shard_map/ppermute | solution.py:828
  236.1 27.2 %collective-permute-start.24 = (bf16[1,528,512]{2,1,0:T(8,128)(2,1)}, bf16[1,528,512]{2,1,0:T(8,128)(2,1)}, u32[]{:S(2)}, u32[]{:S(2)}) collective-permute-start(bf16[1,528,512]{2,1,0:T(8,128)(2,1)} %get-tuple-element.141), channel_id=1, source_target_pairs={{0,12},{4,8},{8,4},{12,0},{16,28},{20,24},{24,20},{28,16},{1,13},{... | collective-permute-start | bytes 1622024 | tf_op jit(solution)/shard_map/ppermute | solution.py:828
  252.5 11.7 %copy-start.19 = (bf16[1,528,512]{2,1,0:T(8,128)(2,1)}, bf16[1,528,512]{2,1,0:T(8,128)(2,1)S(1)}, u32[]{:S(2)}) copy-start(bf16[1,528,512]{2,1,0:T(8,128)(2,1)S(1)} %collective-permute-done.23.refs_3_) | copy-start | bytes 1622020
  264.2 29.9 %all-to-all-start.6 = ((bf16[8,272,128]{2,1,0:T(8,128)(2,1)}), bf16[8,272,128]{2,1,0:T(8,128)(2,1)S(1)}, u32[]{:S(2)}, u32[]{:S(2)}) async-start(bf16[8,272,128]{2,1,0:T(8,128)(2,1)} %broadcast_in_dim.79), calls=%async_computation.6 | async-start | bytes 1114112 | tf_op jit(solution)/shard_map/all_to_all | solution.py:810
  268.9 12.3 %collective-permute-start.18 = (bf16[3,256,512]{2,1,0:T(8,128)(2,1)S(1)}, bf16[3,256,512]{2,1,0:T(8,128)(2,1)S(1)}, u32[]{:S(2)}, u32[]{:S(2)}) collective-permute-start(bf16[3,256,512]{2,1,0:T(8,128)(2,1)S(1)} %copy-done.12), channel_id=1, source_target_pairs={{0,1},{1,0},{2,3},{3,2},{4,5},{5,4},{6,7},{7,6},{8,9},{9,8},{10,11... | collective-permute-start | bytes 2359304 | tf_op jit(solution)/shard_map/ppermute | solution.py:771
  269.0 12.2 %collective-permute-start.20 = (bf16[3,256,512]{2,1,0:T(8,128)(2,1)}, bf16[3,256,512]{2,1,0:T(8,128)(2,1)S(1)}, u32[]{:S(2)}, u32[]{:S(2)}) collective-permute-start(bf16[3,256,512]{2,1,0:T(8,128)(2,1)} %collective-permute-done.19.refs_2_), channel_id=1, source_target_pairs={{0,1},{1,0},{2,3},{3,2},{4,5},{5,4},{6,7},{7,6},{8,9},{9,8},{10,11... | collective-permute-start | bytes 2359304 | tf_op jit(solution)/shard_map/ppermute | solution.py:771
  269.5 18.2 %collective-permute-start.15 = (bf16[3,256,512]{2,1,0:T(8,128)(2,1)S(1)}, bf16[3,256,512]{2,1,0:T(8,128)(2,1)S(1)}, u32[]{:S(2)}, u32[]{:S(2)}) collective-permute-start(bf16[3,256,512]{2,1,0:T(8,128)(2,1)S(1)} %copy-done.1), channel_id=1, source_target_pairs={{0,1},{1,0},{2,3},{3,2},{4,5},{5,4},{6,7},{7,6},{8,9},{9,8},{10,11... | collective-permute-start | bytes 2359304 | tf_op jit(solution)/shard_map/ppermute | solution.py:771
  269.6 18.1 %collective-permute-start.17 = (bf16[3,256,512]{2,1,0:T(8,128)(2,1)}, bf16[3,256,512]{2,1,0:T(8,128)(2,1)S(1)}, u32[]{:S(2)}, u32[]{:S(2)}) collective-permute-start(bf16[3,256,512]{2,1,0:T(8,128)(2,1)} %collective-permute-done.16.refs_2_), channel_id=1, source_target_pairs={{0,1},{1,0},{2,3},{3,2},{4,5},{5,4},{6,7},{7,6},{8,9},{9,8},{10,11... | collective-permute-start | bytes 2359304 | tf_op jit(solution)/shard_map/ppermute | solution.py:771
  294.1 3.9 %collective-permute-start.25 = (bf16[16,128]{1,0:T(8,128)(2,1)S(1)}, bf16[16,128]{1,0:T(8,128)(2,1)S(1)}, u32[]{:S(2)}, u32[]{:S(2)}) collective-permute-start(bf16[16,128]{1,0:T(8,128)(2,1)S(1)} %slice.66), channel_id=1, source_target_pairs={{0,2},{1,3},{2,0},{3,1},{4,6},{5,7},{6,4},{7,5},{8,10},{9,11},{10,... | collective-permute-start | bytes 12296 | tf_op jit(solution)/shard_map/ppermute | solution.py:781
  (18 other events, 44.7 us)

commit v4 on v3

--- a/solution.py
+++ b/solution.py
@@ -279,7 +279,7 @@
 def unmix_kernel(
     part, narrow, relative, spread, rows, cots, probs, controller, row_code, col_code, tile, *refs
 ):
-    back, (grad_out, mixed_out, gain_out, outs, grads) = refs[:narrow], refs[narrow:]
+    back, (sent, gain_out, outs, grads) = refs[:narrow], refs[narrow:]
     count, _, lines, _ = back[0].shape
     for j, piece in enumerate(back):
         for e in range(count):
@@ -292,18 +292,19 @@
     d_weights = mm_nt(pairs, tile[...])
     p = probs[...]
     d_logits = (p * (d_weights - group_totals(p * d_weights, row_code[...], part))).astype(BF16)
-    grad_out[...] = (mm(spread[...], grads[...]) + mm_nt(d_logits, controller[...])).astype(BF16)
-    mixed_out[...] = mm(spread[...], outs[...]).astype(BF16)
+    shape = (sent.shape[0],) + sent.shape[2:]
+    grad = mm(spread[...], grads[...]) + mm_nt(d_logits, controller[...])
+    sent[:, 0] = grad.reshape(shape).astype(BF16)
+    sent[:, 1] = mm(spread[...], outs[...]).reshape(shape).astype(BF16)
     gain_out[...] = mm_tn(d_logits, held)
 
 
-def mix_backward(part, relative, spread, rows, cots, probs, back, controller, row_code, col_code, tile):
+def mix_backward(part, relative, spread, rows, cots, probs, back, controller, row_code, col_code, tile, devices):
     count, width = rows.shape
     experts, columns = tile.shape
     operands = (spread, rows, cots, probs, controller, row_code, col_code, tile) + tuple(back)
     outs = [
-        jax.ShapeDtypeStruct((count, width), BF16),
-        jax.ShapeDtypeStruct((count, width), BF16),
+        jax.ShapeDtypeStruct((devices, 2, count // devices, width), BF16),
         jax.ShapeDtypeStruct((experts, width), F32),
     ]
     return pl.pallas_call(
@@ -380,28 +381,16 @@
     )(*both, w_in, b_in[:, None], w_out, b_out[:, None])
 
 
-def weight_kernel(units, where, first, both, w_in, b_in, w_out, *refs):
-    refs, (merged, grads, turned, total) = refs[:-4], refs[-4:]
-    outs = list(refs[: units - 1]) + [refs[units - 1 :]]
-    p, i = pl.program_id(0), pl.program_id(1)
-    half, unit = where[0], where[1]
+def weight_kernel(units, where, both, w_in, b_in, w_out, *refs):
+    outs, (merged, grads, turned, total) = refs[:units], refs[units:]
+    i, half, unit = pl.program_id(0), where[0], where[1]
+    steps = pl.num_programs(0)
     width = both.shape[-1]
-    block = w_out.shape[1]
     span = turned.shape[0]
     rows = span // units
-    fold = width // block
-    height = refs[0].shape[1]
-
-    def put(lines, at, values, d=None):
-        for u in range(units) if d is None else [d]:
-            if u < units - 1:
-                outs[u][p, lines, at] = values
-            else:
-                for expert, out in enumerate(outs[u]):
-
-                    @pl.when(p == expert)
-                    def _(out=out):
-                        out[0, lines, at] = values
+    height = outs[0].shape[0]
+    block = height - 16 - steps * rows
+    slices = width // block
 
     @pl.when(i == 0)
     def _():
@@ -409,110 +398,100 @@
         grads[...] = both[:, :, 0, 1].reshape(grads.shape)
         turned[...] = merged[:, pl.ds(pl.multiple_of(half * span, span), span)].T
         sums = jnp.sum(grads[...].astype(F32), axis=0, keepdims=True).astype(BF16)
-        put(slice(height - 16, height), slice(0, width), jnp.zeros((16, width), BF16))
-        put(slice(height - 1, height), slice(0, width), sums)
+        for out in outs:
+            out[height - 16 :] = jnp.zeros((16, width), BF16)
+            out[height - 1 :] = sums
 
     act, slope = gelu_pair(mm(merged[...], w_in[0]) + b_in[0])
     d_pre = (mm_nt(grads[...], w_out[0]) * slope).astype(BF16)
     bias = jnp.sum(d_pre.astype(F32), axis=0, keepdims=True).astype(BF16)
     total[...] = mm(turned[...], d_pre)
-    for part in range(fold):
-
-        @pl.when(lax.rem(i, fold) == part)
-        def _(part=part):
-            at = slice(part * block, (part + 1) * block)
-            base = pl.ds(pl.multiple_of(i // fold * rows, rows), rows)
-            for d in range(units):
-                own = pl.multiple_of(lax.bitwise_xor(unit, d) * rows, rows)
-                put(base, at, total[pl.ds(own, rows)].astype(BF16), d)
-
-    for step in range(pl.num_programs(1)):
+    base = pl.ds(pl.multiple_of(i * rows, rows), rows)
+    for d, out in enumerate(outs):
+        own = pl.ds(pl.multiple_of(lax.bitwise_xor(unit, d) * rows, rows), rows)
+        out[base] = total[own].astype(BF16)
+    for step in range(steps):
 
         @pl.when(i == step)
         def _(step=step):
-            line = height - 16 + step // fold
-            put(slice(line, line + 1), slice(step % fold * block, (step % fold + 1) * block), bias)
-
-    @pl.when((i >= half * units) & (i < (half + 1) * units))
+            for out in outs:
+                out[height - 16 + step : height - 15 + step] = bias
+
+    @pl.when(i // (steps // 2) == half)
     def _():
         grad = mm_tn(act.astype(BF16), grads[...]).astype(BF16)
-        start = height - 16 - block
-        for d in range(units):
-
-            @pl.when(i - half * units == lax.bitwise_xor(unit, d))
-            def _(d=d):
-                put(slice(start, start + block), slice(0, width), grad, d)
-
-
-def expert_weights(where, first, both, w_in, b_in, w_out, wide, units):
-    sources, inner_sources, held, _, rows, width = both.shape
+        first = (i - half * (steps // 2)) * slices
+        for s in range(slices):
+            for d, out in enumerate(outs):
+
+                @pl.when(first + s == lax.bitwise_xor(unit, d))
+                def _(s=s, out=out):
+                    out[height - 16 - block : height - 16] = grad[s * block : (s + 1) * block]
+
+
+def expert_weights(where, expert, p, both, w_in, b_in, w_out, wide, units):
+    sources, inner_sources, _, _, rows, width = both.shape
     inner = w_in.shape[2]
-    block = inner // wide
     count = sources * inner_sources * rows
     span = width * units // wide
-    height = inner // width * (width // wide) + block + 16
-    shapes = [(held, height, width)] * (units - 1) + [(1, height, width)] * held
+    height = inner // width * (width // wide) + inner // wide + 16
     return pl.pallas_call(
-        functools.partial(weight_kernel, units),
+        lambda where, expert, *refs: weight_kernel(units, where, *refs),
         grid_spec=pltpu.PrefetchScalarGridSpec(
             num_scalar_prefetch=2,
-            grid=(held, wide),
+            grid=(inner // width,),
             in_specs=[
                 pl.BlockSpec(
-                    (sources, inner_sources, 1, 2, rows, width), lambda p, i, w, f: (0, 0, p, 0, 0, 0)
+                    (sources, inner_sources, 1, 2, rows, width), lambda i, w, e: (0, 0, p, 0, 0, 0)
                 ),
-                pl.BlockSpec((1, width, block), lambda p, i, w, f: (f[0] + p, 0, i)),
-                pl.BlockSpec((1, 1, block), lambda p, i, w, f: (f[0] + p, 0, i)),
-                pl.BlockSpec((1, block, width), lambda p, i, w, f: (f[0] + p, i, 0)),
+                pl.BlockSpec((1, width, width), lambda i, w, e: (e[0], 0, i)),
+                pl.BlockSpec((1, 1, width), lambda i, w, e: (e[0], 0, i)),
+                pl.BlockSpec((1, width, width), lambda i, w, e: (e[0], i, 0)),
             ],
-            out_specs=[whole(x) for x in shapes],
+            out_specs=[whole((height, width))] * units,
             scratch_shapes=[pltpu.VMEM((count, width), BF16)] * 2
-            + [pltpu.VMEM((span, count), BF16), pltpu.VMEM((span, block), F32)],
-        ),
-        out_shape=[jax.ShapeDtypeStruct(x, BF16) for x in shapes],
-        compiler_params=params("arbitrary", "arbitrary"),
+            + [pltpu.VMEM((span, count), BF16), pltpu.VMEM((span, width), F32)],
+        ),
+        out_shape=[jax.ShapeDtypeStruct((height, width), BF16)] * units,
+        compiler_params=params("arbitrary"),
         cost_estimate=pl.CostEstimate(
-            flops=held * 6 * count * width * inner,
-            bytes_accessed=held * (8 * width * inner + 4 * count * width),
-            transcendentals=held * count * inner,
+            flops=6 * count * width * inner,
+            bytes_accessed=8 * width * inner + 4 * count * width,
+            transcendentals=count * inner,
         ),
         name="expert_weights",
-    )(where, first, both, w_in, b_in[:, None], w_out)
-
-
-def owner_kernel(units, held, where, *refs):
+    )(where, expert, both, w_in, b_in[:, None], w_out)
+
+
+def owner_kernel(where, *refs):
     pieces, (g_in, g_out, bias) = refs[:-3], refs[-3:]
     rows, block = g_in.shape[1], g_out.shape[1]
     width = g_out.shape[2]
-    start = pieces[0].shape[1] - 16 - block
-    for d in range(units):
-        for p in range(held):
-
-            @pl.when((pl.program_id(0) == d) & (pl.program_id(1) == p))
-            def _(d=d, p=p):
-                ref, e = (pieces[d], p) if d < units - 1 else (pieces[d + p], 0)
-                for c in range(g_in.shape[2] // width):
-                    at = slice(c * width, (c + 1) * width)
-                    g_in[0, :, at] = ref[e, c * rows : (c + 1) * rows].astype(F32)
-                g_out[0] = ref[e, start : start + block].astype(F32)
-                bias[0] = ref[e, start + block :].astype(F32)
-
-
-def owned_weights(pieces, where, inner, wide, units):
-    width = pieces[0].shape[2]
-    held = len(pieces) - units + 1
-    count = units * held
+    start = pieces[0].shape[0] - 16 - block
+    for j, piece in enumerate(pieces):
+
+        @pl.when(pl.program_id(0) == j)
+        def _(piece=piece):
+            for c in range(g_in.shape[2] // width):
+                g_in[0, :, c * width : (c + 1) * width] = piece[c * rows : (c + 1) * rows].astype(F32)
+            g_out[0] = piece[start : start + block].astype(F32)
+            bias[0] = piece[start + block :].astype(F32)
+
+
+def owned_weights(pieces, where, inner, wide):
+    count = len(pieces)
+    width = pieces[0].shape[1]
     shapes = [(1, width // wide, inner), (1, inner // wide, width), (1, 16, width)]
     return pl.pallas_call(
-        functools.partial(owner_kernel, units, held),
+        owner_kernel,
         grid_spec=pltpu.PrefetchScalarGridSpec(
             num_scalar_prefetch=1,
-            grid=(units, held),
+            grid=(count,),
             in_specs=[whole(x.shape) for x in pieces],
-            out_specs=[pl.BlockSpec(x, lambda d, p, where: (where[d] * held + p, 0, 0)) for x in shapes],
+            out_specs=[pl.BlockSpec(x, lambda j, where: (where[j], 0, 0)) for x in shapes],
         ),
         out_shape=[jax.ShapeDtypeStruct((count,) + x[1:], F32) for x in shapes],
-        compiler_params=params("arbitrary", "arbitrary"),
+        compiler_params=params("arbitrary"),
         cost_estimate=pl.CostEstimate(
             flops=0, bytes_accessed=sum(x.size for x in pieces) * 6, transcendentals=0
         ),
@@ -575,9 +554,9 @@
         out[height:] = jnp.concatenate(tail + [jnp.zeros((left, LANES), BF16)], axis=0)
 
 
-def back_far_kernel(blocks, lanes, place, tokens, cots, grads, hidden, joint, context, *refs):
+def back_far_kernel(blocks, lanes, place, tokens, cots, grads, mixed, hidden, joint, context, *refs):
     packs, (gain_attn, gain_mix, controllers), refs = refs[:blocks], refs[blocks : blocks + 3], refs[blocks + 3 :]
-    (partial_out, d_hidden_out, gain_out), outs, total = refs[:3], refs[3:-1], refs[-1]
+    (partial_out, d_hidden_out, mixed_out, gain_out), outs, total = refs[:4], refs[4:-1], refs[-1]
     i = pl.program_id(0)
     length, width = hidden.shape[1:]
     live = (place[0] + i < place[1]).astype(F32)
@@ -597,6 +576,7 @@
         d_normed - normed * jnp.mean(d_normed * normed, axis=-1, keepdims=True)
     )
     d_hidden_out[0] = d_hidden
+    mixed_out[0] = (live * (hidden[0] + mixed[...].astype(F32).reshape(length, width))).astype(BF16)
     rows = tokens[0].astype(F32)
     entry = (rows * inverse_rms(rows) * gain_attn[...]).astype(BF16)
     partial_out[0] = attend_back(
@@ -644,10 +624,11 @@
 
 
 def attention_back_far(
-    place, tokens, cotangent, grads, hidden, joint, context, packs, gain_attn, gain_mix, controllers, height
+    place, tokens, cotangent, back, hidden, joint, context, packs, gain_attn, gain_mix, controllers, height
 ):
     total, length, width = tokens.shape
-    spread, slots, part, _ = grads.shape
+    slots = hidden.shape[0]
+    spread, part = back.shape[0], back.shape[2] // slots
     inner = context.shape[2]
     blocks = len(packs)
     count = controllers.shape[0]
@@ -664,7 +645,8 @@
             in_specs=[
                 pl.BlockSpec((1, length, width), own),
                 pl.BlockSpec((1, length, width), own),
-                pl.BlockSpec((spread, 1, part, width), lambda i, place: (0, i, 0, 0)),
+                pl.BlockSpec((spread, 1, part, width), lambda i, place: (0, 0, i, 0)),
+                pl.BlockSpec((spread, 1, part, width), lambda i, place: (0, 1, i, 0)),
                 rows,
                 pl.BlockSpec((1, length, 3 * inner), local_block),
                 pl.BlockSpec((1, length, inner), local_block),
@@ -672,12 +654,13 @@
             + [whole(p.shape) for p in packs]
             + [whole((1, width))] * 2
             + [whole(controllers.shape)],
-            out_specs=[rows, rows, whole((8, width))] + [whole((height, LANES))] * count,
+            out_specs=[rows, rows, rows, whole((8, width))] + [whole((height, LANES))] * count,
             scratch_shapes=[pltpu.VMEM((blocks, 4 * width, LANES), F32)],
         ),
         out_shape=[
             jax.ShapeDtypeStruct((slots, length, width), F32),
             jax.ShapeDtypeStruct((slots, length, width), F32),
+            jax.ShapeDtypeStruct((slots, length, width), BF16),
             jax.ShapeDtypeStruct((8, width), F32),
         ]
         + [jax.ShapeDtypeStruct((height, LANES), BF16)] * count,
@@ -688,7 +671,7 @@
             transcendentals=slots * length * length * inner // HEAD_WIDTH,
         ),
         name="attention_back_far",
-    )(place, tokens, cotangent, grads, hidden, joint, context, *packs, gain_attn, gain_mix, controllers)
+    )(place, tokens, cotangent, back, back, hidden, joint, context, *packs, gain_attn, gain_mix, controllers)
 
 
 def attention_back_near(
@@ -737,35 +720,6 @@
     )(place, tokens, d_hidden, partial, joint, context, *packs, gain_attn, gain_in, controllers)
 
 
-def output_kernel(place, hidden, mixed, out):
-    live = (place[0] + pl.program_id(0) < place[1]).astype(F32)
-    rows = mixed[...].astype(F32).reshape(hidden.shape[1:])
-    out[0] = (live * (hidden[0] + rows)).astype(BF16)
-
-
-def layer_output(place, hidden, mixed):
-    spread, slots, part, width = mixed.shape
-    length = hidden.shape[1]
-    return pl.pallas_call(
-        output_kernel,
-        grid_spec=pltpu.PrefetchScalarGridSpec(
-            num_scalar_prefetch=1,
-            grid=(slots,),
-            in_specs=[
-                pl.BlockSpec((1, length, width), lambda i, place: (i, 0, 0)),
-                pl.BlockSpec((spread, 1, part, width), lambda i, place: (0, i, 0, 0)),
-            ],
-            out_specs=pl.BlockSpec((1, length, width), lambda i, place: (i, 0, 0)),
-        ),
-        out_shape=jax.ShapeDtypeStruct((slots, length, width), BF16),
-        compiler_params=params("arbitrary"),
-        cost_estimate=pl.CostEstimate(
-            flops=slots * length * width * 3, bytes_accessed=slots * length * width * 8, transcendentals=0
-        ),
-        name="layer_output",
-    )(place, hidden, mixed)
-
-
 def swap_core(x):
     narrow = lax.axis_size("narrow")
     return lax.ppermute(x, "narrow", [(n, n ^ 1) for n in range(narrow)])
@@ -800,15 +754,21 @@
     return [(x.astype(F32) + y.astype(F32)).astype(BF16) for x, y in pairs]
 
 
-def sum_wide(x, *others):
+def after(x, *others):
+    return lax.optimization_barrier((x, others))[0]
+
+
+def wide_parts(x):
     wide = lax.axis_size("wide")
     parts = x.astype(BF16).reshape(wide, x.shape[0] // wide, x.shape[1])
     parts = lax.all_to_all(parts, "wide", split_axis=0, concat_axis=0, tiled=True)
-    part = jnp.sum(parts.astype(F32), axis=0).astype(BF16)
-    part, others = lax.optimization_barrier((part, others))
-    parts = jnp.broadcast_to(part[None], parts.shape)
+    return jnp.sum(parts.astype(F32), axis=0).astype(BF16)
+
+
+def from_parts(part):
+    parts = jnp.broadcast_to(part[None], (lax.axis_size("wide"),) + part.shape)
     parts = lax.all_to_all(parts, "wide", split_axis=0, concat_axis=0, tiled=True)
-    return parts.reshape(x.shape).astype(F32), others
+    return parts.reshape(-1, part.shape[-1]).astype(F32)
 
 
 def to_relative(x, j):
@@ -828,31 +788,30 @@
     return lax.ppermute(x, "wide", [(w, w ^ d) for w in range(wide)])
 
 
-def place_kernel(count, where, *refs):
-    out = refs[count]
-    for j in range(count):
+def place_kernel(where, *refs):
+    pieces, out = refs[:-1], refs[-1]
+    for j, piece in enumerate(pieces):
 
         @pl.when(pl.program_id(0) == j)
-        def _(j=j):
-            out[...] = refs[j][...].astype(out.dtype)
-
-
-def place_blocks(pieces, where, dtype):
+        def _(piece=piece):
+            out[...] = piece[...]
+
+
+def place_blocks(pieces, where):
     count = len(pieces)
     shape = pieces[0].shape
-    zeros = (0,) * (len(shape) - 1)
     return pl.pallas_call(
-        functools.partial(place_kernel, count),
+        place_kernel,
         grid_spec=pltpu.PrefetchScalarGridSpec(
             num_scalar_prefetch=1,
             grid=(count,),
             in_specs=[whole(shape)] * count,
-            out_specs=pl.BlockSpec(shape, lambda i, where: (where[i],) + zeros),
-        ),
-        out_shape=jax.ShapeDtypeStruct((count * shape[0],) + shape[1:], dtype),
+            out_specs=pl.BlockSpec(shape, lambda j, where: (where[j], 0, 0)),
+        ),
+        out_shape=jax.ShapeDtypeStruct((count * shape[0],) + shape[1:], pieces[0].dtype),
         compiler_params=params("arbitrary"),
         cost_estimate=pl.CostEstimate(
-            flops=0, bytes_accessed=pieces[0].size * 8 * count, transcendentals=0
+            flops=0, bytes_accessed=pieces[0].size * 4 * count, transcendentals=0
         ),
         name="place_blocks",
     )(where, *pieces)
@@ -927,7 +886,8 @@
         return x.reshape(-1, model_width)
 
     def to_slots(x):
-        x = x.reshape(spread, slots, padded_part, model_width)[:, :, :part]
+        x = x.reshape(spread, 2, slots, padded_part, model_width)[:, :, :, :part]
+        x = x.reshape(spread, 2, slots * part, model_width)
         return lax.all_to_all(x, BOTH, split_axis=0, concat_axis=0, tiled=True)
 
     cots, *packs = lax.optimization_barrier((cotangent, *packs))
@@ -982,30 +942,40 @@
         back = [back[:, :, j] for j in range(narrow)]
 
     where = jnp.stack([wide_index // units, unit]).astype(jnp.int32)
-    first = (unit * held // share).astype(jnp.int32)[None]
-    expert_grads = expert_weights(where, first, tokens_all, w_in, b_in, w_out, wide, units)
+    first = (unit * held // share).astype(jnp.int32)
+    expert_grads = [
+        expert_weights(where, (first + p)[None], p, tokens_all, w_in, b_in, w_out, wide, units)
+        for p in range(held)
+    ]
 
     back = [untrim(x if j == 0 else from_relative(x, j)) for j, x in enumerate(back)]
-    grad_rows, mixed_rows, grad_controller = mix_backward(
-        padded_part, relative, spread_probs, mix_rows, cot_rows, probs, back, controllers, row_code, col_code, tile
-    )
-    grads = to_slots(grad_rows)
-    mixed_rows, expert_grads, grads = lax.optimization_barrier((mixed_rows, expert_grads, grads))
-    mixed = to_slots(mixed_rows)
-
-    expert_grads = list(expert_grads[:1]) + [
-        to_unit(x, min(d, units - 1)) for d, x in enumerate(expert_grads) if d
-    ]
+    slot_rows, grad_controller = mix_backward(
+        padded_part,
+        relative,
+        spread_probs,
+        mix_rows,
+        cot_rows,
+        probs,
+        back,
+        controllers,
+        row_code,
+        col_code,
+        tile,
+        spread,
+    )
+    slot_rows = to_slots(slot_rows)
+    expert_grads = [[x[0]] + [to_unit(x[d], d) for d in range(1, units)] for x in expert_grads]
+    slot_rows = after(slot_rows, expert_grads[0][:-1], [x[0] for x in expert_grads])
 
     height = 4 * model_width
     grad_controller = grad_controller.astype(BF16).reshape(narrow, -1, LANES)[relative]
     end = height + grad_controller.shape[1]
     rows_sent = -(-(end + 16) // (16 * wide)) * 16 * wide
-    partial, d_hidden, gain_mix_part, *far = attention_back_far(
+    partial, d_hidden, mixed_part, gain_mix_part, *far = attention_back_far(
         place,
         tokens,
         cotangent,
-        grads,
+        slot_rows,
         hidden,
         joint_far,
         context_far,
@@ -1015,6 +985,10 @@
         grad_controller[2:],
         rows_sent,
     )
+    early = [x[1:-1] for x in expert_grads[1:]]
+    far, early = lax.optimization_barrier((far, early))
+    for x, pieces in zip(expert_grads[1:], early):
+        x[1:-1] = pieces
     partial, far = lax.optimization_barrier((partial, far_sums(far)))
     far = sum([to_chip(x, k + 1).astype(F32) for k, x in enumerate(far)], 0.0)
     d_tokens, kept, sent = attention_back_near(
@@ -1030,27 +1004,42 @@
         grad_controller[:2],
         rows_sent,
     )
-    d_tokens, kept, sent, mixed, expert_grads[:3] = lax.optimization_barrier(
-        (d_tokens, kept, sent, mixed, expert_grads[:3])
+    d_tokens, kept, sent, far, expert_grads[0][-1] = lax.optimization_barrier(
+        (d_tokens, kept, sent, far, expert_grads[0][-1])
     )
     weights = kept.astype(F32) + swap_core(sent).astype(F32) + far
-    weights, expert_grads = sum_wide(weights, *expert_grads)
+    part_sums = wide_parts(weights)
+
+    d_tokens = [d_tokens] + [from_chip(d_tokens, k) for k in range(1, narrow // 2)]
+    swapped = [swap_core(d_tokens[0]), swap_core(mixed_part)]
+    mixed_part, d_tokens[1:], swapped, expert_grads = lax.optimization_barrier(
+        (mixed_part, d_tokens[1:], swapped, expert_grads)
+    )
+    mixed_part = [mixed_part] + [from_chip(mixed_part, k) for k in range(1, narrow // 2)]
+    order = lax.bitwise_xor(unit, jnp.arange(units)) * held
+    order = (order[None] + jnp.arange(held)[:, None]).reshape(-1)
+    pieces = [piece for x in expert_grads for piece in x]
+    g_w_in, g_w_out, bias = owned_weights(pieces, order, w_in.shape[2], wide)
+    swapped = swapped + [swap_core(x) for x in d_tokens[1:]]
+    part_sums, bias, swapped = lax.optimization_barrier((part_sums, bias, swapped))
+
+    def placed(pieces, others):
+        pieces = [x for pair in zip(pieces, others) for x in pair]
+        return place_blocks(pieces, relative)[:slot_count]
+
+    d_tokens = placed(d_tokens, swapped[:1] + swapped[2:])
+    mixed_part[1:], d_tokens = lax.optimization_barrier((mixed_part[1:], d_tokens))
+    mixed_part = placed(mixed_part, swapped[1:2] + [swap_core(x) for x in mixed_part[1:]])
+    weights = from_parts(part_sums)
     gains = weights[end : end + 16].astype(BF16)
     gains = sum([to_chip(gains, k).astype(F32) for k in range(1, narrow // 2)], gains.astype(F32))
     projections = weights[: 3 * model_width, :head_columns].reshape(3, model_width, head_columns)
     output_weight_gradient = weights[3 * model_width : height].reshape(-1, LANES, LANES)[:, :head_columns]
     output_weight_gradient = output_weight_gradient.transpose(1, 0, 2).reshape(head_columns, -1)
     g_controller = weights[height:end].reshape(local_experts, model_width).T
-    pieces = model_width // LANES
-    g_gain_attn = gains[:pieces].reshape(-1)
-    g_gain_mix = gains[pieces : 2 * pieces].reshape(-1)
-
-    d_tokens = place_blocks(gather_narrow(d_tokens), relative, BF16)[:slot_count]
-    mixed_part = layer_output(place, hidden, mixed)
-    mixed_part = place_blocks(gather_narrow(mixed_part), relative, BF16)[:slot_count]
-
-    order = lax.bitwise_xor(unit, jnp.arange(units))
-    g_w_in, g_w_out, bias = owned_weights(expert_grads, order, w_in.shape[2], wide, units)
+    lines = model_width // LANES
+    g_gain_attn = gains[:lines].reshape(-1)
+    g_gain_mix = gains[lines : 2 * lines].reshape(-1)
 
     def over_share(x):
         return jnp.sum(x.reshape((local_experts, share) + x.shape[1:]), axis=1)

time: 300 us -> 278 us (0.927)
  waiting for transfers between devices: 88.4 us -> 81.4 us
  starting transfers between devices: 54 us -> 47.6 us
  Pallas kernels: 122 us -> 116 us
    ppermute x4 -> x6, waiting for transfers between devices: 29.7 us -> 12.9 us  [to_unit(): return lax.ppermute(x, 'wide', [(w, w ^ d) for w in range(wide)])]
    all_to_all x2 -> x1, waiting for transfers between devices: 0.01 us -> 10.6 us  [to_slots(): return lax.all_to_all(x, BOTH, split_axis=0, concat_axis=0, tiled=True)]
    pallas_call x5, Pallas kernels: 44.6 us -> 38 us  [the longest x2 21.2 us: expert_weights(): pl.pallas_call(lambda where, expert, *refs: weight_kernel(units, where, *...]
    all_to_all x2 -> x1, starting transfers between devices: 9.18 us -> 3.6 us  [to_slots(): return lax.all_to_all(x, BOTH, split_axis=0, concat_axis=0, tiled=True)]
    all_to_all x2, waiting for transfers between devices: 6.63 us -> 1.86 us  [the longest x1 1.85 us: from_parts(): lax.all_to_all(parts, 'wide', split_axis=0, concat_axis=0, tiled=True)]
    ppermute x4, waiting for transfers between devices: 1.45 us -> 4.7 us  [from_chip(): lax.ppermute(x, 'narrow', [((n + 2 * k) % narrow, n) for n in range(narro...]
    unnamed x70 -> x66, local copies, waits for them, and re-layouts: 9.02 us -> 7.59 us
    ppermute x4 -> x6, starting transfers between devices: 6.1 us -> 5.87 us  [to_unit(): return lax.ppermute(x, 'wide', [(w, w ^ d) for w in range(wide)])]
  transfers between devices with their start and end apart: 33 -> 34, of which waited for: 15 -> 18; matrix products, arithmetic and copies ran while one was open for 6% -> 7% of each run, Pallas kernels for 39% -> 39%
where the time goes in v4:
time: 278 us; the launch traced here: 277 us
  Pallas kernels  116 us (42%)
  waiting for transfers between devices  81.4 us (29%)
  starting transfers between devices  47.6 us (17%)
  local copies, waits for them, and re-layouts  20.8 us (7%)
  other arithmetic  10.1 us (4%)
    pallas_call x2, Pallas kernels, expert_weights(): pl.pallas_call(lambda where, expert, *refs: weight_kernel(units, where, *...  21.2 us
    pallas_call x1, Pallas kernels, experts_at_positions(): pl.pallas_call(functools.partial(expert_kernel, sources), grid=(experts,)...  20.8 us
    all_to_all x1, waiting for transfers between devices, to_positions(): x = lax.all_to_all(x, BOTH, split_axis=0, concat_axis=0, tiled=True)  16.5 us
    pallas_call x1, Pallas kernels, attention_back_far(): pl.pallas_call(functools.partial(back_far_kernel, blocks, inner // count)...  13.7 us
    ppermute x6, waiting for transfers between devices, to_unit(): return lax.ppermute(x, 'wide', [(w, w ^ d) for w in range(wide)])  12.9 us
    ppermute x3, waiting for transfers between devices, to_relative(): lax.ppermute(x, 'narrow', [(n, (n + 2 * k) % narrow ^ other) for n in ran...  12.6 us
    pallas_call x1, Pallas kernels, attention_back_near(): pl.pallas_call(functools.partial(back_near_kernel, blocks, inner // count...  12.5 us
    ppermute x3, waiting for transfers between devices, from_relative(): lax.ppermute(x, 'narrow', [((n + 2 * k) % narrow ^ other, n) for n in ran...  12.2 us
  transfers between devices with their start and end apart: 34, of which 18 were waited for; matrix products, arithmetic and copies ran while one was open for 7% of the time, Pallas kernels for 39%

profile of v4, /device:TPU:0, one launch (start us, length us, event | category | flops | bytes accessed | tf_op | source)
XLA Modules:
  0.0 277.3 jit_solution(15071830833644384894)
XLA Ops:
  0.6 2.0 pack_weights.1.refs_0_
  3.1 1.7 collective-permute-done.refs_1_
  4.8 2.3 copy_bitcast_fusion
  7.2 7.2 %all-to-all-start.1 = ((bf16[8,12,8,512]{3,2,1,0:T(8,128)(2,1)}), bf16[8,12,8,512]{3,2,1,0:T(8,128)(2,1)S(1)}, u32[]{:S(2)}, u32[]{:S(2)}) async-start(bf16[8,12,8,512]{3,2,1,0:T(8,128)(2,1)} %copy_bitcast_fusion), calls=%async_computation.1 | async-start | bytes 1572864 | tf_op jit(solution)/shard_map/all_to_all | solution.py:897
  14.4 1.6 collective-permute-start.1
  17.2 1.2 pad_add_fusion.1.place
  18.5 8.2 %attention_near.1 = (f32[3,256,512]{2,1,0:T(8,128)}, bf16[3,256,768]{2,1,0:T(8,128)(2,1)}, bf16[3,256,256]{2,1,0:T(8,128)(2,1)}) custom-call(s32[2]{0:T(128)} %pad_add_fusion.1.place, bf16[12,256,512]{2,1,0:T(8,128)(2,1)} %tokens.7, bf16[512,512]{1,0:T(8,128)(2,1)} %pack_weights.1.refs_0_, bf16[512,512]{1,0:T(8,128)(2,1)} %copy-done.19, f32[1,512]{1,0:T(1,128)} %bitcast.83), custom_call_target="tpu_custom_call" | custom-call | flops 1207959552 | bytes 4980736 | tf_op jit(solution)/shard_map/attention_near/pallas_call | solution.py:119
  26.7 1.5 collective-permute-done.1.refs_0_
  30.9 8.9 %attention_far.1 = (bf16[32,3,8,512]{3,2,1,0:T(8,128)(2,1)}, f32[3,256,512]{2,1,0:T(8,128)}, bf16[3,256,768]{2,1,0:T(8,128)(2,1)}, bf16[3,256,256]{2,1,0:T(8,128)(2,1)}) custom-call(s32[2]{0:T(128)} %pad_add_fusion.1.place, bf16[12,256,512]{2,1,0:T(8,128)(2,1)} %tokens.7, f32[3,256,512]{2,1,0:T(8,128)} %get-tuple-element.97.partial, ...), custom_call_target="tpu_custom_call" | custom-call | flops 1207959552 | bytes 7340032 | tf_op jit(solution)/shard_map/attention_far/pallas_call | solution.py:154
  39.8 5.7 %all-to-all-start = ((bf16[32,3,8,512]{3,2,1,0:T(8,128)(2,1)}), bf16[32,3,8,512]{3,2,1,0:T(8,128)(2,1)S(1)}, u32[]{:S(2)}, u32[]{:S(2)}) async-start(bf16[32,3,8,512]{3,2,1,0:T(8,128)(2,1)} %get-tuple-element.99), calls=%async_computation | async-start | bytes 1572864 | tf_op jit(solution)/shard_map/all_to_all | solution.py:884
  49.6 16.5 %all-to-all-done = bf16[32,3,8,512]{3,2,1,0:T(8,128)(2,1)S(1)} async-done(((bf16[32,3,8,512]{3,2,1,0:T(8,128)(2,1)}), bf16[32,3,8,512]{3,2,1,0:T(8,128)(2,1)S(1)}, u32[]{:S(2)}, u32[]{:S(2)}) %all-to-all-start) | async-done | bytes 786464 | tf_op jit(solution)/shard_map/all_to_all | solution.py:884
  67.0 5.4 %mix_forward.1 = (f32[768,32]{1,0:T(8,128)}, bf16[768,512]{1,0:T(8,128)(2,1)}, bf16[8,2,16,512]{3,2,1,0:T(8,128)(2,1)}, bf16[8,2,16,512]{3,2,1,0:T(8,128)(2,1)},...) custom-call(s32[4]{0:T(128)} %copy-done.24, bf16[768,512]{1,0:T(8,128)(2,1)} %bitcast.75, ...), custom_call_target="tpu_custom_call" | custom-call | flops 805306368 | bytes 4718592 | tf_op jit(solution)/shard_map/mix_forward/pallas_call | solution.py:254
  72.4 1.2 collective-permute-start.8
  74.2 6.9 %collective-permute-done.8.refs_3_ = bf16[8,2,16,512]{3,2,1,0:T(8,128)(2,1)S(1)} collective-permute-done((bf16[8,2,16,512]{3,2,1,0:T(8,128)(2,1)}, bf16[8,2,16,512]{3,2,1,0:T(8,128)(2,1)S(1)}, u32[]{:S(2)}, u32[]{:S(2)}) %collective-permute-start.8) | collective-permute-done | bytes 262176 | tf_op jit(solution)/shard_map/ppermute | solution.py:777
  81.2 5.6 %collective-permute-done.7.refs_2_ = bf16[8,2,16,512]{3,2,1,0:T(8,128)(2,1)S(1)} collective-permute-done((bf16[8,2,16,512]{3,2,1,0:T(8,128)(2,1)}, bf16[8,2,16,512]{3,2,1,0:T(8,128)(2,1)S(1)}, u32[]{:S(2)}, u32[]{:S(2)}) %collective-permute-start.7) | collective-permute-done | bytes 262176 | tf_op jit(solution)/shard_map/ppermute | solution.py:777
  86.8 1.2 maximum_bitcast_fusion
  88.1 1.5 pad_maximum_fusion
  89.6 3.8 %all-to-all-start.3 = ((bf16[8,4,2,2,16,512]{5,4,3,2,1,0:T(8,128)(2,1)}), bf16[8,4,2,2,16,512]{5,4,3,2,1,0:T(8,128)(2,1)S(1)}, u32[]{:S(2)}, u32[]{:S(2)}) async-start(bf16[8,4,2,2,16,512]{5,4,3,2,1,0:T(8,128)(2,1)} %pad_maximum_fusion), calls=%async_computation.3 | async-start | bytes 4194304 | tf_op jit(solution)/shard_map/all_to_all | solution.py:935
  94.7 20.8 %experts.1 = (bf16[8,2,16,512]{3,2,1,0:T(8,128)(2,1)}, bf16[8,2,16,512]{3,2,1,0:T(8,128)(2,1)}, bf16[8,2,16,512]{3,2,1,0:T(8,128)(2,1)}, bf16[8,2,16,512]{3,2,1,0:T(8,128)(2,1)}) custom-call(bf16[8,2,16,512]{3,2,1,0:T(8,128)(2,1)} %get-tuple-element.108.refs_0_, bf16[8,2,16,512]{3,2,1,0:T(8,128)(2,1)} %copy-done.6, bf16[8,2,16,512]{3,2,1,0:T(8,128)(2,1)} %copy-done.5, ...), custom_call_target="tpu_custom_call" | custom-call | flops 4294967296 | bytes 35651584 | tf_op jit(solution)/shard_map/experts/pallas_call | solution.py:362
  115.6 1.5 collective-permute-start.10
  117.4 7.5 %collective-permute-done.10.refs_2_ = bf16[8,2,16,512]{3,2,1,0:T(8,128)(2,1)S(1)} collective-permute-done((bf16[8,2,16,512]{3,2,1,0:T(8,128)(2,1)}, bf16[8,2,16,512]{3,2,1,0:T(8,128)(2,1)S(1)}, u32[]{:S(2)}, u32[]{:S(2)}) %collective-permute-start.10) | collective-permute-done | bytes 262176 | tf_op jit(solution)/shard_map/ppermute | solution.py:783
  124.9 4.7 %collective-permute-done.11.refs_3_ = bf16[8,2,16,512]{3,2,1,0:T(8,128)(2,1)S(1)} collective-permute-done((bf16[8,2,16,512]{3,2,1,0:T(8,128)(2,1)}, bf16[8,2,16,512]{3,2,1,0:T(8,128)(2,1)S(1)}, u32[]{:S(2)}, u32[]{:S(2)}) %collective-permute-start.11) | collective-permute-done | bytes 262176 | tf_op jit(solution)/shard_map/ppermute | solution.py:783
  130.4 6.9 %mix_backward.1 = (bf16[32,2,24,512]{3,2,1,0:T(8,128)(2,1)}, f32[32,512]{1,0:T(8,128)}) custom-call(s32[4]{0:T(128)} %copy-done.24, bf16[768,512]{1,0:T(8,128)(2,1)} %get-tuple-element.102.spread, bf16[768,512]{1,0:T(8,128)(2,1)} %bitcast.76, bf16[768,512]{1,0:T(8,128)(2,1)} %bitcast.74, f32[768,32]{1,0:T(8,128)} %get-tuple-element.103.probs, ...), custom_call_target="tpu_custom_call" | custom-call | flops 1610612736 | bytes 6291456 | tf_op jit(solution)/shard_map/mix_backward/pallas_call | solution.py:310
  137.3 4.7 %all-to-all-done.3.refs_0_ = bf16[8,4,2,2,16,512]{5,4,3,2,1,0:T(8,128)(2,1)S(1)} async-done(((bf16[8,4,2,2,16,512]{5,4,3,2,1,0:T(8,128)(2,1)}), bf16[8,4,2,2,16,512]{5,4,3,2,1,0:T(8,128)(2,1)S(1)}, u32[]{:S(2)}, u32[]{:S(2)}) %all-to-all-start.3) | async-done | bytes 2097184 | tf_op jit(solution)/shard_map/all_to_all | solution.py:935
  142.0 1.3 copy-done
  143.4 3.6 %all-to-all-start.2 = ((bf16[32,2,24,512]{3,2,1,0:T(8,128)(2,1)}), bf16[32,2,24,512]{3,2,1,0:T(8,128)(2,1)}, u32[]{:S(2)}, u32[]{:S(2)}) async-start(bf16[32,2,24,512]{3,2,1,0:T(8,128)(2,1)} %get-tuple-element.116), calls=%async_computation.2 | async-start | bytes 3145728 | tf_op jit(solution)/shard_map/all_to_all | solution.py:891
  147.6 10.5 %expert_weights.2 = (bf16[528,512]{1,0:T(8,128)(2,1)}, bf16[528,512]{1,0:T(8,128)(2,1)}, bf16[528,512]{1,0:T(8,128)(2,1)}, bf16[528,512]{1,0:T(8,128)(2,1)}) custom-call(s32[2]{0:T(128)} %pad_add_fusion.2.where, s32[1]{0:T(128)} %bitcast.30.expert, bf16[8,4,2,2,16,512]{5,4,3,2,1,0:T(8,128)(2,1)} %copy-done, bf16[8,512,2048]{2,1,0:T(8,128)(2,1)} %refs_1_.3, ...), custom_call_target="tpu_custom_call" | custom-call | flops 3221225472 | bytes 9437184 | tf_op jit(solution)/shard_map/expert_weights/pallas_call | solution.py:438
  158.1 1.5 collective-permute-start.12
  159.6 1.5 collective-permute-start.13
  161.1 10.6 %expert_weights.3 = (bf16[528,512]{1,0:T(8,128)(2,1)}, bf16[528,512]{1,0:T(8,128)(2,1)}, bf16[528,512]{1,0:T(8,128)(2,1)}, bf16[528,512]{1,0:T(8,128)(2,1)}) custom-call(s32[2]{0:T(128)} %pad_add_fusion.2.where, s32[1]{0:T(128)} %bitcast.31.expert, bf16[8,4,2,2,16,512]{5,4,3,2,1,0:T(8,128)(2,1)} %copy-done, bf16[8,512,2048]{2,1,0:T(8,128)(2,1)} %refs_1_.3, ...), custom_call_target="tpu_custom_call" | custom-call | flops 3221225472 | bytes 9437184 | tf_op jit(solution)/shard_map/expert_weights/pallas_call | solution.py:438
  174.1 10.6 %all-to-all-done.2.grads.mixed = bf16[32,2,24,512]{3,2,1,0:T(8,128)(2,1)} async-done(((bf16[32,2,24,512]{3,2,1,0:T(8,128)(2,1)}), bf16[32,2,24,512]{3,2,1,0:T(8,128)(2,1)}, u32[]{:S(2)}, u32[]{:S(2)}) %all-to-all-start.2) | async-done | bytes 1572896 | tf_op jit(solution)/shard_map/all_to_all | solution.py:891
  184.7 2.1 collective-permute-done.13.refs_2_
  186.9 13.7 %attention_back_far.1 = (f32[3,256,512]{2,1,0:T(8,128)}, f32[3,256,512]{2,1,0:T(8,128)}, bf16[3,256,512]{2,1,0:T(8,128)(2,1)}, f32[8,512]{1,0:T(8,128)}, bf16[21...) custom-call(s32[2]{0:T(128)} %pad_add_fusion.1.place, bf16[12,256,512]{2,1,0:T(8,128)(2,1)} %tokens.7, ...), custom_call_target="tpu_custom_call" | custom-call | bytes 10747904 | tf_op jit(solution)/shard_map/attention_back_far/pallas_call | solution.py:640
  200.7 2.2 collective-permute-done.16
  202.9 1.2 add_convert_fusion.1
  204.1 2.1 collective-permute-start.17
  207.1 12.5 %attention_back_near.1 = (bf16[3,256,512]{2,1,0:T(8,128)(2,1)}, bf16[2176,128]{1,0:T(8,128)(2,1)}, bf16[2176,128]{1,0:T(8,128)(2,1)}) custom-call(s32[2]{0:T(128)} %pad_add_fusion.1.place, bf16[12,256,512]{2,1,0:T(8,128)(2,1)} %tokens.7, f32[3,256,512]{2,1,0:T(8,128)} %get-tuple-element.128.d_hidden, f32[3,256,512]{2,1,0:T(8,128)} %get-tuple-element.136.partial, ...), custom_call_target="tpu_custom_call" | custom-call | bytes 8388608 | tf_op jit(solution)/shard_map/attention_back_near/pallas_call | solution.py:689
  219.8 1.4 collective-permute-done.18.refs_3_
  223.3 2.1 add_convert_fusion
  225.4 4.3 %all-to-all-start.4 = ((bf16[8,272,128]{2,1,0:T(8,128)(2,1)}), bf16[8,272,128]{2,1,0:T(8,128)(2,1)S(1)}, u32[]{:S(2)}, u32[]{:S(2)}) async-start(bf16[8,272,128]{2,1,0:T(8,128)(2,1)} %bitcast.37), calls=%async_computation.4 | async-start | bytes 1114112 | tf_op jit(solution)/shard_map/all_to_all | solution.py:764
  229.7 9.4 %collective-permute-done.22.refs_7_ = bf16[528,512]{1,0:T(8,128)(2,1)} collective-permute-done((bf16[528,512]{1,0:T(8,128)(2,1)}, bf16[528,512]{1,0:T(8,128)(2,1)}, u32[]{:S(2)}, u32[]{:S(2)}) %collective-permute-start.22) | collective-permute-done | bytes 540704 | tf_op jit(solution)/shard_map/ppermute | solution.py:788
  239.1 3.0 %collective-permute-done.19.refs_2_ = bf16[3,256,512]{2,1,0:T(8,128)(2,1)} collective-permute-done((bf16[3,256,512]{2,1,0:T(8,128)(2,1)S(1)}, bf16[3,256,512]{2,1,0:T(8,128)(2,1)}, u32[]{:S(2)}, u32[]{:S(2)}) %collective-permute-start.19) | collective-permute-done | bytes 786464 | tf_op jit(solution)/shard_map/ppermute | solution.py:730
  243.4 7.5 %owned_weights.1 = (f32[8,64,2048]{2,1,0:T(8,128)}, f32[8,256,512]{2,1,0:T(8,128)}, f32[8,16,512]{2,1,0:T(8,128)}) custom-call(s32[8]{0:T(128)} %add.142.where, bf16[528,512]{1,0:T(8,128)(2,1)} %get-tuple-element.154.refs_0_, bf16[528,512]{1,0:T(8,128)(2,1)} %copy-done.14, bf16[528,512]{1,0:T(8,128)(2,1)} %copy-done.15, bf16[528,512]{1,0:T(8,128)(2,1)} %copy-done.18, ...), custom_call_target="tpu_custom_call" | custom-call | bytes 12976128 | tf_op jit(solution)/shard_map/owned_weights/pallas_call | solution.py:485
  251.9 5.4 %all-to-all-start.5 = ((bf16[8,272,128]{2,1,0:T(8,128)(2,1)}), bf16[8,272,128]{2,1,0:T(8,128)(2,1)S(1)}, u32[]{:S(2)}, u32[]{:S(2)}) async-start(bf16[8,272,128]{2,1,0:T(8,128)(2,1)} %broadcast_in_dim.86), calls=%async_computation.5 | async-start | bytes 1114112 | tf_op jit(solution)/shard_map/all_to_all | solution.py:770
  257.3 4.7 %place_blocks.2 = bf16[12,256,512]{2,1,0:T(8,128)(2,1)} custom-call(s32[4]{0:T(128)} %copy-done.24, bf16[3,256,512]{2,1,0:T(8,128)(2,1)} %get-tuple-element.145.refs_0_, bf16[3,256,512]{2,1,0:T(8,128)(2,1)} %collective-permute-done.20.refs_1_, bf16[3,256,512]{2,1,0:T(8,128)(2,1)} %collective-permute-done.19.refs_2_, ...), custom_call_target="tpu_custom_call" | custom-call | bytes 6291456 | tf_op jit(solution)/shard_map/place_blocks/pallas_call | solution.py:803
  266.2 4.7 %place_blocks.3 = bf16[12,256,512]{2,1,0:T(8,128)(2,1)} custom-call(s32[4]{0:T(128)} %copy-done.24, bf16[3,256,512]{2,1,0:T(8,128)(2,1)} %get-tuple-element.150.refs_0_, bf16[3,256,512]{2,1,0:T(8,128)(2,1)} %copy-done.9, bf16[3,256,512]{2,1,0:T(8,128)(2,1)} %copy-done.10, bf16[3,256,512]{2,1,0:T(8,128)(2,1)} %copy-done.11), custom_call_target="tpu_custom_call" | custom-call | bytes 6291456 | tf_op jit(solution)/shard_map/place_blocks/pallas_call | solution.py:803
  270.9 1.9 all-to-all-done.5
  272.8 1.4 collective-permute-start.27
  (152 shorter events, 28.4 us)
Async XLA Ops:
  2.6 2.2 collective-permute-start
  4.8 9.5 %copy-start.1 = (bf16[512,512]{1,0:T(8,128)(2,1)S(1)}, bf16[512,512]{1,0:T(8,128)(2,1)}, u32[]{:S(2)}) copy-start(bf16[512,512]{1,0:T(8,128)(2,1)} %pack_weights.1.refs_0_) | copy-start | bytes 1572868
  4.8 11.1 %copy-start.23 = (bf16[512,8]{0,1:T(8,128)(2,1)S(1)}, bf16[512,8]{0,1:T(8,128)(2,1)}, u32[]{:S(2)}) copy-start(bf16[512,8]{0,1:T(8,128)(2,1)} %param.25) | copy-start | bytes 24580
  4.8 11.6 %copy-start.25 = (s32[8]{0:T(128)S(1)}, s32[8]{0:T(128)}, u32[]{:S(2)}) copy-start(s32[8]{0:T(128)} %param.17) | copy-start | bytes 100
  7.2 32.6 %all-to-all-start.1 = ((bf16[8,12,8,512]{3,2,1,0:T(8,128)(2,1)}), bf16[8,12,8,512]{3,2,1,0:T(8,128)(2,1)S(1)}, u32[]{:S(2)}, u32[]{:S(2)}) async-start(bf16[8,12,8,512]{3,2,1,0:T(8,128)(2,1)} %copy_bitcast_fusion), calls=%async_computation.1 | async-start | bytes 1572864 | tf_op jit(solution)/shard_map/all_to_all | solution.py:897
  14.4 13.8 %collective-permute-start.1 = (bf16[512,512]{1,0:T(8,128)(2,1)S(1)}, bf16[512,512]{1,0:T(8,128)(2,1)S(1)}, u32[]{:S(2)}, u32[]{:S(2)}) collective-permute-start(bf16[512,512]{1,0:T(8,128)(2,1)S(1)} %copy-done.1), channel_id=1, source_target_pairs={{2,0},{3,1},{0,2},{1,3},{6,4},{7,5},{4,6},{5,7},{10,8},{11,9},{8,1... | collective-permute-start | bytes 1572872 | tf_op jit(solution)/shard_map/ppermute | solution.py:730
  15.9 29.8 %collective-permute-start.4 = (bf16[8,512]{1,0:T(8,128)(2,1)S(1)}, bf16[8,512]{1,0:T(8,128)(2,1)S(1)}, u32[]{:S(2)}, u32[]{:S(2)}) collective-permute-start(bf16[8,512]{1,0:T(8,128)(2,1)S(1)} %bitcast.91), channel_id=1, source_target_pairs={{2,0},{3,1},{0,2},{1,3},{6,4},{7,5},{4,6},{5,7},{10,8},{11,9},{8,1... | collective-permute-start | bytes 24584 | tf_op jit(solution)/shard_map/ppermute | solution.py:730
  16.5 31.8 %collective-permute-start.3 = (bf16[8,512]{1,0:T(8,128)(2,1)S(1)}, bf16[8,512]{1,0:T(8,128)(2,1)S(1)}, u32[]{:S(2)}, u32[]{:S(2)}) collective-permute-start(bf16[8,512]{1,0:T(8,128)(2,1)S(1)} %bitcast.92), channel_id=1, source_target_pairs={{0,1},{1,0},{2,3},{3,2},{4,5},{5,4},{6,7},{7,6},{8,9},{9,8},{10,11... | collective-permute-start | bytes 24584 | tf_op jit(solution)/shard_map/ppermute | solution.py:725
  28.2 1.9 collective-permute-start.2
  28.5 11.3 %copy-start.24 = (s32[4]{0:T(128)}, s32[4]{0:T(128)S(1)}, u32[]{:S(2)}) copy-start(s32[4]{0:T(128)S(1)} %pad_add_fusion.relative.where) | copy-start | bytes 52
  39.8 5.7 %copy-start.26 = (s32[64]{0:T(128)S(1)}, s32[64]{0:T(128)}, u32[]{:S(2)}) copy-start(s32[64]{0:T(128)} %param.18) | copy-start | bytes 772
  39.8 26.3 %copy-start.12 = (bf16[8,12,8,512]{3,2,1,0:T(8,128)(2,1)}, bf16[8,12,8,512]{3,2,1,0:T(8,128)(2,1)S(1)}, u32[]{:S(2)}) copy-start(bf16[8,12,8,512]{3,2,1,0:T(8,128)(2,1)S(1)} %all-to-all-done.1) | copy-start | bytes 2359300
  39.8 26.3 %all-to-all-start = ((bf16[32,3,8,512]{3,2,1,0:T(8,128)(2,1)}), bf16[32,3,8,512]{3,2,1,0:T(8,128)(2,1)S(1)}, u32[]{:S(2)}, u32[]{:S(2)}) async-start(bf16[32,3,8,512]{3,2,1,0:T(8,128)(2,1)} %get-tuple-element.99), calls=%async_computation | async-start | bytes 1572864 | tf_op jit(solution)/shard_map/all_to_all | solution.py:884
  45.8 2.5 collective-permute-start.5
  72.4 8.8 %collective-permute-start.8 = (bf16[8,2,16,512]{3,2,1,0:T(8,128)(2,1)}, bf16[8,2,16,512]{3,2,1,0:T(8,128)(2,1)S(1)}, u32[]{:S(2)}, u32[]{:S(2)}) collective-permute-start(bf16[8,2,16,512]{3,2,1,0:T(8,128)(2,1)} %get-tuple-element.107), channel_id=1, source_target_pairs={{0,3},{1,2},{2,1},{3,0},{4,7},{5,6},{6,5},{7,4},{8,11},{9,10},{10,... | collective-permute-start | bytes 786440 | tf_op jit(solution)/shard_map/ppermute | solution.py:777
  73.6 13.2 %collective-permute-start.7 = (bf16[8,2,16,512]{3,2,1,0:T(8,128)(2,1)}, bf16[8,2,16,512]{3,2,1,0:T(8,128)(2,1)S(1)}, u32[]{:S(2)}, u32[]{:S(2)}) collective-permute-start(bf16[8,2,16,512]{3,2,1,0:T(8,128)(2,1)} %get-tuple-element.106), channel_id=1, source_target_pairs={{0,2},{1,3},{2,0},{3,1},{4,6},{5,7},{6,4},{7,5},{8,10},{9,11},{10,... | collective-permute-start | bytes 786440 | tf_op jit(solution)/shard_map/ppermute | solution.py:777
  73.9 12.9 %collective-permute-start.6 = (bf16[8,2,16,512]{3,2,1,0:T(8,128)(2,1)}, bf16[8,2,16,512]{3,2,1,0:T(8,128)(2,1)S(1)}, u32[]{:S(2)}, u32[]{:S(2)}) collective-permute-start(bf16[8,2,16,512]{3,2,1,0:T(8,128)(2,1)} %get-tuple-element.105), channel_id=1, source_target_pairs={{0,1},{1,0},{2,3},{3,2},{4,5},{5,4},{6,7},{7,6},{8,9},{9,8},{10,11... | collective-permute-start | bytes 786440 | tf_op jit(solution)/shard_map/ppermute | solution.py:777
  81.2 8.4 %copy-start.4 = (bf16[8,2,16,512]{3,2,1,0:T(8,128)(2,1)}, bf16[8,2,16,512]{3,2,1,0:T(8,128)(2,1)S(1)}, u32[]{:S(2)}) copy-start(bf16[8,2,16,512]{3,2,1,0:T(8,128)(2,1)S(1)} %collective-permute-done.8.refs_3_) | copy-start | bytes 786436
  89.6 52.4 %all-to-all-start.3 = ((bf16[8,4,2,2,16,512]{5,4,3,2,1,0:T(8,128)(2,1)}), bf16[8,4,2,2,16,512]{5,4,3,2,1,0:T(8,128)(2,1)S(1)}, u32[]{:S(2)}, u32[]{:S(2)}) async-start(bf16[8,4,2,2,16,512]{5,4,3,2,1,0:T(8,128)(2,1)} %pad_maximum_fusion), calls=%async_computation.3 | async-start | bytes 4194304 | tf_op jit(solution)/shard_map/all_to_all | solution.py:935
  115.5 1.9 collective-permute-start.9
  115.6 9.4 %collective-permute-start.10 = (bf16[8,2,16,512]{3,2,1,0:T(8,128)(2,1)}, bf16[8,2,16,512]{3,2,1,0:T(8,128)(2,1)S(1)}, u32[]{:S(2)}, u32[]{:S(2)}) collective-permute-start(bf16[8,2,16,512]{3,2,1,0:T(8,128)(2,1)} %get-tuple-element.114), channel_id=1, source_target_pairs={{2,0},{3,1},{0,2},{1,3},{6,4},{7,5},{4,6},{5,7},{10,8},{11,9},{8,1... | collective-permute-start | bytes 786440 | tf_op jit(solution)/shard_map/ppermute | solution.py:783
  117.1 12.6 %collective-permute-start.11 = (bf16[8,2,16,512]{3,2,1,0:T(8,128)(2,1)}, bf16[8,2,16,512]{3,2,1,0:T(8,128)(2,1)S(1)}, u32[]{:S(2)}, u32[]{:S(2)}) collective-permute-start(bf16[8,2,16,512]{3,2,1,0:T(8,128)(2,1)} %get-tuple-element.115), channel_id=1, source_target_pairs={{3,0},{2,1},{1,2},{0,3},{7,4},{6,5},{5,6},{4,7},{11,8},{10,9},{9,1... | collective-permute-start | bytes 786440 | tf_op jit(solution)/shard_map/ppermute | solution.py:783
  117.4 12.2 %copy-start.28 = (bf16[8,2,16,512]{3,2,1,0:T(8,128)(2,1)}, bf16[8,2,16,512]{3,2,1,0:T(8,128)(2,1)S(1)}, u32[]{:S(2)}) copy-start(bf16[8,2,16,512]{3,2,1,0:T(8,128)(2,1)S(1)} %collective-permute-done.9.refs_1_) | copy-start | bytes 786436
  143.4 41.4 %all-to-all-start.2 = ((bf16[32,2,24,512]{3,2,1,0:T(8,128)(2,1)}), bf16[32,2,24,512]{3,2,1,0:T(8,128)(2,1)}, u32[]{:S(2)}, u32[]{:S(2)}) async-start(bf16[32,2,24,512]{3,2,1,0:T(8,128)(2,1)} %get-tuple-element.116), calls=%async_computation.2 | async-start | bytes 3145728 | tf_op jit(solution)/shard_map/all_to_all | solution.py:891
  158.1 26.6 %collective-permute-start.12 = (bf16[528,512]{1,0:T(8,128)(2,1)}, bf16[528,512]{1,0:T(8,128)(2,1)S(1)}, u32[]{:S(2)}, u32[]{:S(2)}) collective-permute-start(bf16[528,512]{1,0:T(8,128)(2,1)} %get-tuple-element.119), channel_id=1, source_target_pairs={{0,4},{4,0},{8,12},{12,8},{16,20},{20,16},{24,28},{28,24},{1,5},{5... | collective-permute-start | bytes 1622024 | tf_op jit(solution)/shard_map/ppermute | solution.py:788
  159.6 27.3 %collective-permute-start.13 = (bf16[528,512]{1,0:T(8,128)(2,1)}, bf16[528,512]{1,0:T(8,128)(2,1)S(1)}, u32[]{:S(2)}, u32[]{:S(2)}) collective-permute-start(bf16[528,512]{1,0:T(8,128)(2,1)} %get-tuple-element.120), channel_id=1, source_target_pairs={{0,8},{4,12},{8,0},{12,4},{16,24},{20,28},{24,16},{28,20},{1,9},{5... | collective-permute-start | bytes 1622024 | tf_op jit(solution)/shard_map/ppermute | solution.py:788
  161.1 11.8 %copy-start.20 = (f32[32,512]{1,0:T(8,128)S(1)}, f32[32,512]{1,0:T(8,128)}, u32[]{:S(2)}) copy-start(f32[32,512]{1,0:T(8,128)} %get-tuple-element.126) | copy-start | bytes 196612
  171.7 28.9 %collective-permute-start.14 = (bf16[528,512]{1,0:T(8,128)(2,1)}, bf16[528,512]{1,0:T(8,128)(2,1)S(1)}, u32[]{:S(2)}, u32[]{:S(2)}) collective-permute-start(bf16[528,512]{1,0:T(8,128)(2,1)} %get-tuple-element.132), channel_id=1, source_target_pairs={{0,4},{4,0},{8,12},{12,8},{16,20},{20,16},{24,28},{28,24},{1,5},{5... | collective-permute-start | bytes 1622024 | tf_op jit(solution)/shard_map/ppermute | solution.py:788
  172.3 28.4 %collective-permute-start.15 = (bf16[528,512]{1,0:T(8,128)(2,1)}, bf16[528,512]{1,0:T(8,128)(2,1)S(1)}, u32[]{:S(2)}, u32[]{:S(2)}) collective-permute-start(bf16[528,512]{1,0:T(8,128)(2,1)} %get-tuple-element.133), channel_id=1, source_target_pairs={{0,8},{4,12},{8,0},{12,4},{16,24},{20,28},{24,16},{28,20},{1,9},{5... | collective-permute-start | bytes 1622024 | tf_op jit(solution)/shard_map/ppermute | solution.py:788
  184.7 15.9 %copy-start.14 = (bf16[528,512]{1,0:T(8,128)(2,1)}, bf16[528,512]{1,0:T(8,128)(2,1)S(1)}, u32[]{:S(2)}) copy-start(bf16[528,512]{1,0:T(8,128)(2,1)S(1)} %collective-permute-done.12.refs_1_) | copy-start | bytes 1622020
  186.8 13.7 %copy-start.15 = (bf16[528,512]{1,0:T(8,128)(2,1)}, bf16[528,512]{1,0:T(8,128)(2,1)S(1)}, u32[]{:S(2)}) copy-start(bf16[528,512]{1,0:T(8,128)(2,1)S(1)} %collective-permute-done.13.refs_2_) | copy-start | bytes 1622020
  200.6 6.5 %copy-start.16 = (bf16[528,512]{1,0:T(8,128)(2,1)}, bf16[528,512]{1,0:T(8,128)(2,1)S(1)}, u32[]{:S(2)}) copy-start(bf16[528,512]{1,0:T(8,128)(2,1)S(1)} %collective-permute-done.14.refs_5_) | copy-start | bytes 1622020
  200.6 19.0 %copy-start.17 = (bf16[528,512]{1,0:T(8,128)(2,1)}, bf16[528,512]{1,0:T(8,128)(2,1)S(1)}, u32[]{:S(2)}) copy-start(bf16[528,512]{1,0:T(8,128)(2,1)S(1)} %collective-permute-done.15.refs_6_) | copy-start | bytes 1622020
  200.7 2.2 collective-permute-start.16
  204.1 15.6 %collective-permute-start.17 = (bf16[2176,128]{1,0:T(8,128)(2,1)S(1)}, bf16[2176,128]{1,0:T(8,128)(2,1)S(1)}, u32[]{:S(2)}, u32[]{:S(2)}) collective-permute-start(bf16[2176,128]{1,0:T(8,128)(2,1)S(1)} %add_convert_fusion.1), channel_id=1, source_target_pairs={{0,2},{1,3},{2,0},{3,1},{4,6},{5,7},{6,4},{7,5},{8,10},{9,11},{10,... | collective-permute-start | bytes 1671176 | tf_op jit(solution)/shard_map/ppermute | solution.py:735
  206.2 14.9 %collective-permute-start.18 = (bf16[528,512]{1,0:T(8,128)(2,1)S(1)}, bf16[528,512]{1,0:T(8,128)(2,1)S(1)}, u32[]{:S(2)}, u32[]{:S(2)}) collective-permute-start(bf16[528,512]{1,0:T(8,128)(2,1)S(1)} %copy-done.27), channel_id=1, source_target_pairs={{0,12},{4,8},{8,4},{12,0},{16,28},{20,24},{24,20},{28,16},{1,13},{... | collective-permute-start | bytes 1622024 | tf_op jit(solution)/shard_map/ppermute | solution.py:788
  221.2 2.2 collective-permute-start.23
  221.2 18.0 %collective-permute-start.22 = (bf16[528,512]{1,0:T(8,128)(2,1)}, bf16[528,512]{1,0:T(8,128)(2,1)}, u32[]{:S(2)}, u32[]{:S(2)}) collective-permute-start(bf16[528,512]{1,0:T(8,128)(2,1)} %get-tuple-element.149), channel_id=1, source_target_pairs={{0,12},{4,8},{8,4},{12,0},{16,28},{20,24},{24,20},{28,16},{1,13},{... | collective-permute-start | bytes 1622024 | tf_op jit(solution)/shard_map/ppermute | solution.py:788
  222.1 17.0 %collective-permute-start.21 = (bf16[3,256,512]{2,1,0:T(8,128)(2,1)S(1)}, bf16[3,256,512]{2,1,0:T(8,128)(2,1)S(1)}, u32[]{:S(2)}, u32[]{:S(2)}) collective-permute-start(bf16[3,256,512]{2,1,0:T(8,128)(2,1)S(1)} %copy-done.7), channel_id=1, source_target_pairs={{0,1},{1,0},{2,3},{3,2},{4,5},{5,4},{6,7},{7,6},{8,9},{9,8},{10,11... | collective-permute-start | bytes 2359304 | tf_op jit(solution)/shard_map/ppermute | solution.py:725
  222.3 19.8 %collective-permute-start.19 = (bf16[3,256,512]{2,1,0:T(8,128)(2,1)S(1)}, bf16[3,256,512]{2,1,0:T(8,128)(2,1)}, u32[]{:S(2)}, u32[]{:S(2)}) collective-permute-start(bf16[3,256,512]{2,1,0:T(8,128)(2,1)S(1)} %copy-done.8), channel_id=1, source_target_pairs={{2,0},{3,1},{0,2},{1,3},{6,4},{7,5},{4,6},{5,7},{10,8},{11,9},{8,1... | collective-permute-start | bytes 2359304 | tf_op jit(solution)/shard_map/ppermute | solution.py:730
  222.9 19.2 %collective-permute-start.20 = (bf16[3,256,512]{2,1,0:T(8,128)(2,1)S(1)}, bf16[3,256,512]{2,1,0:T(8,128)(2,1)}, u32[]{:S(2)}, u32[]{:S(2)}) collective-permute-start(bf16[3,256,512]{2,1,0:T(8,128)(2,1)S(1)} %copy-done.8), channel_id=1, source_target_pairs={{0,1},{1,0},{2,3},{3,2},{4,5},{5,4},{6,7},{7,6},{8,9},{9,8},{10,11... | collective-permute-start | bytes 2359304 | tf_op jit(solution)/shard_map/ppermute | solution.py:725
  225.4 25.4 %all-to-all-start.4 = ((bf16[8,272,128]{2,1,0:T(8,128)(2,1)}), bf16[8,272,128]{2,1,0:T(8,128)(2,1)S(1)}, u32[]{:S(2)}, u32[]{:S(2)}) async-start(bf16[8,272,128]{2,1,0:T(8,128)(2,1)} %bitcast.37), calls=%async_computation.4 | async-start | bytes 1114112 | tf_op jit(solution)/shard_map/all_to_all | solution.py:764
  239.1 11.7 %copy-start.9 = (bf16[3,256,512]{2,1,0:T(8,128)(2,1)}, bf16[3,256,512]{2,1,0:T(8,128)(2,1)S(1)}, u32[]{:S(2)}) copy-start(bf16[3,256,512]{2,1,0:T(8,128)(2,1)S(1)} %collective-permute-done.21.refs_1_) | copy-start | bytes 2359300
  242.2 8.8 %collective-permute-start.24 = (bf16[3,256,512]{2,1,0:T(8,128)(2,1)}, bf16[3,256,512]{2,1,0:T(8,128)(2,1)}, u32[]{:S(2)}, u32[]{:S(2)}) collective-permute-start(bf16[3,256,512]{2,1,0:T(8,128)(2,1)} %collective-permute-done.19.refs_2_), channel_id=1, source_target_pairs={{0,1},{1,0},{2,3},{3,2},{4,5},{5,4},{6,7},{7,6},{8,9},{9,8},{10,11... | collective-permute-start | bytes 2359304 | tf_op jit(solution)/shard_map/ppermute | solution.py:725
  242.2 20.0 %collective-permute-start.25 = (bf16[3,256,512]{2,1,0:T(8,128)(2,1)S(1)}, bf16[3,256,512]{2,1,0:T(8,128)(2,1)S(1)}, u32[]{:S(2)}, u32[]{:S(2)}) collective-permute-start(bf16[3,256,512]{2,1,0:T(8,128)(2,1)S(1)} %copy-done.7), channel_id=1, source_target_pairs={{2,0},{3,1},{0,2},{1,3},{6,4},{7,5},{4,6},{5,7},{10,8},{11,9},{8,1... | collective-permute-start | bytes 2359304 | tf_op jit(solution)/shard_map/ppermute | solution.py:730
  251.9 20.9 %all-to-all-start.5 = ((bf16[8,272,128]{2,1,0:T(8,128)(2,1)}), bf16[8,272,128]{2,1,0:T(8,128)(2,1)S(1)}, u32[]{:S(2)}, u32[]{:S(2)}) async-start(bf16[8,272,128]{2,1,0:T(8,128)(2,1)} %broadcast_in_dim.86), calls=%async_computation.5 | async-start | bytes 1114112 | tf_op jit(solution)/shard_map/all_to_all | solution.py:770
  262.1 3.2 %collective-permute-start.26 = (bf16[3,256,512]{2,1,0:T(8,128)(2,1)S(1)}, bf16[3,256,512]{2,1,0:T(8,128)(2,1)S(1)}, u32[]{:S(2)}, u32[]{:S(2)}) collective-permute-start(bf16[3,256,512]{2,1,0:T(8,128)(2,1)S(1)} %collective-permute-done.25.refs_2_), channel_id=1, source_target_pairs={{0,1},{1,0},{2,3},{3,2},{4,5},{5,4},{6,7},{7,6},{8,9},{9,8},{10,11... | collective-permute-start | bytes 2359304 | tf_op jit(solution)/shard_map/ppermute | solution.py:725
  272.8 3.9 %collective-permute-start.27 = (bf16[16,128]{1,0:T(8,128)(2,1)S(1)}, bf16[16,128]{1,0:T(8,128)(2,1)S(1)}, u32[]{:S(2)}, u32[]{:S(2)}) collective-permute-start(bf16[16,128]{1,0:T(8,128)(2,1)S(1)} %slice.66), channel_id=1, source_target_pairs={{0,2},{1,3},{2,0},{3,1},{4,6},{5,7},{6,4},{7,5},{8,10},{9,11},{10,... | collective-permute-start | bytes 12296 | tf_op jit(solution)/shard_map/ppermute | solution.py:735
  (17 other events, 45.6 us)

commit v5 on v4

--- a/solution.py
+++ b/solution.py
@@ -463,8 +463,8 @@
     )(where, expert, both, w_in, b_in[:, None], w_out)
 
 
-def owner_kernel(where, *refs):
-    pieces, (g_in, g_out, bias) = refs[:-3], refs[-3:]
+def owner_kernel(count, where, *refs):
+    pieces, (g_in, g_out, bias) = refs[:count], refs[-3:]
     rows, block = g_in.shape[1], g_out.shape[1]
     width = g_out.shape[2]
     start = pieces[0].shape[0] - 16 - block
@@ -478,25 +478,26 @@
             bias[0] = piece[start + block :].astype(F32)
 
 
-def owned_weights(pieces, where, inner, wide):
+def owned_weights(pieces, where, total, inner, wide, rest=()):
     count = len(pieces)
     width = pieces[0].shape[1]
     shapes = [(1, width // wide, inner), (1, inner // wide, width), (1, 16, width)]
     return pl.pallas_call(
-        owner_kernel,
+        functools.partial(owner_kernel, count),
         grid_spec=pltpu.PrefetchScalarGridSpec(
             num_scalar_prefetch=1,
             grid=(count,),
-            in_specs=[whole(x.shape) for x in pieces],
+            in_specs=[whole(x.shape) for x in pieces] + [pl.BlockSpec(memory_space=pl.ANY)] * len(rest),
             out_specs=[pl.BlockSpec(x, lambda j, where: (where[j], 0, 0)) for x in shapes],
         ),
-        out_shape=[jax.ShapeDtypeStruct((count,) + x[1:], F32) for x in shapes],
+        out_shape=[jax.ShapeDtypeStruct((total,) + x[1:], F32) for x in shapes],
+        input_output_aliases={1 + count + i: i for i in range(len(rest))},
         compiler_params=params("arbitrary"),
         cost_estimate=pl.CostEstimate(
             flops=0, bytes_accessed=sum(x.size for x in pieces) * 6, transcendentals=0
         ),
         name="owned_weights",
-    )(where, *pieces)
+    )(where, *pieces, *rest)
 
 
 def attend_back(entry, d_low, packs, joint_in, context_in, causal, masks, total):
@@ -788,8 +789,8 @@
     return lax.ppermute(x, "wide", [(w, w ^ d) for w in range(wide)])
 
 
-def place_kernel(where, *refs):
-    pieces, out = refs[:-1], refs[-1]
+def place_kernel(count, where, *refs):
+    pieces, out = refs[:count], refs[-1]
     for j, piece in enumerate(pieces):
 
         @pl.when(pl.program_id(0) == j)
@@ -797,24 +798,25 @@
             out[...] = piece[...]
 
 
-def place_blocks(pieces, where):
+def place_blocks(pieces, where, total, *rest):
     count = len(pieces)
     shape = pieces[0].shape
     return pl.pallas_call(
-        place_kernel,
+        functools.partial(place_kernel, count),
         grid_spec=pltpu.PrefetchScalarGridSpec(
             num_scalar_prefetch=1,
             grid=(count,),
-            in_specs=[whole(shape)] * count,
+            in_specs=[whole(shape)] * count + [pl.BlockSpec(memory_space=pl.ANY)] * len(rest),
             out_specs=pl.BlockSpec(shape, lambda j, where: (where[j], 0, 0)),
         ),
-        out_shape=jax.ShapeDtypeStruct((count * shape[0],) + shape[1:], pieces[0].dtype),
+        out_shape=jax.ShapeDtypeStruct((total * shape[0],) + shape[1:], pieces[0].dtype),
+        input_output_aliases={1 + count: 0} if rest else {},
         compiler_params=params("arbitrary"),
         cost_estimate=pl.CostEstimate(
             flops=0, bytes_accessed=pieces[0].size * 4 * count, transcendentals=0
         ),
         name="place_blocks",
-    )(where, *pieces)
+    )(where, *pieces, *rest)
 
 
 def body(
@@ -928,9 +930,13 @@
     held, share = max(local_experts // units, 1), max(units // local_experts, 1)
     unit = lax.rem(wide_index, units)
     shape = (held, 2, rows, model_width)
-    tokens_sent = jnp.stack(both).reshape((share, narrow // share, units // share) + shape)
-    tokens_sent = tokens_sent.transpose(2, 0, 1, 3, 4, 5, 6).reshape((units, narrow // share) + shape)
-    tokens_sent = jnp.concatenate([tokens_sent] * halves)
+    if share == 1:
+        tokens_sent = [x.reshape((units, 1) + shape) for x in both]
+        tokens_sent = jnp.concatenate([jnp.concatenate([x] * halves) for x in tokens_sent], axis=1)
+    else:
+        tokens_sent = jnp.stack(both).reshape((share, narrow // share, units // share) + shape)
+        tokens_sent = tokens_sent.transpose(2, 0, 1, 3, 4, 5, 6).reshape((units, narrow // share) + shape)
+        tokens_sent = jnp.concatenate([tokens_sent] * halves)
     tokens_sent, both = lax.optimization_barrier((tokens_sent, both))
     tokens_all = lax.all_to_all(tokens_sent, "wide", split_axis=0, concat_axis=0, tiled=True)
     if rows % 16 == 0:
@@ -1010,26 +1016,25 @@
     weights = kept.astype(F32) + swap_core(sent).astype(F32) + far
     part_sums = wide_parts(weights)
 
-    d_tokens = [d_tokens] + [from_chip(d_tokens, k) for k in range(1, narrow // 2)]
-    swapped = [swap_core(d_tokens[0]), swap_core(mixed_part)]
-    mixed_part, d_tokens[1:], swapped, expert_grads = lax.optimization_barrier(
-        (mixed_part, d_tokens[1:], swapped, expert_grads)
-    )
-    mixed_part = [mixed_part] + [from_chip(mixed_part, k) for k in range(1, narrow // 2)]
+    far_tokens = [from_chip(d_tokens, k) for k in range(1, narrow // 2)]
+    swapped = [swap_core(d_tokens), swap_core(mixed_part)]
     order = lax.bitwise_xor(unit, jnp.arange(units)) * held
-    order = (order[None] + jnp.arange(held)[:, None]).reshape(-1)
-    pieces = [piece for x in expert_grads for piece in x]
-    g_w_in, g_w_out, bias = owned_weights(pieces, order, w_in.shape[2], wide)
-    swapped = swapped + [swap_core(x) for x in d_tokens[1:]]
-    part_sums, bias, swapped = lax.optimization_barrier((part_sums, bias, swapped))
-
-    def placed(pieces, others):
-        pieces = [x for pair in zip(pieces, others) for x in pair]
-        return place_blocks(pieces, relative)[:slot_count]
-
-    d_tokens = placed(d_tokens, swapped[:1] + swapped[2:])
-    mixed_part[1:], d_tokens = lax.optimization_barrier((mixed_part[1:], d_tokens))
-    mixed_part = placed(mixed_part, swapped[1:2] + [swap_core(x) for x in mixed_part[1:]])
+    order = order[None] + jnp.arange(held)[:, None]
+    order = jnp.concatenate([order[:, :-1].reshape(-1), order[:, -1]])
+    pieces = [piece for x in expert_grads for piece in x[:-1]] + [x[-1] for x in expert_grads]
+    owned = owned_weights(pieces[:-1], order[:-1], units * held, w_in.shape[2], wide)
+    mixed_part, far_tokens, swapped, owned, pieces[-1] = lax.optimization_barrier(
+        (mixed_part, far_tokens, swapped, owned, pieces[-1])
+    )
+    far_mixed = [from_chip(mixed_part, k) for k in range(1, narrow // 2)]
+    far_tokens = [y for x in far_tokens for y in (x, swap_core(x))]
+    part_sums, far_tokens = lax.optimization_barrier((part_sums, far_tokens))
+    d_tokens = place_blocks([d_tokens, swapped[0]] + far_tokens, relative, narrow)
+    g_w_in, g_w_out, bias = owned_weights(after(pieces[-1:], part_sums), order[-1:], units * held, w_in.shape[2], wide, owned)
+    far_mixed, d_tokens, bias = lax.optimization_barrier((far_mixed, d_tokens, bias))
+    far_mixed = [y for x in far_mixed for y in (x, swap_core(x))]
+    mixed_part = place_blocks([mixed_part, swapped[1]] + far_mixed, relative, narrow)
+    d_tokens, mixed_part = d_tokens[:slot_count], mixed_part[:slot_count]
     weights = from_parts(part_sums)
     gains = weights[end : end + 16].astype(BF16)
     gains = sum([to_chip(gains, k).astype(F32) for k in range(1, narrow // 2)], gains.astype(F32))

time: 278 us -> 275 us (0.989)
  waiting for transfers between devices: 81.4 us -> 77.7 us
  Pallas kernels: 116 us -> 119 us
    ppermute x6, waiting for transfers between devices: 12.9 us -> 5.07 us  [to_unit(): return lax.ppermute(x, 'wide', [(w, w ^ d) for w in range(wide)])]
    all_to_all x1, waiting for transfers between devices: 0.01 us -> 3.38 us  [wide_parts(): lax.all_to_all(parts, 'wide', split_axis=0, concat_axis=0, tiled=True)]
    pallas_call x3 -> x4, Pallas kernels: 16.8 us -> 19 us  [the longest x2 9.64 us: owned_weights(): pl.pallas_call(functools.partial(owner_kernel, count), grid_spec=pltpu.Pr...]
  transfers between devices with their start and end apart: 34 -> 34, of which waited for: 18 -> 19; matrix products, arithmetic and copies ran while one was open for 7% -> 7% of each run, Pallas kernels for 39% -> 41%
where the time goes in v5:
time: 275 us; the launch traced here: 274 us
  Pallas kernels  119 us (43%)
  waiting for transfers between devices  77.7 us (28%)
  starting transfers between devices  46.4 us (17%)
  local copies, waits for them, and re-layouts  19.6 us (7%)
  other arithmetic  10.5 us (4%)
    pallas_call x2, Pallas kernels, expert_weights(): pl.pallas_call(lambda where, expert, *refs: weight_kernel(units, where, *...  21.2 us
    pallas_call x1, Pallas kernels, experts_at_positions(): pl.pallas_call(functools.partial(expert_kernel, sources), grid=(experts,)...  20.8 us
    all_to_all x1, waiting for transfers between devices, to_positions(): x = lax.all_to_all(x, BOTH, split_axis=0, concat_axis=0, tiled=True)  16.5 us
    pallas_call x1, Pallas kernels, attention_back_far(): pl.pallas_call(functools.partial(back_far_kernel, blocks, inner // count)...  13.8 us
    pallas_call x1, Pallas kernels, attention_back_near(): pl.pallas_call(functools.partial(back_near_kernel, blocks, inner // count...  12.6 us
    ppermute x3, waiting for transfers between devices, to_relative(): lax.ppermute(x, 'narrow', [(n, (n + 2 * k) % narrow ^ other) for n in ran...  12.3 us
    ppermute x3, waiting for transfers between devices, from_relative(): lax.ppermute(x, 'narrow', [((n + 2 * k) % narrow ^ other, n) for n in ran...  11.4 us
    all_to_all x1, waiting for transfers between devices, to_slots(): return lax.all_to_all(x, BOTH, split_axis=0, concat_axis=0, tiled=True)  10.5 us
  transfers between devices with their start and end apart: 34, of which 19 were waited for; matrix products, arithmetic and copies ran while one was open for 7% of the time, Pallas kernels for 41%

profile of v5, /device:TPU:0, one launch (start us, length us, event | category | flops | bytes accessed | tf_op | source)
XLA Modules:
  0.0 274.1 jit_solution(15675958576456582436)
XLA Ops:
  0.7 2.0 pack_weights.1.refs_0_
  3.1 1.7 collective-permute-done.refs_1_
  4.9 2.3 copy_bitcast_fusion
  7.2 7.2 %all-to-all-start.1 = ((bf16[8,12,8,512]{3,2,1,0:T(8,128)(2,1)}), bf16[8,12,8,512]{3,2,1,0:T(8,128)(2,1)S(1)}, u32[]{:S(2)}, u32[]{:S(2)}) async-start(bf16[8,12,8,512]{3,2,1,0:T(8,128)(2,1)} %copy_bitcast_fusion), calls=%async_computation.1 | async-start | bytes 1572864 | tf_op jit(solution)/shard_map/all_to_all | solution.py:899
  14.4 1.6 collective-permute-start.1
  17.2 1.2 pad_add_fusion.1.place
  18.5 8.2 %attention_near.1 = (f32[3,256,512]{2,1,0:T(8,128)}, bf16[3,256,768]{2,1,0:T(8,128)(2,1)}, bf16[3,256,256]{2,1,0:T(8,128)(2,1)}) custom-call(s32[2]{0:T(128)} %pad_add_fusion.1.place, bf16[12,256,512]{2,1,0:T(8,128)(2,1)} %tokens.7, bf16[512,512]{1,0:T(8,128)(2,1)} %pack_weights.1.refs_0_, bf16[512,512]{1,0:T(8,128)(2,1)} %copy-done.19, f32[1,512]{1,0:T(1,128)} %bitcast.84), custom_call_target="tpu_custom_call" | custom-call | flops 1207959552 | bytes 4980736 | tf_op jit(solution)/shard_map/attention_near/pallas_call | solution.py:119
  26.7 1.5 collective-permute-done.1.refs_0_
  30.9 9.0 %attention_far.1 = (bf16[32,3,8,512]{3,2,1,0:T(8,128)(2,1)}, f32[3,256,512]{2,1,0:T(8,128)}, bf16[3,256,768]{2,1,0:T(8,128)(2,1)}, bf16[3,256,256]{2,1,0:T(8,128)(2,1)}) custom-call(s32[2]{0:T(128)} %pad_add_fusion.1.place, bf16[12,256,512]{2,1,0:T(8,128)(2,1)} %tokens.7, f32[3,256,512]{2,1,0:T(8,128)} %get-tuple-element.96.partial, ...), custom_call_target="tpu_custom_call" | custom-call | flops 1207959552 | bytes 7340032 | tf_op jit(solution)/shard_map/attention_far/pallas_call | solution.py:154
  39.9 5.7 %all-to-all-start = ((bf16[32,3,8,512]{3,2,1,0:T(8,128)(2,1)}), bf16[32,3,8,512]{3,2,1,0:T(8,128)(2,1)S(1)}, u32[]{:S(2)}, u32[]{:S(2)}) async-start(bf16[32,3,8,512]{3,2,1,0:T(8,128)(2,1)} %get-tuple-element.98), calls=%async_computation | async-start | bytes 1572864 | tf_op jit(solution)/shard_map/all_to_all | solution.py:886
  49.8 16.5 %all-to-all-done = bf16[32,3,8,512]{3,2,1,0:T(8,128)(2,1)S(1)} async-done(((bf16[32,3,8,512]{3,2,1,0:T(8,128)(2,1)}), bf16[32,3,8,512]{3,2,1,0:T(8,128)(2,1)S(1)}, u32[]{:S(2)}, u32[]{:S(2)}) %all-to-all-start) | async-done | bytes 786464 | tf_op jit(solution)/shard_map/all_to_all | solution.py:886
  67.1 5.4 %mix_forward.1 = (f32[768,32]{1,0:T(8,128)}, bf16[768,512]{1,0:T(8,128)(2,1)}, bf16[8,2,16,512]{3,2,1,0:T(8,128)(2,1)}, bf16[8,2,16,512]{3,2,1,0:T(8,128)(2,1)},...) custom-call(s32[4]{0:T(128)} %copy-done.24, bf16[768,512]{1,0:T(8,128)(2,1)} %bitcast.76, ...), custom_call_target="tpu_custom_call" | custom-call | flops 805306368 | bytes 4718592 | tf_op jit(solution)/shard_map/mix_forward/pallas_call | solution.py:254
  72.5 1.6 collective-permute-start.7
  74.4 7.5 %collective-permute-done.7.refs_2_ = bf16[8,2,16,512]{3,2,1,0:T(8,128)(2,1)S(1)} collective-permute-done((bf16[8,2,16,512]{3,2,1,0:T(8,128)(2,1)}, bf16[8,2,16,512]{3,2,1,0:T(8,128)(2,1)S(1)}, u32[]{:S(2)}, u32[]{:S(2)}) %collective-permute-start.7) | collective-permute-done | bytes 262176 | tf_op jit(solution)/shard_map/ppermute | solution.py:778
  81.8 4.8 %collective-permute-done.8.refs_3_ = bf16[8,2,16,512]{3,2,1,0:T(8,128)(2,1)S(1)} collective-permute-done((bf16[8,2,16,512]{3,2,1,0:T(8,128)(2,1)}, bf16[8,2,16,512]{3,2,1,0:T(8,128)(2,1)S(1)}, u32[]{:S(2)}, u32[]{:S(2)}) %collective-permute-start.8) | collective-permute-done | bytes 262176 | tf_op jit(solution)/shard_map/ppermute | solution.py:778
  86.6 2.5 maximum_maximum_fusion
  89.2 3.8 %all-to-all-start.3 = ((bf16[8,4,2,2,16,512]{5,4,3,2,1,0:T(8,128)(2,1)}), bf16[8,4,2,2,16,512]{5,4,3,2,1,0:T(8,128)(2,1)S(1)}, u32[]{:S(2)}, u32[]{:S(2)}) async-start(bf16[8,4,2,2,16,512]{5,4,3,2,1,0:T(8,128)(2,1)} %maximum_maximum_fusion), calls=%async_computation.3 | async-start | bytes 4194304 | tf_op jit(solution)/shard_map/all_to_all | solution.py:941
  94.2 20.8 %experts.1 = (bf16[8,2,16,512]{3,2,1,0:T(8,128)(2,1)}, bf16[8,2,16,512]{3,2,1,0:T(8,128)(2,1)}, bf16[8,2,16,512]{3,2,1,0:T(8,128)(2,1)}, bf16[8,2,16,512]{3,2,1,0:T(8,128)(2,1)}) custom-call(bf16[8,2,16,512]{3,2,1,0:T(8,128)(2,1)} %get-tuple-element.107.refs_0_, bf16[8,2,16,512]{3,2,1,0:T(8,128)(2,1)} %copy-done.4, bf16[8,2,16,512]{3,2,1,0:T(8,128)(2,1)} %copy-done.5, ...), custom_call_target="tpu_custom_call" | custom-call | flops 4294967296 | bytes 35651584 | tf_op jit(solution)/shard_map/experts/pallas_call | solution.py:362
  115.0 1.5 collective-permute-start.10
  117.2 7.2 %collective-permute-done.10.refs_2_ = bf16[8,2,16,512]{3,2,1,0:T(8,128)(2,1)S(1)} collective-permute-done((bf16[8,2,16,512]{3,2,1,0:T(8,128)(2,1)}, bf16[8,2,16,512]{3,2,1,0:T(8,128)(2,1)S(1)}, u32[]{:S(2)}, u32[]{:S(2)}) %collective-permute-start.10) | collective-permute-done | bytes 262176 | tf_op jit(solution)/shard_map/ppermute | solution.py:784
  124.4 4.2 %collective-permute-done.11.refs_3_ = bf16[8,2,16,512]{3,2,1,0:T(8,128)(2,1)S(1)} collective-permute-done((bf16[8,2,16,512]{3,2,1,0:T(8,128)(2,1)}, bf16[8,2,16,512]{3,2,1,0:T(8,128)(2,1)S(1)}, u32[]{:S(2)}, u32[]{:S(2)}) %collective-permute-start.11) | collective-permute-done | bytes 262176 | tf_op jit(solution)/shard_map/ppermute | solution.py:784
  129.4 6.9 %mix_backward.1 = (bf16[32,2,24,512]{3,2,1,0:T(8,128)(2,1)}, f32[32,512]{1,0:T(8,128)}) custom-call(s32[4]{0:T(128)} %copy-done.24, bf16[768,512]{1,0:T(8,128)(2,1)} %get-tuple-element.101.spread, bf16[768,512]{1,0:T(8,128)(2,1)} %bitcast.77, bf16[768,512]{1,0:T(8,128)(2,1)} %bitcast.75, f32[768,32]{1,0:T(8,128)} %get-tuple-element.102.probs, ...), custom_call_target="tpu_custom_call" | custom-call | flops 1610612736 | bytes 6291456 | tf_op jit(solution)/shard_map/mix_backward/pallas_call | solution.py:310
  136.4 5.4 %all-to-all-done.3.refs_0_ = bf16[8,4,2,2,16,512]{5,4,3,2,1,0:T(8,128)(2,1)S(1)} async-done(((bf16[8,4,2,2,16,512]{5,4,3,2,1,0:T(8,128)(2,1)}), bf16[8,4,2,2,16,512]{5,4,3,2,1,0:T(8,128)(2,1)S(1)}, u32[]{:S(2)}, u32[]{:S(2)}) %all-to-all-start.3) | async-done | bytes 2097184 | tf_op jit(solution)/shard_map/all_to_all | solution.py:941
  141.8 3.9 %all-to-all-start.2 = ((bf16[32,2,24,512]{3,2,1,0:T(8,128)(2,1)}), bf16[32,2,24,512]{3,2,1,0:T(8,128)(2,1)}, u32[]{:S(2)}, u32[]{:S(2)}) async-start(bf16[32,2,24,512]{3,2,1,0:T(8,128)(2,1)} %get-tuple-element.115), calls=%async_computation.2 | async-start | bytes 3145728 | tf_op jit(solution)/shard_map/all_to_all | solution.py:893
  146.3 10.6 %expert_weights.2 = (bf16[528,512]{1,0:T(8,128)(2,1)}, bf16[528,512]{1,0:T(8,128)(2,1)}, bf16[528,512]{1,0:T(8,128)(2,1)}, bf16[528,512]{1,0:T(8,128)(2,1)}) custom-call(s32[2]{0:T(128)} %pad_add_fusion.2.where, s32[1]{0:T(128)} %bitcast.28.expert, bf16[8,4,2,2,16,512]{5,4,3,2,1,0:T(8,128)(2,1)} %copy-done, bf16[8,512,2048]{2,1,0:T(8,128)(2,1)} %refs_1_.3, ...), custom_call_target="tpu_custom_call" | custom-call | flops 3221225472 | bytes 9437184 | tf_op jit(solution)/shard_map/expert_weights/pallas_call | solution.py:438
  156.8 1.5 collective-permute-start.12
  158.4 1.5 collective-permute-start.13
  159.8 10.6 %expert_weights.3 = (bf16[528,512]{1,0:T(8,128)(2,1)}, bf16[528,512]{1,0:T(8,128)(2,1)}, bf16[528,512]{1,0:T(8,128)(2,1)}, bf16[528,512]{1,0:T(8,128)(2,1)}) custom-call(s32[2]{0:T(128)} %pad_add_fusion.2.where, s32[1]{0:T(128)} %bitcast.29.expert, bf16[8,4,2,2,16,512]{5,4,3,2,1,0:T(8,128)(2,1)} %copy-done, bf16[8,512,2048]{2,1,0:T(8,128)(2,1)} %refs_1_.3, ...), custom_call_target="tpu_custom_call" | custom-call | flops 3221225472 | bytes 9437184 | tf_op jit(solution)/shard_map/expert_weights/pallas_call | solution.py:438
  172.9 10.5 %all-to-all-done.2.grads.mixed = bf16[32,2,24,512]{3,2,1,0:T(8,128)(2,1)} async-done(((bf16[32,2,24,512]{3,2,1,0:T(8,128)(2,1)}), bf16[32,2,24,512]{3,2,1,0:T(8,128)(2,1)}, u32[]{:S(2)}, u32[]{:S(2)}) %all-to-all-start.2) | async-done | bytes 1572896 | tf_op jit(solution)/shard_map/all_to_all | solution.py:893
  183.4 2.1 collective-permute-done.13.refs_2_
  185.6 13.8 %attention_back_far.1 = (f32[3,256,512]{2,1,0:T(8,128)}, f32[3,256,512]{2,1,0:T(8,128)}, bf16[3,256,512]{2,1,0:T(8,128)(2,1)}, f32[8,512]{1,0:T(8,128)}, bf16[21...) custom-call(s32[2]{0:T(128)} %pad_add_fusion.1.place, bf16[12,256,512]{2,1,0:T(8,128)(2,1)} %tokens.7, ...), custom_call_target="tpu_custom_call" | custom-call | bytes 10747904 | tf_op jit(solution)/shard_map/attention_back_far/pallas_call | solution.py:641
  199.6 2.2 collective-permute-done.16
  201.7 1.2 add_convert_fusion.1
  202.9 2.1 collective-permute-start.17
  206.0 12.6 %attention_back_near.1 = (bf16[3,256,512]{2,1,0:T(8,128)(2,1)}, bf16[2176,128]{1,0:T(8,128)(2,1)}, bf16[2176,128]{1,0:T(8,128)(2,1)}) custom-call(s32[2]{0:T(128)} %pad_add_fusion.1.place, bf16[12,256,512]{2,1,0:T(8,128)(2,1)} %tokens.7, f32[3,256,512]{2,1,0:T(8,128)} %get-tuple-element.127.d_hidden, f32[3,256,512]{2,1,0:T(8,128)} %get-tuple-element.135.partial, ...), custom_call_target="tpu_custom_call" | custom-call | bytes 8388608 | tf_op jit(solution)/shard_map/attention_back_near/pallas_call | solution.py:690
  218.7 1.3 collective-permute-done.18.refs_6_
  222.2 2.1 add_convert_fusion
  224.2 4.4 %all-to-all-start.4 = ((bf16[8,272,128]{2,1,0:T(8,128)(2,1)}), bf16[8,272,128]{2,1,0:T(8,128)(2,1)S(1)}, u32[]{:S(2)}, u32[]{:S(2)}) async-start(bf16[8,272,128]{2,1,0:T(8,128)(2,1)} %bitcast.36), calls=%async_computation.4 | async-start | bytes 1114112 | tf_op jit(solution)/shard_map/all_to_all | solution.py:765
  229.4 6.9 %owned_weights.2 = (f32[8,64,2048]{2,1,0:T(8,128)}, f32[8,256,512]{2,1,0:T(8,128)}, f32[8,16,512]{2,1,0:T(8,128)}) custom-call(s32[7]{0:T(128)} %bitcast.99, bf16[528,512]{1,0:T(8,128)(2,1)} %get-tuple-element.117.refs_0_, bf16[528,512]{1,0:T(8,128)(2,1)} %copy-done.14, bf16[528,512]{1,0:T(8,128)(2,1)} %copy-done.15, ...), custom_call_target="tpu_custom_call" | custom-call | bytes 11354112 | tf_op jit(solution)/shard_map/owned_weights/pallas_call | solution.py:485
  236.3 1.6 collective-permute-done.22.refs_0_
  238.0 3.2 %collective-permute-done.19.refs_2_ = bf16[3,256,512]{2,1,0:T(8,128)(2,1)S(1)} collective-permute-done((bf16[3,256,512]{2,1,0:T(8,128)(2,1)}, bf16[3,256,512]{2,1,0:T(8,128)(2,1)S(1)}, u32[]{:S(2)}, u32[]{:S(2)}) %collective-permute-start.19) | collective-permute-done | bytes 786464 | tf_op jit(solution)/shard_map/ppermute | solution.py:731
  241.9 3.4 %all-to-all-done.4 = bf16[8,272,128]{2,1,0:T(8,128)(2,1)S(1)} async-done(((bf16[8,272,128]{2,1,0:T(8,128)(2,1)}), bf16[8,272,128]{2,1,0:T(8,128)(2,1)S(1)}, u32[]{:S(2)}, u32[]{:S(2)}) %all-to-all-start.4) | async-done | bytes 557088 | tf_op jit(solution)/shard_map/all_to_all | solution.py:765
  246.2 4.3 %all-to-all-start.5 = ((bf16[8,272,128]{2,1,0:T(8,128)(2,1)}), bf16[8,272,128]{2,1,0:T(8,128)(2,1)S(1)}, u32[]{:S(2)}, u32[]{:S(2)}) async-start(bf16[8,272,128]{2,1,0:T(8,128)(2,1)} %broadcast_in_dim.86), calls=%async_computation.5 | async-start | bytes 1114112 | tf_op jit(solution)/shard_map/all_to_all | solution.py:771
  251.1 4.7 %place_blocks.2 = bf16[12,256,512]{2,1,0:T(8,128)(2,1)} custom-call(s32[4]{0:T(128)} %copy-done.24, bf16[3,256,512]{2,1,0:T(8,128)(2,1)} %get-tuple-element.144.refs_0_, bf16[3,256,512]{2,1,0:T(8,128)(2,1)} %collective-permute-done.20.refs_1_, bf16[3,256,512]{2,1,0:T(8,128)(2,1)} %copy-done.9, bf16[3,256,512]{2,1,0:T(8,128)(2,1)} %collective-permute-done.25.refs_3_), custom_call_target="tpu_custom_call" | custom-call | bytes 6291456 | tf_op jit(solution)/shard_map/place_blocks/pallas_call | solution.py:804
  255.8 2.7 owned_weights.3
  258.5 2.7 %collective-permute-done.23.refs_2_ = bf16[3,256,512]{2,1,0:T(8,128)(2,1)} collective-permute-done((bf16[3,256,512]{2,1,0:T(8,128)(2,1)S(1)}, bf16[3,256,512]{2,1,0:T(8,128)(2,1)}, u32[]{:S(2)}, u32[]{:S(2)}) %collective-permute-start.23) | collective-permute-done | bytes 786464 | tf_op jit(solution)/shard_map/ppermute | solution.py:731
  261.2 0.9 slice.76
  265.2 4.7 %place_blocks.3 = bf16[12,256,512]{2,1,0:T(8,128)(2,1)} custom-call(s32[4]{0:T(128)} %copy-done.24, bf16[3,256,512]{2,1,0:T(8,128)(2,1)} %get-tuple-element.152.refs_0_, bf16[3,256,512]{2,1,0:T(8,128)(2,1)} %copy-done.8, bf16[3,256,512]{2,1,0:T(8,128)(2,1)} %collective-permute-done.23.refs_2_, bf16[3,256,512]{2,1,0:T(8,128)(2,1)} %copy-done.10), custom_call_target="tpu_custom_call" | custom-call | bytes 6291456 | tf_op jit(solution)/shard_map/place_blocks/pallas_call | solution.py:804
  (156 shorter events, 29.0 us)
Async XLA Ops:
  0.6 15.3 %copy-start.23 = (bf16[512,8]{0,1:T(8,128)(2,1)S(1)}, bf16[512,8]{0,1:T(8,128)(2,1)}, u32[]{:S(2)}) copy-start(bf16[512,8]{0,1:T(8,128)(2,1)} %param.25) | copy-start | bytes 24580
  0.7 15.8 %copy-start.25 = (s32[8]{0:T(128)S(1)}, s32[8]{0:T(128)}, u32[]{:S(2)}) copy-start(s32[8]{0:T(128)} %param.17) | copy-start | bytes 100
  2.7 2.2 collective-permute-start
  4.9 13.6 %copy-start.19 = (bf16[512,512]{1,0:T(8,128)(2,1)}, bf16[512,512]{1,0:T(8,128)(2,1)S(1)}, u32[]{:S(2)}) copy-start(bf16[512,512]{1,0:T(8,128)(2,1)S(1)} %collective-permute-done.refs_1_) | copy-start | bytes 1572868
  7.2 32.8 %all-to-all-start.1 = ((bf16[8,12,8,512]{3,2,1,0:T(8,128)(2,1)}), bf16[8,12,8,512]{3,2,1,0:T(8,128)(2,1)S(1)}, u32[]{:S(2)}, u32[]{:S(2)}) async-start(bf16[8,12,8,512]{3,2,1,0:T(8,128)(2,1)} %copy_bitcast_fusion), calls=%async_computation.1 | async-start | bytes 1572864 | tf_op jit(solution)/shard_map/all_to_all | solution.py:899
  14.4 13.8 %collective-permute-start.1 = (bf16[512,512]{1,0:T(8,128)(2,1)S(1)}, bf16[512,512]{1,0:T(8,128)(2,1)S(1)}, u32[]{:S(2)}, u32[]{:S(2)}) collective-permute-start(bf16[512,512]{1,0:T(8,128)(2,1)S(1)} %copy-done.1), channel_id=1, source_target_pairs={{2,0},{3,1},{0,2},{1,3},{6,4},{7,5},{4,6},{5,7},{10,8},{11,9},{8,1... | collective-permute-start | bytes 1572872 | tf_op jit(solution)/shard_map/ppermute | solution.py:731
  15.9 30.0 %collective-permute-start.4 = (bf16[8,512]{1,0:T(8,128)(2,1)S(1)}, bf16[8,512]{1,0:T(8,128)(2,1)S(1)}, u32[]{:S(2)}, u32[]{:S(2)}) collective-permute-start(bf16[8,512]{1,0:T(8,128)(2,1)S(1)} %bitcast.93), channel_id=1, source_target_pairs={{2,0},{3,1},{0,2},{1,3},{6,4},{7,5},{4,6},{5,7},{10,8},{11,9},{8,1... | collective-permute-start | bytes 24584 | tf_op jit(solution)/shard_map/ppermute | solution.py:731
  16.5 32.0 %collective-permute-start.3 = (bf16[8,512]{1,0:T(8,128)(2,1)S(1)}, bf16[8,512]{1,0:T(8,128)(2,1)S(1)}, u32[]{:S(2)}, u32[]{:S(2)}) collective-permute-start(bf16[8,512]{1,0:T(8,128)(2,1)S(1)} %bitcast.94), channel_id=1, source_target_pairs={{0,1},{1,0},{2,3},{3,2},{4,5},{5,4},{6,7},{7,6},{8,9},{9,8},{10,11... | collective-permute-start | bytes 24584 | tf_op jit(solution)/shard_map/ppermute | solution.py:726
  28.2 1.9 collective-permute-start.2
  30.9 14.7 %copy-start.26 = (s32[64]{0:T(128)S(1)}, s32[64]{0:T(128)}, u32[]{:S(2)}) copy-start(s32[64]{0:T(128)} %param.18) | copy-start | bytes 772
  39.9 26.3 %copy-start.11 = (bf16[8,12,8,512]{3,2,1,0:T(8,128)(2,1)}, bf16[8,12,8,512]{3,2,1,0:T(8,128)(2,1)S(1)}, u32[]{:S(2)}) copy-start(bf16[8,12,8,512]{3,2,1,0:T(8,128)(2,1)S(1)} %all-to-all-done.1) | copy-start | bytes 2359300
  39.9 26.3 %all-to-all-start = ((bf16[32,3,8,512]{3,2,1,0:T(8,128)(2,1)}), bf16[32,3,8,512]{3,2,1,0:T(8,128)(2,1)S(1)}, u32[]{:S(2)}, u32[]{:S(2)}) async-start(bf16[32,3,8,512]{3,2,1,0:T(8,128)(2,1)} %get-tuple-element.98), calls=%async_computation | async-start | bytes 1572864 | tf_op jit(solution)/shard_map/all_to_all | solution.py:886
  45.9 2.5 collective-permute-start.5
  72.5 1.9 collective-permute-start.6
  72.5 9.3 %collective-permute-start.7 = (bf16[8,2,16,512]{3,2,1,0:T(8,128)(2,1)}, bf16[8,2,16,512]{3,2,1,0:T(8,128)(2,1)S(1)}, u32[]{:S(2)}, u32[]{:S(2)}) collective-permute-start(bf16[8,2,16,512]{3,2,1,0:T(8,128)(2,1)} %get-tuple-element.105), channel_id=1, source_target_pairs={{0,2},{1,3},{2,0},{3,1},{4,6},{5,7},{6,4},{7,5},{8,10},{9,11},{10,... | collective-permute-start | bytes 786440 | tf_op jit(solution)/shard_map/ppermute | solution.py:778
  74.1 12.5 %collective-permute-start.8 = (bf16[8,2,16,512]{3,2,1,0:T(8,128)(2,1)}, bf16[8,2,16,512]{3,2,1,0:T(8,128)(2,1)S(1)}, u32[]{:S(2)}, u32[]{:S(2)}) collective-permute-start(bf16[8,2,16,512]{3,2,1,0:T(8,128)(2,1)} %get-tuple-element.106), channel_id=1, source_target_pairs={{0,3},{1,2},{2,1},{3,0},{4,7},{5,6},{6,5},{7,4},{8,11},{9,10},{10,... | collective-permute-start | bytes 786440 | tf_op jit(solution)/shard_map/ppermute | solution.py:778
  74.4 14.8 %copy-start.4 = (bf16[8,2,16,512]{3,2,1,0:T(8,128)(2,1)}, bf16[8,2,16,512]{3,2,1,0:T(8,128)(2,1)S(1)}, u32[]{:S(2)}) copy-start(bf16[8,2,16,512]{3,2,1,0:T(8,128)(2,1)S(1)} %collective-permute-done.6.refs_1_) | copy-start | bytes 786436
  89.2 52.6 %all-to-all-start.3 = ((bf16[8,4,2,2,16,512]{5,4,3,2,1,0:T(8,128)(2,1)}), bf16[8,4,2,2,16,512]{5,4,3,2,1,0:T(8,128)(2,1)S(1)}, u32[]{:S(2)}, u32[]{:S(2)}) async-start(bf16[8,4,2,2,16,512]{5,4,3,2,1,0:T(8,128)(2,1)} %maximum_maximum_fusion), calls=%async_computation.3 | async-start | bytes 4194304 | tf_op jit(solution)/shard_map/all_to_all | solution.py:941
  115.0 9.4 %collective-permute-start.10 = (bf16[8,2,16,512]{3,2,1,0:T(8,128)(2,1)}, bf16[8,2,16,512]{3,2,1,0:T(8,128)(2,1)S(1)}, u32[]{:S(2)}, u32[]{:S(2)}) collective-permute-start(bf16[8,2,16,512]{3,2,1,0:T(8,128)(2,1)} %get-tuple-element.113), channel_id=1, source_target_pairs={{2,0},{3,1},{0,2},{1,3},{6,4},{7,5},{4,6},{5,7},{10,8},{11,9},{8,1... | collective-permute-start | bytes 786440 | tf_op jit(solution)/shard_map/ppermute | solution.py:784
  116.5 12.1 %collective-permute-start.11 = (bf16[8,2,16,512]{3,2,1,0:T(8,128)(2,1)}, bf16[8,2,16,512]{3,2,1,0:T(8,128)(2,1)S(1)}, u32[]{:S(2)}, u32[]{:S(2)}) collective-permute-start(bf16[8,2,16,512]{3,2,1,0:T(8,128)(2,1)} %get-tuple-element.114), channel_id=1, source_target_pairs={{3,0},{2,1},{1,2},{0,3},{7,4},{6,5},{5,6},{4,7},{11,8},{10,9},{9,1... | collective-permute-start | bytes 786440 | tf_op jit(solution)/shard_map/ppermute | solution.py:784
  116.7 12.0 %collective-permute-start.9 = (bf16[8,2,16,512]{3,2,1,0:T(8,128)(2,1)}, bf16[8,2,16,512]{3,2,1,0:T(8,128)(2,1)S(1)}, u32[]{:S(2)}, u32[]{:S(2)}) collective-permute-start(bf16[8,2,16,512]{3,2,1,0:T(8,128)(2,1)} %get-tuple-element.112), channel_id=1, source_target_pairs={{1,0},{0,1},{3,2},{2,3},{5,4},{4,5},{7,6},{6,7},{9,8},{8,9},{11,10... | collective-permute-start | bytes 786440 | tf_op jit(solution)/shard_map/ppermute | solution.py:784
  141.8 41.7 %all-to-all-start.2 = ((bf16[32,2,24,512]{3,2,1,0:T(8,128)(2,1)}), bf16[32,2,24,512]{3,2,1,0:T(8,128)(2,1)}, u32[]{:S(2)}, u32[]{:S(2)}) async-start(bf16[32,2,24,512]{3,2,1,0:T(8,128)(2,1)} %get-tuple-element.115), calls=%async_computation.2 | async-start | bytes 3145728 | tf_op jit(solution)/shard_map/all_to_all | solution.py:893
  156.8 26.6 %collective-permute-start.12 = (bf16[528,512]{1,0:T(8,128)(2,1)}, bf16[528,512]{1,0:T(8,128)(2,1)S(1)}, u32[]{:S(2)}, u32[]{:S(2)}) collective-permute-start(bf16[528,512]{1,0:T(8,128)(2,1)} %get-tuple-element.118), channel_id=1, source_target_pairs={{0,4},{4,0},{8,12},{12,8},{16,20},{20,16},{24,28},{28,24},{1,5},{5... | collective-permute-start | bytes 1622024 | tf_op jit(solution)/shard_map/ppermute | solution.py:789
  158.4 27.2 %collective-permute-start.13 = (bf16[528,512]{1,0:T(8,128)(2,1)}, bf16[528,512]{1,0:T(8,128)(2,1)S(1)}, u32[]{:S(2)}, u32[]{:S(2)}) collective-permute-start(bf16[528,512]{1,0:T(8,128)(2,1)} %get-tuple-element.119), channel_id=1, source_target_pairs={{0,8},{4,12},{8,0},{12,4},{16,24},{20,28},{24,16},{28,20},{1,9},{5... | collective-permute-start | bytes 1622024 | tf_op jit(solution)/shard_map/ppermute | solution.py:789
  170.5 29.0 %collective-permute-start.14 = (bf16[528,512]{1,0:T(8,128)(2,1)}, bf16[528,512]{1,0:T(8,128)(2,1)S(1)}, u32[]{:S(2)}, u32[]{:S(2)}) collective-permute-start(bf16[528,512]{1,0:T(8,128)(2,1)} %get-tuple-element.131), channel_id=1, source_target_pairs={{0,4},{4,0},{8,12},{12,8},{16,20},{20,16},{24,28},{28,24},{1,5},{5... | collective-permute-start | bytes 1622024 | tf_op jit(solution)/shard_map/ppermute | solution.py:789
  171.1 28.4 %collective-permute-start.15 = (bf16[528,512]{1,0:T(8,128)(2,1)}, bf16[528,512]{1,0:T(8,128)(2,1)S(1)}, u32[]{:S(2)}, u32[]{:S(2)}) collective-permute-start(bf16[528,512]{1,0:T(8,128)(2,1)} %get-tuple-element.132), channel_id=1, source_target_pairs={{0,8},{4,12},{8,0},{12,4},{16,24},{20,28},{24,16},{28,20},{1,9},{5... | collective-permute-start | bytes 1622024 | tf_op jit(solution)/shard_map/ppermute | solution.py:789
  183.4 16.0 %copy-start.14 = (bf16[528,512]{1,0:T(8,128)(2,1)}, bf16[528,512]{1,0:T(8,128)(2,1)S(1)}, u32[]{:S(2)}) copy-start(bf16[528,512]{1,0:T(8,128)(2,1)S(1)} %collective-permute-done.12.refs_1_) | copy-start | bytes 1622020
  185.6 13.9 %copy-start.15 = (bf16[528,512]{1,0:T(8,128)(2,1)}, bf16[528,512]{1,0:T(8,128)(2,1)S(1)}, u32[]{:S(2)}) copy-start(bf16[528,512]{1,0:T(8,128)(2,1)S(1)} %collective-permute-done.13.refs_2_) | copy-start | bytes 1622020
  185.6 19.5 %copy-start.27 = (bf16[528,512]{1,0:T(8,128)(2,1)S(1)}, bf16[528,512]{1,0:T(8,128)(2,1)}, u32[]{:S(2)}) copy-start(bf16[528,512]{1,0:T(8,128)(2,1)} %get-tuple-element.143) | copy-start | bytes 1622020
  199.5 19.2 %copy-start.16 = (bf16[528,512]{1,0:T(8,128)(2,1)}, bf16[528,512]{1,0:T(8,128)(2,1)S(1)}, u32[]{:S(2)}) copy-start(bf16[528,512]{1,0:T(8,128)(2,1)S(1)} %collective-permute-done.14.refs_4_) | copy-start | bytes 1622020
  199.5 19.2 %copy-start.17 = (bf16[528,512]{1,0:T(8,128)(2,1)}, bf16[528,512]{1,0:T(8,128)(2,1)S(1)}, u32[]{:S(2)}) copy-start(bf16[528,512]{1,0:T(8,128)(2,1)S(1)} %collective-permute-done.15.refs_5_) | copy-start | bytes 1622020
  199.5 2.2 collective-permute-start.16
  202.9 15.7 %collective-permute-start.17 = (bf16[2176,128]{1,0:T(8,128)(2,1)S(1)}, bf16[2176,128]{1,0:T(8,128)(2,1)S(1)}, u32[]{:S(2)}, u32[]{:S(2)}) collective-permute-start(bf16[2176,128]{1,0:T(8,128)(2,1)S(1)} %add_convert_fusion.1), channel_id=1, source_target_pairs={{0,2},{1,3},{2,0},{3,1},{4,6},{5,7},{6,4},{7,5},{8,10},{9,11},{10,... | collective-permute-start | bytes 1671176 | tf_op jit(solution)/shard_map/ppermute | solution.py:736
  205.1 14.9 %collective-permute-start.18 = (bf16[528,512]{1,0:T(8,128)(2,1)S(1)}, bf16[528,512]{1,0:T(8,128)(2,1)S(1)}, u32[]{:S(2)}, u32[]{:S(2)}) collective-permute-start(bf16[528,512]{1,0:T(8,128)(2,1)S(1)} %copy-done.27), channel_id=1, source_target_pairs={{0,12},{4,8},{8,4},{12,0},{16,28},{20,24},{24,20},{28,16},{1,13},{... | collective-permute-start | bytes 1622024 | tf_op jit(solution)/shard_map/ppermute | solution.py:789
  206.0 15.0 %copy-start.7 = (bf16[3,256,512]{2,1,0:T(8,128)(2,1)S(1)}, bf16[3,256,512]{2,1,0:T(8,128)(2,1)}, u32[]{:S(2)}) copy-start(bf16[3,256,512]{2,1,0:T(8,128)(2,1)} %get-tuple-element.152.refs_0_) | copy-start | bytes 2359300
  220.0 2.2 collective-permute-start.24
  220.1 17.9 %collective-permute-start.22 = (bf16[528,512]{1,0:T(8,128)(2,1)}, bf16[528,512]{1,0:T(8,128)(2,1)S(1)}, u32[]{:S(2)}, u32[]{:S(2)}) collective-permute-start(bf16[528,512]{1,0:T(8,128)(2,1)} %get-tuple-element.151), channel_id=1, source_target_pairs={{0,12},{4,8},{8,4},{12,0},{16,28},{20,24},{24,20},{28,16},{1,13},{... | collective-permute-start | bytes 1622024 | tf_op jit(solution)/shard_map/ppermute | solution.py:789
  221.0 17.0 %collective-permute-start.21 = (bf16[3,256,512]{2,1,0:T(8,128)(2,1)S(1)}, bf16[3,256,512]{2,1,0:T(8,128)(2,1)S(1)}, u32[]{:S(2)}, u32[]{:S(2)}) collective-permute-start(bf16[3,256,512]{2,1,0:T(8,128)(2,1)S(1)} %copy-done.7), channel_id=1, source_target_pairs={{0,1},{1,0},{2,3},{3,2},{4,5},{5,4},{6,7},{7,6},{8,9},{9,8},{10,11... | collective-permute-start | bytes 2359304 | tf_op jit(solution)/shard_map/ppermute | solution.py:726
  221.2 19.9 %collective-permute-start.19 = (bf16[3,256,512]{2,1,0:T(8,128)(2,1)}, bf16[3,256,512]{2,1,0:T(8,128)(2,1)S(1)}, u32[]{:S(2)}, u32[]{:S(2)}) collective-permute-start(bf16[3,256,512]{2,1,0:T(8,128)(2,1)} %get-tuple-element.144.refs_0_), channel_id=1, source_target_pairs={{2,0},{3,1},{0,2},{1,3},{6,4},{7,5},{4,6},{5,7},{10,8},{11,9},{8,1... | collective-permute-start | bytes 2359304 | tf_op jit(solution)/shard_map/ppermute | solution.py:731
  221.8 19.3 %collective-permute-start.20 = (bf16[3,256,512]{2,1,0:T(8,128)(2,1)}, bf16[3,256,512]{2,1,0:T(8,128)(2,1)}, u32[]{:S(2)}, u32[]{:S(2)}) collective-permute-start(bf16[3,256,512]{2,1,0:T(8,128)(2,1)} %get-tuple-element.144.refs_0_), channel_id=1, source_target_pairs={{0,1},{1,0},{2,3},{3,2},{4,5},{5,4},{6,7},{7,6},{8,9},{9,8},{10,11... | collective-permute-start | bytes 2359304 | tf_op jit(solution)/shard_map/ppermute | solution.py:726
  224.2 21.0 %all-to-all-start.4 = ((bf16[8,272,128]{2,1,0:T(8,128)(2,1)}), bf16[8,272,128]{2,1,0:T(8,128)(2,1)S(1)}, u32[]{:S(2)}, u32[]{:S(2)}) async-start(bf16[8,272,128]{2,1,0:T(8,128)(2,1)} %bitcast.36), calls=%async_computation.4 | async-start | bytes 1114112 | tf_op jit(solution)/shard_map/all_to_all | solution.py:765
  238.0 17.8 %copy-start.13 = (bf16[528,512]{1,0:T(8,128)(2,1)}, bf16[528,512]{1,0:T(8,128)(2,1)S(1)}, u32[]{:S(2)}) copy-start(bf16[528,512]{1,0:T(8,128)(2,1)S(1)} %collective-permute-done.22.refs_0_) | copy-start | bytes 1622020
  238.0 17.8 %copy-start.8 = (bf16[3,256,512]{2,1,0:T(8,128)(2,1)}, bf16[3,256,512]{2,1,0:T(8,128)(2,1)S(1)}, u32[]{:S(2)}) copy-start(bf16[3,256,512]{2,1,0:T(8,128)(2,1)S(1)} %collective-permute-done.21.refs_1_) | copy-start | bytes 2359300
  241.2 4.1 %collective-permute-start.25 = (bf16[3,256,512]{2,1,0:T(8,128)(2,1)S(1)}, bf16[3,256,512]{2,1,0:T(8,128)(2,1)}, u32[]{:S(2)}, u32[]{:S(2)}) collective-permute-start(bf16[3,256,512]{2,1,0:T(8,128)(2,1)S(1)} %collective-permute-done.19.refs_2_), channel_id=1, source_target_pairs={{0,1},{1,0},{2,3},{3,2},{4,5},{5,4},{6,7},{7,6},{8,9},{9,8},{10,11... | collective-permute-start | bytes 2359304 | tf_op jit(solution)/shard_map/ppermute | solution.py:726
  241.2 20.1 %collective-permute-start.23 = (bf16[3,256,512]{2,1,0:T(8,128)(2,1)S(1)}, bf16[3,256,512]{2,1,0:T(8,128)(2,1)}, u32[]{:S(2)}, u32[]{:S(2)}) collective-permute-start(bf16[3,256,512]{2,1,0:T(8,128)(2,1)S(1)} %copy-done.7), channel_id=1, source_target_pairs={{2,0},{3,1},{0,2},{1,3},{6,4},{7,5},{4,6},{5,7},{10,8},{11,9},{8,1... | collective-permute-start | bytes 2359304 | tf_op jit(solution)/shard_map/ppermute | solution.py:731
  246.2 23.7 %all-to-all-start.5 = ((bf16[8,272,128]{2,1,0:T(8,128)(2,1)}), bf16[8,272,128]{2,1,0:T(8,128)(2,1)S(1)}, u32[]{:S(2)}, u32[]{:S(2)}) async-start(bf16[8,272,128]{2,1,0:T(8,128)(2,1)} %broadcast_in_dim.86), calls=%async_computation.5 | async-start | bytes 1114112 | tf_op jit(solution)/shard_map/all_to_all | solution.py:771
  261.2 3.1 %collective-permute-start.26 = (bf16[3,256,512]{2,1,0:T(8,128)(2,1)}, bf16[3,256,512]{2,1,0:T(8,128)(2,1)S(1)}, u32[]{:S(2)}, u32[]{:S(2)}) collective-permute-start(bf16[3,256,512]{2,1,0:T(8,128)(2,1)} %collective-permute-done.23.refs_2_), channel_id=1, source_target_pairs={{0,1},{1,0},{2,3},{3,2},{4,5},{5,4},{6,7},{7,6},{8,9},{9,8},{10,11... | collective-permute-start | bytes 2359304 | tf_op jit(solution)/shard_map/ppermute | solution.py:726
  269.9 3.6 %collective-permute-start.27 = (bf16[16,128]{1,0:T(8,128)(2,1)S(1)}, bf16[16,128]{1,0:T(8,128)(2,1)S(1)}, u32[]{:S(2)}, u32[]{:S(2)}) collective-permute-start(bf16[16,128]{1,0:T(8,128)(2,1)S(1)} %slice.87), channel_id=1, source_target_pairs={{0,2},{1,3},{2,0},{3,1},{4,6},{5,7},{6,4},{7,5},{8,10},{9,11},{10,... | collective-permute-start | bytes 12296 | tf_op jit(solution)/shard_map/ppermute | solution.py:736
  (17 other events, 81.9 us)

commit v6 on v5

--- a/solution.py
+++ b/solution.py
@@ -41,9 +41,13 @@
     return pl.BlockSpec(tuple(shape), lambda *_: zeros)
 
 
-def head_masks(rows):
-    lane = lax.broadcasted_iota(jnp.int32, (rows, LANES), 1)
+def head_masks(shape, axis):
+    lane = lax.broadcasted_iota(jnp.int32, shape, axis)
     return [(lane >= h * HEAD_WIDTH) & (lane < (h + 1) * HEAD_WIDTH) for h in range(LANES // HEAD_WIDTH)]
+
+
+def masks_of(length):
+    return list(zip(head_masks((length, LANES), 1), head_masks((LANES, length), 0)))
 
 
 def keep(mask, rows):
@@ -51,14 +55,14 @@
 
 
 def causal_probs(query_head, keys, causal):
-    scores = mm_nt(query_head, keys) * (float(HEAD_WIDTH) ** -0.5)
+    scores = mm_nt(keys, query_head) * (float(HEAD_WIDTH) ** -0.5)
     scores = jnp.where(causal, scores, NEGATIVE)
-    powers = jnp.exp(scores - jnp.max(scores, axis=-1, keepdims=True))
-    return powers * (1.0 / jnp.sum(powers, axis=-1, keepdims=True))
+    powers = jnp.exp(scores - jnp.max(scores, axis=0, keepdims=True))
+    return powers * (1.0 / jnp.sum(powers, axis=0, keepdims=True))
 
 
 def causal_mask(length):
-    return lax.broadcasted_iota(jnp.int32, (length, length), 0) >= lax.broadcasted_iota(
+    return lax.broadcasted_iota(jnp.int32, (length, length), 0) <= lax.broadcasted_iota(
         jnp.int32, (length, length), 1
     )
 
@@ -73,12 +77,12 @@
         joint = mm(entry, pack[:, : 3 * LANES]).astype(BF16)
         joint_out[0, :, j * 3 * LANES : (j + 1) * 3 * LANES] = joint
         q, k, v = (joint[:, i * LANES : (i + 1) * LANES] for i in range(3))
-        context = None
-        for mask in masks:
+        turned, context = v.T, None
+        for mask, across in masks:
             probs = causal_probs(keep(mask, q), k, causal)
-            term = mm(probs.astype(BF16), keep(mask, v))
+            term = mm(keep(across, turned), probs.astype(BF16))
             context = term if context is None else context + term
-        context = context.astype(BF16)
+        context = context.astype(BF16).T
         context_out[0, :, j * LANES : (j + 1) * LANES] = context
         term = mm_nt(context, pack[:, 3 * LANES :])
         attention = term if attention is None else attention + term
@@ -91,7 +95,7 @@
     entry = (rows * inverse_rms(rows) * gain_attn[...]).astype(BF16)
     length = rows.shape[0]
     partial_out[0] = rows + attend(
-        entry, packs, causal_mask(length), head_masks(length), joint_out, context_out
+        entry, packs, causal_mask(length), masks_of(length), joint_out, context_out
     )
 
 
@@ -102,7 +106,7 @@
     entry = (rows * inverse_rms(rows) * gain_attn[...]).astype(BF16)
     length = rows.shape[0]
     hidden = partial[0] + attend(
-        entry, packs, causal_mask(length), head_masks(length), joint_out, context_out
+        entry, packs, causal_mask(length), masks_of(length), joint_out, context_out
     )
     mixed = hidden * inverse_rms(hidden) * gain_mix[...]
     mix_out[...] = mixed.reshape(mix_out.shape).astype(BF16)
@@ -500,71 +504,76 @@
     )(where, *pieces, *rest)
 
 
-def attend_back(entry, d_low, packs, joint_in, context_in, causal, masks, total):
-    width = entry.shape[1]
+def attend_back(i, entry, d_low, packs, joint_in, context_in, causal, masks, held):
+    length = entry.shape[0]
+    lines = pl.ds(pl.multiple_of(i * length, length), length)
+    for ref, rows in zip(held, (entry, d_low, None, context_in[0])):
+        if rows is not None:
+            ref[lines] = rows
     scale = float(HEAD_WIDTH) ** -0.5
     d_entry = None
     for j, pack in enumerate(packs):
         base = j * 3 * LANES
         q, k, v = (joint_in[0, :, base + i * LANES : base + (i + 1) * LANES] for i in range(3))
-        context = context_in[0, :, j * LANES : (j + 1) * LANES]
         d_context = mm(d_low, pack[:, 3 * LANES :]).astype(BF16)
         d_q, d_k, d_v = [], [], []
-        for mask in masks:
+        turned = k.T
+        for mask, across in masks:
             q_head = keep(mask, q)
             d_head = keep(mask, d_context)
             probs = causal_probs(q_head, k, causal)
-            d_probs = mm_nt(d_head, v).astype(BF16).astype(F32)
-            d_scores = probs * (d_probs - jnp.sum(probs * d_probs, axis=-1, keepdims=True))
+            d_probs = mm_nt(v, d_head).astype(BF16).astype(F32)
+            d_scores = probs * (d_probs - jnp.sum(probs * d_probs, axis=0, keepdims=True))
             d_scores = d_scores.astype(BF16)
-            d_v.append(mm_tn(probs.astype(BF16), d_head))
-            d_q.append(mm(d_scores, keep(mask, k)))
-            d_k.append(mm_tn(d_scores, q_head))
-        joint = [sum(d_q) * scale, sum(d_k) * scale, sum(d_v)]
-        joint = jnp.concatenate(joint, axis=1).astype(BF16)
+            d_v.append(mm(probs.astype(BF16), d_head))
+            d_q.append(mm(keep(across, turned), d_scores))
+            d_k.append(mm(d_scores, q_head))
+        joint = [(sum(d_q) * scale).astype(BF16).T, (sum(d_k) * scale).astype(BF16), sum(d_v).astype(BF16)]
+        joint = jnp.concatenate(joint, axis=1)
         term = mm_nt(joint, pack[:, : 3 * LANES])
         d_entry = term if d_entry is None else d_entry + term
-        grad = mm_tn(entry, joint)
-        for c in range(3):
-            total[j, c * width : (c + 1) * width] += grad[:, c * LANES : (c + 1) * LANES]
-        grad = mm_tn(context, d_low)
-        for c in range(width // LANES):
-            at = slice(3 * width + c * LANES, 3 * width + (c + 1) * LANES)
-            total[j, at] += grad[:, c * LANES : (c + 1) * LANES]
+        held[2][lines, base : base + 3 * LANES] = joint
     return d_entry
 
 
-def store_weights(total, controllers, outs, lanes, gains=None):
-    height = total.shape[1]
+def store_weights(held, controllers, outs, lanes, gains=None):
+    entry, d_low, joint, context = held
+    width = entry.shape[1]
     for o, out in enumerate(outs):
         j, at = divmod(o, LANES // lanes)
-        piece = total[j].astype(BF16)
-        if lanes < LANES:
-            own = slice(at * lanes, (at + 1) * lanes)
-            split = height // 4 * 3
-            piece = [jnp.pad(piece[:split, own], ((0, 0), (0, LANES - lanes)))] + [
-                jnp.pad(piece[c : c + LANES][own], ((0, LANES - lanes), (0, 0)))
-                for c in range(split, height, LANES)
-            ]
-            piece = jnp.concatenate(piece, axis=0)
-        out[:height] = piece
+        own = slice(at * lanes, (at + 1) * lanes)
+        grad = mm_tn(entry[...], joint[:, j * 3 * LANES : (j + 1) * 3 * LANES]).astype(BF16)
+        for c in range(3):
+            piece = grad[:, c * LANES : (c + 1) * LANES]
+            if lanes < LANES:
+                piece = jnp.pad(piece[:, own], ((0, 0), (0, LANES - lanes)))
+            out[c * width : (c + 1) * width] = piece
+        grad = mm_tn(context[:, j * LANES : (j + 1) * LANES], d_low[...]).astype(BF16)
+        for c in range(width // LANES):
+            piece = grad[:, c * LANES : (c + 1) * LANES]
+            if lanes < LANES:
+                piece = jnp.pad(piece[own], ((0, LANES - lanes), (0, 0)))
+            out[3 * width + c * LANES : 3 * width + (c + 1) * LANES] = piece
         tail = [controllers[o]]
         if gains is not None:
             tail.append(gains)
-        left = out.shape[0] - height - sum(x.shape[0] for x in tail)
-        out[height:] = jnp.concatenate(tail + [jnp.zeros((left, LANES), BF16)], axis=0)
+        left = out.shape[0] - 4 * width - sum(x.shape[0] for x in tail)
+        out[4 * width :] = jnp.concatenate(tail + [jnp.zeros((left, LANES), BF16)], axis=0)
+
+
+def held_rows(slots, length, width, inner):
+    return [pltpu.VMEM((slots * length, columns), BF16) for columns in (width, width, 3 * inner, inner)]
 
 
 def back_far_kernel(blocks, lanes, place, tokens, cots, grads, mixed, hidden, joint, context, *refs):
     packs, (gain_attn, gain_mix, controllers), refs = refs[:blocks], refs[blocks : blocks + 3], refs[blocks + 3 :]
-    (partial_out, d_hidden_out, mixed_out, gain_out), outs, total = refs[:4], refs[4:-1], refs[-1]
+    (partial_out, d_hidden_out, mixed_out, gain_out), outs, held = refs[:4], refs[4:-4], refs[-4:]
     i = pl.program_id(0)
     length, width = hidden.shape[1:]
     live = (place[0] + i < place[1]).astype(F32)
 
     @pl.when(i == 0)
     def _():
-        total[...] = jnp.zeros_like(total)
         gain_out[...] = jnp.zeros_like(gain_out)
 
     rows = hidden[0]
@@ -581,23 +590,22 @@
     rows = tokens[0].astype(F32)
     entry = (rows * inverse_rms(rows) * gain_attn[...]).astype(BF16)
     partial_out[0] = attend_back(
-        entry, d_hidden.astype(BF16), packs, joint, context, causal_mask(length), head_masks(length), total
+        i, entry, d_hidden.astype(BF16), packs, joint, context, causal_mask(length), masks_of(length), held
     )
 
     @pl.when(i == pl.num_programs(0) - 1)
     def _():
-        store_weights(total, controllers, outs, lanes)
+        store_weights(held, controllers, outs, lanes)
 
 
 def back_near_kernel(blocks, lanes, place, tokens, d_hidden, partial, joint, context, *refs):
     packs, (gain_attn, gain_in, controllers), refs = refs[:blocks], refs[blocks : blocks + 3], refs[blocks + 3 :]
-    d_tokens_out, outs, (total, gain) = refs[0], refs[1:-2], refs[-2:]
+    d_tokens_out, outs, held, gain = refs[0], refs[1:-5], refs[-5:-1], refs[-1]
     i = pl.program_id(0)
     length, width = d_hidden.shape[1:]
 
     @pl.when(i == 0)
     def _():
-        total[...] = jnp.zeros_like(total)
         gain[...] = jnp.zeros_like(gain)
 
     rows = tokens[0].astype(F32)
@@ -605,7 +613,7 @@
     normed = rows * inverse
     entry = (normed * gain_attn[...]).astype(BF16)
     d_entry = partial[0] + attend_back(
-        entry, d_hidden[0].astype(BF16), packs, joint, context, causal_mask(length), head_masks(length), total
+        i, entry, d_hidden[0].astype(BF16), packs, joint, context, causal_mask(length), masks_of(length), held
     )
     d_entry = d_entry.astype(BF16).astype(F32)
     gain[0:1] += jnp.sum(d_entry * normed, axis=0, keepdims=True)
@@ -621,7 +629,7 @@
         pieces = width // LANES
         tail = [x[0:1, c * LANES : (c + 1) * LANES] for x in (gain, gain_in) for c in range(pieces)]
         tail.append(jnp.zeros((16 - 2 * pieces, LANES), F32))
-        store_weights(total, controllers, outs, lanes, jnp.concatenate(tail, axis=0).astype(BF16))
+        store_weights(held, controllers, outs, lanes, jnp.concatenate(tail, axis=0).astype(BF16))
 
 
 def attention_back_far(
@@ -656,7 +664,7 @@
             + [whole((1, width))] * 2
             + [whole(controllers.shape)],
             out_specs=[rows, rows, rows, whole((8, width))] + [whole((height, LANES))] * count,
-            scratch_shapes=[pltpu.VMEM((blocks, 4 * width, LANES), F32)],
+            scratch_shapes=held_rows(slots, length, width, inner),
         ),
         out_shape=[
             jax.ShapeDtypeStruct((slots, length, width), F32),
@@ -702,10 +710,7 @@
             + [whole(p.shape) for p in packs]
             + [whole((1, width)), whole((8, width)), whole(controllers.shape)],
             out_specs=[rows] + [whole((height, LANES))] * count,
-            scratch_shapes=[
-                pltpu.VMEM((blocks, 4 * width, LANES), F32),
-                pltpu.VMEM((8, width), F32),
-            ],
+            scratch_shapes=held_rows(slots, length, width, inner) + [pltpu.VMEM((8, width), F32)],
         ),
         out_shape=[
             jax.ShapeDtypeStruct((slots, length, width), BF16),

time: 275 us -> 274 us (level)
  Pallas kernels: 119 us -> 116 us
  transfers between devices with their start and end apart: 34 -> 34, of which waited for: 19 -> 20; matrix products, arithmetic and copies ran while one was open for 7% -> 7% of each run, Pallas kernels for 41% -> 40%
where the time goes in v6:
time: 274 us; the launch traced here: 272 us
  Pallas kernels  116 us (42%)
  waiting for transfers between devices  79.3 us (29%)
  starting transfers between devices  46.3 us (17%)
  local copies, waits for them, and re-layouts  19.6 us (7%)
  other arithmetic  10.5 us (4%)
    pallas_call x2, Pallas kernels, expert_weights(): pl.pallas_call(lambda where, expert, *refs: weight_kernel(units, where, *...  21.2 us
    pallas_call x1, Pallas kernels, experts_at_positions(): pl.pallas_call(functools.partial(expert_kernel, sources), grid=(experts,)...  20.8 us
    all_to_all x1, waiting for transfers between devices, to_positions(): x = lax.all_to_all(x, BOTH, split_axis=0, concat_axis=0, tiled=True)  16.5 us
    pallas_call x1, Pallas kernels, attention_back_far(): pl.pallas_call(functools.partial(back_far_kernel, blocks, inner // count)...  12.4 us
    ppermute x3, waiting for transfers between devices, to_relative(): lax.ppermute(x, 'narrow', [(n, (n + 2 * k) % narrow ^ other) for n in ran...  12.3 us
    pallas_call x1, Pallas kernels, attention_back_near(): pl.pallas_call(functools.partial(back_near_kernel, blocks, inner // count...  11.4 us
    ppermute x3, waiting for transfers between devices, from_relative(): lax.ppermute(x, 'narrow', [((n + 2 * k) % narrow ^ other, n) for n in ran...  11.4 us
    all_to_all x1, waiting for transfers between devices, to_slots(): return lax.all_to_all(x, BOTH, split_axis=0, concat_axis=0, tiled=True)  10.5 us
  transfers between devices with their start and end apart: 34, of which 20 were waited for; matrix products, arithmetic and copies ran while one was open for 7% of the time, Pallas kernels for 40%

profile of v6, /device:TPU:0, one launch (start us, length us, event | category | flops | bytes accessed | tf_op | source)
XLA Modules:
  0.0 272.3 jit_solution(9349898254318156863)
XLA Ops:
  0.7 2.0 pack_weights.1.refs_0_
  3.1 1.7 collective-permute-done.refs_1_
  4.9 2.3 copy_bitcast_fusion
  7.2 7.2 %all-to-all-start.1 = ((bf16[8,12,8,512]{3,2,1,0:T(8,128)(2,1)}), bf16[8,12,8,512]{3,2,1,0:T(8,128)(2,1)S(1)}, u32[]{:S(2)}, u32[]{:S(2)}) async-start(bf16[8,12,8,512]{3,2,1,0:T(8,128)(2,1)} %copy_bitcast_fusion), calls=%async_computation.1 | async-start | bytes 1572864 | tf_op jit(solution)/shard_map/all_to_all | solution.py:904
  14.4 1.6 collective-permute-start.1
  17.2 1.2 pad_add_fusion.1.place
  18.5 7.9 %attention_near.1 = (f32[3,256,512]{2,1,0:T(8,128)}, bf16[3,256,768]{2,1,0:T(8,128)(2,1)}, bf16[3,256,256]{2,1,0:T(8,128)(2,1)}) custom-call(s32[2]{0:T(128)} %pad_add_fusion.1.place, bf16[12,256,512]{2,1,0:T(8,128)(2,1)} %tokens.7, bf16[512,512]{1,0:T(8,128)(2,1)} %pack_weights.1.refs_0_, bf16[512,512]{1,0:T(8,128)(2,1)} %copy-done.19, f32[1,512]{1,0:T(1,128)} %bitcast.84), custom_call_target="tpu_custom_call" | custom-call | flops 1207959552 | bytes 4980736 | tf_op jit(solution)/shard_map/attention_near/pallas_call | solution.py:123
  26.4 1.8 collective-permute-done.1.refs_0_
  30.9 8.6 %attention_far.1 = (bf16[32,3,8,512]{3,2,1,0:T(8,128)(2,1)}, f32[3,256,512]{2,1,0:T(8,128)}, bf16[3,256,768]{2,1,0:T(8,128)(2,1)}, bf16[3,256,256]{2,1,0:T(8,128)(2,1)}) custom-call(s32[2]{0:T(128)} %pad_add_fusion.1.place, bf16[12,256,512]{2,1,0:T(8,128)(2,1)} %tokens.7, f32[3,256,512]{2,1,0:T(8,128)} %get-tuple-element.96.partial, ...), custom_call_target="tpu_custom_call" | custom-call | flops 1207959552 | bytes 7340032 | tf_op jit(solution)/shard_map/attention_far/pallas_call | solution.py:158
  39.6 5.7 %all-to-all-start = ((bf16[32,3,8,512]{3,2,1,0:T(8,128)(2,1)}), bf16[32,3,8,512]{3,2,1,0:T(8,128)(2,1)S(1)}, u32[]{:S(2)}, u32[]{:S(2)}) async-start(bf16[32,3,8,512]{3,2,1,0:T(8,128)(2,1)} %get-tuple-element.98), calls=%async_computation | async-start | bytes 1572864 | tf_op jit(solution)/shard_map/all_to_all | solution.py:891
  49.4 16.5 %all-to-all-done = bf16[32,3,8,512]{3,2,1,0:T(8,128)(2,1)S(1)} async-done(((bf16[32,3,8,512]{3,2,1,0:T(8,128)(2,1)}), bf16[32,3,8,512]{3,2,1,0:T(8,128)(2,1)S(1)}, u32[]{:S(2)}, u32[]{:S(2)}) %all-to-all-start) | async-done | bytes 786464 | tf_op jit(solution)/shard_map/all_to_all | solution.py:891
  66.8 5.4 %mix_forward.1 = (f32[768,32]{1,0:T(8,128)}, bf16[768,512]{1,0:T(8,128)(2,1)}, bf16[8,2,16,512]{3,2,1,0:T(8,128)(2,1)}, bf16[8,2,16,512]{3,2,1,0:T(8,128)(2,1)},...) custom-call(s32[4]{0:T(128)} %copy-done.24, bf16[768,512]{1,0:T(8,128)(2,1)} %bitcast.76, ...), custom_call_target="tpu_custom_call" | custom-call | flops 805306368 | bytes 4718592 | tf_op jit(solution)/shard_map/mix_forward/pallas_call | solution.py:258
  72.2 1.6 collective-permute-start.7
  74.0 7.5 %collective-permute-done.7.refs_2_ = bf16[8,2,16,512]{3,2,1,0:T(8,128)(2,1)S(1)} collective-permute-done((bf16[8,2,16,512]{3,2,1,0:T(8,128)(2,1)}, bf16[8,2,16,512]{3,2,1,0:T(8,128)(2,1)S(1)}, u32[]{:S(2)}, u32[]{:S(2)}) %collective-permute-start.7) | collective-permute-done | bytes 262176 | tf_op jit(solution)/shard_map/ppermute | solution.py:783
  81.5 4.8 %collective-permute-done.8.refs_3_ = bf16[8,2,16,512]{3,2,1,0:T(8,128)(2,1)S(1)} collective-permute-done((bf16[8,2,16,512]{3,2,1,0:T(8,128)(2,1)}, bf16[8,2,16,512]{3,2,1,0:T(8,128)(2,1)S(1)}, u32[]{:S(2)}, u32[]{:S(2)}) %collective-permute-start.8) | collective-permute-done | bytes 262176 | tf_op jit(solution)/shard_map/ppermute | solution.py:783
  86.3 2.5 maximum_maximum_fusion
  88.8 3.8 %all-to-all-start.3 = ((bf16[8,4,2,2,16,512]{5,4,3,2,1,0:T(8,128)(2,1)}), bf16[8,4,2,2,16,512]{5,4,3,2,1,0:T(8,128)(2,1)S(1)}, u32[]{:S(2)}, u32[]{:S(2)}) async-start(bf16[8,4,2,2,16,512]{5,4,3,2,1,0:T(8,128)(2,1)} %maximum_maximum_fusion), calls=%async_computation.3 | async-start | bytes 4194304 | tf_op jit(solution)/shard_map/all_to_all | solution.py:946
  93.9 20.8 %experts.1 = (bf16[8,2,16,512]{3,2,1,0:T(8,128)(2,1)}, bf16[8,2,16,512]{3,2,1,0:T(8,128)(2,1)}, bf16[8,2,16,512]{3,2,1,0:T(8,128)(2,1)}, bf16[8,2,16,512]{3,2,1,0:T(8,128)(2,1)}) custom-call(bf16[8,2,16,512]{3,2,1,0:T(8,128)(2,1)} %get-tuple-element.107.refs_0_, bf16[8,2,16,512]{3,2,1,0:T(8,128)(2,1)} %copy-done.4, bf16[8,2,16,512]{3,2,1,0:T(8,128)(2,1)} %copy-done.5, ...), custom_call_target="tpu_custom_call" | custom-call | flops 4294967296 | bytes 35651584 | tf_op jit(solution)/shard_map/experts/pallas_call | solution.py:366
  114.7 1.5 collective-permute-start.10
  116.9 7.2 %collective-permute-done.10.refs_2_ = bf16[8,2,16,512]{3,2,1,0:T(8,128)(2,1)S(1)} collective-permute-done((bf16[8,2,16,512]{3,2,1,0:T(8,128)(2,1)}, bf16[8,2,16,512]{3,2,1,0:T(8,128)(2,1)S(1)}, u32[]{:S(2)}, u32[]{:S(2)}) %collective-permute-start.10) | collective-permute-done | bytes 262176 | tf_op jit(solution)/shard_map/ppermute | solution.py:789
  124.1 4.2 %collective-permute-done.11.refs_3_ = bf16[8,2,16,512]{3,2,1,0:T(8,128)(2,1)S(1)} collective-permute-done((bf16[8,2,16,512]{3,2,1,0:T(8,128)(2,1)}, bf16[8,2,16,512]{3,2,1,0:T(8,128)(2,1)S(1)}, u32[]{:S(2)}, u32[]{:S(2)}) %collective-permute-start.11) | collective-permute-done | bytes 262176 | tf_op jit(solution)/shard_map/ppermute | solution.py:789
  129.1 6.9 %mix_backward.1 = (bf16[32,2,24,512]{3,2,1,0:T(8,128)(2,1)}, f32[32,512]{1,0:T(8,128)}) custom-call(s32[4]{0:T(128)} %copy-done.24, bf16[768,512]{1,0:T(8,128)(2,1)} %get-tuple-element.101.spread, bf16[768,512]{1,0:T(8,128)(2,1)} %bitcast.77, bf16[768,512]{1,0:T(8,128)(2,1)} %bitcast.75, f32[768,32]{1,0:T(8,128)} %get-tuple-element.102.probs, ...), custom_call_target="tpu_custom_call" | custom-call | flops 1610612736 | bytes 6291456 | tf_op jit(solution)/shard_map/mix_backward/pallas_call | solution.py:314
  136.0 5.4 %all-to-all-done.3.refs_0_ = bf16[8,4,2,2,16,512]{5,4,3,2,1,0:T(8,128)(2,1)S(1)} async-done(((bf16[8,4,2,2,16,512]{5,4,3,2,1,0:T(8,128)(2,1)}), bf16[8,4,2,2,16,512]{5,4,3,2,1,0:T(8,128)(2,1)S(1)}, u32[]{:S(2)}, u32[]{:S(2)}) %all-to-all-start.3) | async-done | bytes 2097184 | tf_op jit(solution)/shard_map/all_to_all | solution.py:946
  141.4 3.9 %all-to-all-start.2 = ((bf16[32,2,24,512]{3,2,1,0:T(8,128)(2,1)}), bf16[32,2,24,512]{3,2,1,0:T(8,128)(2,1)}, u32[]{:S(2)}, u32[]{:S(2)}) async-start(bf16[32,2,24,512]{3,2,1,0:T(8,128)(2,1)} %get-tuple-element.115), calls=%async_computation.2 | async-start | bytes 3145728 | tf_op jit(solution)/shard_map/all_to_all | solution.py:898
  145.9 10.6 %expert_weights.2 = (bf16[528,512]{1,0:T(8,128)(2,1)}, bf16[528,512]{1,0:T(8,128)(2,1)}, bf16[528,512]{1,0:T(8,128)(2,1)}, bf16[528,512]{1,0:T(8,128)(2,1)}) custom-call(s32[2]{0:T(128)} %pad_add_fusion.2.where, s32[1]{0:T(128)} %bitcast.28.expert, bf16[8,4,2,2,16,512]{5,4,3,2,1,0:T(8,128)(2,1)} %copy-done, bf16[8,512,2048]{2,1,0:T(8,128)(2,1)} %refs_1_.3, ...), custom_call_target="tpu_custom_call" | custom-call | flops 3221225472 | bytes 9437184 | tf_op jit(solution)/shard_map/expert_weights/pallas_call | solution.py:442
  156.5 1.5 collective-permute-start.12
  158.0 1.5 collective-permute-start.13
  159.5 10.6 %expert_weights.3 = (bf16[528,512]{1,0:T(8,128)(2,1)}, bf16[528,512]{1,0:T(8,128)(2,1)}, bf16[528,512]{1,0:T(8,128)(2,1)}, bf16[528,512]{1,0:T(8,128)(2,1)}) custom-call(s32[2]{0:T(128)} %pad_add_fusion.2.where, s32[1]{0:T(128)} %bitcast.29.expert, bf16[8,4,2,2,16,512]{5,4,3,2,1,0:T(8,128)(2,1)} %copy-done, bf16[8,512,2048]{2,1,0:T(8,128)(2,1)} %refs_1_.3, ...), custom_call_target="tpu_custom_call" | custom-call | flops 3221225472 | bytes 9437184 | tf_op jit(solution)/shard_map/expert_weights/pallas_call | solution.py:442
  172.5 10.5 %all-to-all-done.2.grads.mixed = bf16[32,2,24,512]{3,2,1,0:T(8,128)(2,1)} async-done(((bf16[32,2,24,512]{3,2,1,0:T(8,128)(2,1)}), bf16[32,2,24,512]{3,2,1,0:T(8,128)(2,1)}, u32[]{:S(2)}, u32[]{:S(2)}) %all-to-all-start.2) | async-done | bytes 1572896 | tf_op jit(solution)/shard_map/all_to_all | solution.py:898
  183.1 2.1 collective-permute-done.13.refs_2_
  185.2 12.4 %attention_back_far.1 = (f32[3,256,512]{2,1,0:T(8,128)}, f32[3,256,512]{2,1,0:T(8,128)}, bf16[3,256,512]{2,1,0:T(8,128)(2,1)}, f32[8,512]{1,0:T(8,128)}, bf16[21...) custom-call(s32[2]{0:T(128)} %pad_add_fusion.1.place, bf16[12,256,512]{2,1,0:T(8,128)(2,1)} %tokens.7, ...), custom_call_target="tpu_custom_call" | custom-call | bytes 10747904 | tf_op jit(solution)/shard_map/attention_back_far/pallas_call | solution.py:649
  197.7 2.2 collective-permute-done.16
  199.9 1.2 add_convert_fusion.1
  201.1 2.1 collective-permute-start.17
  204.2 11.4 %attention_back_near.1 = (bf16[3,256,512]{2,1,0:T(8,128)(2,1)}, bf16[2176,128]{1,0:T(8,128)(2,1)}, bf16[2176,128]{1,0:T(8,128)(2,1)}) custom-call(s32[2]{0:T(128)} %pad_add_fusion.1.place, bf16[12,256,512]{2,1,0:T(8,128)(2,1)} %tokens.7, f32[3,256,512]{2,1,0:T(8,128)} %get-tuple-element.127.d_hidden, f32[3,256,512]{2,1,0:T(8,128)} %get-tuple-element.135.partial, ...), custom_call_target="tpu_custom_call" | custom-call | bytes 8388608 | tf_op jit(solution)/shard_map/attention_back_near/pallas_call | solution.py:698
  216.2 1.9 collective-permute-done.18.refs_6_
  220.4 2.1 add_convert_fusion
  222.4 4.4 %all-to-all-start.4 = ((bf16[8,272,128]{2,1,0:T(8,128)(2,1)}), bf16[8,272,128]{2,1,0:T(8,128)(2,1)S(1)}, u32[]{:S(2)}, u32[]{:S(2)}) async-start(bf16[8,272,128]{2,1,0:T(8,128)(2,1)} %bitcast.36), calls=%async_computation.4 | async-start | bytes 1114112 | tf_op jit(solution)/shard_map/all_to_all | solution.py:770
  227.5 6.9 %owned_weights.2 = (f32[8,64,2048]{2,1,0:T(8,128)}, f32[8,256,512]{2,1,0:T(8,128)}, f32[8,16,512]{2,1,0:T(8,128)}) custom-call(s32[7]{0:T(128)} %bitcast.99, bf16[528,512]{1,0:T(8,128)(2,1)} %get-tuple-element.117.refs_0_, bf16[528,512]{1,0:T(8,128)(2,1)} %copy-done.14, bf16[528,512]{1,0:T(8,128)(2,1)} %copy-done.15, ...), custom_call_target="tpu_custom_call" | custom-call | bytes 11354112 | tf_op jit(solution)/shard_map/owned_weights/pallas_call | solution.py:489
  234.5 1.7 collective-permute-done.22.refs_0_
  236.2 3.2 %collective-permute-done.19.refs_2_ = bf16[3,256,512]{2,1,0:T(8,128)(2,1)S(1)} collective-permute-done((bf16[3,256,512]{2,1,0:T(8,128)(2,1)}, bf16[3,256,512]{2,1,0:T(8,128)(2,1)S(1)}, u32[]{:S(2)}, u32[]{:S(2)}) %collective-permute-start.19) | collective-permute-done | bytes 786464 | tf_op jit(solution)/shard_map/ppermute | solution.py:736
  240.0 3.4 %all-to-all-done.4 = bf16[8,272,128]{2,1,0:T(8,128)(2,1)S(1)} async-done(((bf16[8,272,128]{2,1,0:T(8,128)(2,1)}), bf16[8,272,128]{2,1,0:T(8,128)(2,1)S(1)}, u32[]{:S(2)}, u32[]{:S(2)}) %all-to-all-start.4) | async-done | bytes 557088 | tf_op jit(solution)/shard_map/all_to_all | solution.py:770
  244.4 4.3 %all-to-all-start.5 = ((bf16[8,272,128]{2,1,0:T(8,128)(2,1)}), bf16[8,272,128]{2,1,0:T(8,128)(2,1)S(1)}, u32[]{:S(2)}, u32[]{:S(2)}) async-start(bf16[8,272,128]{2,1,0:T(8,128)(2,1)} %broadcast_in_dim.86), calls=%async_computation.5 | async-start | bytes 1114112 | tf_op jit(solution)/shard_map/all_to_all | solution.py:776
  249.3 4.7 %place_blocks.2 = bf16[12,256,512]{2,1,0:T(8,128)(2,1)} custom-call(s32[4]{0:T(128)} %copy-done.24, bf16[3,256,512]{2,1,0:T(8,128)(2,1)} %get-tuple-element.144.refs_0_, bf16[3,256,512]{2,1,0:T(8,128)(2,1)} %collective-permute-done.20.refs_1_, bf16[3,256,512]{2,1,0:T(8,128)(2,1)} %copy-done.9, bf16[3,256,512]{2,1,0:T(8,128)(2,1)} %collective-permute-done.25.refs_3_), custom_call_target="tpu_custom_call" | custom-call | bytes 6291456 | tf_op jit(solution)/shard_map/place_blocks/pallas_call | solution.py:809
  254.0 2.7 owned_weights.3
  256.7 2.8 %collective-permute-done.23.refs_2_ = bf16[3,256,512]{2,1,0:T(8,128)(2,1)} collective-permute-done((bf16[3,256,512]{2,1,0:T(8,128)(2,1)S(1)}, bf16[3,256,512]{2,1,0:T(8,128)(2,1)}, u32[]{:S(2)}, u32[]{:S(2)}) %collective-permute-start.23) | collective-permute-done | bytes 786464 | tf_op jit(solution)/shard_map/ppermute | solution.py:736
  259.4 0.9 slice.76
  263.4 4.7 %place_blocks.3 = bf16[12,256,512]{2,1,0:T(8,128)(2,1)} custom-call(s32[4]{0:T(128)} %copy-done.24, bf16[3,256,512]{2,1,0:T(8,128)(2,1)} %get-tuple-element.152.refs_0_, bf16[3,256,512]{2,1,0:T(8,128)(2,1)} %copy-done.8, bf16[3,256,512]{2,1,0:T(8,128)(2,1)} %collective-permute-done.23.refs_2_, bf16[3,256,512]{2,1,0:T(8,128)(2,1)} %copy-done.10), custom_call_target="tpu_custom_call" | custom-call | bytes 6291456 | tf_op jit(solution)/shard_map/place_blocks/pallas_call | solution.py:809
  (156 shorter events, 29.6 us)
Async XLA Ops:
  0.6 15.3 %copy-start.23 = (bf16[512,8]{0,1:T(8,128)(2,1)S(1)}, bf16[512,8]{0,1:T(8,128)(2,1)}, u32[]{:S(2)}) copy-start(bf16[512,8]{0,1:T(8,128)(2,1)} %param.25) | copy-start | bytes 24580
  0.7 15.8 %copy-start.25 = (s32[8]{0:T(128)S(1)}, s32[8]{0:T(128)}, u32[]{:S(2)}) copy-start(s32[8]{0:T(128)} %param.17) | copy-start | bytes 100
  2.7 2.2 collective-permute-start
  4.9 13.6 %copy-start.19 = (bf16[512,512]{1,0:T(8,128)(2,1)}, bf16[512,512]{1,0:T(8,128)(2,1)S(1)}, u32[]{:S(2)}) copy-start(bf16[512,512]{1,0:T(8,128)(2,1)S(1)} %collective-permute-done.refs_1_) | copy-start | bytes 1572868
  7.2 32.4 %all-to-all-start.1 = ((bf16[8,12,8,512]{3,2,1,0:T(8,128)(2,1)}), bf16[8,12,8,512]{3,2,1,0:T(8,128)(2,1)S(1)}, u32[]{:S(2)}, u32[]{:S(2)}) async-start(bf16[8,12,8,512]{3,2,1,0:T(8,128)(2,1)} %copy_bitcast_fusion), calls=%async_computation.1 | async-start | bytes 1572864 | tf_op jit(solution)/shard_map/all_to_all | solution.py:904
  14.4 13.8 %collective-permute-start.1 = (bf16[512,512]{1,0:T(8,128)(2,1)S(1)}, bf16[512,512]{1,0:T(8,128)(2,1)S(1)}, u32[]{:S(2)}, u32[]{:S(2)}) collective-permute-start(bf16[512,512]{1,0:T(8,128)(2,1)S(1)} %copy-done.1), channel_id=1, source_target_pairs={{2,0},{3,1},{0,2},{1,3},{6,4},{7,5},{4,6},{5,7},{10,8},{11,9},{8,1... | collective-permute-start | bytes 1572872 | tf_op jit(solution)/shard_map/ppermute | solution.py:736
  15.9 29.6 %collective-permute-start.4 = (bf16[8,512]{1,0:T(8,128)(2,1)S(1)}, bf16[8,512]{1,0:T(8,128)(2,1)S(1)}, u32[]{:S(2)}, u32[]{:S(2)}) collective-permute-start(bf16[8,512]{1,0:T(8,128)(2,1)S(1)} %bitcast.93), channel_id=1, source_target_pairs={{2,0},{3,1},{0,2},{1,3},{6,4},{7,5},{4,6},{5,7},{10,8},{11,9},{8,1... | collective-permute-start | bytes 24584 | tf_op jit(solution)/shard_map/ppermute | solution.py:736
  16.5 31.6 %collective-permute-start.3 = (bf16[8,512]{1,0:T(8,128)(2,1)S(1)}, bf16[8,512]{1,0:T(8,128)(2,1)S(1)}, u32[]{:S(2)}, u32[]{:S(2)}) collective-permute-start(bf16[8,512]{1,0:T(8,128)(2,1)S(1)} %bitcast.94), channel_id=1, source_target_pairs={{0,1},{1,0},{2,3},{3,2},{4,5},{5,4},{6,7},{7,6},{8,9},{9,8},{10,11... | collective-permute-start | bytes 24584 | tf_op jit(solution)/shard_map/ppermute | solution.py:731
  28.2 1.9 collective-permute-start.2
  30.9 14.4 %copy-start.26 = (s32[64]{0:T(128)S(1)}, s32[64]{0:T(128)}, u32[]{:S(2)}) copy-start(s32[64]{0:T(128)} %param.18) | copy-start | bytes 772
  39.6 26.3 %copy-start.11 = (bf16[8,12,8,512]{3,2,1,0:T(8,128)(2,1)}, bf16[8,12,8,512]{3,2,1,0:T(8,128)(2,1)S(1)}, u32[]{:S(2)}) copy-start(bf16[8,12,8,512]{3,2,1,0:T(8,128)(2,1)S(1)} %all-to-all-done.1) | copy-start | bytes 2359300
  39.6 26.3 %all-to-all-start = ((bf16[32,3,8,512]{3,2,1,0:T(8,128)(2,1)}), bf16[32,3,8,512]{3,2,1,0:T(8,128)(2,1)S(1)}, u32[]{:S(2)}, u32[]{:S(2)}) async-start(bf16[32,3,8,512]{3,2,1,0:T(8,128)(2,1)} %get-tuple-element.98), calls=%async_computation | async-start | bytes 1572864 | tf_op jit(solution)/shard_map/all_to_all | solution.py:891
  45.6 2.5 collective-permute-start.5
  72.2 1.9 collective-permute-start.6
  72.2 9.3 %collective-permute-start.7 = (bf16[8,2,16,512]{3,2,1,0:T(8,128)(2,1)}, bf16[8,2,16,512]{3,2,1,0:T(8,128)(2,1)S(1)}, u32[]{:S(2)}, u32[]{:S(2)}) collective-permute-start(bf16[8,2,16,512]{3,2,1,0:T(8,128)(2,1)} %get-tuple-element.105), channel_id=1, source_target_pairs={{0,2},{1,3},{2,0},{3,1},{4,6},{5,7},{6,4},{7,5},{8,10},{9,11},{10,... | collective-permute-start | bytes 786440 | tf_op jit(solution)/shard_map/ppermute | solution.py:783
  73.8 12.5 %collective-permute-start.8 = (bf16[8,2,16,512]{3,2,1,0:T(8,128)(2,1)}, bf16[8,2,16,512]{3,2,1,0:T(8,128)(2,1)S(1)}, u32[]{:S(2)}, u32[]{:S(2)}) collective-permute-start(bf16[8,2,16,512]{3,2,1,0:T(8,128)(2,1)} %get-tuple-element.106), channel_id=1, source_target_pairs={{0,3},{1,2},{2,1},{3,0},{4,7},{5,6},{6,5},{7,4},{8,11},{9,10},{10,... | collective-permute-start | bytes 786440 | tf_op jit(solution)/shard_map/ppermute | solution.py:783
  74.0 14.8 %copy-start.4 = (bf16[8,2,16,512]{3,2,1,0:T(8,128)(2,1)}, bf16[8,2,16,512]{3,2,1,0:T(8,128)(2,1)S(1)}, u32[]{:S(2)}) copy-start(bf16[8,2,16,512]{3,2,1,0:T(8,128)(2,1)S(1)} %collective-permute-done.6.refs_1_) | copy-start | bytes 786436
  88.8 52.6 %all-to-all-start.3 = ((bf16[8,4,2,2,16,512]{5,4,3,2,1,0:T(8,128)(2,1)}), bf16[8,4,2,2,16,512]{5,4,3,2,1,0:T(8,128)(2,1)S(1)}, u32[]{:S(2)}, u32[]{:S(2)}) async-start(bf16[8,4,2,2,16,512]{5,4,3,2,1,0:T(8,128)(2,1)} %maximum_maximum_fusion), calls=%async_computation.3 | async-start | bytes 4194304 | tf_op jit(solution)/shard_map/all_to_all | solution.py:946
  114.7 9.4 %collective-permute-start.10 = (bf16[8,2,16,512]{3,2,1,0:T(8,128)(2,1)}, bf16[8,2,16,512]{3,2,1,0:T(8,128)(2,1)S(1)}, u32[]{:S(2)}, u32[]{:S(2)}) collective-permute-start(bf16[8,2,16,512]{3,2,1,0:T(8,128)(2,1)} %get-tuple-element.113), channel_id=1, source_target_pairs={{2,0},{3,1},{0,2},{1,3},{6,4},{7,5},{4,6},{5,7},{10,8},{11,9},{8,1... | collective-permute-start | bytes 786440 | tf_op jit(solution)/shard_map/ppermute | solution.py:789
  116.2 12.1 %collective-permute-start.11 = (bf16[8,2,16,512]{3,2,1,0:T(8,128)(2,1)}, bf16[8,2,16,512]{3,2,1,0:T(8,128)(2,1)S(1)}, u32[]{:S(2)}, u32[]{:S(2)}) collective-permute-start(bf16[8,2,16,512]{3,2,1,0:T(8,128)(2,1)} %get-tuple-element.114), channel_id=1, source_target_pairs={{3,0},{2,1},{1,2},{0,3},{7,4},{6,5},{5,6},{4,7},{11,8},{10,9},{9,1... | collective-permute-start | bytes 786440 | tf_op jit(solution)/shard_map/ppermute | solution.py:789
  116.3 12.0 %collective-permute-start.9 = (bf16[8,2,16,512]{3,2,1,0:T(8,128)(2,1)}, bf16[8,2,16,512]{3,2,1,0:T(8,128)(2,1)S(1)}, u32[]{:S(2)}, u32[]{:S(2)}) collective-permute-start(bf16[8,2,16,512]{3,2,1,0:T(8,128)(2,1)} %get-tuple-element.112), channel_id=1, source_target_pairs={{1,0},{0,1},{3,2},{2,3},{5,4},{4,5},{7,6},{6,7},{9,8},{8,9},{11,10... | collective-permute-start | bytes 786440 | tf_op jit(solution)/shard_map/ppermute | solution.py:789
  141.4 41.7 %all-to-all-start.2 = ((bf16[32,2,24,512]{3,2,1,0:T(8,128)(2,1)}), bf16[32,2,24,512]{3,2,1,0:T(8,128)(2,1)}, u32[]{:S(2)}, u32[]{:S(2)}) async-start(bf16[32,2,24,512]{3,2,1,0:T(8,128)(2,1)} %get-tuple-element.115), calls=%async_computation.2 | async-start | bytes 3145728 | tf_op jit(solution)/shard_map/all_to_all | solution.py:898
  156.5 26.6 %collective-permute-start.12 = (bf16[528,512]{1,0:T(8,128)(2,1)}, bf16[528,512]{1,0:T(8,128)(2,1)S(1)}, u32[]{:S(2)}, u32[]{:S(2)}) collective-permute-start(bf16[528,512]{1,0:T(8,128)(2,1)} %get-tuple-element.118), channel_id=1, source_target_pairs={{0,4},{4,0},{8,12},{12,8},{16,20},{20,16},{24,28},{28,24},{1,5},{5... | collective-permute-start | bytes 1622024 | tf_op jit(solution)/shard_map/ppermute | solution.py:794
  158.0 27.2 %collective-permute-start.13 = (bf16[528,512]{1,0:T(8,128)(2,1)}, bf16[528,512]{1,0:T(8,128)(2,1)S(1)}, u32[]{:S(2)}, u32[]{:S(2)}) collective-permute-start(bf16[528,512]{1,0:T(8,128)(2,1)} %get-tuple-element.119), channel_id=1, source_target_pairs={{0,8},{4,12},{8,0},{12,4},{16,24},{20,28},{24,16},{28,20},{1,9},{5... | collective-permute-start | bytes 1622024 | tf_op jit(solution)/shard_map/ppermute | solution.py:794
  170.1 27.5 %collective-permute-start.14 = (bf16[528,512]{1,0:T(8,128)(2,1)}, bf16[528,512]{1,0:T(8,128)(2,1)S(1)}, u32[]{:S(2)}, u32[]{:S(2)}) collective-permute-start(bf16[528,512]{1,0:T(8,128)(2,1)} %get-tuple-element.131), channel_id=1, source_target_pairs={{0,4},{4,0},{8,12},{12,8},{16,20},{20,16},{24,28},{28,24},{1,5},{5... | collective-permute-start | bytes 1622024 | tf_op jit(solution)/shard_map/ppermute | solution.py:794
  170.7 26.9 %collective-permute-start.15 = (bf16[528,512]{1,0:T(8,128)(2,1)}, bf16[528,512]{1,0:T(8,128)(2,1)S(1)}, u32[]{:S(2)}, u32[]{:S(2)}) collective-permute-start(bf16[528,512]{1,0:T(8,128)(2,1)} %get-tuple-element.132), channel_id=1, source_target_pairs={{0,8},{4,12},{8,0},{12,4},{16,24},{20,28},{24,16},{28,20},{1,9},{5... | collective-permute-start | bytes 1622024 | tf_op jit(solution)/shard_map/ppermute | solution.py:794
  183.1 14.5 %copy-start.14 = (bf16[528,512]{1,0:T(8,128)(2,1)}, bf16[528,512]{1,0:T(8,128)(2,1)S(1)}, u32[]{:S(2)}) copy-start(bf16[528,512]{1,0:T(8,128)(2,1)S(1)} %collective-permute-done.12.refs_1_) | copy-start | bytes 1622020
  185.2 12.4 %copy-start.15 = (bf16[528,512]{1,0:T(8,128)(2,1)}, bf16[528,512]{1,0:T(8,128)(2,1)S(1)}, u32[]{:S(2)}) copy-start(bf16[528,512]{1,0:T(8,128)(2,1)S(1)} %collective-permute-done.13.refs_2_) | copy-start | bytes 1622020
  185.2 18.0 %copy-start.27 = (bf16[528,512]{1,0:T(8,128)(2,1)S(1)}, bf16[528,512]{1,0:T(8,128)(2,1)}, u32[]{:S(2)}) copy-start(bf16[528,512]{1,0:T(8,128)(2,1)} %get-tuple-element.143) | copy-start | bytes 1622020
  197.6 17.9 %copy-start.16 = (bf16[528,512]{1,0:T(8,128)(2,1)}, bf16[528,512]{1,0:T(8,128)(2,1)S(1)}, u32[]{:S(2)}) copy-start(bf16[528,512]{1,0:T(8,128)(2,1)S(1)} %collective-permute-done.14.refs_4_) | copy-start | bytes 1622020
  197.7 17.9 %copy-start.17 = (bf16[528,512]{1,0:T(8,128)(2,1)}, bf16[528,512]{1,0:T(8,128)(2,1)S(1)}, u32[]{:S(2)}) copy-start(bf16[528,512]{1,0:T(8,128)(2,1)S(1)} %collective-permute-done.15.refs_5_) | copy-start | bytes 1622020
  197.7 2.2 collective-permute-start.16
  201.1 15.1 %collective-permute-start.17 = (bf16[2176,128]{1,0:T(8,128)(2,1)S(1)}, bf16[2176,128]{1,0:T(8,128)(2,1)S(1)}, u32[]{:S(2)}, u32[]{:S(2)}) collective-permute-start(bf16[2176,128]{1,0:T(8,128)(2,1)S(1)} %add_convert_fusion.1), channel_id=1, source_target_pairs={{0,2},{1,3},{2,0},{3,1},{4,6},{5,7},{6,4},{7,5},{8,10},{9,11},{10,... | collective-permute-start | bytes 1671176 | tf_op jit(solution)/shard_map/ppermute | solution.py:741
  203.2 14.9 %collective-permute-start.18 = (bf16[528,512]{1,0:T(8,128)(2,1)S(1)}, bf16[528,512]{1,0:T(8,128)(2,1)S(1)}, u32[]{:S(2)}, u32[]{:S(2)}) collective-permute-start(bf16[528,512]{1,0:T(8,128)(2,1)S(1)} %copy-done.27), channel_id=1, source_target_pairs={{0,12},{4,8},{8,4},{12,0},{16,28},{20,24},{24,20},{28,16},{1,13},{... | collective-permute-start | bytes 1622024 | tf_op jit(solution)/shard_map/ppermute | solution.py:794
  204.2 15.0 %copy-start.7 = (bf16[3,256,512]{2,1,0:T(8,128)(2,1)S(1)}, bf16[3,256,512]{2,1,0:T(8,128)(2,1)}, u32[]{:S(2)}) copy-start(bf16[3,256,512]{2,1,0:T(8,128)(2,1)} %get-tuple-element.152.refs_0_) | copy-start | bytes 2359300
  218.2 2.2 collective-permute-start.24
  218.3 17.9 %collective-permute-start.22 = (bf16[528,512]{1,0:T(8,128)(2,1)}, bf16[528,512]{1,0:T(8,128)(2,1)S(1)}, u32[]{:S(2)}, u32[]{:S(2)}) collective-permute-start(bf16[528,512]{1,0:T(8,128)(2,1)} %get-tuple-element.151), channel_id=1, source_target_pairs={{0,12},{4,8},{8,4},{12,0},{16,28},{20,24},{24,20},{28,16},{1,13},{... | collective-permute-start | bytes 1622024 | tf_op jit(solution)/shard_map/ppermute | solution.py:794
  219.2 17.0 %collective-permute-start.21 = (bf16[3,256,512]{2,1,0:T(8,128)(2,1)S(1)}, bf16[3,256,512]{2,1,0:T(8,128)(2,1)S(1)}, u32[]{:S(2)}, u32[]{:S(2)}) collective-permute-start(bf16[3,256,512]{2,1,0:T(8,128)(2,1)S(1)} %copy-done.7), channel_id=1, source_target_pairs={{0,1},{1,0},{2,3},{3,2},{4,5},{5,4},{6,7},{7,6},{8,9},{9,8},{10,11... | collective-permute-start | bytes 2359304 | tf_op jit(solution)/shard_map/ppermute | solution.py:731
  219.4 19.9 %collective-permute-start.19 = (bf16[3,256,512]{2,1,0:T(8,128)(2,1)}, bf16[3,256,512]{2,1,0:T(8,128)(2,1)S(1)}, u32[]{:S(2)}, u32[]{:S(2)}) collective-permute-start(bf16[3,256,512]{2,1,0:T(8,128)(2,1)} %get-tuple-element.144.refs_0_), channel_id=1, source_target_pairs={{2,0},{3,1},{0,2},{1,3},{6,4},{7,5},{4,6},{5,7},{10,8},{11,9},{8,1... | collective-permute-start | bytes 2359304 | tf_op jit(solution)/shard_map/ppermute | solution.py:736
  220.0 19.3 %collective-permute-start.20 = (bf16[3,256,512]{2,1,0:T(8,128)(2,1)}, bf16[3,256,512]{2,1,0:T(8,128)(2,1)}, u32[]{:S(2)}, u32[]{:S(2)}) collective-permute-start(bf16[3,256,512]{2,1,0:T(8,128)(2,1)} %get-tuple-element.144.refs_0_), channel_id=1, source_target_pairs={{0,1},{1,0},{2,3},{3,2},{4,5},{5,4},{6,7},{7,6},{8,9},{9,8},{10,11... | collective-permute-start | bytes 2359304 | tf_op jit(solution)/shard_map/ppermute | solution.py:731
  222.4 21.0 %all-to-all-start.4 = ((bf16[8,272,128]{2,1,0:T(8,128)(2,1)}), bf16[8,272,128]{2,1,0:T(8,128)(2,1)S(1)}, u32[]{:S(2)}, u32[]{:S(2)}) async-start(bf16[8,272,128]{2,1,0:T(8,128)(2,1)} %bitcast.36), calls=%async_computation.4 | async-start | bytes 1114112 | tf_op jit(solution)/shard_map/all_to_all | solution.py:770
  236.1 17.8 %copy-start.13 = (bf16[528,512]{1,0:T(8,128)(2,1)}, bf16[528,512]{1,0:T(8,128)(2,1)S(1)}, u32[]{:S(2)}) copy-start(bf16[528,512]{1,0:T(8,128)(2,1)S(1)} %collective-permute-done.22.refs_0_) | copy-start | bytes 1622020
  236.1 17.8 %copy-start.8 = (bf16[3,256,512]{2,1,0:T(8,128)(2,1)}, bf16[3,256,512]{2,1,0:T(8,128)(2,1)S(1)}, u32[]{:S(2)}) copy-start(bf16[3,256,512]{2,1,0:T(8,128)(2,1)S(1)} %collective-permute-done.21.refs_1_) | copy-start | bytes 2359300
  239.4 4.1 %collective-permute-start.25 = (bf16[3,256,512]{2,1,0:T(8,128)(2,1)S(1)}, bf16[3,256,512]{2,1,0:T(8,128)(2,1)}, u32[]{:S(2)}, u32[]{:S(2)}) collective-permute-start(bf16[3,256,512]{2,1,0:T(8,128)(2,1)S(1)} %collective-permute-done.19.refs_2_), channel_id=1, source_target_pairs={{0,1},{1,0},{2,3},{3,2},{4,5},{5,4},{6,7},{7,6},{8,9},{9,8},{10,11... | collective-permute-start | bytes 2359304 | tf_op jit(solution)/shard_map/ppermute | solution.py:731
  239.4 20.1 %collective-permute-start.23 = (bf16[3,256,512]{2,1,0:T(8,128)(2,1)S(1)}, bf16[3,256,512]{2,1,0:T(8,128)(2,1)}, u32[]{:S(2)}, u32[]{:S(2)}) collective-permute-start(bf16[3,256,512]{2,1,0:T(8,128)(2,1)S(1)} %copy-done.7), channel_id=1, source_target_pairs={{2,0},{3,1},{0,2},{1,3},{6,4},{7,5},{4,6},{5,7},{10,8},{11,9},{8,1... | collective-permute-start | bytes 2359304 | tf_op jit(solution)/shard_map/ppermute | solution.py:736
  244.4 23.7 %all-to-all-start.5 = ((bf16[8,272,128]{2,1,0:T(8,128)(2,1)}), bf16[8,272,128]{2,1,0:T(8,128)(2,1)S(1)}, u32[]{:S(2)}, u32[]{:S(2)}) async-start(bf16[8,272,128]{2,1,0:T(8,128)(2,1)} %broadcast_in_dim.86), calls=%async_computation.5 | async-start | bytes 1114112 | tf_op jit(solution)/shard_map/all_to_all | solution.py:776
  259.4 3.1 %collective-permute-start.26 = (bf16[3,256,512]{2,1,0:T(8,128)(2,1)}, bf16[3,256,512]{2,1,0:T(8,128)(2,1)S(1)}, u32[]{:S(2)}, u32[]{:S(2)}) collective-permute-start(bf16[3,256,512]{2,1,0:T(8,128)(2,1)} %collective-permute-done.23.refs_2_), channel_id=1, source_target_pairs={{0,1},{1,0},{2,3},{3,2},{4,5},{5,4},{6,7},{7,6},{8,9},{9,8},{10,11... | collective-permute-start | bytes 2359304 | tf_op jit(solution)/shard_map/ppermute | solution.py:731
  268.1 3.6 %collective-permute-start.27 = (bf16[16,128]{1,0:T(8,128)(2,1)S(1)}, bf16[16,128]{1,0:T(8,128)(2,1)S(1)}, u32[]{:S(2)}, u32[]{:S(2)}) collective-permute-start(bf16[16,128]{1,0:T(8,128)(2,1)S(1)} %slice.87), channel_id=1, source_target_pairs={{0,2},{1,3},{2,0},{3,1},{4,6},{5,7},{6,4},{7,5},{8,10},{9,11},{10,... | collective-permute-start | bytes 12296 | tf_op jit(solution)/shard_map/ppermute | solution.py:741
  (17 other events, 81.6 us)

commit v7 on v6

--- a/solution.py
+++ b/solution.py
@@ -897,8 +897,7 @@
         x = x.reshape(spread, 2, slots * part, model_width)
         return lax.all_to_all(x, BOTH, split_axis=0, concat_axis=0, tiled=True)
 
-    cots, *packs = lax.optimization_barrier((cotangent, *packs))
-    cots = jnp.pad(cots, ((0, slots * narrow - slot_count), (0, 0), (0, 0)))
+    cots = jnp.pad(cotangent, ((0, slots * narrow - slot_count), (0, 0), (0, 0)))
     cots = cots.reshape(slots * narrow, wide, narrow, part, model_width)
     cots = lax.dynamic_index_in_dim(cots, narrow_index, axis=2, keepdims=False).transpose(1, 0, 2, 3)
     cots = lax.all_to_all(cots, "wide", split_axis=0, concat_axis=0, tiled=True)
@@ -1028,8 +1027,9 @@
     order = jnp.concatenate([order[:, :-1].reshape(-1), order[:, -1]])
     pieces = [piece for x in expert_grads for piece in x[:-1]] + [x[-1] for x in expert_grads]
     owned = owned_weights(pieces[:-1], order[:-1], units * held, w_in.shape[2], wide)
-    mixed_part, far_tokens, swapped, owned, pieces[-1] = lax.optimization_barrier(
-        (mixed_part, far_tokens, swapped, owned, pieces[-1])
+    mixed_near = place_blocks([mixed_part, swapped[1]], relative[:2], narrow)
+    mixed_part, far_tokens, swapped, owned, pieces[-1], mixed_near = lax.optimization_barrier(
+        (mixed_part, far_tokens, swapped, owned, pieces[-1], mixed_near)
     )
     far_mixed = [from_chip(mixed_part, k) for k in range(1, narrow // 2)]
     far_tokens = [y for x in far_tokens for y in (x, swap_core(x))]
@@ -1038,7 +1038,7 @@
     g_w_in, g_w_out, bias = owned_weights(after(pieces[-1:], part_sums), order[-1:], units * held, w_in.shape[2], wide, owned)
     far_mixed, d_tokens, bias = lax.optimization_barrier((far_mixed, d_tokens, bias))
     far_mixed = [y for x in far_mixed for y in (x, swap_core(x))]
-    mixed_part = place_blocks([mixed_part, swapped[1]] + far_mixed, relative, narrow)
+    mixed_part = place_blocks(far_mixed, relative[2:], narrow, mixed_near)
     d_tokens, mixed_part = d_tokens[:slot_count], mixed_part[:slot_count]
     weights = from_parts(part_sums)
     gains = weights[end : end + 16].astype(BF16)

time: 274 us -> 272 us (level)
  waiting for transfers between devices: 79.3 us -> 73.7 us
    pallas_call x2 -> x3, Pallas kernels: 9.35 us -> 11.2 us  [place_blocks(): pl.pallas_call(functools.partial(place_kernel, count), grid_spec=pltpu.Pr...]
    unnamed x66 -> x62, local copies, waits for them, and re-layouts: 6.34 us -> 7.1 us
  transfers between devices with their start and end apart: 34 -> 34, of which waited for: 20 -> 17; matrix products, arithmetic and copies ran while one was open for 7% -> 8% of each run, Pallas kernels for 40% -> 41%
where the time goes in v7:
time: 272 us; the launch traced here: 271 us
  Pallas kernels  118 us (43%)
  waiting for transfers between devices  73.7 us (27%)
  starting transfers between devices  46.4 us (17%)
  local copies, waits for them, and re-layouts  20.2 us (7%)
  other arithmetic  11.8 us (4%)
    pallas_call x2, Pallas kernels, expert_weights(): pl.pallas_call(lambda where, expert, *refs: weight_kernel(units, where, *...  21.3 us
    pallas_call x1, Pallas kernels, experts_at_positions(): pl.pallas_call(functools.partial(expert_kernel, sources), grid=(experts,)...  20.8 us
    all_to_all x1, waiting for transfers between devices, to_positions(): x = lax.all_to_all(x, BOTH, split_axis=0, concat_axis=0, tiled=True)  16.5 us
    pallas_call x1, Pallas kernels, attention_back_far(): pl.pallas_call(functools.partial(back_far_kernel, blocks, inner // count)...  12.4 us
    ppermute x3, waiting for transfers between devices, to_relative(): lax.ppermute(x, 'narrow', [(n, (n + 2 * k) % narrow ^ other) for n in ran...  12.3 us
    ppermute x3, waiting for transfers between devices, from_relative(): lax.ppermute(x, 'narrow', [((n + 2 * k) % narrow ^ other, n) for n in ran...  12.1 us
    pallas_call x1, Pallas kernels, attention_back_near(): pl.pallas_call(functools.partial(back_near_kernel, blocks, inner // count...  11.4 us
    pallas_call x3, Pallas kernels, place_blocks(): pl.pallas_call(functools.partial(place_kernel, count), grid_spec=pltpu.Pr...  11.2 us
  transfers between devices with their start and end apart: 34, of which 17 were waited for; matrix products, arithmetic and copies ran while one was open for 8% of the time, Pallas kernels for 41%

profile of v7, /device:TPU:0, one launch (start us, length us, event | category | flops | bytes accessed | tf_op | source)
XLA Modules:
  0.0 270.8 jit_solution(16552354809997854696)
XLA Ops:
  0.7 2.1 copy_bitcast_fusion
  2.8 7.3 %all-to-all-start.1 = ((bf16[8,12,8,512]{3,2,1,0:T(8,128)(2,1)}), bf16[8,12,8,512]{3,2,1,0:T(8,128)(2,1)S(1)}, u32[]{:S(2)}, u32[]{:S(2)}) async-start(bf16[8,12,8,512]{3,2,1,0:T(8,128)(2,1)} %copy_bitcast_fusion), calls=%async_computation.1 | async-start | bytes 1572864 | tf_op jit(solution)/shard_map/all_to_all | solution.py:903
  10.1 2.0 pack_weights.1.refs_0_
  12.0 1.5 collective-permute-start.1
  15.1 1.2 pad_add_fusion.1.place
  17.2 7.9 %attention_near.1 = (f32[3,256,512]{2,1,0:T(8,128)}, bf16[3,256,768]{2,1,0:T(8,128)(2,1)}, bf16[3,256,256]{2,1,0:T(8,128)(2,1)}) custom-call(s32[2]{0:T(128)} %pad_add_fusion.1.place, bf16[12,256,512]{2,1,0:T(8,128)(2,1)} %tokens.7, bf16[512,512]{1,0:T(8,128)(2,1)} %pack_weights.1.refs_0_, bf16[512,512]{1,0:T(8,128)(2,1)} %copy-done.17, f32[1,512]{1,0:T(1,128)} %bitcast.84), custom_call_target="tpu_custom_call" | custom-call | flops 1207959552 | bytes 4980736 | tf_op jit(solution)/shard_map/attention_near/pallas_call | solution.py:123
  25.1 1.6 collective-permute-done.1.refs_0_
  29.4 8.7 %attention_far.1 = (bf16[32,3,8,512]{3,2,1,0:T(8,128)(2,1)}, f32[3,256,512]{2,1,0:T(8,128)}, bf16[3,256,768]{2,1,0:T(8,128)(2,1)}, bf16[3,256,256]{2,1,0:T(8,128)(2,1)}) custom-call(s32[2]{0:T(128)} %pad_add_fusion.1.place, bf16[12,256,512]{2,1,0:T(8,128)(2,1)} %tokens.7, f32[3,256,512]{2,1,0:T(8,128)} %get-tuple-element.91.partial, ...), custom_call_target="tpu_custom_call" | custom-call | flops 1207959552 | bytes 7340032 | tf_op jit(solution)/shard_map/attention_far/pallas_call | solution.py:158
  38.1 6.0 %all-to-all-start = ((bf16[32,3,8,512]{3,2,1,0:T(8,128)(2,1)}), bf16[32,3,8,512]{3,2,1,0:T(8,128)(2,1)S(1)}, u32[]{:S(2)}, u32[]{:S(2)}) async-start(bf16[32,3,8,512]{3,2,1,0:T(8,128)(2,1)} %get-tuple-element.93), calls=%async_computation | async-start | bytes 1572864 | tf_op jit(solution)/shard_map/all_to_all | solution.py:891
  46.0 0.9 select_n.87.row_code
  48.2 16.5 %all-to-all-done = bf16[32,3,8,512]{3,2,1,0:T(8,128)(2,1)S(1)} async-done(((bf16[32,3,8,512]{3,2,1,0:T(8,128)(2,1)}), bf16[32,3,8,512]{3,2,1,0:T(8,128)(2,1)S(1)}, u32[]{:S(2)}, u32[]{:S(2)}) %all-to-all-start) | async-done | bytes 786464 | tf_op jit(solution)/shard_map/all_to_all | solution.py:891
  65.6 5.4 %mix_forward.1 = (f32[768,32]{1,0:T(8,128)}, bf16[768,512]{1,0:T(8,128)(2,1)}, bf16[8,2,16,512]{3,2,1,0:T(8,128)(2,1)}, bf16[8,2,16,512]{3,2,1,0:T(8,128)(2,1)},...) custom-call(s32[4]{0:T(128)} %copy-done.22, bf16[768,512]{1,0:T(8,128)(2,1)} %bitcast.76, ...), custom_call_target="tpu_custom_call" | custom-call | flops 805306368 | bytes 4718592 | tf_op jit(solution)/shard_map/mix_forward/pallas_call | solution.py:258
  71.0 1.6 collective-permute-start.7
  72.8 7.5 %collective-permute-done.7.refs_2_ = bf16[8,2,16,512]{3,2,1,0:T(8,128)(2,1)S(1)} collective-permute-done((bf16[8,2,16,512]{3,2,1,0:T(8,128)(2,1)}, bf16[8,2,16,512]{3,2,1,0:T(8,128)(2,1)S(1)}, u32[]{:S(2)}, u32[]{:S(2)}) %collective-permute-start.7) | collective-permute-done | bytes 262176 | tf_op jit(solution)/shard_map/ppermute | solution.py:783
  80.3 4.8 %collective-permute-done.8.refs_3_ = bf16[8,2,16,512]{3,2,1,0:T(8,128)(2,1)S(1)} collective-permute-done((bf16[8,2,16,512]{3,2,1,0:T(8,128)(2,1)}, bf16[8,2,16,512]{3,2,1,0:T(8,128)(2,1)S(1)}, u32[]{:S(2)}, u32[]{:S(2)}) %collective-permute-start.8) | collective-permute-done | bytes 262176 | tf_op jit(solution)/shard_map/ppermute | solution.py:783
  85.1 2.5 maximum_maximum_fusion
  87.6 3.8 %all-to-all-start.3 = ((bf16[8,4,2,2,16,512]{5,4,3,2,1,0:T(8,128)(2,1)}), bf16[8,4,2,2,16,512]{5,4,3,2,1,0:T(8,128)(2,1)S(1)}, u32[]{:S(2)}, u32[]{:S(2)}) async-start(bf16[8,4,2,2,16,512]{5,4,3,2,1,0:T(8,128)(2,1)} %maximum_maximum_fusion), calls=%async_computation.3 | async-start | bytes 4194304 | tf_op jit(solution)/shard_map/all_to_all | solution.py:945
  92.7 20.8 %experts.1 = (bf16[8,2,16,512]{3,2,1,0:T(8,128)(2,1)}, bf16[8,2,16,512]{3,2,1,0:T(8,128)(2,1)}, bf16[8,2,16,512]{3,2,1,0:T(8,128)(2,1)}, bf16[8,2,16,512]{3,2,1,0:T(8,128)(2,1)}) custom-call(bf16[8,2,16,512]{3,2,1,0:T(8,128)(2,1)} %get-tuple-element.101.refs_0_, bf16[8,2,16,512]{3,2,1,0:T(8,128)(2,1)} %copy-done.3, bf16[8,2,16,512]{3,2,1,0:T(8,128)(2,1)} %copy-done.4, ...), custom_call_target="tpu_custom_call" | custom-call | flops 4294967296 | bytes 35651584 | tf_op jit(solution)/shard_map/experts/pallas_call | solution.py:366
  113.8 1.5 collective-permute-start.10
  115.4 7.7 %collective-permute-done.10.refs_2_ = bf16[8,2,16,512]{3,2,1,0:T(8,128)(2,1)S(1)} collective-permute-done((bf16[8,2,16,512]{3,2,1,0:T(8,128)(2,1)}, bf16[8,2,16,512]{3,2,1,0:T(8,128)(2,1)S(1)}, u32[]{:S(2)}, u32[]{:S(2)}) %collective-permute-start.10) | collective-permute-done | bytes 262176 | tf_op jit(solution)/shard_map/ppermute | solution.py:789
  123.1 4.4 %collective-permute-done.11.refs_3_ = bf16[8,2,16,512]{3,2,1,0:T(8,128)(2,1)S(1)} collective-permute-done((bf16[8,2,16,512]{3,2,1,0:T(8,128)(2,1)}, bf16[8,2,16,512]{3,2,1,0:T(8,128)(2,1)S(1)}, u32[]{:S(2)}, u32[]{:S(2)}) %collective-permute-start.11) | collective-permute-done | bytes 262176 | tf_op jit(solution)/shard_map/ppermute | solution.py:789
  128.2 6.9 %mix_backward.1 = (bf16[32,2,24,512]{3,2,1,0:T(8,128)(2,1)}, f32[32,512]{1,0:T(8,128)}) custom-call(s32[4]{0:T(128)} %copy-done.22, bf16[768,512]{1,0:T(8,128)(2,1)} %get-tuple-element.95.spread, bf16[768,512]{1,0:T(8,128)(2,1)} %bitcast.77, bf16[768,512]{1,0:T(8,128)(2,1)} %bitcast.75, f32[768,32]{1,0:T(8,128)} %get-tuple-element.96.probs, ...), custom_call_target="tpu_custom_call" | custom-call | flops 1610612736 | bytes 6291456 | tf_op jit(solution)/shard_map/mix_backward/pallas_call | solution.py:314
  135.1 5.1 %all-to-all-done.3.refs_0_ = bf16[8,4,2,2,16,512]{5,4,3,2,1,0:T(8,128)(2,1)S(1)} async-done(((bf16[8,4,2,2,16,512]{5,4,3,2,1,0:T(8,128)(2,1)}), bf16[8,4,2,2,16,512]{5,4,3,2,1,0:T(8,128)(2,1)S(1)}, u32[]{:S(2)}, u32[]{:S(2)}) %all-to-all-start.3) | async-done | bytes 2097184 | tf_op jit(solution)/shard_map/all_to_all | solution.py:945
  140.2 3.9 %all-to-all-start.2 = ((bf16[32,2,24,512]{3,2,1,0:T(8,128)(2,1)}), bf16[32,2,24,512]{3,2,1,0:T(8,128)(2,1)}, u32[]{:S(2)}, u32[]{:S(2)}) async-start(bf16[32,2,24,512]{3,2,1,0:T(8,128)(2,1)} %get-tuple-element.109), calls=%async_computation.2 | async-start | bytes 3145728 | tf_op jit(solution)/shard_map/all_to_all | solution.py:898
  144.7 10.6 %expert_weights.2 = (bf16[528,512]{1,0:T(8,128)(2,1)}, bf16[528,512]{1,0:T(8,128)(2,1)}, bf16[528,512]{1,0:T(8,128)(2,1)}, bf16[528,512]{1,0:T(8,128)(2,1)}) custom-call(s32[2]{0:T(128)} %pad_add_fusion.3.where, s32[1]{0:T(128)} %bitcast.28.expert, bf16[8,4,2,2,16,512]{5,4,3,2,1,0:T(8,128)(2,1)} %copy-done, bf16[8,512,2048]{2,1,0:T(8,128)(2,1)} %refs_1_.3, ...), custom_call_target="tpu_custom_call" | custom-call | flops 3221225472 | bytes 9437184 | tf_op jit(solution)/shard_map/expert_weights/pallas_call | solution.py:442
  155.4 1.5 collective-permute-start.12
  156.9 1.5 collective-permute-start.13
  158.4 10.7 %expert_weights.3 = (bf16[528,512]{1,0:T(8,128)(2,1)}, bf16[528,512]{1,0:T(8,128)(2,1)}, bf16[528,512]{1,0:T(8,128)(2,1)}, bf16[528,512]{1,0:T(8,128)(2,1)}) custom-call(s32[2]{0:T(128)} %pad_add_fusion.3.where, s32[1]{0:T(128)} %bitcast.29.expert, bf16[8,4,2,2,16,512]{5,4,3,2,1,0:T(8,128)(2,1)} %copy-done, bf16[8,512,2048]{2,1,0:T(8,128)(2,1)} %refs_1_.3, ...), custom_call_target="tpu_custom_call" | custom-call | flops 3221225472 | bytes 9437184 | tf_op jit(solution)/shard_map/expert_weights/pallas_call | solution.py:442
  171.5 10.4 %all-to-all-done.2.grads.mixed = bf16[32,2,24,512]{3,2,1,0:T(8,128)(2,1)} async-done(((bf16[32,2,24,512]{3,2,1,0:T(8,128)(2,1)}), bf16[32,2,24,512]{3,2,1,0:T(8,128)(2,1)}, u32[]{:S(2)}, u32[]{:S(2)}) %all-to-all-start.2) | async-done | bytes 1572896 | tf_op jit(solution)/shard_map/all_to_all | solution.py:898
  181.9 2.1 collective-permute-done.13.refs_2_
  184.0 12.4 %attention_back_far.1 = (f32[3,256,512]{2,1,0:T(8,128)}, f32[3,256,512]{2,1,0:T(8,128)}, bf16[3,256,512]{2,1,0:T(8,128)(2,1)}, f32[8,512]{1,0:T(8,128)}, bf16[21...) custom-call(s32[2]{0:T(128)} %pad_add_fusion.1.place, bf16[12,256,512]{2,1,0:T(8,128)(2,1)} %tokens.7, ...), custom_call_target="tpu_custom_call" | custom-call | bytes 10747904 | tf_op jit(solution)/shard_map/attention_back_far/pallas_call | solution.py:649
  196.6 2.2 collective-permute-done.16
  198.7 1.2 add_convert_fusion.1
  199.9 2.1 collective-permute-start.17
  203.0 11.4 %attention_back_near.1 = (bf16[3,256,512]{2,1,0:T(8,128)(2,1)}, bf16[2176,128]{1,0:T(8,128)(2,1)}, bf16[2176,128]{1,0:T(8,128)(2,1)}) custom-call(s32[2]{0:T(128)} %pad_add_fusion.1.place, bf16[12,256,512]{2,1,0:T(8,128)(2,1)} %tokens.7, f32[3,256,512]{2,1,0:T(8,128)} %get-tuple-element.121.d_hidden, f32[3,256,512]{2,1,0:T(8,128)} %get-tuple-element.129.partial, ...), custom_call_target="tpu_custom_call" | custom-call | bytes 8388608 | tf_op jit(solution)/shard_map/attention_back_near/pallas_call | solution.py:698
  215.1 2.0 collective-permute-done.18.refs_6_
  219.4 2.2 add_convert_fusion
  221.6 4.7 %all-to-all-start.4 = ((bf16[8,272,128]{2,1,0:T(8,128)(2,1)}), bf16[8,272,128]{2,1,0:T(8,128)(2,1)S(1)}, u32[]{:S(2)}, u32[]{:S(2)}) async-start(bf16[8,272,128]{2,1,0:T(8,128)(2,1)} %bitcast.36), calls=%async_computation.4 | async-start | bytes 1114112 | tf_op jit(solution)/shard_map/all_to_all | solution.py:770
  227.5 3.3 %place_blocks.3.refs_2_ = bf16[12,256,512]{2,1,0:T(8,128)(2,1)} custom-call(s32[2]{0:T(128)} %pad_add_fusion.5.where, bf16[3,256,512]{2,1,0:T(8,128)(2,1)} %get-tuple-element.146.refs_0_, bf16[3,256,512]{2,1,0:T(8,128)(2,1)} %collective-permute-done.21.refs_1_), custom_call_target="tpu_custom_call" | custom-call | bytes 3145728 | tf_op jit(solution)/shard_map/place_blocks/pallas_call | solution.py:809
  230.7 7.1 %owned_weights.2 = (f32[8,64,2048]{2,1,0:T(8,128)}, f32[8,256,512]{2,1,0:T(8,128)}, f32[8,16,512]{2,1,0:T(8,128)}) custom-call(s32[7]{0:T(128)} %bitcast.99, bf16[528,512]{1,0:T(8,128)(2,1)} %get-tuple-element.111.refs_0_, bf16[528,512]{1,0:T(8,128)(2,1)} %copy-done.13, bf16[528,512]{1,0:T(8,128)(2,1)} %copy-done.14, ...), custom_call_target="tpu_custom_call" | custom-call | bytes 11354112 | tf_op jit(solution)/shard_map/owned_weights/pallas_call | solution.py:489
  239.4 3.6 %all-to-all-done.4 = bf16[8,272,128]{2,1,0:T(8,128)(2,1)S(1)} async-done(((bf16[8,272,128]{2,1,0:T(8,128)(2,1)}), bf16[8,272,128]{2,1,0:T(8,128)(2,1)S(1)}, u32[]{:S(2)}, u32[]{:S(2)}) %all-to-all-start.4) | async-done | bytes 557088 | tf_op jit(solution)/shard_map/all_to_all | solution.py:770
  243.9 3.9 %all-to-all-start.5 = ((bf16[8,272,128]{2,1,0:T(8,128)(2,1)}), bf16[8,272,128]{2,1,0:T(8,128)(2,1)S(1)}, u32[]{:S(2)}, u32[]{:S(2)}) async-start(bf16[8,272,128]{2,1,0:T(8,128)(2,1)} %broadcast_in_dim.86), calls=%async_computation.5 | async-start | bytes 1114112 | tf_op jit(solution)/shard_map/all_to_all | solution.py:776
  248.4 4.7 %place_blocks.4 = bf16[12,256,512]{2,1,0:T(8,128)(2,1)} custom-call(s32[4]{0:T(128)} %copy-done.22, bf16[3,256,512]{2,1,0:T(8,128)(2,1)} %get-tuple-element.138.refs_0_, bf16[3,256,512]{2,1,0:T(8,128)(2,1)} %copy-done.8, bf16[3,256,512]{2,1,0:T(8,128)(2,1)} %copy-done.9, bf16[3,256,512]{2,1,0:T(8,128)(2,1)} %collective-permute-done.25.refs_3_), custom_call_target="tpu_custom_call" | custom-call | bytes 6291456 | tf_op jit(solution)/shard_map/place_blocks/pallas_call | solution.py:809
  253.1 2.7 owned_weights.3
  255.8 3.0 %collective-permute-done.23.refs_0_ = bf16[3,256,512]{2,1,0:T(8,128)(2,1)} collective-permute-done((bf16[3,256,512]{2,1,0:T(8,128)(2,1)S(1)}, bf16[3,256,512]{2,1,0:T(8,128)(2,1)}, u32[]{:S(2)}, u32[]{:S(2)}) %collective-permute-start.23) | collective-permute-done | bytes 786464 | tf_op jit(solution)/shard_map/ppermute | solution.py:736
  259.4 0.9 slice.80
  260.3 0.9 slice_bitcast_fusion
  263.4 3.3 %place_blocks.5 = bf16[12,256,512]{2,1,0:T(8,128)(2,1)} custom-call(s32[2]{0:T(128)} %pad_add_fusion.where, bf16[3,256,512]{2,1,0:T(8,128)(2,1)} %collective-permute-done.23.refs_0_, bf16[3,256,512]{2,1,0:T(8,128)(2,1)} %copy-done.12, bf16[12,256,512]{2,1,0:T(8,128)(2,1)} %place_blocks.3.refs_2_), custom_call_target="tpu_custom_call", output_to_operand_aliasing={{}: (3, {})} | custom-call | bytes 3145728 | tf_op jit(solution)/shard_map/place_blocks/pallas_call | solution.py:809
  (155 shorter events, 30.0 us)
Async XLA Ops:
  0.6 12.9 %copy-start.21 = (bf16[512,8]{0,1:T(8,128)(2,1)S(1)}, bf16[512,8]{0,1:T(8,128)(2,1)}, u32[]{:S(2)}) copy-start(bf16[512,8]{0,1:T(8,128)(2,1)} %param.25) | copy-start | bytes 24580
  0.7 13.6 %copy-start.23 = (s32[8]{0:T(128)S(1)}, s32[8]{0:T(128)}, u32[]{:S(2)}) copy-start(s32[8]{0:T(128)} %param.17) | copy-start | bytes 100
  2.8 35.2 %all-to-all-start.1 = ((bf16[8,12,8,512]{3,2,1,0:T(8,128)(2,1)}), bf16[8,12,8,512]{3,2,1,0:T(8,128)(2,1)S(1)}, u32[]{:S(2)}, u32[]{:S(2)}) async-start(bf16[8,12,8,512]{3,2,1,0:T(8,128)(2,1)} %copy_bitcast_fusion), calls=%async_computation.1 | async-start | bytes 1572864 | tf_op jit(solution)/shard_map/all_to_all | solution.py:903
  12.0 4.3 %collective-permute-start = (bf16[512,512]{1,0:T(8,128)(2,1)}, bf16[512,512]{1,0:T(8,128)(2,1)S(1)}, u32[]{:S(2)}, u32[]{:S(2)}) collective-permute-start(bf16[512,512]{1,0:T(8,128)(2,1)} %pack_weights.1.refs_0_), channel_id=1, source_target_pairs={{0,1},{1,0},{2,3},{3,2},{4,5},{5,4},{6,7},{7,6},{8,9},{9,8},{10,11... | collective-permute-start | bytes 1572872 | tf_op jit(solution)/shard_map/ppermute | solution.py:731
  12.0 14.6 %collective-permute-start.1 = (bf16[512,512]{1,0:T(8,128)(2,1)}, bf16[512,512]{1,0:T(8,128)(2,1)S(1)}, u32[]{:S(2)}, u32[]{:S(2)}) collective-permute-start(bf16[512,512]{1,0:T(8,128)(2,1)} %pack_weights.1.refs_0_), channel_id=1, source_target_pairs={{2,0},{3,1},{0,2},{1,3},{6,4},{7,5},{4,6},{5,7},{10,8},{11,9},{8,1... | collective-permute-start | bytes 1572872 | tf_op jit(solution)/shard_map/ppermute | solution.py:736
  13.5 33.4 %collective-permute-start.3 = (bf16[8,512]{1,0:T(8,128)(2,1)S(1)}, bf16[8,512]{1,0:T(8,128)(2,1)S(1)}, u32[]{:S(2)}, u32[]{:S(2)}) collective-permute-start(bf16[8,512]{1,0:T(8,128)(2,1)S(1)} %bitcast.93), channel_id=1, source_target_pairs={{0,1},{1,0},{2,3},{3,2},{4,5},{5,4},{6,7},{7,6},{8,9},{9,8},{10,11... | collective-permute-start | bytes 24584 | tf_op jit(solution)/shard_map/ppermute | solution.py:731
  13.8 30.6 %collective-permute-start.4 = (bf16[8,512]{1,0:T(8,128)(2,1)S(1)}, bf16[8,512]{1,0:T(8,128)(2,1)S(1)}, u32[]{:S(2)}, u32[]{:S(2)}) collective-permute-start(bf16[8,512]{1,0:T(8,128)(2,1)S(1)} %bitcast.94), channel_id=1, source_target_pairs={{2,0},{3,1},{0,2},{1,3},{6,4},{7,5},{4,6},{5,7},{10,8},{11,9},{8,1... | collective-permute-start | bytes 24584 | tf_op jit(solution)/shard_map/ppermute | solution.py:736
  26.7 1.9 collective-permute-start.2
  26.9 11.1 %copy-start.22 = (s32[4]{0:T(128)}, s32[4]{0:T(128)S(1)}, u32[]{:S(2)}) copy-start(s32[4]{0:T(128)S(1)} %pad_add_fusion.2.relative.where) | copy-start | bytes 52
  29.4 14.7 %copy-start.24 = (s32[64]{0:T(128)S(1)}, s32[64]{0:T(128)}, u32[]{:S(2)}) copy-start(s32[64]{0:T(128)} %param.18) | copy-start | bytes 772
  38.1 26.7 %copy-start.10 = (bf16[8,12,8,512]{3,2,1,0:T(8,128)(2,1)}, bf16[8,12,8,512]{3,2,1,0:T(8,128)(2,1)S(1)}, u32[]{:S(2)}) copy-start(bf16[8,12,8,512]{3,2,1,0:T(8,128)(2,1)S(1)} %all-to-all-done.1) | copy-start | bytes 2359300
  38.1 26.6 %all-to-all-start = ((bf16[32,3,8,512]{3,2,1,0:T(8,128)(2,1)}), bf16[32,3,8,512]{3,2,1,0:T(8,128)(2,1)S(1)}, u32[]{:S(2)}, u32[]{:S(2)}) async-start(bf16[32,3,8,512]{3,2,1,0:T(8,128)(2,1)} %get-tuple-element.93), calls=%async_computation | async-start | bytes 1572864 | tf_op jit(solution)/shard_map/all_to_all | solution.py:891
  44.4 2.5 collective-permute-start.5
  71.0 1.9 collective-permute-start.6
  71.0 9.3 %collective-permute-start.7 = (bf16[8,2,16,512]{3,2,1,0:T(8,128)(2,1)}, bf16[8,2,16,512]{3,2,1,0:T(8,128)(2,1)S(1)}, u32[]{:S(2)}, u32[]{:S(2)}) collective-permute-start(bf16[8,2,16,512]{3,2,1,0:T(8,128)(2,1)} %get-tuple-element.99), channel_id=1, source_target_pairs={{0,2},{1,3},{2,0},{3,1},{4,6},{5,7},{6,4},{7,5},{8,10},{9,11},{10,... | collective-permute-start | bytes 786440 | tf_op jit(solution)/shard_map/ppermute | solution.py:783
  72.6 12.5 %collective-permute-start.8 = (bf16[8,2,16,512]{3,2,1,0:T(8,128)(2,1)}, bf16[8,2,16,512]{3,2,1,0:T(8,128)(2,1)S(1)}, u32[]{:S(2)}, u32[]{:S(2)}) collective-permute-start(bf16[8,2,16,512]{3,2,1,0:T(8,128)(2,1)} %get-tuple-element.100), channel_id=1, source_target_pairs={{0,3},{1,2},{2,1},{3,0},{4,7},{5,6},{6,5},{7,4},{8,11},{9,10},{10,... | collective-permute-start | bytes 786440 | tf_op jit(solution)/shard_map/ppermute | solution.py:783
  72.8 14.8 %copy-start.3 = (bf16[8,2,16,512]{3,2,1,0:T(8,128)(2,1)}, bf16[8,2,16,512]{3,2,1,0:T(8,128)(2,1)S(1)}, u32[]{:S(2)}) copy-start(bf16[8,2,16,512]{3,2,1,0:T(8,128)(2,1)S(1)} %collective-permute-done.6.refs_1_) | copy-start | bytes 786436
  87.6 52.6 %all-to-all-start.3 = ((bf16[8,4,2,2,16,512]{5,4,3,2,1,0:T(8,128)(2,1)}), bf16[8,4,2,2,16,512]{5,4,3,2,1,0:T(8,128)(2,1)S(1)}, u32[]{:S(2)}, u32[]{:S(2)}) async-start(bf16[8,4,2,2,16,512]{5,4,3,2,1,0:T(8,128)(2,1)} %maximum_maximum_fusion), calls=%async_computation.3 | async-start | bytes 4194304 | tf_op jit(solution)/shard_map/all_to_all | solution.py:945
  113.5 1.9 collective-permute-start.9
  113.8 9.3 %collective-permute-start.10 = (bf16[8,2,16,512]{3,2,1,0:T(8,128)(2,1)}, bf16[8,2,16,512]{3,2,1,0:T(8,128)(2,1)S(1)}, u32[]{:S(2)}, u32[]{:S(2)}) collective-permute-start(bf16[8,2,16,512]{3,2,1,0:T(8,128)(2,1)} %get-tuple-element.107), channel_id=1, source_target_pairs={{2,0},{3,1},{0,2},{1,3},{6,4},{7,5},{4,6},{5,7},{10,8},{11,9},{8,1... | collective-permute-start | bytes 786440 | tf_op jit(solution)/shard_map/ppermute | solution.py:789
  115.3 12.2 %collective-permute-start.11 = (bf16[8,2,16,512]{3,2,1,0:T(8,128)(2,1)}, bf16[8,2,16,512]{3,2,1,0:T(8,128)(2,1)S(1)}, u32[]{:S(2)}, u32[]{:S(2)}) collective-permute-start(bf16[8,2,16,512]{3,2,1,0:T(8,128)(2,1)} %get-tuple-element.108), channel_id=1, source_target_pairs={{3,0},{2,1},{1,2},{0,3},{7,4},{6,5},{5,6},{4,7},{11,8},{10,9},{9,1... | collective-permute-start | bytes 786440 | tf_op jit(solution)/shard_map/ppermute | solution.py:789
  115.4 12.1 %copy-start.26 = (bf16[8,2,16,512]{3,2,1,0:T(8,128)(2,1)}, bf16[8,2,16,512]{3,2,1,0:T(8,128)(2,1)S(1)}, u32[]{:S(2)}) copy-start(bf16[8,2,16,512]{3,2,1,0:T(8,128)(2,1)S(1)} %collective-permute-done.9.refs_1_) | copy-start | bytes 786436
  140.2 41.7 %all-to-all-start.2 = ((bf16[32,2,24,512]{3,2,1,0:T(8,128)(2,1)}), bf16[32,2,24,512]{3,2,1,0:T(8,128)(2,1)}, u32[]{:S(2)}, u32[]{:S(2)}) async-start(bf16[32,2,24,512]{3,2,1,0:T(8,128)(2,1)} %get-tuple-element.109), calls=%async_computation.2 | async-start | bytes 3145728 | tf_op jit(solution)/shard_map/all_to_all | solution.py:898
  155.4 26.5 %collective-permute-start.12 = (bf16[528,512]{1,0:T(8,128)(2,1)}, bf16[528,512]{1,0:T(8,128)(2,1)S(1)}, u32[]{:S(2)}, u32[]{:S(2)}) collective-permute-start(bf16[528,512]{1,0:T(8,128)(2,1)} %get-tuple-element.112), channel_id=1, source_target_pairs={{0,4},{4,0},{8,12},{12,8},{16,20},{20,16},{24,28},{28,24},{1,5},{5... | collective-permute-start | bytes 1622024 | tf_op jit(solution)/shard_map/ppermute | solution.py:794
  156.9 27.1 %collective-permute-start.13 = (bf16[528,512]{1,0:T(8,128)(2,1)}, bf16[528,512]{1,0:T(8,128)(2,1)S(1)}, u32[]{:S(2)}, u32[]{:S(2)}) collective-permute-start(bf16[528,512]{1,0:T(8,128)(2,1)} %get-tuple-element.113), channel_id=1, source_target_pairs={{0,8},{4,12},{8,0},{12,4},{16,24},{20,28},{24,16},{28,20},{1,9},{5... | collective-permute-start | bytes 1622024 | tf_op jit(solution)/shard_map/ppermute | solution.py:794
  158.4 11.8 %copy-start.18 = (f32[32,512]{1,0:T(8,128)S(1)}, f32[32,512]{1,0:T(8,128)}, u32[]{:S(2)}) copy-start(f32[32,512]{1,0:T(8,128)} %get-tuple-element.119) | copy-start | bytes 196612
  169.1 27.4 %collective-permute-start.14 = (bf16[528,512]{1,0:T(8,128)(2,1)}, bf16[528,512]{1,0:T(8,128)(2,1)S(1)}, u32[]{:S(2)}, u32[]{:S(2)}) collective-permute-start(bf16[528,512]{1,0:T(8,128)(2,1)} %get-tuple-element.125), channel_id=1, source_target_pairs={{0,4},{4,0},{8,12},{12,8},{16,20},{20,16},{24,28},{28,24},{1,5},{5... | collective-permute-start | bytes 1622024 | tf_op jit(solution)/shard_map/ppermute | solution.py:794
  169.6 26.8 %collective-permute-start.15 = (bf16[528,512]{1,0:T(8,128)(2,1)}, bf16[528,512]{1,0:T(8,128)(2,1)S(1)}, u32[]{:S(2)}, u32[]{:S(2)}) collective-permute-start(bf16[528,512]{1,0:T(8,128)(2,1)} %get-tuple-element.126), channel_id=1, source_target_pairs={{0,8},{4,12},{8,0},{12,4},{16,24},{20,28},{24,16},{28,20},{1,9},{5... | collective-permute-start | bytes 1622024 | tf_op jit(solution)/shard_map/ppermute | solution.py:794
  181.9 14.5 %copy-start.13 = (bf16[528,512]{1,0:T(8,128)(2,1)}, bf16[528,512]{1,0:T(8,128)(2,1)S(1)}, u32[]{:S(2)}) copy-start(bf16[528,512]{1,0:T(8,128)(2,1)S(1)} %collective-permute-done.12.refs_1_) | copy-start | bytes 1622020
  184.0 12.4 %copy-start.14 = (bf16[528,512]{1,0:T(8,128)(2,1)}, bf16[528,512]{1,0:T(8,128)(2,1)S(1)}, u32[]{:S(2)}) copy-start(bf16[528,512]{1,0:T(8,128)(2,1)S(1)} %collective-permute-done.13.refs_2_) | copy-start | bytes 1622020
  184.0 18.0 %copy-start.25 = (bf16[528,512]{1,0:T(8,128)(2,1)S(1)}, bf16[528,512]{1,0:T(8,128)(2,1)}, u32[]{:S(2)}) copy-start(bf16[528,512]{1,0:T(8,128)(2,1)} %get-tuple-element.137) | copy-start | bytes 1622020
  196.5 2.2 collective-permute-start.16
  199.9 15.1 %collective-permute-start.17 = (bf16[2176,128]{1,0:T(8,128)(2,1)S(1)}, bf16[2176,128]{1,0:T(8,128)(2,1)S(1)}, u32[]{:S(2)}, u32[]{:S(2)}) collective-permute-start(bf16[2176,128]{1,0:T(8,128)(2,1)S(1)} %add_convert_fusion.1), channel_id=1, source_target_pairs={{0,2},{1,3},{2,0},{3,1},{4,6},{5,7},{6,4},{7,5},{8,10},{9,11},{10,... | collective-permute-start | bytes 1671176 | tf_op jit(solution)/shard_map/ppermute | solution.py:741
  202.1 15.0 %collective-permute-start.18 = (bf16[528,512]{1,0:T(8,128)(2,1)S(1)}, bf16[528,512]{1,0:T(8,128)(2,1)}, u32[]{:S(2)}, u32[]{:S(2)}) collective-permute-start(bf16[528,512]{1,0:T(8,128)(2,1)S(1)} %copy-done.25), channel_id=1, source_target_pairs={{0,12},{4,8},{8,4},{12,0},{16,28},{20,24},{24,20},{28,16},{1,13},{... | collective-permute-start | bytes 1622024 | tf_op jit(solution)/shard_map/ppermute | solution.py:794
  203.0 15.3 %copy-start.6 = (bf16[3,256,512]{2,1,0:T(8,128)(2,1)S(1)}, bf16[3,256,512]{2,1,0:T(8,128)(2,1)}, u32[]{:S(2)}) copy-start(bf16[3,256,512]{2,1,0:T(8,128)(2,1)} %get-tuple-element.146.refs_0_) | copy-start | bytes 2359300
  217.1 2.3 collective-permute-start.24
  217.4 20.4 %collective-permute-start.22 = (bf16[528,512]{1,0:T(8,128)(2,1)}, bf16[528,512]{1,0:T(8,128)(2,1)}, u32[]{:S(2)}, u32[]{:S(2)}) collective-permute-start(bf16[528,512]{1,0:T(8,128)(2,1)} %get-tuple-element.145), channel_id=1, source_target_pairs={{0,12},{4,8},{8,4},{12,0},{16,28},{20,24},{24,20},{28,16},{1,13},{... | collective-permute-start | bytes 1622024 | tf_op jit(solution)/shard_map/ppermute | solution.py:794
  218.3 9.2 %collective-permute-start.21 = (bf16[3,256,512]{2,1,0:T(8,128)(2,1)S(1)}, bf16[3,256,512]{2,1,0:T(8,128)(2,1)}, u32[]{:S(2)}, u32[]{:S(2)}) collective-permute-start(bf16[3,256,512]{2,1,0:T(8,128)(2,1)S(1)} %copy-done.6), channel_id=1, source_target_pairs={{0,1},{1,0},{2,3},{3,2},{4,5},{5,4},{6,7},{7,6},{8,9},{9,8},{10,11... | collective-permute-start | bytes 2359304 | tf_op jit(solution)/shard_map/ppermute | solution.py:731
  218.5 19.3 %collective-permute-start.20 = (bf16[3,256,512]{2,1,0:T(8,128)(2,1)}, bf16[3,256,512]{2,1,0:T(8,128)(2,1)S(1)}, u32[]{:S(2)}, u32[]{:S(2)}) collective-permute-start(bf16[3,256,512]{2,1,0:T(8,128)(2,1)} %get-tuple-element.138.refs_0_), channel_id=1, source_target_pairs={{0,1},{1,0},{2,3},{3,2},{4,5},{5,4},{6,7},{7,6},{8,9},{9,8},{10,11... | collective-permute-start | bytes 2359304 | tf_op jit(solution)/shard_map/ppermute | solution.py:731
  218.8 19.9 %collective-permute-start.19 = (bf16[3,256,512]{2,1,0:T(8,128)(2,1)}, bf16[3,256,512]{2,1,0:T(8,128)(2,1)S(1)}, u32[]{:S(2)}, u32[]{:S(2)}) collective-permute-start(bf16[3,256,512]{2,1,0:T(8,128)(2,1)} %get-tuple-element.138.refs_0_), channel_id=1, source_target_pairs={{2,0},{3,1},{0,2},{1,3},{6,4},{7,5},{4,6},{5,7},{10,8},{11,9},{8,1... | collective-permute-start | bytes 2359304 | tf_op jit(solution)/shard_map/ppermute | solution.py:736
  221.6 21.3 %all-to-all-start.4 = ((bf16[8,272,128]{2,1,0:T(8,128)(2,1)}), bf16[8,272,128]{2,1,0:T(8,128)(2,1)S(1)}, u32[]{:S(2)}, u32[]{:S(2)}) async-start(bf16[8,272,128]{2,1,0:T(8,128)(2,1)} %bitcast.36), calls=%async_computation.4 | async-start | bytes 1114112 | tf_op jit(solution)/shard_map/all_to_all | solution.py:770
  237.8 10.6 %copy-start.8 = (bf16[3,256,512]{2,1,0:T(8,128)(2,1)}, bf16[3,256,512]{2,1,0:T(8,128)(2,1)S(1)}, u32[]{:S(2)}) copy-start(bf16[3,256,512]{2,1,0:T(8,128)(2,1)S(1)} %collective-permute-done.20.refs_1_) | copy-start | bytes 2359300
  238.7 9.7 %copy-start.9 = (bf16[3,256,512]{2,1,0:T(8,128)(2,1)}, bf16[3,256,512]{2,1,0:T(8,128)(2,1)S(1)}, u32[]{:S(2)}) copy-start(bf16[3,256,512]{2,1,0:T(8,128)(2,1)S(1)} %collective-permute-done.19.refs_2_) | copy-start | bytes 2359300
  238.7 4.4 %collective-permute-start.25 = (bf16[3,256,512]{2,1,0:T(8,128)(2,1)S(1)}, bf16[3,256,512]{2,1,0:T(8,128)(2,1)}, u32[]{:S(2)}, u32[]{:S(2)}) collective-permute-start(bf16[3,256,512]{2,1,0:T(8,128)(2,1)S(1)} %collective-permute-done.19.refs_2_), channel_id=1, source_target_pairs={{0,1},{1,0},{2,3},{3,2},{4,5},{5,4},{6,7},{7,6},{8,9},{9,8},{10,11... | collective-permute-start | bytes 2359304 | tf_op jit(solution)/shard_map/ppermute | solution.py:731
  238.7 20.1 %collective-permute-start.23 = (bf16[3,256,512]{2,1,0:T(8,128)(2,1)S(1)}, bf16[3,256,512]{2,1,0:T(8,128)(2,1)}, u32[]{:S(2)}, u32[]{:S(2)}) collective-permute-start(bf16[3,256,512]{2,1,0:T(8,128)(2,1)S(1)} %copy-done.7), channel_id=1, source_target_pairs={{2,0},{3,1},{0,2},{1,3},{6,4},{7,5},{4,6},{5,7},{10,8},{11,9},{8,1... | collective-permute-start | bytes 2359304 | tf_op jit(solution)/shard_map/ppermute | solution.py:736
  243.9 22.7 %all-to-all-start.5 = ((bf16[8,272,128]{2,1,0:T(8,128)(2,1)}), bf16[8,272,128]{2,1,0:T(8,128)(2,1)S(1)}, u32[]{:S(2)}, u32[]{:S(2)}) async-start(bf16[8,272,128]{2,1,0:T(8,128)(2,1)} %broadcast_in_dim.86), calls=%async_computation.5 | async-start | bytes 1114112 | tf_op jit(solution)/shard_map/all_to_all | solution.py:776
  258.8 3.7 %collective-permute-start.26 = (bf16[3,256,512]{2,1,0:T(8,128)(2,1)}, bf16[3,256,512]{2,1,0:T(8,128)(2,1)S(1)}, u32[]{:S(2)}, u32[]{:S(2)}) collective-permute-start(bf16[3,256,512]{2,1,0:T(8,128)(2,1)} %collective-permute-done.23.refs_0_), channel_id=1, source_target_pairs={{0,1},{1,0},{2,3},{3,2},{4,5},{5,4},{6,7},{7,6},{8,9},{9,8},{10,11... | collective-permute-start | bytes 2359304 | tf_op jit(solution)/shard_map/ppermute | solution.py:731
  266.6 3.6 %collective-permute-start.27 = (bf16[16,128]{1,0:T(8,128)(2,1)S(1)}, bf16[16,128]{1,0:T(8,128)(2,1)S(1)}, u32[]{:S(2)}, u32[]{:S(2)}) collective-permute-start(bf16[16,128]{1,0:T(8,128)(2,1)S(1)} %slice.91), channel_id=1, source_target_pairs={{0,2},{1,3},{2,0},{3,1},{4,6},{5,7},{6,4},{7,5},{8,10},{9,11},{10,... | collective-permute-start | bytes 12296 | tf_op jit(solution)/shard_map/ppermute | solution.py:741
  (15 other events, 54.0 us)
